TPU v7x, 32 devices: a whole 2x2x4 slice. The times are simulated.
32 devices in a mesh: slab: 4 (over y, x), brick: 8 (over z, core).
Axes of the slice: x: 2, y: 2, z: 4, core: 2. Of those that a mesh axis runs over, the one named last changes fastest.
Arguments:
- embed: bfloat16 [32768, 512], P(('slab', 'brick')), may hold values from -6 to 6
- cotangent: bfloat16 [32768, 512], P(('slab', 'brick')), may hold values from -6 to 6
- basis: bfloat16 [16, 16, 32768], P(None, None, ('slab', 'brick')), may hold values from -4 to 4
- triplet_row_index: int32 [16, 32768], P(None, ('slab', 'brick')), may hold values from 0 to 1535
- triplet_slot_count: int32 [32768], P(('slab', 'brick')), may hold values from 1 to 16, as said below
- outgoing_edge_rows: int32 [4, 4096], P(None, ('slab', 'brick')), may hold values from 0 to 1023
- residual_weight: bfloat16 [512, 512], replicated, may hold values from -0.25 to 0.25
- down_weight: bfloat16 [512, 64], replicated, may hold values from -0.25 to 0.25
- up_weight: bfloat16 [64, 512], replicated, may hold values from -0.75 to 0.75
- basis_weight: bfloat16 [16, 64], replicated, may hold values from -1.5 to 1.5
Outputs:
- edge_embedding_gradient: bfloat16 [32768, 512], P(('slab', 'brick'))
- residual_weight_gradient: float32 [512, 512], replicated
- down_weight_gradient: float32 [512, 64], replicated
- up_weight_gradient: float32 [64, 512], replicated
- basis_weight_gradient: float32 [16, 64], replicated
Inputs may be any that keep to these rules, and one draw needn't show every extreme that they name: `triplet_row_index`: indices refer to the extended table of the edge's own brick. `triplet_slot_count`: slots at or past the count are empty; in every brick some edge fills all 16 slots; bricks differ in density. `outgoing_edge_rows`: local row numbers within the sending brick; a row may appear more than once.
All inputs are finite; a program needn't handle non-finite values.
Results may differ from a plain program's by a relative error of at most 0.006.
Values may be sent and summed in bfloat16 or wider, within the bound.
No kernel may reach another device: no remote copies, remote signals or barrier semaphores. Data moves between devices by JAX's collectives and lax.ppermute only.
A program may use at most 64 MiB of HBM per device.

v0:
```python
import jax
import jax.numpy as jnp
from jax import lax
from jax.sharding import PartitionSpec as P


def passed_along(value, axis, steps):
    count = lax.axis_size(axis)
    pairs = [(source, (source + steps) % count) for source in range(count)]
    return lax.ppermute(value, axis, pairs)


def silu_grad(value):
    sig = jax.nn.sigmoid(value)
    return sig * (1.0 + value * (1.0 - sig))


def selector(index_row, count_rows, dtype):
    positions = lax.broadcasted_iota(jnp.int32, (count_rows, index_row.shape[0]), 0)
    return (positions == index_row[None, :]).astype(dtype)


def shards(
    embed,
    cotangent,
    basis,
    triplet_row_index,
    triplet_slot_count,
    outgoing_edge_rows,
    residual_weight,
    down_weight,
    up_weight,
    basis_weight,
):
    rows = embed.shape[0]
    ghost = outgoing_edge_rows.shape[1]
    trips = triplet_row_index.shape[0]
    res_pre = jnp.dot(embed, residual_weight, preferred_element_type=jnp.float32)
    dres = (cotangent.astype(jnp.float32) * silu_grad(res_pre)).astype(jnp.bfloat16)
    residual_weight_gradient = lax.dot_general(
        embed, dres, (((0,), (0,)), ((), ())), preferred_element_type=jnp.float32
    )
    res_term = lax.dot_general(
        dres, residual_weight, (((1,), (1,)), ((), ())), preferred_element_type=jnp.float32
    )
    pre = lax.dot_general(
        down_weight, embed, (((0,), (1,)), ((), ())), preferred_element_type=jnp.float32
    )
    proj = jax.nn.silu(pre).astype(jnp.bfloat16)
    picks = [selector(outgoing_edge_rows[step], rows, jnp.bfloat16) for step in range(4)]
    received = []
    for step, by in enumerate((1, -1)):
        chosen = jnp.dot(proj, picks[step], preferred_element_type=jnp.float32).astype(jnp.bfloat16)
        received.append(passed_along(chosen, "slab", by))
    for step, by in enumerate((1, -1)):
        chosen = jnp.dot(proj, picks[step + 2], preferred_element_type=jnp.float32).astype(
            jnp.bfloat16
        )
        received.append(passed_along(chosen, "brick", by))
    ghost_proj = jnp.concatenate(received, axis=1)
    edge_table_rows = jnp.concatenate([proj, ghost_proj], axis=1)
    table_rows = edge_table_rows.shape[1]
    weight_list = jnp.einsum("unz,nh->uhz", basis, basis_weight, preferred_element_type=jnp.float32)
    live = (lax.broadcasted_iota(jnp.int32, (trips, rows), 0) < triplet_slot_count[None, :]).astype(
        jnp.float32
    )

    def gather_slot(carry, index_row):
        onehot = selector(index_row, table_rows, jnp.bfloat16)
        picked = jnp.dot(edge_table_rows, onehot, preferred_element_type=jnp.float32).astype(
            jnp.bfloat16
        )
        return (carry, picked)

    _, gathered = lax.scan(gather_slot, jnp.zeros((), jnp.float32), triplet_row_index)
    gathered = gathered.astype(jnp.float32)
    tsum = jnp.sum(weight_list * gathered * live[:, None, :], axis=0)
    activation_value = jax.nn.silu(tsum).astype(jnp.bfloat16)
    dsum = lax.dot_general(
        up_weight, cotangent, (((1,), (1,)), ((), ())), preferred_element_type=jnp.float32
    )
    dt = dsum * silu_grad(tsum)
    up_weight_gradient = lax.dot_general(
        activation_value, cotangent, (((1,), (0,)), ((), ())), preferred_element_type=jnp.float32
    )
    weight_gradient_list = (dt[None, :, :] * gathered * live[:, None, :]).astype(jnp.bfloat16)
    basis_weight_gradient = jnp.einsum(
        "yqi,ywi->qw", basis, weight_gradient_list, preferred_element_type=jnp.float32
    )
    dhx = dt[None, :, :] * weight_list * live[:, None, :]

    def scatter_slot(total, inputs):
        index_row, slot_terms = inputs
        onehot = selector(index_row, table_rows, jnp.float32)
        added = lax.dot_general(
            slot_terms,
            onehot,
            (((1,), (1,)), ((), ())),
            precision=lax.Precision.HIGHEST,
            preferred_element_type=jnp.float32,
        )
        return (total + added, None)

    table_gradient, _ = lax.scan(
        scatter_slot,
        jnp.zeros((edge_table_rows.shape[0], table_rows), jnp.float32),
        (triplet_row_index, dhx),
    )
    dproj = table_gradient[:, :rows]
    for step, by in enumerate((1, -1)):
        block = table_gradient[:, rows + step * ghost : rows + (step + 1) * ghost]
        back = passed_along(block, "slab", -by)
        dproj = dproj + lax.dot_general(
            back,
            picks[step].astype(jnp.float32),
            (((1,), (1,)), ((), ())),
            precision=lax.Precision.HIGHEST,
            preferred_element_type=jnp.float32,
        )
    for step, by in enumerate((1, -1)):
        block = table_gradient[:, rows + (step + 2) * ghost : rows + (step + 3) * ghost]
        back = passed_along(block, "brick", -by)
        dproj = dproj + lax.dot_general(
            back,
            picks[step + 2].astype(jnp.float32),
            (((1,), (1,)), ((), ())),
            precision=lax.Precision.HIGHEST,
            preferred_element_type=jnp.float32,
        )
    dpre = (dproj * silu_grad(pre)).astype(jnp.bfloat16)
    down_weight_gradient = lax.dot_general(
        embed, dpre, (((0,), (1,)), ((), ())), preferred_element_type=jnp.float32
    )
    down_term = lax.dot_general(
        dpre, down_weight, (((0,), (1,)), ((), ())), preferred_element_type=jnp.float32
    )
    edge_embedding_gradient = (res_term + down_term).astype(jnp.bfloat16)
    reduced_total = lax.psum(
        (residual_weight_gradient, down_weight_gradient, up_weight_gradient, basis_weight_gradient),
        ("slab", "brick"),
    )
    return (
        edge_embedding_gradient,
        reduced_total[0],
        reduced_total[1],
        reduced_total[2],
        reduced_total[3],
    )


def solution(mesh):
    in_specs = (
        P(("slab", "brick"), None),
        P(("slab", "brick"), None),
        P(None, None, ("slab", "brick")),
        P(None, ("slab", "brick")),
        P(("slab", "brick")),
        P(None, ("slab", "brick")),
        P(),
        P(),
        P(),
        P(),
    )
    out_specs = (P(("slab", "brick"), None), P(), P(), P(), P())
    return jax.shard_map(shards, mesh=mesh, in_specs=in_specs, out_specs=out_specs, check_vma=False)
```

profile of v0, /device:TPU:0, one launch (start us, length us, event | category | flops | bytes accessed | tf_op | source)
XLA Modules:
  0.0 308.2 jit_solution(8073968531589642934)
XLA Ops:
  8.5 2.0 constant_dynamic-update-slice_fusion.4
  11.3 2.9 collective-permute-start
  16.0 3.6 %collective-permute-start.3 = (bf16[64,128]{1,0:T(8,128)(2,1)S(1)}, bf16[64,128]{1,0:T(8,128)(2,1)S(1)}, u32[]{:S(2)}, u32[]{:S(2)}) collective-permute-start(bf16[64,128]{1,0:T(8,128)(2,1)S(1)} %convolution_convert_fusion), channel_id=1, source_target_pairs={{0,7},{1,0},{2,1},{3,2},{4,3},{5,4},{6,5},{7,6},{8,15},{9,8},{10,9... | collective-permute-start | bytes 49160 | tf_op jit(solution)/shard_map/ppermute | solution.py:10
  20.9 1.7 convolution_bitcast_fusion
  22.8 30.5 %while.21 = (s32[]{:T(128)}, bf16[16,64,1024]{2,1,0:T(8,128)(2,1)S(1)}, s32[16,1024]{1,0:T(8,128)}, bf16[64,1536]{1,0:T(8,128)(2,1)S(1)}, s32[]{:T(128)}) while((s32[]{:T(128)}, bf16[16,64,1024]{2,1,0:T(8,128)(2,1)S(1)}, s32[16,1024]{1,0:T(8,128)}, bf16[64,1536]{1,0:T(8,128)(2,1)S(1)}, s32[]{:T(128)}) %tuple.49), condition=%wide.region_1.2_spmd, body=%wide.region_0.1_spmd.sunk | while | flops 202964992 | bytes 340037 | solution.py:75
  53.3 2.3 fusion.12
  56.1 2.9 fusion.15
  59.1 93.6 %while.22 = (s32[]{:T(128)}, f32[64,1536]{1,0:T(8,128)}, f32[16,64,1024]{2,1,0:T(8,128)}, s32[16,1024]{1,0:T(8,128)}, s32[]{:T(128)}, /*index=5*/s32[]{:T(128)}) while((s32[]{:T(128)}, f32[64,1536]{1,0:T(8,128)}, f32[16,64,1024]{2,1,0:T(8,128)}, s32[16,1024]{1,0:T(8,128)}, s32[]{:T(128)}, /*index=5*/s32[]{:T(128)}) %tuple.59), condition=%wide.region_4.5_spmd.clone, body=%wide.region_3.4_spmd.clone.sunk | while | flops 1209729024 | bytes 1061459 | solution.py:104
  59.8 5.0 %fusion.80 = f32[64,1536]{1,0:T(8,128)} fusion(s32[1024]{0:T(1024)S(1)} %bitcast.73, f32[64,1536]{1,0:T(8,128)} %get-tuple-element.175, f32[16,64,1024]{2,1,0:T(8,128)} %get-tuple-element.182, s32[]{:T(128)} %get-tuple-element.174, pred[]{:T(512)S(6)} %compare.3), kind=kOutput, calls=%fused_computation.10.clone.1 | convolution fusion | flops 1209729024 | bytes 1053185 | tf_op jit(solution)/shard_map/while/body/eval_jaxpr/dot_general | solution.py:95
  65.6 5.1 %fusion.80 = f32[64,1536]{1,0:T(8,128)} fusion(s32[1024]{0:T(1024)S(1)} %bitcast.73, f32[64,1536]{1,0:T(8,128)} %get-tuple-element.175, f32[16,64,1024]{2,1,0:T(8,128)} %get-tuple-element.182, s32[]{:T(128)} %get-tuple-element.174, pred[]{:T(512)S(6)} %compare.3), kind=kOutput, calls=%fused_computation.10.clone.1 | convolution fusion | flops 1209729024 | bytes 1053185 | tf_op jit(solution)/shard_map/while/body/eval_jaxpr/dot_general | solution.py:95
  71.4 5.1 %fusion.80 = f32[64,1536]{1,0:T(8,128)} fusion(s32[1024]{0:T(1024)S(1)} %bitcast.73, f32[64,1536]{1,0:T(8,128)} %get-tuple-element.175, f32[16,64,1024]{2,1,0:T(8,128)} %get-tuple-element.182, s32[]{:T(128)} %get-tuple-element.174, pred[]{:T(512)S(6)} %compare.3), kind=kOutput, calls=%fused_computation.10.clone.1 | convolution fusion | flops 1209729024 | bytes 1053185 | tf_op jit(solution)/shard_map/while/body/eval_jaxpr/dot_general | solution.py:95
  77.3 5.1 %fusion.80 = f32[64,1536]{1,0:T(8,128)} fusion(s32[1024]{0:T(1024)S(1)} %bitcast.73, f32[64,1536]{1,0:T(8,128)} %get-tuple-element.175, f32[16,64,1024]{2,1,0:T(8,128)} %get-tuple-element.182, s32[]{:T(128)} %get-tuple-element.174, pred[]{:T(512)S(6)} %compare.3), kind=kOutput, calls=%fused_computation.10.clone.1 | convolution fusion | flops 1209729024 | bytes 1053185 | tf_op jit(solution)/shard_map/while/body/eval_jaxpr/dot_general | solution.py:95
  83.1 5.1 %fusion.80 = f32[64,1536]{1,0:T(8,128)} fusion(s32[1024]{0:T(1024)S(1)} %bitcast.73, f32[64,1536]{1,0:T(8,128)} %get-tuple-element.175, f32[16,64,1024]{2,1,0:T(8,128)} %get-tuple-element.182, s32[]{:T(128)} %get-tuple-element.174, pred[]{:T(512)S(6)} %compare.3), kind=kOutput, calls=%fused_computation.10.clone.1 | convolution fusion | flops 1209729024 | bytes 1053185 | tf_op jit(solution)/shard_map/while/body/eval_jaxpr/dot_general | solution.py:95
  89.0 5.1 %fusion.80 = f32[64,1536]{1,0:T(8,128)} fusion(s32[1024]{0:T(1024)S(1)} %bitcast.73, f32[64,1536]{1,0:T(8,128)} %get-tuple-element.175, f32[16,64,1024]{2,1,0:T(8,128)} %get-tuple-element.182, s32[]{:T(128)} %get-tuple-element.174, pred[]{:T(512)S(6)} %compare.3), kind=kOutput, calls=%fused_computation.10.clone.1 | convolution fusion | flops 1209729024 | bytes 1053185 | tf_op jit(solution)/shard_map/while/body/eval_jaxpr/dot_general | solution.py:95
  94.8 5.1 %fusion.80 = f32[64,1536]{1,0:T(8,128)} fusion(s32[1024]{0:T(1024)S(1)} %bitcast.73, f32[64,1536]{1,0:T(8,128)} %get-tuple-element.175, f32[16,64,1024]{2,1,0:T(8,128)} %get-tuple-element.182, s32[]{:T(128)} %get-tuple-element.174, pred[]{:T(512)S(6)} %compare.3), kind=kOutput, calls=%fused_computation.10.clone.1 | convolution fusion | flops 1209729024 | bytes 1053185 | tf_op jit(solution)/shard_map/while/body/eval_jaxpr/dot_general | solution.py:95
  100.7 5.1 %fusion.80 = f32[64,1536]{1,0:T(8,128)} fusion(s32[1024]{0:T(1024)S(1)} %bitcast.73, f32[64,1536]{1,0:T(8,128)} %get-tuple-element.175, f32[16,64,1024]{2,1,0:T(8,128)} %get-tuple-element.182, s32[]{:T(128)} %get-tuple-element.174, pred[]{:T(512)S(6)} %compare.3), kind=kOutput, calls=%fused_computation.10.clone.1 | convolution fusion | flops 1209729024 | bytes 1053185 | tf_op jit(solution)/shard_map/while/body/eval_jaxpr/dot_general | solution.py:95
  106.6 5.1 %fusion.80 = f32[64,1536]{1,0:T(8,128)} fusion(s32[1024]{0:T(1024)S(1)} %bitcast.73, f32[64,1536]{1,0:T(8,128)} %get-tuple-element.175, f32[16,64,1024]{2,1,0:T(8,128)} %get-tuple-element.182, s32[]{:T(128)} %get-tuple-element.174, pred[]{:T(512)S(6)} %compare.3), kind=kOutput, calls=%fused_computation.10.clone.1 | convolution fusion | flops 1209729024 | bytes 1053185 | tf_op jit(solution)/shard_map/while/body/eval_jaxpr/dot_general | solution.py:95
  112.4 5.1 %fusion.80 = f32[64,1536]{1,0:T(8,128)} fusion(s32[1024]{0:T(1024)S(1)} %bitcast.73, f32[64,1536]{1,0:T(8,128)} %get-tuple-element.175, f32[16,64,1024]{2,1,0:T(8,128)} %get-tuple-element.182, s32[]{:T(128)} %get-tuple-element.174, pred[]{:T(512)S(6)} %compare.3), kind=kOutput, calls=%fused_computation.10.clone.1 | convolution fusion | flops 1209729024 | bytes 1053185 | tf_op jit(solution)/shard_map/while/body/eval_jaxpr/dot_general | solution.py:95
  118.3 5.1 %fusion.80 = f32[64,1536]{1,0:T(8,128)} fusion(s32[1024]{0:T(1024)S(1)} %bitcast.73, f32[64,1536]{1,0:T(8,128)} %get-tuple-element.175, f32[16,64,1024]{2,1,0:T(8,128)} %get-tuple-element.182, s32[]{:T(128)} %get-tuple-element.174, pred[]{:T(512)S(6)} %compare.3), kind=kOutput, calls=%fused_computation.10.clone.1 | convolution fusion | flops 1209729024 | bytes 1053185 | tf_op jit(solution)/shard_map/while/body/eval_jaxpr/dot_general | solution.py:95
  124.1 5.1 %fusion.80 = f32[64,1536]{1,0:T(8,128)} fusion(s32[1024]{0:T(1024)S(1)} %bitcast.73, f32[64,1536]{1,0:T(8,128)} %get-tuple-element.175, f32[16,64,1024]{2,1,0:T(8,128)} %get-tuple-element.182, s32[]{:T(128)} %get-tuple-element.174, pred[]{:T(512)S(6)} %compare.3), kind=kOutput, calls=%fused_computation.10.clone.1 | convolution fusion | flops 1209729024 | bytes 1053185 | tf_op jit(solution)/shard_map/while/body/eval_jaxpr/dot_general | solution.py:95
  130.0 5.1 %fusion.80 = f32[64,1536]{1,0:T(8,128)} fusion(s32[1024]{0:T(1024)S(1)} %bitcast.73, f32[64,1536]{1,0:T(8,128)} %get-tuple-element.175, f32[16,64,1024]{2,1,0:T(8,128)} %get-tuple-element.182, s32[]{:T(128)} %get-tuple-element.174, pred[]{:T(512)S(6)} %compare.3), kind=kOutput, calls=%fused_computation.10.clone.1 | convolution fusion | flops 1209729024 | bytes 1053185 | tf_op jit(solution)/shard_map/while/body/eval_jaxpr/dot_general | solution.py:95
  135.9 5.1 %fusion.80 = f32[64,1536]{1,0:T(8,128)} fusion(s32[1024]{0:T(1024)S(1)} %bitcast.73, f32[64,1536]{1,0:T(8,128)} %get-tuple-element.175, f32[16,64,1024]{2,1,0:T(8,128)} %get-tuple-element.182, s32[]{:T(128)} %get-tuple-element.174, pred[]{:T(512)S(6)} %compare.3), kind=kOutput, calls=%fused_computation.10.clone.1 | convolution fusion | flops 1209729024 | bytes 1053185 | tf_op jit(solution)/shard_map/while/body/eval_jaxpr/dot_general | solution.py:95
  141.7 5.1 %fusion.80 = f32[64,1536]{1,0:T(8,128)} fusion(s32[1024]{0:T(1024)S(1)} %bitcast.73, f32[64,1536]{1,0:T(8,128)} %get-tuple-element.175, f32[16,64,1024]{2,1,0:T(8,128)} %get-tuple-element.182, s32[]{:T(128)} %get-tuple-element.174, pred[]{:T(512)S(6)} %compare.3), kind=kOutput, calls=%fused_computation.10.clone.1 | convolution fusion | flops 1209729024 | bytes 1053185 | tf_op jit(solution)/shard_map/while/body/eval_jaxpr/dot_general | solution.py:95
  147.6 5.1 %fusion.80 = f32[64,1536]{1,0:T(8,128)} fusion(s32[1024]{0:T(1024)S(1)} %bitcast.73, f32[64,1536]{1,0:T(8,128)} %get-tuple-element.175, f32[16,64,1024]{2,1,0:T(8,128)} %get-tuple-element.182, s32[]{:T(128)} %get-tuple-element.174, pred[]{:T(512)S(6)} %compare.3), kind=kOutput, calls=%fused_computation.10.clone.1 | convolution fusion | flops 1209729024 | bytes 1053185 | tf_op jit(solution)/shard_map/while/body/eval_jaxpr/dot_general | solution.py:95
  153.6 1.8 collective-permute-start.6
  155.4 2.2 fusion.39
  158.6 1.9 collective-permute-start.4
  165.7 1.8 fusion.25
  167.5 37.9 %psum.31 = f32[16,64]{1,0:T(8,128)} all-reduce(f32[16,64]{1,0:T(8,128)S(1)} %fusion.25), channel_id=1, replica_groups=mesh['slab'=4,'brick'=8] {'slab','brick'}, use_global_device_ids=true, to_apply=%region_8.9 | all-reduce | flops 1024 | bytes 8192 | tf_op jit(solution)/shard_map/psum | solution.py:138
  205.8 1.7 add_convert_fusion
  207.5 89.9 %all-reduce.3.cloned.1.call-done = (f32[512,512]{0,1:T(8,128)}, f32[512,64]{0,1:T(8,128)}, f32[64,512]{1,0:T(8,128)}) async-done(((f32[512,512]{0,1:T(8,128)}, f32[512,64]{0,1:T(8,128)}, f32[64,512]{1,0:T(8,128)}), (f32[512,512]{0,1:T(8,128)}, f32[512,64]{0,1:T(8,128)}, f32[64,512]{1,0:T(8,128)})) %all-reduce.3.cloned.1.call-update) | async-done | bytes 1310736 | tf_op jit(solution)/shard_map/psum | solution.py:138
  297.4 2.6 copy.15
  (117 shorter events, 57.0 us)
Async XLA Ops:
  7.2 1.3 copy-start
  7.2 12.5 %copy-start.12 = (bf16[1024,512]{1,0:T(8,128)(2,1)S(1)}, bf16[1024,512]{1,0:T(8,128)(2,1)}, u32[]{:S(2)}) copy-start(bf16[1024,512]{1,0:T(8,128)(2,1)} %param.15) | copy-start | bytes 3145732
  7.2 12.4 %copy-start.3 = (bf16[512,512]{1,0:T(8,128)(2,1)S(1)}, bf16[512,512]{1,0:T(8,128)(2,1)}, u32[]{:S(2)}) copy-start(bf16[512,512]{1,0:T(8,128)(2,1)} %param.20) | copy-start | bytes 1572868
  7.2 290.2 %all-reduce.3.cloned.1.call-start = ((), (), s32[]{:S(2)}) async-start(), calls=%async_computation | async-start | bytes 2621440 | tf_op jit(solution)/shard_map/psum | solution.py:138
  11.3 11.4 %collective-permute-start = (bf16[64,128]{1,0:T(8,128)(2,1)}, bf16[64,128]{1,0:T(8,128)(2,1)S(1)}, u32[]{:S(2)}, u32[]{:S(2)}) collective-permute-start(bf16[64,128]{1,0:T(8,128)(2,1)} %convolution_convert_fusion.3), channel_id=1, source_target_pairs={{0,8},{8,16},{16,24},{24,0},{1,9},{9,17},{17,25},{25,1},{2,10},{10... | collective-permute-start | bytes 49160 | tf_op jit(solution)/shard_map/ppermute | solution.py:10
  14.5 8.3 %collective-permute-start.1 = (bf16[64,128]{1,0:T(8,128)(2,1)S(1)}, bf16[64,128]{1,0:T(8,128)(2,1)S(1)}, u32[]{:S(2)}, u32[]{:S(2)}) collective-permute-start(bf16[64,128]{1,0:T(8,128)(2,1)S(1)} %convolution_convert_fusion.2), channel_id=1, source_target_pairs={{0,24},{8,0},{16,8},{24,16},{1,25},{9,1},{17,9},{25,17},{2,26},{10... | collective-permute-start | bytes 49160 | tf_op jit(solution)/shard_map/ppermute | solution.py:10
  15.7 7.0 %collective-permute-start.2 = (bf16[64,128]{1,0:T(8,128)(2,1)S(1)}, bf16[64,128]{1,0:T(8,128)(2,1)S(1)}, u32[]{:S(2)}, u32[]{:S(2)}) collective-permute-start(bf16[64,128]{1,0:T(8,128)(2,1)S(1)} %convolution_convert_fusion.1), channel_id=1, source_target_pairs={{0,1},{1,2},{2,3},{3,4},{4,5},{5,6},{6,7},{7,0},{8,9},{9,10},{10,1... | collective-permute-start | bytes 49160 | tf_op jit(solution)/shard_map/ppermute | solution.py:10
  16.0 6.7 %collective-permute-start.3 = (bf16[64,128]{1,0:T(8,128)(2,1)S(1)}, bf16[64,128]{1,0:T(8,128)(2,1)S(1)}, u32[]{:S(2)}, u32[]{:S(2)}) collective-permute-start(bf16[64,128]{1,0:T(8,128)(2,1)S(1)} %convolution_convert_fusion), channel_id=1, source_target_pairs={{0,7},{1,0},{2,1},{3,2},{4,3},{5,4},{6,5},{7,6},{8,15},{9,8},{10,9... | collective-permute-start | bytes 49160 | tf_op jit(solution)/shard_map/ppermute | solution.py:10
  20.9 1.8 copy-start.1
  20.9 1.8 copy-start.11
  22.8 30.5 %copy-start.10 = (bf16[16,64]{1,0:T(8,128)(2,1)S(1)}, bf16[16,64]{1,0:T(8,128)(2,1)}, u32[]{:S(2)}) copy-start(bf16[16,64]{1,0:T(8,128)(2,1)} %param.23) | copy-start | bytes 6148
  53.3 2.3 copy-start.13
  53.3 2.3 copy-start.14
  56.1 2.9 copy-start.5
  152.7 11.5 %copy-start.9 = (f32[64,1536]{1,0:T(8,128)S(1)}, f32[64,1536]{1,0:T(8,128)}, u32[]{:S(2)}) copy-start(f32[64,1536]{1,0:T(8,128)} %get-tuple-element.50) | copy-start | bytes 1179652
  152.7 11.5 %copy-start.15 = (f32[64,1024]{1,0:T(8,128)S(1)}, f32[64,1024]{1,0:T(8,128)}, u32[]{:S(2)}) copy-start(f32[64,1024]{1,0:T(8,128)} %get-tuple-element.100) | copy-start | bytes 786436
  153.6 6.9 %collective-permute-start.6 = (f32[64,128]{1,0:T(8,128)S(1)}, f32[64,128]{1,0:T(8,128)S(1)}, u32[]{:S(2)}, u32[]{:S(2)}) collective-permute-start(f32[64,128]{1,0:T(8,128)S(1)} %get-tuple-element.95), channel_id=1, source_target_pairs={{0,7},{1,0},{2,1},{3,2},{4,3},{5,4},{6,5},{7,6},{8,15},{9,8},{10,9... | collective-permute-start | bytes 98312 | tf_op jit(solution)/shard_map/ppermute | solution.py:10
  157.6 4.8 %collective-permute-start.5 = (f32[64,128]{1,0:T(8,128)S(1)}, f32[64,128]{1,0:T(8,128)S(1)}, u32[]{:S(2)}, u32[]{:S(2)}) collective-permute-start(f32[64,128]{1,0:T(8,128)S(1)} %get-tuple-element.93), channel_id=1, source_target_pairs={{0,8},{8,16},{16,24},{24,0},{1,9},{9,17},{17,25},{25,1},{2,10},{10... | collective-permute-start | bytes 98312 | tf_op jit(solution)/shard_map/ppermute | solution.py:10
  158.6 5.1 %collective-permute-start.7 = (f32[64,128]{1,0:T(8,128)S(1)}, f32[64,128]{1,0:T(8,128)S(1)}, u32[]{:S(2)}, u32[]{:S(2)}) collective-permute-start(f32[64,128]{1,0:T(8,128)S(1)} %get-tuple-element.94), channel_id=1, source_target_pairs={{0,1},{1,2},{2,3},{3,4},{4,5},{5,6},{6,7},{7,0},{8,9},{9,10},{10,1... | collective-permute-start | bytes 98312 | tf_op jit(solution)/shard_map/ppermute | solution.py:10
  158.6 5.5 %collective-permute-start.4 = (f32[64,128]{1,0:T(8,128)S(1)}, f32[64,128]{1,0:T(8,128)S(1)}, u32[]{:S(2)}, u32[]{:S(2)}) collective-permute-start(f32[64,128]{1,0:T(8,128)S(1)} %get-tuple-element.92), channel_id=1, source_target_pairs={{0,24},{8,0},{16,8},{24,16},{1,25},{9,1},{17,9},{25,17},{2,26},{10... | collective-permute-start | bytes 98312 | tf_op jit(solution)/shard_map/ppermute | solution.py:10
  165.7 39.7 %copy-start.8 = (bf16[512,64]{0,1:T(8,128)(2,1)S(1)}, bf16[512,64]{0,1:T(8,128)(2,1)}, u32[]{:S(2)}) copy-start(bf16[512,64]{0,1:T(8,128)(2,1)} %param.21) | copy-start | bytes 196612
  167.5 38.3 %copy-start.2 = (bf16[1024,512]{1,0:T(8,128)(2,1)S(1)}, bf16[1024,512]{1,0:T(8,128)(2,1)}, u32[]{:S(2)}) copy-start(bf16[1024,512]{1,0:T(8,128)(2,1)} %copy-done.1) | copy-start | bytes 3145732
  167.5 38.3 %copy-start.4 = (bf16[512,512]{1,0:T(8,128)(2,1)S(1)}, bf16[512,512]{1,0:T(8,128)(2,1)}, u32[]{:S(2)}) copy-start(bf16[512,512]{1,0:T(8,128)(2,1)} %param.20) | copy-start | bytes 1572868
  297.4 2.6 copy-start.7
  297.4 3.2 %copy-start.6 = (f32[64,512]{1,0:T(8,128)S(1)}, f32[64,512]{1,0:T(8,128)}, u32[]{:S(2)}) copy-start(f32[64,512]{1,0:T(8,128)} %get-tuple-element.189) | copy-start | bytes 393220
Sparse Core Ops, SparseCore 0:
  165.8 131.5 all-reduce.2
where the time goes:
time: 311 us; the launch traced here: 308 us
  matrix products  117 us (38%)
  waiting for transfers between devices  92.4 us (30%)
  blocking collectives  37.9 us (12%)
  local copies, waits for them, and re-layouts  30.6 us (10%)
  between operations  14.3 us (5%)
  starting transfers between devices  12.4 us (4%)
    psum x1, waiting for transfers between devices, shards(): lax.psum((residual_weight_gradient, down_weight_gradient, up_weight_gradi...  89.9 us
    dot_general x16, matrix products, scatter_slot(): lax.dot_general(slot_terms, onehot, (((1,), (1,)), ((), ())), precision=l...  81.4 us
    psum x1, blocking collectives, shards(): lax.psum((residual_weight_gradient, down_weight_gradient, up_weight_gradi...  37.9 us
    dynamic_slice x32, local copies, waits for them, and re-layouts, shards(): lax.scan(gather_slot, jnp.zeros((), jnp.float32), triplet_row_index)  24.5 us
    dot_general x16, matrix products, gather_slot(): jnp.dot(edge_table_rows, onehot, preferred_element_type=jnp.float32)  18 us
    ppermute x8, starting transfers between devices, passed_along(): return lax.ppermute(value, axis, pairs)  12.4 us
  transfers between devices with their start and end apart: 9, of which 3 were waited for; matrix products, arithmetic and copies ran while one was open for 4% of the time, Pallas kernels for 0%

commit v1 on v0

v1 whole, which is shorter than its diff:
```python
import functools

import jax
import jax.numpy as jnp
from jax import lax
from jax.experimental import pallas as pl
from jax.experimental.pallas import tpu as pltpu
from jax.sharding import PartitionSpec as P

AXES = ("slab", "brick")
LANES = 256
F32 = jnp.float32
BF16 = jnp.bfloat16


def dot(a, b, dims, precision=None):
    return lax.dot_general(a, b, (dims, ((), ())), precision=precision, preferred_element_type=F32)


NN = ((1,), (0,))
NT = ((1,), (1,))
TN = ((0,), (0,))


def sigmoid(value):
    return 1.0 / (1.0 + jnp.exp(-value))


def silu_grad(value):
    sig = sigmoid(value)
    return sig * (1.0 + value * (1.0 - sig))


def onehot(low):
    rows = lax.broadcasted_iota(jnp.int32, (LANES, low.shape[1]), 0)
    return jnp.where(rows == low, 1.0, 0.0).astype(BF16)


def stacked(table):
    return jnp.concatenate(
        [table[:, g * LANES : (g + 1) * LANES] for g in range(table.shape[1] // LANES)], axis=0
    )


def unstacked(blocks, width):
    return jnp.concatenate(
        [blocks[g * width : (g + 1) * width] for g in range(blocks.shape[0] // width)], axis=1
    )


def chosen(blocks, high, width):
    total = jnp.zeros((width, blocks.shape[1]), F32)
    for g in range(blocks.shape[0] // width):
        total = jnp.where(high == g, blocks[g * width : (g + 1) * width], total)
    return total


def spread(values, high, groups):
    zero = jnp.zeros_like(values)
    return jnp.concatenate([jnp.where(high == g, values, zero) for g in range(groups)], axis=0)


def project_kernel(embed_ref, down_ref, rows_ref, pre_ref, proj_ref, *send_refs):
    pre = dot(down_ref[...], embed_ref[...], NT)
    pre_ref[...] = pre
    proj = (pre * sigmoid(pre)).astype(BF16)
    proj_ref[...] = proj
    table = stacked(proj)
    width = proj.shape[0]
    for k, send_ref in enumerate(send_refs):
        index = rows_ref[k : k + 1, :]
        picked = dot(table, onehot(index & (LANES - 1)), NN)
        send_ref[...] = chosen(picked, index // LANES, width).astype(BF16)


def project(embed, down_t, outgoing):
    rows, width = embed.shape[0], down_t.shape[0]
    ghost = outgoing.shape[1]
    return pl.pallas_call(
        project_kernel,
        out_shape=[
            jax.ShapeDtypeStruct((width, rows), F32),
            jax.ShapeDtypeStruct((width, rows), BF16),
        ]
        + [jax.ShapeDtypeStruct((width, ghost), BF16)] * 4,
        compiler_params=pltpu.CompilerParams(vmem_limit_bytes=16 * 2**20),
        name="project",
    )(embed, down_t, outgoing)


def triplet_kernel(
    proj_ref,
    g0_ref,
    g1_ref,
    g2_ref,
    g3_ref,
    basis_ref,
    index_ref,
    count_ref,
    up_ref,
    cotangent_ref,
    bw_ref,
    own_ref,
    ghost_ref,
    grads_ref,
    table_ref,
    weight_ref,
    hot_ref,
    picked_ref,
    dw_ref,
    tsum_ref,
    dt_ref,
    acc_ref,
):
    width, rows = proj_ref.shape
    trips = index_ref.shape[0]
    nbasis = bw_ref.shape[0]
    own_groups = rows // LANES
    ghosts = jnp.concatenate([g0_ref[...], g1_ref[...], g2_ref[...], g3_ref[...]], axis=1)
    table_ref[: own_groups * width, :] = stacked(proj_ref[...])
    table_ref[own_groups * width :, :] = stacked(ghosts)
    groups = table_ref.shape[0] // width
    tiles = rows // LANES

    span = trips * nbasis
    fold = jnp.where(
        lax.broadcasted_iota(jnp.int32, (nbasis, span), 1) % nbasis
        == lax.broadcasted_iota(jnp.int32, (nbasis, span), 0),
        1.0,
        0.0,
    )
    wide = dot(bw_ref[...], fold.astype(BF16), TN).astype(BF16)
    own_slot = lax.broadcasted_iota(jnp.int32, (trips, width, span), 0) == (
        lax.broadcasted_iota(jnp.int32, (trips, width, span), 2) // nbasis
    )
    diagonal = jnp.where(own_slot, wide[None], jnp.zeros((), BF16)).reshape(trips * width, span)
    weight_ref[...] = dot(diagonal, basis_ref[...], NN)

    tsum_ref[...] = jnp.zeros_like(tsum_ref)

    def lookup(j, t):
        at = pl.ds(t * LANES, LANES)
        index = index_ref[pl.ds(j, 1), at]
        high = jnp.where(j < count_ref[:, at], index // LANES, -1)
        return at, index & (LANES - 1), high

    def forward(j, carry):
        for t in range(tiles):
            at, low, high = lookup(j, t)
            hot = onehot(low)
            hot_ref[j, :, at] = hot
            picked = chosen(dot(table_ref[...], hot, NN), high, width)
            picked_ref[j, :, at] = picked.astype(BF16)
            tsum_ref[:, at] += weight_ref[pl.ds(j * width, width), at] * picked
        return carry

    lax.fori_loop(0, trips, forward, 0)

    tsum = tsum_ref[...]
    sig = sigmoid(tsum)
    act = (tsum * sig).astype(BF16)
    cotangent = cotangent_ref[...]
    inner = cotangent.shape[1]
    grads_ref[:, :inner] = dot(act, cotangent, NN).astype(BF16)
    dsum = dot(up_ref[...], cotangent, NT)
    dt_ref[...] = dsum * (sig * (1.0 + tsum * (1.0 - sig)))
    acc_ref[...] = jnp.zeros_like(acc_ref)

    def backward(j, carry):
        parts = []
        for t in range(tiles):
            at, low, high = lookup(j, t)
            dt = dt_ref[:, at]
            dw_ref[pl.ds(j * width, width), at] = (dt * picked_ref[j, :, at].astype(F32)).astype(BF16)
            terms = (dt * weight_ref[pl.ds(j * width, width), at]).astype(BF16)
            parts.append(spread(terms, high, groups))
        acc_ref[...] += dot(jnp.concatenate(parts, axis=1), hot_ref[j], NT)
        return carry

    lax.fori_loop(0, trips, backward, 0)

    own_ref[...] = unstacked(acc_ref[: own_groups * width, :], width)
    ghost_ref[...] = unstacked(acc_ref[own_groups * width :, :], width).astype(BF16)
    full = dot(dw_ref[...], basis_ref[...], NT).reshape(trips, width, span)
    kept = jnp.sum(jnp.where(own_slot, full, 0.0), axis=0)
    folded = dot(kept, fold, NT, lax.Precision.HIGHEST)
    pad = grads_ref.shape[1] - inner - nbasis
    grads_ref[:, inner:] = jnp.concatenate(
        [folded, jnp.zeros((width, pad), F32)], axis=1
    ).astype(BF16)


def triplets(proj, ghosts, basis, index, count, up_weight, cotangent, basis_weight):
    width, rows = proj.shape
    trips, nbasis = basis.shape[:2]
    ghost = ghosts[0].shape[1]
    inner = cotangent.shape[1]
    table_rows = rows + 4 * ghost
    groups = table_rows // LANES
    return pl.pallas_call(
        triplet_kernel,
        out_shape=[
            jax.ShapeDtypeStruct((width, rows), F32),
            jax.ShapeDtypeStruct((width, 4 * ghost), BF16),
            jax.ShapeDtypeStruct((width, inner + 128), BF16),
        ],
        scratch_shapes=[
            pltpu.VMEM((groups * width, LANES), BF16),
            pltpu.VMEM((trips * width, rows), F32),
            pltpu.VMEM((trips, LANES, rows), BF16),
            pltpu.VMEM((trips, width, rows), BF16),
            pltpu.VMEM((trips * width, rows), BF16),
            pltpu.VMEM((width, rows), F32),
            pltpu.VMEM((width, rows), F32),
            pltpu.VMEM((groups * width, LANES), F32),
        ],
        compiler_params=pltpu.CompilerParams(vmem_limit_bytes=40 * 2**20),
        name="triplets",
    )(
        proj,
        *ghosts,
        basis.reshape(trips * nbasis, rows),
        index,
        count.reshape(1, rows),
        up_weight,
        cotangent,
        basis_weight,
    )


def collect_kernel(
    own_ref, b0_ref, b1_ref, b2_ref, b3_ref, rows_ref, pre_ref, embed_ref, dpre_ref, grad_ref
):
    width, rows = own_ref.shape
    groups = rows // LANES
    acc = jnp.zeros((groups * width, LANES), F32)
    for k, back_ref in enumerate((b0_ref, b1_ref, b2_ref, b3_ref)):
        index = rows_ref[k : k + 1, :]
        acc += dot(spread(back_ref[...], index // LANES, groups), onehot(index & (LANES - 1)), NT)
    dproj = own_ref[...] + unstacked(acc, width)
    dpre = (dproj * silu_grad(pre_ref[...])).astype(BF16)
    dpre_ref[...] = dpre
    grad_ref[...] = dot(dpre, embed_ref[...], NN).astype(BF16)


def collect(own, backs, outgoing, pre, embed):
    return pl.pallas_call(
        collect_kernel,
        out_shape=[
            jax.ShapeDtypeStruct(own.shape, BF16),
            jax.ShapeDtypeStruct((own.shape[0], embed.shape[1]), BF16),
        ],
        compiler_params=pltpu.CompilerParams(vmem_limit_bytes=16 * 2**20),
        name="collect",
    )(own, *backs, outgoing, pre, embed)


def passed_along(value, axis, steps):
    count = lax.axis_size(axis)
    return lax.ppermute(value, axis, [(i, (i + steps) % count) for i in range(count)])


def swapped(value, axis, bit):
    return lax.ppermute(value, axis, [(i, i ^ bit) for i in range(lax.axis_size(axis))])


def bits_of(axis):
    bit, bits = 1, []
    while bit < lax.axis_size(axis):
        bits.append((axis, bit))
        bit *= 2
    return bits


def side(step):
    axis, bit = step
    return (lax.axis_index(axis) // bit) % 2


def halved(value, step):
    rows = value.shape[0] // 2
    upper = side(step)
    mine = lax.dynamic_slice_in_dim(value, upper * rows, rows, 0)
    other = lax.dynamic_slice_in_dim(value, (1 - upper) * rows, rows, 0)
    return mine + swapped(other, *step)


def doubled(value, step):
    other = swapped(value, *step)
    upper = side(step)
    return jnp.where(
        upper == 1,
        jnp.concatenate([other, value], axis=0),
        jnp.concatenate([value, other], axis=0),
    )


def shards(
    embed,
    cotangent,
    basis,
    triplet_row_index,
    triplet_slot_count,
    outgoing_edge_rows,
    residual_weight,
    down_weight,
    up_weight,
    basis_weight,
):
    inner = embed.shape[1]
    ghost = outgoing_edge_rows.shape[1]
    nbasis = basis.shape[1]
    down_t = down_weight.T
    moves = (("slab", 1), ("slab", -1), ("brick", 1), ("brick", -1))

    pre, proj, *sends = project(embed, down_t, outgoing_edge_rows)
    ghosts = [passed_along(sends[k], *moves[k]) for k in range(4)]

    res_pre = jnp.dot(embed, residual_weight, preferred_element_type=F32)
    dres = (cotangent.astype(F32) * silu_grad(res_pre)).astype(BF16)
    residual_grad = dot(embed, dres, TN).astype(BF16)

    scattered = [("brick", 1)] + bits_of("slab")
    summed = bits_of("brick")[1:]
    for step in scattered:
        residual_grad = halved(residual_grad, step)

    own, ghost_terms, grads = triplets(
        proj, ghosts, basis, triplet_row_index, triplet_slot_count, up_weight, cotangent, basis_weight
    )
    backs = [
        passed_along(ghost_terms[:, k * ghost : (k + 1) * ghost], moves[k][0], -moves[k][1])
        for k in range(4)
    ]
    dpre, down_grad = collect(own, backs, outgoing_edge_rows, pre, embed)

    rest = jnp.concatenate([down_grad, grads], axis=1)
    for step in summed[::-1]:
        residual_grad = residual_grad + swapped(residual_grad, *step)
        rest = rest + swapped(rest, *step)
    for step in scattered[::-1]:
        residual_grad = doubled(residual_grad, step)
        rest = rest + swapped(rest, *step)

    res_term = dot(dres, residual_weight, NT)
    down_term = dot(dpre, down_weight, ((0,), (1,)))
    edge_grad = (res_term + down_term).astype(BF16)
    rest = rest.astype(F32)
    return (
        edge_grad,
        residual_grad.astype(F32),
        rest[:, :inner].T,
        rest[:, inner : 2 * inner],
        rest[:, 2 * inner : 2 * inner + nbasis].T,
    )


def solution(mesh):
    both = P(AXES, None)
    in_specs = (both, both, P(None, None, AXES), P(None, AXES), P(AXES), P(None, AXES)) + (P(),) * 4
    out_specs = (both, P(), P(), P(), P())
    return jax.shard_map(shards, mesh=mesh, in_specs=in_specs, out_specs=out_specs, check_vma=False)
```

time: 311 us -> 88.7 us (0.29)
  matrix products: 117 us -> 7.84 us
  waiting for transfers between devices: 92.4 us -> 23 us
  blocking collectives: 37.9 us -> 0 us
  Pallas kernels: 0 us -> 18.4 us
  local copies, waits for them, and re-layouts: 30.6 us -> 13.8 us
  between operations: 14.3 us -> 0.95 us
  starting transfers between devices: 12.4 us -> 21.6 us
    dot_general x50 -> x4, matrix products: 117 us -> 7.84 us  [the longest x3 4.95 us: dot(): lax.dot_general(a, b, (dims, ((), ())), precision=precision, preferred_el...]
    psum x1 -> x0, waiting for transfers between devices: 89.9 us -> none  [shards(): lax.psum((residual_weight_gradient, down_weight_gradient, up_weight_gradi...]
    psum x1 -> x0, blocking collectives: 37.9 us -> none  [shards(): lax.psum((residual_weight_gradient, down_weight_gradient, up_weight_gradi...]
    dynamic_slice x32 -> x3, local copies, waits for them, and re-layouts: 24.5 us -> 1.7 us  [halved(): other = lax.dynamic_slice_in_dim(value, (1 - upper) * rows, rows, 0)]
    ppermute x8 -> x21, waiting for transfers between devices: 2.45 us -> 23 us  [the longest x13 18 us: swapped(): lax.ppermute(value, axis, [(i, i ^ bit) for i in range(lax.axis_size(axis...]
    pallas_call x0 -> x3, Pallas kernels: none -> 18.4 us  [the longest x1 16.3 us: triplets(): pl.pallas_call(triplet_kernel, out_shape=[jax.ShapeDtypeStruct((width, ro...]
    ppermute x8 -> x21, starting transfers between devices: 12.4 us -> 21.6 us  [the longest x8 11.4 us: passed_along(): lax.ppermute(value, axis, [(i, (i + steps) % count) for i in range(count)])]
    unnamed x38, local copies, waits for them, and re-layouts: 4.32 us -> 10.5 us
  transfers between devices with their start and end apart: 9 -> 21, of which waited for: 3 -> 10; matrix products, arithmetic and copies ran while one was open for 4% -> 15% of each run, Pallas kernels for 0% -> 19%
where the time goes in v1:
time: 88.7 us; the launch traced here: 88.1 us
  waiting for transfers between devices  23 us (26%)
  starting transfers between devices  21.6 us (24%)
  Pallas kernels  18.4 us (21%)
  local copies, waits for them, and re-layouts  13.8 us (16%)
  matrix products  7.84 us (9%)
  other arithmetic  2.55 us (3%)
  between operations  0.95 us (1%)
    ppermute x13, waiting for transfers between devices, swapped(): lax.ppermute(value, axis, [(i, i ^ bit) for i in range(lax.axis_size(axis...  18 us
    pallas_call x1, Pallas kernels, triplets(): pl.pallas_call(triplet_kernel, out_shape=[jax.ShapeDtypeStruct((width, ro...  16.3 us
    ppermute x8, starting transfers between devices, passed_along(): lax.ppermute(value, axis, [(i, (i + steps) % count) for i in range(count)])  11.4 us
    unnamed x38, local copies, waits for them, and re-layouts  10.5 us
    ppermute x13, starting transfers between devices, swapped(): lax.ppermute(value, axis, [(i, i ^ bit) for i in range(lax.axis_size(axis...  10.3 us
    ppermute x8, waiting for transfers between devices, passed_along(): lax.ppermute(value, axis, [(i, (i + steps) % count) for i in range(count)])  4.97 us
    dot_general x3, matrix products, dot(): lax.dot_general(a, b, (dims, ((), ())), precision=precision, preferred_el...  4.95 us
    dot_general x1, matrix products, shards(): res_pre = jnp.dot(embed, residual_weight, preferred_element_type=F32)  2.89 us
  transfers between devices with their start and end apart: 21, of which 10 were waited for; matrix products, arithmetic and copies ran while one was open for 15% of the time, Pallas kernels for 19%

profile of v1, /device:TPU:0, one launch (start us, length us, event | category | flops | bytes accessed | tf_op | source)
XLA Modules:
  0.0 88.1 jit_solution(5567274403440878337)
XLA Ops:
  0.7 1.3 %copy-done.1 = bf16[1024,512]{1,0:T(8,128)(2,1)S(1)} copy-done((bf16[1024,512]{1,0:T(8,128)(2,1)S(1)}, bf16[1024,512]{1,0:T(8,128)(2,1)}, u32[]{:S(2)}) %copy-start.1) | copy-done | bytes 1048600
  3.5 1.3 %project.1 = (f32[64,1024]{1,0:T(8,128)S(1)}, bf16[64,1024]{1,0:T(8,128)(2,1)S(1)}, bf16[64,128]{1,0:T(8,128)(2,1)}, bf16[64,128]{1,0:T(8,128)(2,1)}, bf16[64,128]{1,0:T(8,128)(2,1)}, /*index=5*/bf16[64,128]{1,0:T(8,128)(2,1)}) custom-call(bf16[1024,512]{1,0:T(8,128)(2,1)S(1)} %copy-done.1, bf16[64,512]{1,0:T(8,128)(2,1)S(1)} %bitcast.20, ...), custom_call_target="tpu_custom_call" | custom-call | tf_op jit(solution)/shard_map/project/pallas_call | solution.py:79
  4.8 2.9 %collective-permute-start = (bf16[64,128]{1,0:T(8,128)(2,1)}, bf16[64,128]{1,0:T(8,128)(2,1)S(1)}, u32[]{:S(2)}, u32[]{:S(2)}) collective-permute-start(bf16[64,128]{1,0:T(8,128)(2,1)} %get-tuple-element.17), channel_id=1, source_target_pairs={{0,8},{8,16},{16,24},{24,0},{1,9},{9,17},{17,25},{25,1},{2,10},{10... | collective-permute-start | bytes 49160 | tf_op jit(solution)/shard_map/ppermute | solution.py:260
  7.7 1.0 %collective-permute-start.1 = (bf16[64,128]{1,0:T(8,128)(2,1)}, bf16[64,128]{1,0:T(8,128)(2,1)}, u32[]{:S(2)}, u32[]{:S(2)}) collective-permute-start(bf16[64,128]{1,0:T(8,128)(2,1)} %get-tuple-element.18), channel_id=1, source_target_pairs={{0,24},{8,0},{16,8},{24,16},{1,25},{9,1},{17,9},{25,17},{2,26},{10... | collective-permute-start | bytes 49160 | tf_op jit(solution)/shard_map/ppermute | solution.py:260
  8.7 3.5 %collective-permute-start.3 = (bf16[64,128]{1,0:T(8,128)(2,1)}, bf16[64,128]{1,0:T(8,128)(2,1)}, u32[]{:S(2)}, u32[]{:S(2)}) collective-permute-start(bf16[64,128]{1,0:T(8,128)(2,1)} %get-tuple-element.20), channel_id=1, source_target_pairs={{0,7},{1,0},{2,1},{3,2},{4,3},{5,4},{6,5},{7,6},{8,15},{9,8},{10,9... | collective-permute-start | bytes 49160 | tf_op jit(solution)/shard_map/ppermute | solution.py:260
  12.2 2.9 %multiply_convert_fusion = bf16[1024,512]{1,0:T(8,128)(2,1)S(1)} fusion(bf16[1024,512]{1,0:T(8,128)(2,1)} %cotangent_ref.1, bf16[1024,512]{1,0:T(8,128)(2,1)} %embed_ref.3, bf16[512,512]{1,0:T(8,128)(2,1)S(1)} %copy-done), kind=kOutput, calls=%fused_computation.1 | convolution fusion | flops 542113792 | bytes 3670016 | tf_op jit(solution)/shard_map/dot_general | solution.py:319
  15.1 1.0 %copy-done.16 = bf16[1024,512]{1,0:T(8,128)(2,1)} copy-done((bf16[1024,512]{1,0:T(8,128)(2,1)}, bf16[1024,512]{1,0:T(8,128)(2,1)S(1)}, u32[]{:S(2)}) %copy-start.16) | copy-done | bytes 1048600
  16.1 1.6 %convolution_convert_fusion = bf16[512,512]{0,1:T(8,128)(2,1)} fusion(bf16[1024,512]{1,0:T(8,128)(2,1)S(1)} %multiply_convert_fusion, bf16[1024,512]{1,0:T(8,128)(2,1)S(1)} %copy-done.2), kind=kOutput, calls=%fused_computation.2 | convolution fusion | flops 537133056 | bytes 2621440 | tf_op jit(solution)/shard_map/dot_general | solution.py:17
  17.7 1.7 %dynamic-slice_bitcast_fusion = bf16[256,512]{1,0:T(8,128)(2,1)} fusion(bf16[512,512]{0,1:T(8,128)(2,1)} %convolution_convert_fusion, s32[]{:T(128)S(6)} %select_n.80), kind=kLoop, calls=%fused_computation.7 | loop fusion | bytes 524292 | tf_op jit(solution)/shard_map/dynamic_slice | solution.py:284
  22.4 16.3 %triplets.1 = (f32[64,1024]{1,0:T(8,128)S(1)}, bf16[64,512]{1,0:T(8,128)(2,1)S(1)}, bf16[64,640]{1,0:T(8,128)(2,1)S(1)}) custom-call(bf16[64,1024]{1,0:T(8,128)(2,1)S(1)} %get-tuple-element.16.proj_ref, bf16[64,128]{1,0:T(8,128)(2,1)S(1)} %collective-permute-done.g0_ref, bf16[64,128]{1,0:T(8,128)(2,1)} %collective-permute-done.1.g1_ref, ...), custom_call_target="tpu_custom_call" | custom-call | tf_op jit(solution)/shard_map/triplets/pallas_call | solution.py:200
  40.1 2.1 %collective-permute-start.4 = (bf16[64,128]{1,0:T(8,128)(2,1)S(1)}, bf16[64,128]{1,0:T(8,128)(2,1)S(1)}, u32[]{:S(2)}, u32[]{:S(2)}) collective-permute-start(bf16[64,128]{1,0:T(8,128)(2,1)S(1)} %get-tuple-element.37), channel_id=1, source_target_pairs={{0,24},{8,0},{16,8},{24,16},{1,25},{9,1},{17,9},{25,17},{2,26},{10... | collective-permute-start | bytes 49160 | tf_op jit(solution)/shard_map/ppermute | solution.py:260
  42.2 1.8 %collective-permute-start.6 = (bf16[64,128]{1,0:T(8,128)(2,1)S(1)}, bf16[64,128]{1,0:T(8,128)(2,1)S(1)}, u32[]{:S(2)}, u32[]{:S(2)}) collective-permute-start(bf16[64,128]{1,0:T(8,128)(2,1)S(1)} %get-tuple-element.35), channel_id=1, source_target_pairs={{0,7},{1,0},{2,1},{3,2},{4,3},{5,4},{6,5},{7,6},{8,15},{9,8},{10,9... | collective-permute-start | bytes 49160 | tf_op jit(solution)/shard_map/ppermute | solution.py:260
  44.0 2.8 %collective-permute-done.5.b1_ref = bf16[64,128]{1,0:T(8,128)(2,1)S(1)} collective-permute-done((bf16[64,128]{1,0:T(8,128)(2,1)S(1)}, bf16[64,128]{1,0:T(8,128)(2,1)S(1)}, u32[]{:S(2)}, u32[]{:S(2)}) %collective-permute-start.5) | collective-permute-done | bytes 16416 | tf_op jit(solution)/shard_map/ppermute | solution.py:260
  46.8 2.2 %collective-permute-done.7.b3_ref = bf16[64,128]{1,0:T(8,128)(2,1)S(1)} collective-permute-done((bf16[64,128]{1,0:T(8,128)(2,1)S(1)}, bf16[64,128]{1,0:T(8,128)(2,1)S(1)}, u32[]{:S(2)}, u32[]{:S(2)}) %collective-permute-start.7) | collective-permute-done | bytes 16416 | tf_op jit(solution)/shard_map/ppermute | solution.py:260
  49.0 0.9 %copy-done.6 = f32[64,1024]{1,0:T(8,128)S(1)} copy-done((f32[64,1024]{1,0:T(8,128)S(1)}, f32[64,1024]{1,0:T(8,128)}, u32[]{:S(2)}) %copy-start.6) | copy-done | bytes 262168
  52.4 1.0 %bitcast_add_fusion = bf16[256,512]{1,0:T(8,128)(2,1)S(1)} fusion(bf16[256,512]{1,0:T(8,128)(2,1)} %collective-permute-done.8, bf16[512,512]{0,1:T(8,128)(2,1)S(1)} %copy-done.17, s32[]{:T(128)S(6)} %select_n.79), kind=kLoop, calls=%fused_computation.6 | loop fusion | flops 524288 | bytes 786436 | tf_op jit(solution)/shard_map/add | solution.py:285
  53.4 1.5 %collective-permute-start.9 = (bf16[128,512]{1,0:T(8,128)(2,1)S(1)}, bf16[128,512]{1,0:T(8,128)(2,1)S(1)}, u32[]{:S(2)}, u32[]{:S(2)}) collective-permute-start(bf16[128,512]{1,0:T(8,128)(2,1)S(1)} %constant_dynamic-slice_fusion.1), channel_id=1, source_target_pairs={{0,8},{8,0},{16,24},{24,16},{1,9},{9,1},{17,25},{25,17},{2,10},{10... | collective-permute-start | bytes 393224 | tf_op jit(solution)/shard_map/ppermute | solution.py:264
  55.0 4.1 %collective-permute-done.16 = bf16[64,1152]{1,0:T(8,128)(2,1)S(1)} collective-permute-done((bf16[64,1152]{1,0:T(8,128)(2,1)S(1)}, bf16[64,1152]{1,0:T(8,128)(2,1)S(1)}, u32[]{:S(2)}, u32[]{:S(2)}) %collective-permute-start.16) | collective-permute-done | bytes 147488 | tf_op jit(solution)/shard_map/ppermute | solution.py:264
  59.3 1.6 %collective-permute-start.10 = (bf16[64,512]{1,0:T(8,128)(2,1)S(1)}, bf16[64,512]{1,0:T(8,128)(2,1)S(1)}, u32[]{:S(2)}, u32[]{:S(2)}) collective-permute-start(bf16[64,512]{1,0:T(8,128)(2,1)S(1)} %constant_dynamic-slice_fusion), channel_id=1, source_target_pairs={{0,16},{8,24},{16,0},{24,8},{1,17},{9,25},{17,1},{25,9},{2,18},{10... | collective-permute-start | bytes 196616 | tf_op jit(solution)/shard_map/ppermute | solution.py:264
  60.9 3.4 %collective-permute-done.17 = bf16[64,1152]{1,0:T(8,128)(2,1)S(1)} collective-permute-done((bf16[64,1152]{1,0:T(8,128)(2,1)S(1)}, bf16[64,1152]{1,0:T(8,128)(2,1)S(1)}, u32[]{:S(2)}, u32[]{:S(2)}) %collective-permute-start.17) | collective-permute-done | bytes 147488 | tf_op jit(solution)/shard_map/ppermute | solution.py:264
  64.4 1.6 %collective-permute-start.18 = (bf16[64,1152]{1,0:T(8,128)(2,1)S(1)}, bf16[64,1152]{1,0:T(8,128)(2,1)S(1)}, u32[]{:S(2)}, u32[]{:S(2)}) collective-permute-start(bf16[64,1152]{1,0:T(8,128)(2,1)S(1)} %add.91), channel_id=1, source_target_pairs={{0,16},{8,24},{16,0},{24,8},{1,17},{9,25},{17,1},{25,9},{2,18},{10... | collective-permute-start | bytes 442376 | tf_op jit(solution)/shard_map/ppermute | solution.py:264
  66.0 1.2 %collective-permute-start.11 = (bf16[64,512]{1,0:T(8,128)(2,1)S(1)}, bf16[64,512]{1,0:T(8,128)(2,1)S(1)}, u32[]{:S(2)}, u32[]{:S(2)}) collective-permute-start(bf16[64,512]{1,0:T(8,128)(2,1)S(1)} %dynamic-slice_add_fusion.1), channel_id=1, source_target_pairs={{0,4},{1,5},{2,6},{3,7},{4,0},{5,1},{6,2},{7,3},{8,12},{9,13},{10,... | collective-permute-start | bytes 196616 | tf_op jit(solution)/shard_map/ppermute | solution.py:264
  67.2 2.4 %collective-permute-done.18 = bf16[64,1152]{1,0:T(8,128)(2,1)S(1)} collective-permute-done((bf16[64,1152]{1,0:T(8,128)(2,1)S(1)}, bf16[64,1152]{1,0:T(8,128)(2,1)S(1)}, u32[]{:S(2)}, u32[]{:S(2)}) %collective-permute-start.18) | collective-permute-done | bytes 147488 | tf_op jit(solution)/shard_map/ppermute | solution.py:264
  69.6 1.4 %collective-permute-start.19 = (bf16[64,1152]{1,0:T(8,128)(2,1)S(1)}, bf16[64,1152]{1,0:T(8,128)(2,1)S(1)}, u32[]{:S(2)}, u32[]{:S(2)}) collective-permute-start(bf16[64,1152]{1,0:T(8,128)(2,1)S(1)} %add.92), channel_id=1, source_target_pairs={{0,8},{8,0},{16,24},{24,16},{1,9},{9,1},{17,25},{25,17},{2,10},{10... | collective-permute-start | bytes 442376 | tf_op jit(solution)/shard_map/ppermute | solution.py:264
  71.6 2.0 %fusion.3 = f32[1024,512]{1,0:T(8,128)S(1)} fusion(bf16[1024,512]{1,0:T(8,128)(2,1)} %copy-done.16, bf16[512,512]{1,0:T(8,128)(2,1)S(1)} %copy-done), kind=kOutput, calls=%fused_computation.20 | convolution fusion | flops 536870912 | bytes 3670016 | tf_op jit(solution)/shard_map/dot_general | solution.py:17
  73.6 2.3 %collective-permute-done.12 = bf16[64,512]{1,0:T(8,128)(2,1)S(1)} collective-permute-done((bf16[64,512]{1,0:T(8,128)(2,1)S(1)}, bf16[64,512]{1,0:T(8,128)(2,1)S(1)}, u32[]{:S(2)}, u32[]{:S(2)}) %collective-permute-start.12) | collective-permute-done | bytes 65568 | tf_op jit(solution)/shard_map/ppermute | solution.py:264
  75.9 1.1 %collective-permute-start.13 = (bf16[64,512]{1,0:T(8,128)(2,1)S(1)}, bf16[64,512]{1,0:T(8,128)(2,1)S(1)}, u32[]{:S(2)}, u32[]{:S(2)}) collective-permute-start(bf16[64,512]{1,0:T(8,128)(2,1)S(1)} %add.89), channel_id=1, source_target_pairs={{0,16},{8,24},{16,0},{24,8},{1,17},{9,25},{17,1},{25,9},{2,18},{10... | collective-permute-start | bytes 196616 | tf_op jit(solution)/shard_map/ppermute | solution.py:264
  77.1 1.4 %add_convert_fusion = bf16[1024,512]{1,0:T(8,128)(2,1)} fusion(f32[1024,512]{1,0:T(8,128)S(1)} %fusion.3, bf16[64,1024]{1,0:T(8,128)(2,1)S(1)} %get-tuple-element.24, bf16[512,64]{0,1:T(8,128)(2,1)S(1)} %copy-done.8), kind=kOutput, calls=%fused_computation | convolution fusion | flops 68157440 | bytes 3342336 | tf_op jit(solution)/shard_map/dot_general | solution.py:17
  78.6 1.7 %collective-permute-done.13 = bf16[64,512]{1,0:T(8,128)(2,1)S(1)} collective-permute-done((bf16[64,512]{1,0:T(8,128)(2,1)S(1)}, bf16[64,512]{1,0:T(8,128)(2,1)S(1)}, u32[]{:S(2)}, u32[]{:S(2)}) %collective-permute-start.13) | collective-permute-done | bytes 65568 | tf_op jit(solution)/shard_map/ppermute | solution.py:264
  80.3 1.5 %collective-permute-start.14 = (bf16[128,512]{1,0:T(8,128)(2,1)S(1)}, bf16[128,512]{1,0:T(8,128)(2,1)S(1)}, u32[]{:S(2)}, u32[]{:S(2)}) collective-permute-start(bf16[128,512]{1,0:T(8,128)(2,1)S(1)} %maximum_select_fusion.2), channel_id=1, source_target_pairs={{0,8},{8,0},{16,24},{24,16},{1,9},{9,1},{17,25},{25,17},{2,10},{10... | collective-permute-start | bytes 393224 | tf_op jit(solution)/shard_map/ppermute | solution.py:264
  81.8 3.5 %collective-permute-done.14 = bf16[128,512]{1,0:T(8,128)(2,1)S(1)} collective-permute-done((bf16[128,512]{1,0:T(8,128)(2,1)S(1)}, bf16[128,512]{1,0:T(8,128)(2,1)S(1)}, u32[]{:S(2)}, u32[]{:S(2)}) %collective-permute-start.14) | collective-permute-done | bytes 131104 | tf_op jit(solution)/shard_map/ppermute | solution.py:264
  87.0 1.2 %fusion = f32[512,512]{1,0:T(8,128)} fusion(bf16[256,512]{1,0:T(8,128)(2,1)S(1)} %maximum_select_fusion.1, bf16[256,512]{1,0:T(8,128)(2,1)S(1)} %collective-permute-done.15, pred[]{:T(512)S(6)} %eq.16), kind=kLoop, calls=%fused_computation.4 | loop fusion | flops 2621440 | bytes 1572865 | tf_op jit(solution)/shard_map/convert_element_type | solution.py:351
  (75 shorter events, 11.1 us)
Async XLA Ops:
  0.6 11.6 %copy-start = (bf16[512,512]{1,0:T(8,128)(2,1)S(1)}, bf16[512,512]{1,0:T(8,128)(2,1)}, u32[]{:S(2)}) copy-start(bf16[512,512]{1,0:T(8,128)(2,1)} %param.16) | copy-start | bytes 1572868
  0.6 1.3 %copy-start.1 = (bf16[1024,512]{1,0:T(8,128)(2,1)S(1)}, bf16[1024,512]{1,0:T(8,128)(2,1)}, u32[]{:S(2)}) copy-start(bf16[1024,512]{1,0:T(8,128)(2,1)} %embed_ref.3) | copy-start | bytes 3145732
  1.9 0.8 copy-start.7
  4.8 14.6 %collective-permute-start = (bf16[64,128]{1,0:T(8,128)(2,1)}, bf16[64,128]{1,0:T(8,128)(2,1)S(1)}, u32[]{:S(2)}, u32[]{:S(2)}) collective-permute-start(bf16[64,128]{1,0:T(8,128)(2,1)} %get-tuple-element.17), channel_id=1, source_target_pairs={{0,8},{8,16},{16,24},{24,0},{1,9},{9,17},{17,25},{25,1},{2,10},{10... | collective-permute-start | bytes 49160 | tf_op jit(solution)/shard_map/ppermute | solution.py:260
  7.7 11.6 %collective-permute-start.1 = (bf16[64,128]{1,0:T(8,128)(2,1)}, bf16[64,128]{1,0:T(8,128)(2,1)}, u32[]{:S(2)}, u32[]{:S(2)}) collective-permute-start(bf16[64,128]{1,0:T(8,128)(2,1)} %get-tuple-element.18), channel_id=1, source_target_pairs={{0,24},{8,0},{16,8},{24,16},{1,25},{9,1},{17,9},{25,17},{2,26},{10... | collective-permute-start | bytes 49160 | tf_op jit(solution)/shard_map/ppermute | solution.py:260
  8.7 10.7 %collective-permute-start.2 = (bf16[64,128]{1,0:T(8,128)(2,1)}, bf16[64,128]{1,0:T(8,128)(2,1)}, u32[]{:S(2)}, u32[]{:S(2)}) collective-permute-start(bf16[64,128]{1,0:T(8,128)(2,1)} %get-tuple-element.19), channel_id=1, source_target_pairs={{0,1},{1,2},{2,3},{3,4},{4,5},{5,6},{6,7},{7,0},{8,9},{9,10},{10,1... | collective-permute-start | bytes 49160 | tf_op jit(solution)/shard_map/ppermute | solution.py:260
  8.7 10.7 %collective-permute-start.3 = (bf16[64,128]{1,0:T(8,128)(2,1)}, bf16[64,128]{1,0:T(8,128)(2,1)}, u32[]{:S(2)}, u32[]{:S(2)}) collective-permute-start(bf16[64,128]{1,0:T(8,128)(2,1)} %get-tuple-element.20), channel_id=1, source_target_pairs={{0,7},{1,0},{2,1},{3,2},{4,3},{5,4},{6,5},{7,6},{8,15},{9,8},{10,9... | collective-permute-start | bytes 49160 | tf_op jit(solution)/shard_map/ppermute | solution.py:260
  12.2 3.9 %copy-start.2 = (bf16[1024,512]{1,0:T(8,128)(2,1)S(1)}, bf16[1024,512]{1,0:T(8,128)(2,1)}, u32[]{:S(2)}) copy-start(bf16[1024,512]{1,0:T(8,128)(2,1)} %embed_ref.3) | copy-start | bytes 3145732
  15.1 1.0 %copy-start.16 = (bf16[1024,512]{1,0:T(8,128)(2,1)}, bf16[1024,512]{1,0:T(8,128)(2,1)S(1)}, u32[]{:S(2)}) copy-start(bf16[1024,512]{1,0:T(8,128)(2,1)S(1)} %multiply_convert_fusion) | copy-start | bytes 3145732
  16.1 3.3 %copy-start.3 = (bf16[1024,512]{1,0:T(8,128)(2,1)S(1)}, bf16[1024,512]{1,0:T(8,128)(2,1)}, u32[]{:S(2)}) copy-start(bf16[1024,512]{1,0:T(8,128)(2,1)} %cotangent_ref.1) | copy-start | bytes 3145732
  16.1 3.3 %copy-start.4 = (bf16[16,16,1024]{2,1,0:T(8,128)(2,1)S(1)}, bf16[16,16,1024]{2,1,0:T(8,128)(2,1)}, u32[]{:S(2)}) copy-start(bf16[16,16,1024]{2,1,0:T(8,128)(2,1)} %param.12) | copy-start | bytes 1572868
  19.3 33.0 %collective-permute-start.8 = (bf16[256,512]{1,0:T(8,128)(2,1)}, bf16[256,512]{1,0:T(8,128)(2,1)}, u32[]{:S(2)}, u32[]{:S(2)}) collective-permute-start(bf16[256,512]{1,0:T(8,128)(2,1)} %dynamic-slice_bitcast_fusion), channel_id=1, source_target_pairs={{0,1},{1,0},{2,3},{3,2},{4,5},{5,4},{6,7},{7,6},{8,9},{9,8},{10,11... | collective-permute-start | bytes 786440 | tf_op jit(solution)/shard_map/ppermute | solution.py:264
  19.4 0.8 copy-start.10
  40.1 3.9 %collective-permute-start.4 = (bf16[64,128]{1,0:T(8,128)(2,1)S(1)}, bf16[64,128]{1,0:T(8,128)(2,1)S(1)}, u32[]{:S(2)}, u32[]{:S(2)}) collective-permute-start(bf16[64,128]{1,0:T(8,128)(2,1)S(1)} %get-tuple-element.37), channel_id=1, source_target_pairs={{0,24},{8,0},{16,8},{24,16},{1,25},{9,1},{17,9},{25,17},{2,26},{10... | collective-permute-start | bytes 49160 | tf_op jit(solution)/shard_map/ppermute | solution.py:260
  42.2 4.6 %collective-permute-start.5 = (bf16[64,128]{1,0:T(8,128)(2,1)S(1)}, bf16[64,128]{1,0:T(8,128)(2,1)S(1)}, u32[]{:S(2)}, u32[]{:S(2)}) collective-permute-start(bf16[64,128]{1,0:T(8,128)(2,1)S(1)} %get-tuple-element.36), channel_id=1, source_target_pairs={{0,8},{8,16},{16,24},{24,0},{1,9},{9,17},{17,25},{25,1},{2,10},{10... | collective-permute-start | bytes 49160 | tf_op jit(solution)/shard_map/ppermute | solution.py:260
  42.2 4.6 %collective-permute-start.6 = (bf16[64,128]{1,0:T(8,128)(2,1)S(1)}, bf16[64,128]{1,0:T(8,128)(2,1)S(1)}, u32[]{:S(2)}, u32[]{:S(2)}) collective-permute-start(bf16[64,128]{1,0:T(8,128)(2,1)S(1)} %get-tuple-element.35), channel_id=1, source_target_pairs={{0,7},{1,0},{2,1},{3,2},{4,3},{5,4},{6,5},{7,6},{8,15},{9,8},{10,9... | collective-permute-start | bytes 49160 | tf_op jit(solution)/shard_map/ppermute | solution.py:260
  44.0 5.0 %collective-permute-start.7 = (bf16[64,128]{1,0:T(8,128)(2,1)S(1)}, bf16[64,128]{1,0:T(8,128)(2,1)S(1)}, u32[]{:S(2)}, u32[]{:S(2)}) collective-permute-start(bf16[64,128]{1,0:T(8,128)(2,1)S(1)} %get-tuple-element.34), channel_id=1, source_target_pairs={{0,1},{1,2},{2,3},{3,4},{4,5},{5,6},{6,7},{7,0},{8,9},{9,10},{10,1... | collective-permute-start | bytes 49160 | tf_op jit(solution)/shard_map/ppermute | solution.py:260
  49.0 1.0 %copy-start.6 = (f32[64,1024]{1,0:T(8,128)S(1)}, f32[64,1024]{1,0:T(8,128)}, u32[]{:S(2)}) copy-start(f32[64,1024]{1,0:T(8,128)} %copy-done.5) | copy-start | bytes 786436
  50.6 1.8 %copy-start.17 = (bf16[512,512]{0,1:T(8,128)(2,1)S(1)}, bf16[512,512]{0,1:T(8,128)(2,1)}, u32[]{:S(2)}) copy-start(bf16[512,512]{0,1:T(8,128)(2,1)} %convolution_convert_fusion) | copy-start | bytes 1572868
  52.3 6.8 %collective-permute-start.16 = (bf16[64,1152]{1,0:T(8,128)(2,1)S(1)}, bf16[64,1152]{1,0:T(8,128)(2,1)S(1)}, u32[]{:S(2)}, u32[]{:S(2)}) collective-permute-start(bf16[64,1152]{1,0:T(8,128)(2,1)S(1)} %constant_dynamic-update-slice_fusion), channel_id=1, source_target_pairs={{0,4},{1,5},{2,6},{3,7},{4,0},{5,1},{6,2},{7,3},{8,12},{9,13},{10,... | collective-permute-start | bytes 442376 | tf_op jit(solution)/shard_map/ppermute | solution.py:264
  53.4 5.8 %collective-permute-start.9 = (bf16[128,512]{1,0:T(8,128)(2,1)S(1)}, bf16[128,512]{1,0:T(8,128)(2,1)S(1)}, u32[]{:S(2)}, u32[]{:S(2)}) collective-permute-start(bf16[128,512]{1,0:T(8,128)(2,1)S(1)} %constant_dynamic-slice_fusion.1), channel_id=1, source_target_pairs={{0,8},{8,0},{16,24},{24,16},{1,9},{9,1},{17,25},{25,17},{2,10},{10... | collective-permute-start | bytes 393224 | tf_op jit(solution)/shard_map/ppermute | solution.py:264
  59.1 5.2 %collective-permute-start.17 = (bf16[64,1152]{1,0:T(8,128)(2,1)S(1)}, bf16[64,1152]{1,0:T(8,128)(2,1)S(1)}, u32[]{:S(2)}, u32[]{:S(2)}) collective-permute-start(bf16[64,1152]{1,0:T(8,128)(2,1)S(1)} %add.90), channel_id=1, source_target_pairs={{0,2},{1,3},{2,0},{3,1},{4,6},{5,7},{6,4},{7,5},{8,10},{9,11},{10,... | collective-permute-start | bytes 442376 | tf_op jit(solution)/shard_map/ppermute | solution.py:264
  59.3 6.7 %collective-permute-start.10 = (bf16[64,512]{1,0:T(8,128)(2,1)S(1)}, bf16[64,512]{1,0:T(8,128)(2,1)S(1)}, u32[]{:S(2)}, u32[]{:S(2)}) collective-permute-start(bf16[64,512]{1,0:T(8,128)(2,1)S(1)} %constant_dynamic-slice_fusion), channel_id=1, source_target_pairs={{0,16},{8,24},{16,0},{24,8},{1,17},{9,25},{17,1},{25,9},{2,18},{10... | collective-permute-start | bytes 196616 | tf_op jit(solution)/shard_map/ppermute | solution.py:264
  64.4 5.2 %collective-permute-start.18 = (bf16[64,1152]{1,0:T(8,128)(2,1)S(1)}, bf16[64,1152]{1,0:T(8,128)(2,1)S(1)}, u32[]{:S(2)}, u32[]{:S(2)}) collective-permute-start(bf16[64,1152]{1,0:T(8,128)(2,1)S(1)} %add.91), channel_id=1, source_target_pairs={{0,16},{8,24},{16,0},{24,8},{1,17},{9,25},{17,1},{25,9},{2,18},{10... | collective-permute-start | bytes 442376 | tf_op jit(solution)/shard_map/ppermute | solution.py:264
  66.0 5.5 %collective-permute-start.11 = (bf16[64,512]{1,0:T(8,128)(2,1)S(1)}, bf16[64,512]{1,0:T(8,128)(2,1)S(1)}, u32[]{:S(2)}, u32[]{:S(2)}) collective-permute-start(bf16[64,512]{1,0:T(8,128)(2,1)S(1)} %dynamic-slice_add_fusion.1), channel_id=1, source_target_pairs={{0,4},{1,5},{2,6},{3,7},{4,0},{5,1},{6,2},{7,3},{8,12},{9,13},{10,... | collective-permute-start | bytes 196616 | tf_op jit(solution)/shard_map/ppermute | solution.py:264
  69.6 7.4 %collective-permute-start.19 = (bf16[64,1152]{1,0:T(8,128)(2,1)S(1)}, bf16[64,1152]{1,0:T(8,128)(2,1)S(1)}, u32[]{:S(2)}, u32[]{:S(2)}) collective-permute-start(bf16[64,1152]{1,0:T(8,128)(2,1)S(1)} %add.92), channel_id=1, source_target_pairs={{0,8},{8,0},{16,24},{24,16},{1,9},{9,1},{17,25},{25,17},{2,10},{10... | collective-permute-start | bytes 442376 | tf_op jit(solution)/shard_map/ppermute | solution.py:264
  71.5 5.6 %copy-start.8 = (bf16[512,64]{0,1:T(8,128)(2,1)S(1)}, bf16[512,64]{0,1:T(8,128)(2,1)}, u32[]{:S(2)}) copy-start(bf16[512,64]{0,1:T(8,128)(2,1)} %param.17) | copy-start | bytes 196612
  71.6 4.3 %collective-permute-start.12 = (bf16[64,512]{1,0:T(8,128)(2,1)S(1)}, bf16[64,512]{1,0:T(8,128)(2,1)S(1)}, u32[]{:S(2)}, u32[]{:S(2)}) collective-permute-start(bf16[64,512]{1,0:T(8,128)(2,1)S(1)} %add.88), channel_id=1, source_target_pairs={{0,2},{1,3},{2,0},{3,1},{4,6},{5,7},{6,4},{7,5},{8,10},{9,11},{10,... | collective-permute-start | bytes 196616 | tf_op jit(solution)/shard_map/ppermute | solution.py:264
  75.9 4.3 %collective-permute-start.13 = (bf16[64,512]{1,0:T(8,128)(2,1)S(1)}, bf16[64,512]{1,0:T(8,128)(2,1)S(1)}, u32[]{:S(2)}, u32[]{:S(2)}) collective-permute-start(bf16[64,512]{1,0:T(8,128)(2,1)S(1)} %add.89), channel_id=1, source_target_pairs={{0,16},{8,24},{16,0},{24,8},{1,17},{9,25},{17,1},{25,9},{2,18},{10... | collective-permute-start | bytes 196616 | tf_op jit(solution)/shard_map/ppermute | solution.py:264
  77.1 4.7 %collective-permute-start.20 = (bf16[64,1152]{1,0:T(8,128)(2,1)S(1)}, bf16[64,1152]{1,0:T(8,128)(2,1)S(1)}, u32[]{:S(2)}, u32[]{:S(2)}) collective-permute-start(bf16[64,1152]{1,0:T(8,128)(2,1)S(1)} %add.93), channel_id=1, source_target_pairs={{0,1},{1,0},{2,3},{3,2},{4,5},{5,4},{6,7},{7,6},{8,9},{9,8},{10,11... | collective-permute-start | bytes 442376 | tf_op jit(solution)/shard_map/ppermute | solution.py:264
  80.3 5.0 %collective-permute-start.14 = (bf16[128,512]{1,0:T(8,128)(2,1)S(1)}, bf16[128,512]{1,0:T(8,128)(2,1)S(1)}, u32[]{:S(2)}, u32[]{:S(2)}) collective-permute-start(bf16[128,512]{1,0:T(8,128)(2,1)S(1)} %maximum_select_fusion.2), channel_id=1, source_target_pairs={{0,8},{8,0},{16,24},{24,16},{1,9},{9,1},{17,25},{25,17},{2,10},{10... | collective-permute-start | bytes 393224 | tf_op jit(solution)/shard_map/ppermute | solution.py:264
  85.4 1.6 %collective-permute-start.15 = (bf16[256,512]{1,0:T(8,128)(2,1)S(1)}, bf16[256,512]{1,0:T(8,128)(2,1)S(1)}, u32[]{:S(2)}, u32[]{:S(2)}) collective-permute-start(bf16[256,512]{1,0:T(8,128)(2,1)S(1)} %maximum_select_fusion.1), channel_id=1, source_target_pairs={{0,1},{1,0},{2,3},{3,2},{4,5},{5,4},{6,7},{7,6},{8,9},{9,8},{10,11... | collective-permute-start | bytes 786440 | tf_op jit(solution)/shard_map/ppermute | solution.py:264
  (7 other events, 4.9 us)

commit v2 on v1

v2 whole, which is shorter than its diff:
```python
import jax
import jax.numpy as jnp
from jax import lax
from jax.experimental import pallas as pl
from jax.experimental.pallas import tpu as pltpu
from jax.sharding import PartitionSpec as P

AXES = ("slab", "brick")
LANES = 256
F32 = jnp.float32
BF16 = jnp.bfloat16
NN = ((1,), (0,))
NT = ((1,), (1,))
TN = ((0,), (0,))
VMEM = pl.BlockSpec(memory_space=pltpu.VMEM)
HBM = pl.BlockSpec(memory_space=pltpu.HBM)


def dot(a, b, dims, precision=None):
    return lax.dot_general(a, b, (dims, ((), ())), precision=precision, preferred_element_type=F32)


def like(*arrays):
    return [jax.ShapeDtypeStruct(a.shape, a.dtype) for a in arrays]


def limits(mib):
    return pltpu.CompilerParams(vmem_limit_bytes=mib * 2**20)


def sigmoid(value):
    return 1.0 / (1.0 + jnp.exp(-value))


def silu_grad(value):
    sig = sigmoid(value)
    return sig * (1.0 + value * (1.0 - sig))


def parity(axis):
    return lax.axis_index(axis) % 2 == 1


def onehot(low):
    rows = lax.broadcasted_iota(jnp.int32, (LANES, low.shape[1]), 0).astype(jnp.int16)
    return jnp.where(rows == low.astype(jnp.int16), jnp.ones((), BF16), jnp.zeros((), BF16))


def stacked(table):
    return jnp.concatenate(
        [table[:, g * LANES : (g + 1) * LANES] for g in range(table.shape[1] // LANES)], axis=0
    )


def unstacked(blocks, width):
    return jnp.concatenate(
        [blocks[g * width : (g + 1) * width] for g in range(blocks.shape[0] // width)], axis=1
    )


def chosen(blocks, high, width):
    total = jnp.zeros((width, blocks.shape[1]), F32)
    for g in range(blocks.shape[0] // width):
        total = jnp.where(high == g, blocks[g * width : (g + 1) * width], total)
    return total


def spread(values, high, groups):
    zero = jnp.zeros_like(values)
    return jnp.concatenate([jnp.where(high == g, values, zero) for g in range(groups)], axis=0)


def pair_lists(rows_ref):
    lists = []
    for first, axis in ((0, "slab"), (2, "brick")):
        odd = parity(axis)
        up, down = rows_ref[first : first + 1, :], rows_ref[first + 1 : first + 2, :]
        lists += [jnp.where(odd, down, up), jnp.where(odd, up, down)]
    return lists


def paired(value, axis, first):
    count = lax.axis_size(axis)
    pairs = []
    for i in range(first, count, 2):
        j = (i + 1) % count
        pairs += [(i, j), (j, i)]
    return lax.ppermute(value, axis, pairs)


def pair_exchange(values):
    spots = (("slab", 0), ("slab", 1), ("brick", 0), ("brick", 1))
    sent = {k: paired(values[k], *spots[k]) for k in (3, 1, 0, 2)}
    return [sent[k] for k in range(4)]


def project_kernel(
    embed_ref, down_ref, rows_ref, pre_ref, proj_ref, s0, s1, s2, s3, embed_v, down_v, rows_v, sems
):
    copies = [
        pltpu.make_async_copy(source, target, sems.at[i])
        for i, (source, target) in enumerate(
            ((embed_ref, embed_v), (down_ref, down_v), (rows_ref, rows_v))
        )
    ]
    for copy in copies:
        copy.start()
    for copy in copies:
        copy.wait()
    pre = dot(down_v[...], embed_v[...], NT)
    pre_ref[...] = pre
    proj = (pre * sigmoid(pre)).astype(BF16)
    proj_ref[...] = proj
    table = stacked(proj)
    for index, send_ref in zip(pair_lists(rows_v), (s0, s1, s2, s3)):
        picked = dot(table, onehot(index & (LANES - 1)), NN)
        send_ref[...] = chosen(picked, index // LANES, proj.shape[0]).astype(BF16)


def project(embed, down_t, outgoing):
    rows, width = embed.shape[0], down_t.shape[0]
    ghost = jax.ShapeDtypeStruct((width, outgoing.shape[1]), BF16)
    return pl.pallas_call(
        project_kernel,
        in_specs=[HBM] * 3,
        out_specs=[VMEM] * 9,
        out_shape=[
            jax.ShapeDtypeStruct((width, rows), F32),
            jax.ShapeDtypeStruct((width, rows), BF16),
        ]
        + [ghost] * 4
        + like(embed, down_t, outgoing),
        scratch_shapes=[pltpu.SemaphoreType.DMA((3,))],
        compiler_params=limits(12),
        name="project",
    )(embed, down_t, outgoing)


def residual_kernel(embed_ref, weight_ref, *refs):
    count = (len(refs) - 5) // 2
    sources, targets = refs[:count], refs[count : 2 * count]
    dres_ref, mine_ref, other_ref, grad_ref, sems = refs[2 * count :]
    copies = [
        pltpu.make_async_copy(source, target, sems.at[i])
        for i, (source, target) in enumerate(zip(sources, targets))
    ]
    for copy in copies:
        copy.start()
    copies[0].wait()
    cotangent_v = targets[0]
    rows = embed_ref.shape[0]
    block = min(rows, LANES)
    for start in range(0, rows, block):
        at = pl.ds(start, block)
        res_pre = dot(embed_ref[at, :], weight_ref[...], NN)
        dres_ref[at, :] = (cotangent_v[at, :].astype(F32) * silu_grad(res_pre)).astype(BF16)
    grad_ref[...] = dot(embed_ref[...], dres_ref[...], TN).astype(BF16)
    half = grad_ref.shape[0] // 2
    upper = lax.axis_index("brick") % 2
    mine_ref[...] = grad_ref[pl.ds(upper * half, half), :]
    other_ref[...] = grad_ref[pl.ds((1 - upper) * half, half), :]
    for copy in copies[1:]:
        copy.wait()


def residual(embed, weight, *staged):
    inner = weight.shape[0]
    half = jax.ShapeDtypeStruct((inner // 2, weight.shape[1]), BF16)
    out_shape = like(*staged) + like(embed) + [half] * 2
    return pl.pallas_call(
        residual_kernel,
        in_specs=[VMEM] * 2 + [HBM] * len(staged),
        out_specs=[VMEM] * len(out_shape),
        out_shape=out_shape,
        scratch_shapes=[pltpu.VMEM(weight.shape, BF16), pltpu.SemaphoreType.DMA((len(staged),))],
        compiler_params=limits(16),
        name="residual",
    )(embed, weight, *staged)


def triplet_kernel(
    proj_ref,
    g0_ref,
    g1_ref,
    g2_ref,
    g3_ref,
    basis_ref,
    index_ref,
    count_ref,
    up_ref,
    cotangent_ref,
    bw_ref,
    own_ref,
    t0_ref,
    t1_ref,
    t2_ref,
    t3_ref,
    grads_ref,
    table_ref,
    weight_ref,
    hot_ref,
    picked_ref,
    dw_ref,
    tsum_ref,
    dt_ref,
    acc_ref,
):
    width, rows = proj_ref.shape
    trips = index_ref.shape[0]
    nbasis = bw_ref.shape[0]
    own_groups = rows // LANES
    blocks = []
    for a_ref, b_ref, axis in ((g0_ref, g1_ref, "slab"), (g2_ref, g3_ref, "brick")):
        odd = parity(axis)
        a, b = a_ref[...], b_ref[...]
        blocks += [jnp.where(odd, a, b), jnp.where(odd, b, a)]
    table_ref[: own_groups * width, :] = stacked(proj_ref[...])
    table_ref[own_groups * width :, :] = stacked(jnp.concatenate(blocks, axis=1))
    groups = table_ref.shape[0] // width
    tiles = rows // LANES

    span = trips * nbasis
    fold = jnp.where(
        lax.broadcasted_iota(jnp.int32, (nbasis, span), 1) % nbasis
        == lax.broadcasted_iota(jnp.int32, (nbasis, span), 0),
        1.0,
        0.0,
    )
    wide = dot(bw_ref[...], fold.astype(BF16), TN).astype(BF16)
    own_slot = lax.broadcasted_iota(jnp.int32, (trips, width, span), 0) == (
        lax.broadcasted_iota(jnp.int32, (trips, width, span), 2) // nbasis
    )
    diagonal = jnp.where(own_slot, wide[None], jnp.zeros((), BF16)).reshape(trips * width, span)
    weight_ref[...] = dot(diagonal, basis_ref[...], NN)

    tsum_ref[...] = jnp.zeros_like(tsum_ref)

    def lookup(j, t):
        at = pl.ds(t * LANES, LANES)
        index = index_ref[pl.ds(j, 1), at]
        high = jnp.where(j < count_ref[:, at], index // LANES, -1)
        return at, index & (LANES - 1), high

    def forward(j, carry):
        for t in range(tiles):
            at, low, high = lookup(j, t)
            hot = onehot(low)
            hot_ref[j, :, at] = hot
            picked = chosen(dot(table_ref[...], hot, NN), high, width)
            picked_ref[j, :, at] = picked.astype(BF16)
            tsum_ref[:, at] += weight_ref[pl.ds(j * width, width), at] * picked
        return carry

    lax.fori_loop(0, trips, forward, 0, unroll=8)

    tsum = tsum_ref[...]
    sig = sigmoid(tsum)
    act = (tsum * sig).astype(BF16)
    cotangent = cotangent_ref[...]
    inner = cotangent.shape[1]
    grads_ref[:, :inner] = dot(act, cotangent, NN).astype(BF16)
    dsum = dot(up_ref[...], cotangent, NT)
    dt_ref[...] = dsum * (sig * (1.0 + tsum * (1.0 - sig)))
    acc_ref[...] = jnp.zeros_like(acc_ref)

    def backward(j, carry):
        parts = []
        for t in range(tiles):
            at, low, high = lookup(j, t)
            dt = dt_ref[:, at]
            dw_ref[pl.ds(j * width, width), at] = (dt * picked_ref[j, :, at].astype(F32)).astype(BF16)
            terms = (dt * weight_ref[pl.ds(j * width, width), at]).astype(BF16)
            parts.append(spread(terms, high, groups))
        acc_ref[...] += dot(jnp.concatenate(parts, axis=1), hot_ref[j], NT)
        return carry

    lax.fori_loop(0, trips, backward, 0, unroll=8)

    own_ref[...] = unstacked(acc_ref[: own_groups * width, :], width)
    ghost_terms = unstacked(acc_ref[own_groups * width :, :], width).astype(BF16)
    ghost = t0_ref.shape[1]
    for first, axis, a_ref, b_ref in ((0, "slab", t0_ref, t1_ref), (2, "brick", t2_ref, t3_ref)):
        odd = parity(axis)
        prev = ghost_terms[:, first * ghost : (first + 1) * ghost]
        following = ghost_terms[:, (first + 1) * ghost : (first + 2) * ghost]
        a_ref[...] = jnp.where(odd, prev, following)
        b_ref[...] = jnp.where(odd, following, prev)
    full = dot(dw_ref[...], basis_ref[...], NT).reshape(trips, width, span)
    kept = jnp.sum(jnp.where(own_slot, full, 0.0), axis=0)
    folded = dot(kept, fold, NT, lax.Precision.HIGHEST)
    pad = grads_ref.shape[1] - inner - nbasis
    grads_ref[:, inner:] = jnp.concatenate(
        [folded, jnp.zeros((width, pad), F32)], axis=1
    ).astype(BF16)


def triplets(proj, ghosts, basis, index, count, up_weight, cotangent, basis_weight):
    width, rows = proj.shape
    trips = index.shape[0]
    ghost = ghosts[0].shape[1]
    inner = cotangent.shape[1]
    groups = (rows + 4 * ghost) // LANES
    operands = (proj, *ghosts, basis, index, count, up_weight, cotangent, basis_weight)
    out_shape = (
        [jax.ShapeDtypeStruct((width, rows), F32)]
        + like(*ghosts)
        + [jax.ShapeDtypeStruct((width, inner + 128), BF16)]
    )
    return pl.pallas_call(
        triplet_kernel,
        in_specs=[VMEM] * len(operands),
        out_specs=[VMEM] * len(out_shape),
        out_shape=out_shape,
        scratch_shapes=[
            pltpu.VMEM((groups * width, LANES), BF16),
            pltpu.VMEM((trips * width, rows), F32),
            pltpu.VMEM((trips, LANES, rows), BF16),
            pltpu.VMEM((trips, width, rows), BF16),
            pltpu.VMEM((trips * width, rows), BF16),
            pltpu.VMEM((width, rows), F32),
            pltpu.VMEM((width, rows), F32),
            pltpu.VMEM((groups * width, LANES), F32),
        ],
        compiler_params=limits(28),
        name="triplets",
    )(*operands)


def collect_kernel(
    own_ref,
    b0_ref,
    b1_ref,
    b2_ref,
    b3_ref,
    rows_ref,
    pre_ref,
    embed_ref,
    grads_ref,
    dpre_ref,
    mine_ref,
    other_ref,
    all_ref,
):
    width, rows = own_ref.shape
    groups = rows // LANES
    acc = jnp.zeros((groups * width, LANES), F32)
    for index, back_ref in zip(pair_lists(rows_ref), (b0_ref, b1_ref, b2_ref, b3_ref)):
        acc += dot(spread(back_ref[...], index // LANES, groups), onehot(index & (LANES - 1)), NT)
    dproj = own_ref[...] + unstacked(acc, width)
    dpre = (dproj * silu_grad(pre_ref[...])).astype(BF16)
    dpre_ref[...] = dpre
    inner = embed_ref.shape[1]
    all_ref[:, :inner] = dot(dpre, embed_ref[...], NN).astype(BF16)
    all_ref[:, inner:] = grads_ref[...]
    half = width // 2
    upper = lax.axis_index("brick") % 2
    mine_ref[...] = all_ref[pl.ds(upper * half, half), :]
    other_ref[...] = all_ref[pl.ds((1 - upper) * half, half), :]


def collect(own, backs, outgoing, pre, embed, grads):
    width = own.shape[0]
    total = embed.shape[1] + grads.shape[1]
    half = jax.ShapeDtypeStruct((width // 2, total), BF16)
    operands = (own, *backs, outgoing, pre, embed, grads)
    return pl.pallas_call(
        collect_kernel,
        in_specs=[VMEM] * len(operands),
        out_specs=[VMEM] * 3,
        out_shape=[jax.ShapeDtypeStruct(own.shape, BF16), half, half],
        scratch_shapes=[pltpu.VMEM((width, total), BF16)],
        compiler_params=limits(12),
        name="collect",
    )(*operands)


def edge_kernel(dres_ref, weight_ref, dpre_ref, down_ref, out_ref):
    rows = dres_ref.shape[0]
    block = min(rows, LANES)
    for start in range(0, rows, block):
        at = pl.ds(start, block)
        res_term = dot(dres_ref[at, :], weight_ref[...], NT)
        out_ref[at, :] = (res_term + dot(dpre_ref[:, at], down_ref[...], TN)).astype(BF16)


def edge_gradient(dres, weight, dpre, down_t):
    rows, inner = dres.shape
    return pl.pallas_call(
        edge_kernel,
        in_specs=[VMEM] * 4,
        out_specs=VMEM,
        out_shape=jax.ShapeDtypeStruct((rows, inner), BF16),
        compiler_params=limits(12),
        cost_estimate=pl.CostEstimate(
            flops=2 * rows * inner * (inner + down_t.shape[0]),
            bytes_accessed=4 * rows * inner,
            transcendentals=0,
        ),
        name="edge_gradient",
    )(dres, weight, dpre, down_t)


def finish_kernel(offsets, *refs):
    count = len(offsets)
    kept, sent = refs[:count], refs[count : 2 * count]
    mine_ref, other_ref, residual_ref, down_ref, up_ref, basis_ref, all_ref = refs[2 * count :]
    upper = lax.axis_index("brick") % 2
    slab = lax.axis_index("slab")
    step = kept[0].shape[0]
    half = residual_ref.shape[0] // 2
    for offset, kept_ref, sent_ref in zip(offsets, kept, sent):
        place = (slab ^ offset) * step
        residual_ref[pl.ds(upper * half + place, step), :] = kept_ref[...].astype(F32)
        residual_ref[pl.ds((1 - upper) * half + place, step), :] = sent_ref[...].astype(F32)
    rows, inner = mine_ref.shape[0], down_ref.shape[1]
    all_ref[pl.ds(upper * rows, rows), :] = mine_ref[...].astype(F32)
    all_ref[pl.ds((1 - upper) * rows, rows), :] = other_ref[...].astype(F32)
    down_ref[...] = all_ref[:, :inner]
    up_ref[...] = all_ref[:, inner : 2 * inner]
    basis_ref[...] = all_ref[:, 2 * inner :].T[: basis_ref.shape[0], :]


def finish(kept, sent, mine, other, inner, nbasis):
    offsets = sorted(kept)
    width = 2 * mine.shape[0]
    operands = [kept[o] for o in offsets] + [sent[o] for o in offsets] + [mine, other]
    return pl.pallas_call(
        lambda *refs: finish_kernel(offsets, *refs),
        in_specs=[VMEM] * len(operands),
        out_specs=[VMEM] * 4,
        out_shape=[
            jax.ShapeDtypeStruct((inner, inner), F32),
            jax.ShapeDtypeStruct((width, inner), F32),
            jax.ShapeDtypeStruct((width, inner), F32),
            jax.ShapeDtypeStruct((nbasis, width), F32),
        ],
        scratch_shapes=[pltpu.VMEM((width, mine.shape[1]), F32)],
        compiler_params=limits(12),
        name="finish",
    )(*operands)


def swapped(value, axis, offset):
    return lax.ppermute(value, axis, [(i, i ^ offset) for i in range(lax.axis_size(axis))])


def groups_of(axis, first):
    low, groups = first, []
    while low < lax.axis_size(axis):
        members = min(4, lax.axis_size(axis) // low)
        groups.append((low, members))
        low *= members
    return groups


def total_of(parts):
    return sum(part.astype(F32) for part in parts).astype(BF16)


def scattered_sum(value, axis, low, members):
    digit = (lax.axis_index(axis) // low) % members
    rows = value.shape[0] // members

    def piece(k):
        return lax.dynamic_slice_in_dim(value, (digit ^ k) * rows, rows, 0)

    parts = [swapped(piece(k), axis, k * low) for k in range(members - 1, 0, -1)]
    return total_of([piece(0)] + parts)


def exchanged_sum(values, axis, low, members):
    parts = [[value] for value in values]
    for k in range(members - 1, 0, -1):
        for part, value in zip(parts, values):
            part.append(swapped(value, axis, k * low))
    return [total_of(part) for part in parts]


def shards(
    embed,
    cotangent,
    basis,
    triplet_row_index,
    triplet_slot_count,
    outgoing_edge_rows,
    residual_weight,
    down_weight,
    up_weight,
    basis_weight,
):
    rows, inner = embed.shape
    trips, nbasis = basis.shape[:2]

    pre, proj, *rest = project(embed, down_weight.T, outgoing_edge_rows)
    ghosts = pair_exchange(rest[:4])
    embed_v, down_v, outgoing_v = rest[4:]

    (cotangent_v, basis_v, index_v, count_v, up_v, bw_v, dres, mine, other) = residual(
        embed_v,
        residual_weight,
        cotangent,
        basis.reshape(trips * nbasis, rows),
        triplet_row_index,
        triplet_slot_count.reshape(1, rows),
        up_weight,
        basis_weight,
    )
    share = total_of([mine, swapped(other, "brick", 1)])
    slab_groups = groups_of("slab", 1)
    for low, members in reversed(slab_groups):
        share = scattered_sum(share, "slab", low, members)

    own, *terms, grads = triplets(
        proj, ghosts, basis_v, index_v, count_v, up_v, cotangent_v, bw_v
    )
    backs = pair_exchange(terms)
    dpre, mine, other = collect(own, backs, outgoing_v, pre, embed_v, grads)
    edge_grad = edge_gradient(dres, residual_weight, dpre, down_v)

    mine = total_of([mine, swapped(other, "brick", 1)])
    for low, members in groups_of("brick", 2):
        share, mine = exchanged_sum([share, mine], "brick", low, members)
    pieces = {0: share}
    for low, members in slab_groups:
        received = {}
        for k in range(members - 1, 0, -1):
            for offset, piece in pieces.items():
                received[offset ^ (k * low)] = swapped(piece, "slab", k * low)
        (mine,) = exchanged_sum([mine], "slab", low, members)
        pieces.update(received)
    sent = {offset: swapped(piece, "brick", 1) for offset, piece in pieces.items()}
    residual_grad, down_grad, up_grad, basis_grad = finish(
        pieces, sent, mine, swapped(mine, "brick", 1), inner, nbasis
    )
    return edge_grad, residual_grad, down_grad.T, up_grad, basis_grad


def solution(mesh):
    both = P(AXES, None)
    in_specs = (both, both, P(None, None, AXES), P(None, AXES), P(AXES), P(None, AXES)) + (P(),) * 4
    out_specs = (both, P(), P(), P(), P())
    return jax.shard_map(shards, mesh=mesh, in_specs=in_specs, out_specs=out_specs, check_vma=False)
```

time: 88.7 us -> 72.6 us (0.82)
  waiting for transfers between devices: 23 us -> 9.8 us
  starting transfers between devices: 21.6 us -> 34.4 us
  matrix products: 7.84 us -> 0 us
  local copies, waits for them, and re-layouts: 13.8 us -> 6.96 us
  other arithmetic: 2.55 us -> 1.2 us
    ppermute x21 -> x30, waiting for transfers between devices: 23 us -> 9.8 us  [the longest x22 5.97 us: swapped(): lax.ppermute(value, axis, [(i, i ^ offset) for i in range(lax.axis_size(a...]
    ppermute x21 -> x30, starting transfers between devices: 21.6 us -> 34.4 us  [the longest x22 21.7 us: swapped(): lax.ppermute(value, axis, [(i, i ^ offset) for i in range(lax.axis_size(a...]
    dot_general x4 -> x0, matrix products: 7.84 us -> none  [the longest x3 4.95 us: dot(): lax.dot_general(a, b, (dims, ((), ())), precision=precision, preferred_el...]
    unnamed x38 -> x24, local copies, waits for them, and re-layouts: 10.5 us -> 6.93 us
    dynamic_slice x3 -> x1, local copies, waits for them, and re-layouts: 1.7 us -> 0.02 us  [piece(): return lax.dynamic_slice_in_dim(value, (digit ^ k) * rows, rows, 0)]
    add x9 -> x0, other arithmetic: 1.27 us -> none  [the longest x3 1.08 us: halved(): return mine + swapped(other, *step)]
    concatenate x1 -> x0, local copies, waits for them, and re-layouts: 0.9 us -> none  [shards(): rest = jnp.concatenate([down_grad, grads], axis=1)]
    pallas_call x3 -> x6, Pallas kernels: 18.4 us -> 18.9 us  [the longest x1 10.7 us: triplets(): pl.pallas_call(triplet_kernel, in_specs=[VMEM] * len(operands), out_specs...]
  transfers between devices with their start and end apart: 21 -> 30, of which waited for: 10 -> 7; matrix products, arithmetic and copies ran while one was open for 15% -> 2% of each run, Pallas kernels for 19% -> 20%
where the time goes in v2:
time: 72.6 us; the launch traced here: 72.1 us
  starting transfers between devices  34.4 us (47%)
  Pallas kernels  18.9 us (26%)
  waiting for transfers between devices  9.8 us (13%)
  local copies, waits for them, and re-layouts  6.96 us (10%)
  other arithmetic  1.2 us (2%)
  between operations  0.79 us (1%)
    ppermute x22, starting transfers between devices, swapped(): lax.ppermute(value, axis, [(i, i ^ offset) for i in range(lax.axis_size(a...  21.7 us
    ppermute x8, starting transfers between devices, paired(): return lax.ppermute(value, axis, pairs)  12.7 us
    pallas_call x1, Pallas kernels, triplets(): pl.pallas_call(triplet_kernel, in_specs=[VMEM] * len(operands), out_specs...  10.7 us
    unnamed x24, local copies, waits for them, and re-layouts  6.93 us
    ppermute x22, waiting for transfers between devices, swapped(): lax.ppermute(value, axis, [(i, i ^ offset) for i in range(lax.axis_size(a...  5.97 us
    ppermute x8, waiting for transfers between devices, paired(): return lax.ppermute(value, axis, pairs)  3.83 us
    pallas_call x1, Pallas kernels, residual(): pl.pallas_call(residual_kernel, in_specs=[VMEM] * 2 + [HBM] * len(staged)...  2.72 us
    pallas_call x1, Pallas kernels, edge_gradient(): pl.pallas_call(edge_kernel, in_specs=[VMEM] * 4, out_specs=VMEM, out_shap...  1.98 us
  transfers between devices with their start and end apart: 30, of which 7 were waited for; matrix products, arithmetic and copies ran while one was open for 2% of the time, Pallas kernels for 20%

profile of v2, /device:TPU:0, one launch (start us, length us, event | category | flops | bytes accessed | tf_op | source)
XLA Modules:
  0.0 72.1 jit_solution(5453795409392402327)
XLA Ops:
  0.6 1.2 %copy-done.2 = bf16[1024,512]{1,0:T(8,128)(2,1)S(1)} copy-done((bf16[1024,512]{1,0:T(8,128)(2,1)S(1)}, bf16[1024,512]{1,0:T(8,128)(2,1)}, u32[]{:S(2)}) %copy-start.2) | copy-done | bytes 1048600
  1.9 0.8 %copy-done.4 = bf16[512,64]{0,1:T(8,128)(2,1)S(1)} copy-done((bf16[512,64]{0,1:T(8,128)(2,1)S(1)}, bf16[512,64]{0,1:T(8,128)(2,1)}, u32[]{:S(2)}) %copy-start.4) | copy-done | bytes 65560
  3.4 0.9 %project.1 = (f32[64,1024]{1,0:T(8,128)S(1)}, bf16[64,1024]{1,0:T(8,128)(2,1)S(1)}, bf16[64,128]{1,0:T(8,128)(2,1)S(1)}, bf16[64,128]{1,0:T(8,128)(2,1)S(1)}, bf...) custom-call(bf16[1024,512]{1,0:T(8,128)(2,1)S(1)} %copy-done.2, ...), custom_call_target="tpu_custom_call" | custom-call | tf_op jit(solution)/shard_map/project/pallas_call | solution.py:123
  5.1 1.2 %copy-done.1 = bf16[1024,512]{1,0:T(8,128)(2,1)S(1)} copy-done((bf16[1024,512]{1,0:T(8,128)(2,1)S(1)}, bf16[1024,512]{1,0:T(8,128)(2,1)}, u32[]{:S(2)}) %copy-start.1) | copy-done | bytes 1048600
  6.3 0.8 %copy-done.6 = bf16[64,512]{1,0:T(8,128)(2,1)S(1)} copy-done((bf16[64,512]{1,0:T(8,128)(2,1)S(1)}, bf16[64,512]{1,0:T(8,128)(2,1)}, u32[]{:S(2)}) %copy-start.6) | copy-done | bytes 65560
  7.8 2.7 %residual.1 = (bf16[1024,512]{1,0:T(8,128)(2,1)S(1)}, bf16[256,1024]{1,0:T(8,128)(2,1)S(1)}, s32[16,1024]{1,0:T(8,128)S(1)}, s32[1,1024]{1,0:T(1,128)S(1)}, bf16...) custom-call(bf16[1024,512]{1,0:T(8,128)(2,1)S(1)} %get-tuple-element, ...), custom_call_target="tpu_custom_call" | custom-call | tf_op jit(solution)/shard_map/residual/pallas_call | solution.py:170
  11.1 2.6 %collective-permute-start = (bf16[64,128]{1,0:T(8,128)(2,1)S(1)}, bf16[64,128]{1,0:T(8,128)(2,1)S(1)}, u32[]{:S(2)}, u32[]{:S(2)}) collective-permute-start(bf16[64,128]{1,0:T(8,128)(2,1)S(1)} %get-tuple-element.39), channel_id=1, source_target_pairs={{0,8},{8,0},{16,24},{24,16},{1,9},{9,1},{17,25},{25,17},{2,10},{10... | collective-permute-start | bytes 49160 | tf_op jit(solution)/shard_map/ppermute | solution.py:88
  13.6 1.5 %collective-permute-start.1 = (bf16[64,128]{1,0:T(8,128)(2,1)S(1)}, bf16[64,128]{1,0:T(8,128)(2,1)S(1)}, u32[]{:S(2)}, u32[]{:S(2)}) collective-permute-start(bf16[64,128]{1,0:T(8,128)(2,1)S(1)} %get-tuple-element.40), channel_id=1, source_target_pairs={{8,16},{16,8},{24,0},{0,24},{9,17},{17,9},{25,1},{1,25},{10,18},{1... | collective-permute-start | bytes 49160 | tf_op jit(solution)/shard_map/ppermute | solution.py:88
  15.1 3.7 %collective-permute-start.3 = (bf16[64,128]{1,0:T(8,128)(2,1)S(1)}, bf16[64,128]{1,0:T(8,128)(2,1)S(1)}, u32[]{:S(2)}, u32[]{:S(2)}) collective-permute-start(bf16[64,128]{1,0:T(8,128)(2,1)S(1)} %get-tuple-element.42), channel_id=1, source_target_pairs={{1,2},{2,1},{3,4},{4,3},{5,6},{6,5},{7,0},{0,7},{9,10},{10,9},{11,... | collective-permute-start | bytes 49160 | tf_op jit(solution)/shard_map/ppermute | solution.py:88
  18.8 1.4 %collective-permute-done.3.g3_ref = bf16[64,128]{1,0:T(8,128)(2,1)S(1)} collective-permute-done((bf16[64,128]{1,0:T(8,128)(2,1)S(1)}, bf16[64,128]{1,0:T(8,128)(2,1)S(1)}, u32[]{:S(2)}, u32[]{:S(2)}) %collective-permute-start.3) | collective-permute-done | bytes 16416 | tf_op jit(solution)/shard_map/ppermute | solution.py:88
  20.3 10.7 %triplets.1 = (f32[64,1024]{1,0:T(8,128)S(1)}, bf16[64,128]{1,0:T(8,128)(2,1)}, bf16[64,128]{1,0:T(8,128)(2,1)}, bf16[64,128]{1,0:T(8,128)(2,1)}, bf16[64,128]{1,0:T(8,128)(2,1)}, /*index=5*/bf16[64,640]{1,0:T(8,128)(2,1)S(1)}) custom-call(bf16[64,1024]{1,0:T(8,128)(2,1)S(1)} %get-tuple-element.38.proj_ref, bf16[64,128]{1,0:T(8,128)(2,1)S(1)} %collective-permute-done.g0_ref, ...), custom_call_target="tpu_custom_call" | custom-call | tf_op jit(solution)/shard_map/triplets/pallas_call | solution.py:309
  31.0 1.5 %collective-permute-start.4 = (bf16[64,128]{1,0:T(8,128)(2,1)}, bf16[64,128]{1,0:T(8,128)(2,1)}, u32[]{:S(2)}, u32[]{:S(2)}) collective-permute-start(bf16[64,128]{1,0:T(8,128)(2,1)} %get-tuple-element.50), channel_id=1, source_target_pairs={{0,8},{8,0},{16,24},{24,16},{1,9},{9,1},{17,25},{25,17},{2,10},{10... | collective-permute-start | bytes 49160 | tf_op jit(solution)/shard_map/ppermute | solution.py:88
  32.9 3.0 %collective-permute-start.7 = (bf16[64,128]{1,0:T(8,128)(2,1)}, bf16[64,128]{1,0:T(8,128)(2,1)}, u32[]{:S(2)}, u32[]{:S(2)}) collective-permute-start(bf16[64,128]{1,0:T(8,128)(2,1)} %get-tuple-element.53), channel_id=1, source_target_pairs={{1,2},{2,1},{3,4},{4,3},{5,6},{6,5},{7,0},{0,7},{9,10},{10,9},{11,... | collective-permute-start | bytes 49160 | tf_op jit(solution)/shard_map/ppermute | solution.py:88
  35.9 1.5 %collective-permute-done.5.b1_ref = bf16[64,128]{1,0:T(8,128)(2,1)} collective-permute-done((bf16[64,128]{1,0:T(8,128)(2,1)}, bf16[64,128]{1,0:T(8,128)(2,1)}, u32[]{:S(2)}, u32[]{:S(2)}) %collective-permute-start.5) | collective-permute-done | bytes 16416 | tf_op jit(solution)/shard_map/ppermute | solution.py:88
  37.4 0.9 %collective-permute-done.7.b3_ref = bf16[64,128]{1,0:T(8,128)(2,1)} collective-permute-done((bf16[64,128]{1,0:T(8,128)(2,1)}, bf16[64,128]{1,0:T(8,128)(2,1)}, u32[]{:S(2)}, u32[]{:S(2)}) %collective-permute-start.7) | collective-permute-done | bytes 16416 | tf_op jit(solution)/shard_map/ppermute | solution.py:88
  39.0 1.5 %collect.1 = (bf16[64,1024]{1,0:T(8,128)(2,1)S(1)}, bf16[32,1152]{1,0:T(8,128)(2,1)S(1)}, bf16[32,1152]{1,0:T(8,128)(2,1)S(1)}) custom-call(f32[64,1024]{1,0:T(8,128)S(1)} %get-tuple-element.49.own_ref, bf16[64,128]{1,0:T(8,128)(2,1)} %collective-permute-done.4.b0_ref, bf16[64,128]{1,0:T(8,128)(2,1)} %collective-permute-done.5.b1_ref, ...), custom_call_target="tpu_custom_call" | custom-call | tf_op jit(solution)/shard_map/collect/pallas_call | solution.py:366
  40.6 1.0 %add_convert_fusion = bf16[256,512]{1,0:T(8,128)(2,1)S(1)} fusion(bf16[256,512]{1,0:T(8,128)(2,1)} %collective-permute-done.8, bf16[256,512]{1,0:T(8,128)(2,1)S(1)} %get-tuple-element.59), kind=kLoop, calls=%fused_computation | loop fusion | flops 524288 | bytes 786432 | tf_op jit(solution)/shard_map/convert_element_type | solution.py:457
  41.7 1.6 %collective-permute-start.10 = (bf16[64,512]{1,0:T(8,128)(2,1)S(1)}, bf16[64,512]{1,0:T(8,128)(2,1)S(1)}, u32[]{:S(2)}, u32[]{:S(2)}) collective-permute-start(bf16[64,512]{1,0:T(8,128)(2,1)S(1)} %get-tuple-element.69), channel_id=1, source_target_pairs={{0,16},{8,24},{16,0},{24,8},{1,17},{9,25},{17,1},{25,9},{2,18},{10... | collective-permute-start | bytes 196616 | tf_op jit(solution)/shard_map/ppermute | solution.py:444
  43.2 1.5 %collective-permute-start.11 = (bf16[64,512]{1,0:T(8,128)(2,1)S(1)}, bf16[64,512]{1,0:T(8,128)(2,1)S(1)}, u32[]{:S(2)}, u32[]{:S(2)}) collective-permute-start(bf16[64,512]{1,0:T(8,128)(2,1)S(1)} %get-tuple-element.68), channel_id=1, source_target_pairs={{0,8},{8,0},{16,24},{24,16},{1,9},{9,1},{17,25},{25,17},{2,10},{10... | collective-permute-start | bytes 196616 | tf_op jit(solution)/shard_map/ppermute | solution.py:444
  45.2 3.3 %collective-permute-start.23 = (bf16[32,1152]{1,0:T(8,128)(2,1)S(1)}, bf16[32,1152]{1,0:T(8,128)(2,1)S(1)}, u32[]{:S(2)}, u32[]{:S(2)}) collective-permute-start(bf16[32,1152]{1,0:T(8,128)(2,1)S(1)} %add_convert_fusion.3), channel_id=1, source_target_pairs={{0,6},{1,7},{2,4},{3,5},{4,2},{5,3},{6,0},{7,1},{8,14},{9,15},{10,... | collective-permute-start | bytes 221192 | tf_op jit(solution)/shard_map/ppermute | solution.py:444
  48.6 1.1 %collective-permute-start.25 = (bf16[32,1152]{1,0:T(8,128)(2,1)S(1)}, bf16[32,1152]{1,0:T(8,128)(2,1)S(1)}, u32[]{:S(2)}, u32[]{:S(2)}) collective-permute-start(bf16[32,1152]{1,0:T(8,128)(2,1)S(1)} %add_convert_fusion.3), channel_id=1, source_target_pairs={{0,2},{1,3},{2,0},{3,1},{4,6},{5,7},{6,4},{7,5},{8,10},{9,11},{10,... | collective-permute-start | bytes 221192 | tf_op jit(solution)/shard_map/ppermute | solution.py:444
  50.0 3.3 %collective-permute-start.12 = (bf16[64,512]{1,0:T(8,128)(2,1)S(1)}, bf16[64,512]{1,0:T(8,128)(2,1)S(1)}, u32[]{:S(2)}, u32[]{:S(2)}) collective-permute-start(bf16[64,512]{1,0:T(8,128)(2,1)S(1)} %add_convert_fusion.5), channel_id=1, source_target_pairs={{0,6},{1,7},{2,4},{3,5},{4,2},{5,3},{6,0},{7,1},{8,14},{9,15},{10,... | collective-permute-start | bytes 196616 | tf_op jit(solution)/shard_map/ppermute | solution.py:444
  53.3 1.1 %collective-permute-start.14 = (bf16[64,512]{1,0:T(8,128)(2,1)S(1)}, bf16[64,512]{1,0:T(8,128)(2,1)S(1)}, u32[]{:S(2)}, u32[]{:S(2)}) collective-permute-start(bf16[64,512]{1,0:T(8,128)(2,1)S(1)} %add_convert_fusion.5), channel_id=1, source_target_pairs={{0,2},{1,3},{2,0},{3,1},{4,6},{5,7},{6,4},{7,5},{8,10},{9,11},{10,... | collective-permute-start | bytes 196616 | tf_op jit(solution)/shard_map/ppermute | solution.py:444
  54.4 2.8 %collective-permute-done.24 = bf16[32,1152]{1,0:T(8,128)(2,1)S(1)} collective-permute-done((bf16[32,1152]{1,0:T(8,128)(2,1)S(1)}, bf16[32,1152]{1,0:T(8,128)(2,1)S(1)}, u32[]{:S(2)}, u32[]{:S(2)}) %collective-permute-start.24) | collective-permute-done | bytes 73760 | tf_op jit(solution)/shard_map/ppermute | solution.py:444
  57.3 2.3 %collective-permute-start.26 = (bf16[32,1152]{1,0:T(8,128)(2,1)S(1)}, bf16[32,1152]{1,0:T(8,128)(2,1)S(1)}, u32[]{:S(2)}, u32[]{:S(2)}) collective-permute-start(bf16[32,1152]{1,0:T(8,128)(2,1)S(1)} %add_convert_fusion.2), channel_id=1, source_target_pairs={{0,24},{8,16},{16,8},{24,0},{1,25},{9,17},{17,9},{25,1},{2,26},{10... | collective-permute-start | bytes 221192 | tf_op jit(solution)/shard_map/ppermute | solution.py:444
  60.9 1.4 %collective-permute-start.15 = (bf16[64,512]{1,0:T(8,128)(2,1)S(1)}, bf16[64,512]{1,0:T(8,128)(2,1)S(1)}, u32[]{:S(2)}, u32[]{:S(2)}) collective-permute-start(bf16[64,512]{1,0:T(8,128)(2,1)S(1)} %add_convert_fusion.4.refs_0_), channel_id=1, source_target_pairs={{0,8},{8,0},{16,24},{24,16},{1,9},{9,1},{17,25},{25,17},{2,10},{10... | collective-permute-start | bytes 196616 | tf_op jit(solution)/shard_map/ppermute | solution.py:444
  62.3 1.5 %collective-permute-start.16 = (bf16[64,512]{1,0:T(8,128)(2,1)S(1)}, bf16[64,512]{1,0:T(8,128)(2,1)S(1)}, u32[]{:S(2)}, u32[]{:S(2)}) collective-permute-start(bf16[64,512]{1,0:T(8,128)(2,1)S(1)} %add_convert_fusion.4.refs_0_), channel_id=1, source_target_pairs={{0,16},{8,24},{16,0},{24,8},{1,17},{9,25},{17,1},{25,9},{2,18},{10... | collective-permute-start | bytes 196616 | tf_op jit(solution)/shard_map/ppermute | solution.py:444
  63.8 1.6 %collective-permute-start.17 = (bf16[64,512]{1,0:T(8,128)(2,1)S(1)}, bf16[64,512]{1,0:T(8,128)(2,1)S(1)}, u32[]{:S(2)}, u32[]{:S(2)}) collective-permute-start(bf16[64,512]{1,0:T(8,128)(2,1)S(1)} %add_convert_fusion.4.refs_0_), channel_id=1, source_target_pairs={{0,24},{8,16},{16,8},{24,0},{1,25},{9,17},{17,9},{25,1},{2,26},{10... | collective-permute-start | bytes 196616 | tf_op jit(solution)/shard_map/ppermute | solution.py:444
  66.1 0.9 %collective-permute-done.16.refs_2_ = bf16[64,512]{1,0:T(8,128)(2,1)S(1)} collective-permute-done((bf16[64,512]{1,0:T(8,128)(2,1)S(1)}, bf16[64,512]{1,0:T(8,128)(2,1)S(1)}, u32[]{:S(2)}, u32[]{:S(2)}) %collective-permute-start.16) | collective-permute-done | bytes 65568 | tf_op jit(solution)/shard_map/ppermute | solution.py:444
  67.0 2.0 %collective-permute-done.17.refs_3_ = bf16[64,512]{1,0:T(8,128)(2,1)S(1)} collective-permute-done((bf16[64,512]{1,0:T(8,128)(2,1)S(1)}, bf16[64,512]{1,0:T(8,128)(2,1)S(1)}, u32[]{:S(2)}, u32[]{:S(2)}) %collective-permute-start.17) | collective-permute-done | bytes 65568 | tf_op jit(solution)/shard_map/ppermute | solution.py:444
  69.0 2.0 %edge_gradient.1 = bf16[1024,512]{1,0:T(8,128)(2,1)} custom-call(bf16[1024,512]{1,0:T(8,128)(2,1)S(1)} %get-tuple-element.37.dres_ref, bf16[512,512]{1,0:T(8,128)(2,1)S(1)} %copy-done, bf16[64,1024]{1,0:T(8,128)(2,1)S(1)} %get-tuple-element.57.dpre_ref, bf16[64,512]{1,0:T(8,128)(2,1)S(1)} %get-tuple-element.58.down_ref), custom_call_target="tpu_custom_call" | custom-call | flops 603979776 | bytes 2097152 | tf_op jit(solution)/shard_map/edge_gradient/pallas_call | solution.py:388
  71.0 1.1 %finish.1 = (f32[512,512]{1,0:T(8,128)}, f32[64,512]{1,0:T(8,128)}, f32[64,512]{1,0:T(8,128)}, f32[16,64]{1,0:T(8,128)}) custom-call(bf16[64,512]{1,0:T(8,128)(2,1)S(1)} %add_convert_fusion.4.refs_0_, bf16[64,512]{1,0:T(8,128)(2,1)S(1)} %collective-permute-done.15.refs_1_, bf16[64,512]{1,0:T(8,128)(2,1)S(1)} %collective-permute-done.16.refs_2_, ...), custom_call_target="tpu_custom_call" | custom-call | tf_op jit(solution)/shard_map/finish/pallas_call | solution.py:427
  (65 shorter events, 6.7 us)
Async XLA Ops:
  3.4 1.5 %copy-start.3 = (bf16[16,16,1024]{2,1,0:T(8,128)(2,1)S(1)}, bf16[16,16,1024]{2,1,0:T(8,128)(2,1)}, u32[]{:S(2)}) copy-start(bf16[16,16,1024]{2,1,0:T(8,128)(2,1)} %param.12) | copy-start | bytes 1572868
  3.4 1.5 %copy-start.5 = (s32[16,1024]{1,0:T(8,128)S(1)}, s32[16,1024]{1,0:T(8,128)}, u32[]{:S(2)}) copy-start(s32[16,1024]{1,0:T(8,128)} %refs_2_.1) | copy-start | bytes 196612
  10.5 30.1 %collective-permute-start.8 = (bf16[256,512]{1,0:T(8,128)(2,1)}, bf16[256,512]{1,0:T(8,128)(2,1)}, u32[]{:S(2)}, u32[]{:S(2)}) collective-permute-start(bf16[256,512]{1,0:T(8,128)(2,1)} %get-tuple-element.60), channel_id=1, source_target_pairs={{0,1},{1,0},{2,3},{3,2},{4,5},{5,4},{6,7},{7,6},{8,9},{9,8},{10,11... | collective-permute-start | bytes 786440 | tf_op jit(solution)/shard_map/ppermute | solution.py:444
  11.1 7.8 %collective-permute-start = (bf16[64,128]{1,0:T(8,128)(2,1)S(1)}, bf16[64,128]{1,0:T(8,128)(2,1)S(1)}, u32[]{:S(2)}, u32[]{:S(2)}) collective-permute-start(bf16[64,128]{1,0:T(8,128)(2,1)S(1)} %get-tuple-element.39), channel_id=1, source_target_pairs={{0,8},{8,0},{16,24},{24,16},{1,9},{9,1},{17,25},{25,17},{2,10},{10... | collective-permute-start | bytes 49160 | tf_op jit(solution)/shard_map/ppermute | solution.py:88
  13.6 5.2 %collective-permute-start.1 = (bf16[64,128]{1,0:T(8,128)(2,1)S(1)}, bf16[64,128]{1,0:T(8,128)(2,1)S(1)}, u32[]{:S(2)}, u32[]{:S(2)}) collective-permute-start(bf16[64,128]{1,0:T(8,128)(2,1)S(1)} %get-tuple-element.40), channel_id=1, source_target_pairs={{8,16},{16,8},{24,0},{0,24},{9,17},{17,9},{25,1},{1,25},{10,18},{1... | collective-permute-start | bytes 49160 | tf_op jit(solution)/shard_map/ppermute | solution.py:88
  15.1 3.7 %collective-permute-start.2 = (bf16[64,128]{1,0:T(8,128)(2,1)S(1)}, bf16[64,128]{1,0:T(8,128)(2,1)S(1)}, u32[]{:S(2)}, u32[]{:S(2)}) collective-permute-start(bf16[64,128]{1,0:T(8,128)(2,1)S(1)} %get-tuple-element.41), channel_id=1, source_target_pairs={{0,1},{1,0},{2,3},{3,2},{4,5},{5,4},{6,7},{7,6},{8,9},{9,8},{10,11... | collective-permute-start | bytes 49160 | tf_op jit(solution)/shard_map/ppermute | solution.py:88
  15.1 5.2 %collective-permute-start.3 = (bf16[64,128]{1,0:T(8,128)(2,1)S(1)}, bf16[64,128]{1,0:T(8,128)(2,1)S(1)}, u32[]{:S(2)}, u32[]{:S(2)}) collective-permute-start(bf16[64,128]{1,0:T(8,128)(2,1)S(1)} %get-tuple-element.42), channel_id=1, source_target_pairs={{1,2},{2,1},{3,4},{4,3},{5,6},{6,5},{7,0},{0,7},{9,10},{10,9},{11,... | collective-permute-start | bytes 49160 | tf_op jit(solution)/shard_map/ppermute | solution.py:88
  31.0 4.9 %collective-permute-start.4 = (bf16[64,128]{1,0:T(8,128)(2,1)}, bf16[64,128]{1,0:T(8,128)(2,1)}, u32[]{:S(2)}, u32[]{:S(2)}) collective-permute-start(bf16[64,128]{1,0:T(8,128)(2,1)} %get-tuple-element.50), channel_id=1, source_target_pairs={{0,8},{8,0},{16,24},{24,16},{1,9},{9,1},{17,25},{25,17},{2,10},{10... | collective-permute-start | bytes 49160 | tf_op jit(solution)/shard_map/ppermute | solution.py:88
  32.5 5.0 %collective-permute-start.5 = (bf16[64,128]{1,0:T(8,128)(2,1)}, bf16[64,128]{1,0:T(8,128)(2,1)}, u32[]{:S(2)}, u32[]{:S(2)}) collective-permute-start(bf16[64,128]{1,0:T(8,128)(2,1)} %get-tuple-element.51), channel_id=1, source_target_pairs={{8,16},{16,8},{24,0},{0,24},{9,17},{17,9},{25,1},{1,25},{10,18},{1... | collective-permute-start | bytes 49160 | tf_op jit(solution)/shard_map/ppermute | solution.py:88
  32.9 4.5 %collective-permute-start.6 = (bf16[64,128]{1,0:T(8,128)(2,1)}, bf16[64,128]{1,0:T(8,128)(2,1)}, u32[]{:S(2)}, u32[]{:S(2)}) collective-permute-start(bf16[64,128]{1,0:T(8,128)(2,1)} %get-tuple-element.52), channel_id=1, source_target_pairs={{0,1},{1,0},{2,3},{3,2},{4,5},{5,4},{6,7},{7,6},{8,9},{9,8},{10,11... | collective-permute-start | bytes 49160 | tf_op jit(solution)/shard_map/ppermute | solution.py:88
  32.9 5.3 %collective-permute-start.7 = (bf16[64,128]{1,0:T(8,128)(2,1)}, bf16[64,128]{1,0:T(8,128)(2,1)}, u32[]{:S(2)}, u32[]{:S(2)}) collective-permute-start(bf16[64,128]{1,0:T(8,128)(2,1)} %get-tuple-element.53), channel_id=1, source_target_pairs={{1,2},{2,1},{3,4},{4,3},{5,6},{6,5},{7,0},{0,7},{9,10},{10,9},{11,... | collective-permute-start | bytes 49160 | tf_op jit(solution)/shard_map/ppermute | solution.py:88
  40.5 4.7 %collective-permute-start.22 = (bf16[32,1152]{1,0:T(8,128)(2,1)S(1)}, bf16[32,1152]{1,0:T(8,128)(2,1)S(1)}, u32[]{:S(2)}, u32[]{:S(2)}) collective-permute-start(bf16[32,1152]{1,0:T(8,128)(2,1)S(1)} %get-tuple-element.62), channel_id=1, source_target_pairs={{0,1},{1,0},{2,3},{3,2},{4,5},{5,4},{6,7},{7,6},{8,9},{9,8},{10,11... | collective-permute-start | bytes 221192 | tf_op jit(solution)/shard_map/ppermute | solution.py:444
  41.7 6.9 %collective-permute-start.10 = (bf16[64,512]{1,0:T(8,128)(2,1)S(1)}, bf16[64,512]{1,0:T(8,128)(2,1)S(1)}, u32[]{:S(2)}, u32[]{:S(2)}) collective-permute-start(bf16[64,512]{1,0:T(8,128)(2,1)S(1)} %get-tuple-element.69), channel_id=1, source_target_pairs={{0,16},{8,24},{16,0},{24,8},{1,17},{9,25},{17,1},{25,9},{2,18},{10... | collective-permute-start | bytes 196616 | tf_op jit(solution)/shard_map/ppermute | solution.py:444
  43.2 6.5 %collective-permute-start.11 = (bf16[64,512]{1,0:T(8,128)(2,1)S(1)}, bf16[64,512]{1,0:T(8,128)(2,1)S(1)}, u32[]{:S(2)}, u32[]{:S(2)}) collective-permute-start(bf16[64,512]{1,0:T(8,128)(2,1)S(1)} %get-tuple-element.68), channel_id=1, source_target_pairs={{0,8},{8,0},{16,24},{24,16},{1,9},{9,1},{17,25},{25,17},{2,10},{10... | collective-permute-start | bytes 196616 | tf_op jit(solution)/shard_map/ppermute | solution.py:444
  44.7 5.2 %collective-permute-start.9 = (bf16[64,512]{1,0:T(8,128)(2,1)S(1)}, bf16[64,512]{1,0:T(8,128)(2,1)S(1)}, u32[]{:S(2)}, u32[]{:S(2)}) collective-permute-start(bf16[64,512]{1,0:T(8,128)(2,1)S(1)} %get-tuple-element.67), channel_id=1, source_target_pairs={{0,24},{8,16},{16,8},{24,0},{1,25},{9,17},{17,9},{25,1},{2,26},{10... | collective-permute-start | bytes 196616 | tf_op jit(solution)/shard_map/ppermute | solution.py:444
  45.2 8.0 %collective-permute-start.23 = (bf16[32,1152]{1,0:T(8,128)(2,1)S(1)}, bf16[32,1152]{1,0:T(8,128)(2,1)S(1)}, u32[]{:S(2)}, u32[]{:S(2)}) collective-permute-start(bf16[32,1152]{1,0:T(8,128)(2,1)S(1)} %add_convert_fusion.3), channel_id=1, source_target_pairs={{0,6},{1,7},{2,4},{3,5},{4,2},{5,3},{6,0},{7,1},{8,14},{9,15},{10,... | collective-permute-start | bytes 221192 | tf_op jit(solution)/shard_map/ppermute | solution.py:444
  48.6 8.7 %collective-permute-start.24 = (bf16[32,1152]{1,0:T(8,128)(2,1)S(1)}, bf16[32,1152]{1,0:T(8,128)(2,1)S(1)}, u32[]{:S(2)}, u32[]{:S(2)}) collective-permute-start(bf16[32,1152]{1,0:T(8,128)(2,1)S(1)} %add_convert_fusion.3), channel_id=1, source_target_pairs={{0,4},{1,5},{2,6},{3,7},{4,0},{5,1},{6,2},{7,3},{8,12},{9,13},{10,... | collective-permute-start | bytes 221192 | tf_op jit(solution)/shard_map/ppermute | solution.py:444
  48.6 8.7 %collective-permute-start.25 = (bf16[32,1152]{1,0:T(8,128)(2,1)S(1)}, bf16[32,1152]{1,0:T(8,128)(2,1)S(1)}, u32[]{:S(2)}, u32[]{:S(2)}) collective-permute-start(bf16[32,1152]{1,0:T(8,128)(2,1)S(1)} %add_convert_fusion.3), channel_id=1, source_target_pairs={{0,2},{1,3},{2,0},{3,1},{4,6},{5,7},{6,4},{7,5},{8,10},{9,11},{10,... | collective-permute-start | bytes 221192 | tf_op jit(solution)/shard_map/ppermute | solution.py:444
  50.0 10.2 %collective-permute-start.12 = (bf16[64,512]{1,0:T(8,128)(2,1)S(1)}, bf16[64,512]{1,0:T(8,128)(2,1)S(1)}, u32[]{:S(2)}, u32[]{:S(2)}) collective-permute-start(bf16[64,512]{1,0:T(8,128)(2,1)S(1)} %add_convert_fusion.5), channel_id=1, source_target_pairs={{0,6},{1,7},{2,4},{3,5},{4,2},{5,3},{6,0},{7,1},{8,14},{9,15},{10,... | collective-permute-start | bytes 196616 | tf_op jit(solution)/shard_map/ppermute | solution.py:444
  53.3 7.6 %collective-permute-start.13 = (bf16[64,512]{1,0:T(8,128)(2,1)S(1)}, bf16[64,512]{1,0:T(8,128)(2,1)S(1)}, u32[]{:S(2)}, u32[]{:S(2)}) collective-permute-start(bf16[64,512]{1,0:T(8,128)(2,1)S(1)} %add_convert_fusion.5), channel_id=1, source_target_pairs={{0,4},{1,5},{2,6},{3,7},{4,0},{5,1},{6,2},{7,3},{8,12},{9,13},{10,... | collective-permute-start | bytes 196616 | tf_op jit(solution)/shard_map/ppermute | solution.py:444
  53.3 7.6 %collective-permute-start.14 = (bf16[64,512]{1,0:T(8,128)(2,1)S(1)}, bf16[64,512]{1,0:T(8,128)(2,1)S(1)}, u32[]{:S(2)}, u32[]{:S(2)}) collective-permute-start(bf16[64,512]{1,0:T(8,128)(2,1)S(1)} %add_convert_fusion.5), channel_id=1, source_target_pairs={{0,2},{1,3},{2,0},{3,1},{4,6},{5,7},{6,4},{7,5},{8,10},{9,11},{10,... | collective-permute-start | bytes 196616 | tf_op jit(solution)/shard_map/ppermute | solution.py:444
  57.3 6.5 %collective-permute-start.26 = (bf16[32,1152]{1,0:T(8,128)(2,1)S(1)}, bf16[32,1152]{1,0:T(8,128)(2,1)S(1)}, u32[]{:S(2)}, u32[]{:S(2)}) collective-permute-start(bf16[32,1152]{1,0:T(8,128)(2,1)S(1)} %add_convert_fusion.2), channel_id=1, source_target_pairs={{0,24},{8,16},{16,8},{24,0},{1,25},{9,17},{17,9},{25,1},{2,26},{10... | collective-permute-start | bytes 221192 | tf_op jit(solution)/shard_map/ppermute | solution.py:444
  59.6 5.7 %collective-permute-start.27 = (bf16[32,1152]{1,0:T(8,128)(2,1)S(1)}, bf16[32,1152]{1,0:T(8,128)(2,1)S(1)}, u32[]{:S(2)}, u32[]{:S(2)}) collective-permute-start(bf16[32,1152]{1,0:T(8,128)(2,1)S(1)} %add_convert_fusion.2), channel_id=1, source_target_pairs={{0,16},{8,24},{16,0},{24,8},{1,17},{9,25},{17,1},{25,9},{2,18},{10... | collective-permute-start | bytes 221192 | tf_op jit(solution)/shard_map/ppermute | solution.py:444
  60.1 5.2 %collective-permute-start.28 = (bf16[32,1152]{1,0:T(8,128)(2,1)S(1)}, bf16[32,1152]{1,0:T(8,128)(2,1)S(1)}, u32[]{:S(2)}, u32[]{:S(2)}) collective-permute-start(bf16[32,1152]{1,0:T(8,128)(2,1)S(1)} %add_convert_fusion.2), channel_id=1, source_target_pairs={{0,8},{8,0},{16,24},{24,16},{1,9},{9,1},{17,25},{25,17},{2,10},{10... | collective-permute-start | bytes 221192 | tf_op jit(solution)/shard_map/ppermute | solution.py:444
  60.9 5.1 %collective-permute-start.15 = (bf16[64,512]{1,0:T(8,128)(2,1)S(1)}, bf16[64,512]{1,0:T(8,128)(2,1)S(1)}, u32[]{:S(2)}, u32[]{:S(2)}) collective-permute-start(bf16[64,512]{1,0:T(8,128)(2,1)S(1)} %add_convert_fusion.4.refs_0_), channel_id=1, source_target_pairs={{0,8},{8,0},{16,24},{24,16},{1,9},{9,1},{17,25},{25,17},{2,10},{10... | collective-permute-start | bytes 196616 | tf_op jit(solution)/shard_map/ppermute | solution.py:444
  62.3 4.7 %collective-permute-start.16 = (bf16[64,512]{1,0:T(8,128)(2,1)S(1)}, bf16[64,512]{1,0:T(8,128)(2,1)S(1)}, u32[]{:S(2)}, u32[]{:S(2)}) collective-permute-start(bf16[64,512]{1,0:T(8,128)(2,1)S(1)} %add_convert_fusion.4.refs_0_), channel_id=1, source_target_pairs={{0,16},{8,24},{16,0},{24,8},{1,17},{9,25},{17,1},{25,9},{2,18},{10... | collective-permute-start | bytes 196616 | tf_op jit(solution)/shard_map/ppermute | solution.py:444
  63.8 5.2 %collective-permute-start.17 = (bf16[64,512]{1,0:T(8,128)(2,1)S(1)}, bf16[64,512]{1,0:T(8,128)(2,1)S(1)}, u32[]{:S(2)}, u32[]{:S(2)}) collective-permute-start(bf16[64,512]{1,0:T(8,128)(2,1)S(1)} %add_convert_fusion.4.refs_0_), channel_id=1, source_target_pairs={{0,24},{8,16},{16,8},{24,0},{1,25},{9,17},{17,9},{25,1},{2,26},{10... | collective-permute-start | bytes 196616 | tf_op jit(solution)/shard_map/ppermute | solution.py:444
  65.4 5.5 %collective-permute-start.29 = (bf16[32,1152]{1,0:T(8,128)(2,1)S(1)}, bf16[32,1152]{1,0:T(8,128)(2,1)S(1)}, u32[]{:S(2)}, u32[]{:S(2)}) collective-permute-start(bf16[32,1152]{1,0:T(8,128)(2,1)S(1)} %add_convert_fusion.1.refs_8_), channel_id=1, source_target_pairs={{0,1},{1,0},{2,3},{3,2},{4,5},{5,4},{6,7},{7,6},{8,9},{9,8},{10,11... | collective-permute-start | bytes 221192 | tf_op jit(solution)/shard_map/ppermute | solution.py:444
  65.5 5.5 %collective-permute-start.18 = (bf16[64,512]{1,0:T(8,128)(2,1)S(1)}, bf16[64,512]{1,0:T(8,128)(2,1)S(1)}, u32[]{:S(2)}, u32[]{:S(2)}) collective-permute-start(bf16[64,512]{1,0:T(8,128)(2,1)S(1)} %add_convert_fusion.4.refs_0_), channel_id=1, source_target_pairs={{0,1},{1,0},{2,3},{3,2},{4,5},{5,4},{6,7},{7,6},{8,9},{9,8},{10,11... | collective-permute-start | bytes 196616 | tf_op jit(solution)/shard_map/ppermute | solution.py:444
  66.0 5.0 %collective-permute-start.19 = (bf16[64,512]{1,0:T(8,128)(2,1)S(1)}, bf16[64,512]{1,0:T(8,128)(2,1)S(1)}, u32[]{:S(2)}, u32[]{:S(2)}) collective-permute-start(bf16[64,512]{1,0:T(8,128)(2,1)S(1)} %collective-permute-done.15.refs_1_), channel_id=1, source_target_pairs={{0,1},{1,0},{2,3},{3,2},{4,5},{5,4},{6,7},{7,6},{8,9},{9,8},{10,11... | collective-permute-start | bytes 196616 | tf_op jit(solution)/shard_map/ppermute | solution.py:444
  67.0 4.0 %collective-permute-start.20 = (bf16[64,512]{1,0:T(8,128)(2,1)S(1)}, bf16[64,512]{1,0:T(8,128)(2,1)S(1)}, u32[]{:S(2)}, u32[]{:S(2)}) collective-permute-start(bf16[64,512]{1,0:T(8,128)(2,1)S(1)} %collective-permute-done.16.refs_2_), channel_id=1, source_target_pairs={{0,1},{1,0},{2,3},{3,2},{4,5},{5,4},{6,7},{7,6},{8,9},{9,8},{10,11... | collective-permute-start | bytes 196616 | tf_op jit(solution)/shard_map/ppermute | solution.py:444
  68.9 2.0 %collective-permute-start.21 = (bf16[64,512]{1,0:T(8,128)(2,1)S(1)}, bf16[64,512]{1,0:T(8,128)(2,1)S(1)}, u32[]{:S(2)}, u32[]{:S(2)}) collective-permute-start(bf16[64,512]{1,0:T(8,128)(2,1)S(1)} %collective-permute-done.17.refs_3_), channel_id=1, source_target_pairs={{0,1},{1,0},{2,3},{3,2},{4,5},{5,4},{6,7},{7,6},{8,9},{9,8},{10,11... | collective-permute-start | bytes 196616 | tf_op jit(solution)/shard_map/ppermute | solution.py:444
  (10 other events, 9.0 us)

commit v3 on v2

--- a/solution.py
+++ b/solution.py
@@ -24,8 +24,24 @@
     return [jax.ShapeDtypeStruct(a.shape, a.dtype) for a in arrays]
 
 
+def in_hbm(*arrays):
+    return [pltpu.with_memory_space_constraint(a, pltpu.HBM) for a in arrays]
+
+
 def limits(mib):
     return pltpu.CompilerParams(vmem_limit_bytes=mib * 2**20)
+
+
+def cost(flops):
+    return pl.CostEstimate(flops=flops, bytes_accessed=0, transcendentals=0)
+
+
+def in_vmem(*arrays):
+    return [pltpu.VMEM(a.shape, a.dtype) for a in arrays]
+
+
+def blocks_of(width):
+    return [pl.ds(start, 128) for start in range(0, width, 128)]
 
 
 def sigmoid(value):
@@ -124,58 +140,73 @@
         project_kernel,
         in_specs=[HBM] * 3,
         out_specs=[VMEM] * 9,
-        out_shape=[
-            jax.ShapeDtypeStruct((width, rows), F32),
-            jax.ShapeDtypeStruct((width, rows), BF16),
-        ]
-        + [ghost] * 4
-        + like(embed, down_t, outgoing),
+        out_shape=[pltpu.VMEM((width, rows), F32), pltpu.VMEM((width, rows), BF16)]
+        + in_vmem(*[ghost] * 4, embed, down_t, outgoing),
         scratch_shapes=[pltpu.SemaphoreType.DMA((3,))],
         compiler_params=limits(12),
         name="project",
-    )(embed, down_t, outgoing)
-
-
-def residual_kernel(embed_ref, weight_ref, *refs):
-    count = (len(refs) - 5) // 2
+    )(*in_hbm(embed, down_t, outgoing))
+
+
+def residual_kernel(embed_ref, weight_ref, cotangent_ref, *refs):
+    count = (len(refs) - 7) // 2
     sources, targets = refs[:count], refs[count : 2 * count]
-    dres_ref, mine_ref, other_ref, grad_ref, sems = refs[2 * count :]
+    dres_ref, mine_ref, other_ref, cotangent_v, dres_v, grad_ref, sems = refs[2 * count :]
+    rows = embed_ref.shape[0]
+    block = min(rows, LANES)
+    spans = [pl.ds(start, block) for start in range(0, rows, block)]
+    reads = [
+        pltpu.make_async_copy(cotangent_ref.at[at, :], cotangent_v.at[at, :], sems.at[i])
+        for i, at in enumerate(spans)
+    ]
+    writes = [
+        pltpu.make_async_copy(dres_v.at[at, :], dres_ref.at[at, :], sems.at[len(spans) + i])
+        for i, at in enumerate(spans)
+    ]
     copies = [
-        pltpu.make_async_copy(source, target, sems.at[i])
+        pltpu.make_async_copy(source, target, sems.at[2 * len(spans) + i])
         for i, (source, target) in enumerate(zip(sources, targets))
     ]
-    for copy in copies:
+    for copy in reads + copies:
         copy.start()
-    copies[0].wait()
-    cotangent_v = targets[0]
-    rows = embed_ref.shape[0]
-    block = min(rows, LANES)
-    for start in range(0, rows, block):
-        at = pl.ds(start, block)
+    for at, read, write in zip(spans, reads, writes):
         res_pre = dot(embed_ref[at, :], weight_ref[...], NN)
-        dres_ref[at, :] = (cotangent_v[at, :].astype(F32) * silu_grad(res_pre)).astype(BF16)
-    grad_ref[...] = dot(embed_ref[...], dres_ref[...], TN).astype(BF16)
+        grad = silu_grad(res_pre)
+        read.wait()
+        dres_v[at, :] = (cotangent_v[at, :].astype(F32) * grad).astype(BF16)
+        write.start()
+    grad_ref[...] = dot(embed_ref[...], dres_v[...], TN).astype(BF16)
     half = grad_ref.shape[0] // 2
     upper = lax.axis_index("brick") % 2
-    mine_ref[...] = grad_ref[pl.ds(upper * half, half), :]
-    other_ref[...] = grad_ref[pl.ds((1 - upper) * half, half), :]
-    for copy in copies[1:]:
+    columns = blocks_of(grad_ref.shape[1])
+    step = half // lax.axis_size("slab")
+    for part in range(half // step):
+        for c, column in enumerate(columns):
+            to = pl.ds((part * len(columns) + c) * step, step)
+            mine_ref[to, :] = grad_ref[pl.ds(upper * half + part * step, step), column]
+            other_ref[to, :] = grad_ref[pl.ds((1 - upper) * half + part * step, step), column]
+    for copy in writes + copies:
         copy.wait()
 
 
-def residual(embed, weight, *staged):
-    inner = weight.shape[0]
-    half = jax.ShapeDtypeStruct((inner // 2, weight.shape[1]), BF16)
-    out_shape = like(*staged) + like(embed) + [half] * 2
+def residual(embed, weight, cotangent, *staged):
+    half = jax.ShapeDtypeStruct((weight.size // 256, 128), BF16)
+    blocks = embed.shape[0] // min(embed.shape[0], LANES)
     return pl.pallas_call(
         residual_kernel,
-        in_specs=[VMEM] * 2 + [HBM] * len(staged),
-        out_specs=[VMEM] * len(out_shape),
-        out_shape=out_shape,
-        scratch_shapes=[pltpu.VMEM(weight.shape, BF16), pltpu.SemaphoreType.DMA((len(staged),))],
+        in_specs=[VMEM] * 2 + [HBM] * (1 + len(staged)),
+        out_specs=[VMEM] * len(staged) + [HBM] + [VMEM] * 2,
+        out_shape=in_vmem(*staged) + [pltpu.HBM(embed.shape, BF16)] + in_vmem(half, half),
+        scratch_shapes=[
+            pltpu.VMEM(embed.shape, BF16),
+            pltpu.VMEM(embed.shape, BF16),
+            pltpu.VMEM(weight.shape, BF16),
+            pltpu.SemaphoreType.DMA((2 * blocks + len(staged),)),
+        ],
         compiler_params=limits(16),
+        cost_estimate=cost(6 * embed.size * weight.shape[1]),
         name="residual",
-    )(embed, weight, *staged)
+    )(embed, weight, *in_hbm(cotangent, *staged))
 
 
 def triplet_kernel(
@@ -184,12 +215,12 @@
     g1_ref,
     g2_ref,
     g3_ref,
-    basis_ref,
     index_ref,
     count_ref,
     up_ref,
-    cotangent_ref,
     bw_ref,
+    basis_hbm,
+    cotangent_hbm,
     own_ref,
     t0_ref,
     t1_ref,
@@ -204,7 +235,14 @@
     tsum_ref,
     dt_ref,
     acc_ref,
+    basis_ref,
+    cotangent_ref,
+    sems,
 ):
+    read_basis = pltpu.make_async_copy(basis_hbm, basis_ref, sems.at[0])
+    read_cotangent = pltpu.make_async_copy(cotangent_hbm, cotangent_ref, sems.at[1])
+    read_basis.start()
+    read_cotangent.start()
     width, rows = proj_ref.shape
     trips = index_ref.shape[0]
     nbasis = bw_ref.shape[0]
@@ -231,6 +269,7 @@
         lax.broadcasted_iota(jnp.int32, (trips, width, span), 2) // nbasis
     )
     diagonal = jnp.where(own_slot, wide[None], jnp.zeros((), BF16)).reshape(trips * width, span)
+    read_basis.wait()
     weight_ref[...] = dot(diagonal, basis_ref[...], NN)
 
     tsum_ref[...] = jnp.zeros_like(tsum_ref)
@@ -256,6 +295,7 @@
     tsum = tsum_ref[...]
     sig = sigmoid(tsum)
     act = (tsum * sig).astype(BF16)
+    read_cotangent.wait()
     cotangent = cotangent_ref[...]
     inner = cotangent.shape[1]
     grads_ref[:, :inner] = dot(act, cotangent, NN).astype(BF16)
@@ -300,15 +340,15 @@
     ghost = ghosts[0].shape[1]
     inner = cotangent.shape[1]
     groups = (rows + 4 * ghost) // LANES
-    operands = (proj, *ghosts, basis, index, count, up_weight, cotangent, basis_weight)
+    operands = (proj, *ghosts, index, count, up_weight, basis_weight)
     out_shape = (
-        [jax.ShapeDtypeStruct((width, rows), F32)]
-        + like(*ghosts)
-        + [jax.ShapeDtypeStruct((width, inner + 128), BF16)]
+        [pltpu.VMEM((width, rows), F32)]
+        + in_vmem(*ghosts)
+        + [pltpu.VMEM((width, inner + 128), BF16)]
     )
     return pl.pallas_call(
         triplet_kernel,
-        in_specs=[VMEM] * len(operands),
+        in_specs=[VMEM] * len(operands) + [HBM] * 2,
         out_specs=[VMEM] * len(out_shape),
         out_shape=out_shape,
         scratch_shapes=[
@@ -320,10 +360,14 @@
             pltpu.VMEM((width, rows), F32),
             pltpu.VMEM((width, rows), F32),
             pltpu.VMEM((groups * width, LANES), F32),
+            pltpu.VMEM(basis.shape, BF16),
+            pltpu.VMEM(cotangent.shape, BF16),
+            pltpu.SemaphoreType.DMA((2,)),
         ],
         compiler_params=limits(28),
+        cost_estimate=cost(8 * trips * rows * width * (rows + 4 * ghost)),
         name="triplets",
-    )(*operands)
+    )(*operands, *in_hbm(basis, cotangent))
 
 
 def collect_kernel(
@@ -354,79 +398,86 @@
     all_ref[:, inner:] = grads_ref[...]
     half = width // 2
     upper = lax.axis_index("brick") % 2
-    mine_ref[...] = all_ref[pl.ds(upper * half, half), :]
-    other_ref[...] = all_ref[pl.ds((1 - upper) * half, half), :]
+    for c, column in enumerate(blocks_of(all_ref.shape[1])):
+        to = pl.ds(c * half, half)
+        mine_ref[to, :] = all_ref[pl.ds(upper * half, half), column]
+        other_ref[to, :] = all_ref[pl.ds((1 - upper) * half, half), column]
 
 
 def collect(own, backs, outgoing, pre, embed, grads):
     width = own.shape[0]
     total = embed.shape[1] + grads.shape[1]
-    half = jax.ShapeDtypeStruct((width // 2, total), BF16)
+    half = pltpu.VMEM((width * total // 256, 128), BF16)
     operands = (own, *backs, outgoing, pre, embed, grads)
     return pl.pallas_call(
         collect_kernel,
         in_specs=[VMEM] * len(operands),
         out_specs=[VMEM] * 3,
-        out_shape=[jax.ShapeDtypeStruct(own.shape, BF16), half, half],
+        out_shape=[pltpu.VMEM(own.shape, BF16), half, half],
         scratch_shapes=[pltpu.VMEM((width, total), BF16)],
         compiler_params=limits(12),
         name="collect",
     )(*operands)
 
 
-def edge_kernel(dres_ref, weight_ref, dpre_ref, down_ref, out_ref):
+def edge_kernel(weight_ref, dpre_ref, down_ref, dres_hbm, out_ref, dres_ref, sems):
     rows = dres_ref.shape[0]
     block = min(rows, LANES)
-    for start in range(0, rows, block):
-        at = pl.ds(start, block)
-        res_term = dot(dres_ref[at, :], weight_ref[...], NT)
-        out_ref[at, :] = (res_term + dot(dpre_ref[:, at], down_ref[...], TN)).astype(BF16)
+    spans = [pl.ds(start, block) for start in range(0, rows, block)]
+    reads = [
+        pltpu.make_async_copy(dres_hbm.at[at, :], dres_ref.at[at, :], sems.at[i])
+        for i, at in enumerate(spans)
+    ]
+    for read in reads:
+        read.start()
+    for at, read in zip(spans, reads):
+        down_term = dot(dpre_ref[:, at], down_ref[...], TN)
+        read.wait()
+        out_ref[at, :] = (dot(dres_ref[at, :], weight_ref[...], NT) + down_term).astype(BF16)
 
 
 def edge_gradient(dres, weight, dpre, down_t):
     rows, inner = dres.shape
     return pl.pallas_call(
         edge_kernel,
-        in_specs=[VMEM] * 4,
+        in_specs=[VMEM] * 3 + [HBM],
         out_specs=VMEM,
         out_shape=jax.ShapeDtypeStruct((rows, inner), BF16),
+        scratch_shapes=[
+            pltpu.VMEM((rows, inner), BF16),
+            pltpu.SemaphoreType.DMA((rows // min(rows, LANES),)),
+        ],
         compiler_params=limits(12),
-        cost_estimate=pl.CostEstimate(
-            flops=2 * rows * inner * (inner + down_t.shape[0]),
-            bytes_accessed=4 * rows * inner,
-            transcendentals=0,
-        ),
+        cost_estimate=cost(4 * rows * inner * (inner + down_t.shape[0])),
         name="edge_gradient",
-    )(dres, weight, dpre, down_t)
-
-
-def finish_kernel(offsets, *refs):
-    count = len(offsets)
-    kept, sent = refs[:count], refs[count : 2 * count]
-    mine_ref, other_ref, residual_ref, down_ref, up_ref, basis_ref, all_ref = refs[2 * count :]
+    )(weight, dpre, down_t, *in_hbm(dres))
+
+
+def finish_kernel(offsets, mine_ref, other_ref, residual_ref, down_ref, up_ref, basis_ref, all_ref):
     upper = lax.axis_index("brick") % 2
     slab = lax.axis_index("slab")
-    step = kept[0].shape[0]
+    rows, inner = all_ref.shape[0] // 2, down_ref.shape[1]
     half = residual_ref.shape[0] // 2
-    for offset, kept_ref, sent_ref in zip(offsets, kept, sent):
-        place = (slab ^ offset) * step
-        residual_ref[pl.ds(upper * half + place, step), :] = kept_ref[...].astype(F32)
-        residual_ref[pl.ds((1 - upper) * half + place, step), :] = sent_ref[...].astype(F32)
-    rows, inner = mine_ref.shape[0], down_ref.shape[1]
-    all_ref[pl.ds(upper * rows, rows), :] = mine_ref[...].astype(F32)
-    all_ref[pl.ds((1 - upper) * rows, rows), :] = other_ref[...].astype(F32)
+    step = half // len(offsets)
+    columns = blocks_of(residual_ref.shape[1])
+    for source, side in ((mine_ref, upper), (other_ref, 1 - upper)):
+        for c, column in enumerate(blocks_of(all_ref.shape[1])):
+            all_ref[pl.ds(side * rows, rows), column] = source[pl.ds(c * rows, rows), :].astype(F32)
+        first = rows * all_ref.shape[1] // 128
+        for i, offset in enumerate(offsets):
+            place = pl.ds(side * half + (slab ^ offset) * step, step)
+            for c, column in enumerate(columns):
+                at = pl.ds(first + (i * len(columns) + c) * step, step)
+                residual_ref[place, column] = source[at, :].astype(F32)
     down_ref[...] = all_ref[:, :inner]
     up_ref[...] = all_ref[:, inner : 2 * inner]
     basis_ref[...] = all_ref[:, 2 * inner :].T[: basis_ref.shape[0], :]
 
 
-def finish(kept, sent, mine, other, inner, nbasis):
-    offsets = sorted(kept)
-    width = 2 * mine.shape[0]
-    operands = [kept[o] for o in offsets] + [sent[o] for o in offsets] + [mine, other]
+def finish(offsets, mine, other, inner, width, nbasis):
     return pl.pallas_call(
         lambda *refs: finish_kernel(offsets, *refs),
-        in_specs=[VMEM] * len(operands),
+        in_specs=[VMEM] * 2,
         out_specs=[VMEM] * 4,
         out_shape=[
             jax.ShapeDtypeStruct((inner, inner), F32),
@@ -434,10 +485,10 @@
             jax.ShapeDtypeStruct((width, inner), F32),
             jax.ShapeDtypeStruct((nbasis, width), F32),
         ],
-        scratch_shapes=[pltpu.VMEM((width, mine.shape[1]), F32)],
+        scratch_shapes=[pltpu.VMEM((width, 2 * inner + 128), F32)],
         compiler_params=limits(12),
         name="finish",
-    )(*operands)
+    )(mine, other)
 
 
 def swapped(value, axis, offset):
@@ -468,12 +519,8 @@
     return total_of([piece(0)] + parts)
 
 
-def exchanged_sum(values, axis, low, members):
-    parts = [[value] for value in values]
-    for k in range(members - 1, 0, -1):
-        for part, value in zip(parts, values):
-            part.append(swapped(value, axis, k * low))
-    return [total_of(part) for part in parts]
+def exchanged(value, axis, low, members):
+    return {k * low: swapped(value, axis, k * low) for k in range(members - 1, 0, -1)}
 
 
 def shards(
@@ -495,42 +542,55 @@
     ghosts = pair_exchange(rest[:4])
     embed_v, down_v, outgoing_v = rest[4:]
 
-    (cotangent_v, basis_v, index_v, count_v, up_v, bw_v, dres, mine, other) = residual(
+    index_v, count_v, up_v, bw_v, dres, mine, other = residual(
         embed_v,
         residual_weight,
         cotangent,
-        basis.reshape(trips * nbasis, rows),
         triplet_row_index,
         triplet_slot_count.reshape(1, rows),
         up_weight,
         basis_weight,
     )
     share = total_of([mine, swapped(other, "brick", 1)])
+
+    own, *terms, grads = triplets(
+        proj,
+        ghosts,
+        basis.reshape(trips * nbasis, rows),
+        index_v,
+        count_v,
+        up_v,
+        cotangent,
+        bw_v,
+    )
+    *terms, share = lax.optimization_barrier((*terms, share))
+    backs = pair_exchange(terms)
     slab_groups = groups_of("slab", 1)
     for low, members in reversed(slab_groups):
         share = scattered_sum(share, "slab", low, members)
-
-    own, *terms, grads = triplets(
-        proj, ghosts, basis_v, index_v, count_v, up_v, cotangent_v, bw_v
-    )
-    backs = pair_exchange(terms)
+    *backs, share = lax.optimization_barrier((*backs, share))
     dpre, mine, other = collect(own, backs, outgoing_v, pre, embed_v, grads)
+
+    mine = total_of([mine, swapped(other, "brick", 1)])
+    mine, dpre = lax.optimization_barrier((mine, dpre))
     edge_grad = edge_gradient(dres, residual_weight, dpre, down_v)
-
-    mine = total_of([mine, swapped(other, "brick", 1)])
+    count = mine.shape[0]
+    value = jnp.concatenate([mine, share], axis=0)
     for low, members in groups_of("brick", 2):
-        share, mine = exchanged_sum([share, mine], "brick", low, members)
-    pieces = {0: share}
+        value = total_of([value, *exchanged(value, "brick", low, members).values()])
+    value, edge_grad = lax.optimization_barrier((value, edge_grad))
+    pieces = {0: value[count:]}
     for low, members in slab_groups:
-        received = {}
-        for k in range(members - 1, 0, -1):
-            for offset, piece in pieces.items():
-                received[offset ^ (k * low)] = swapped(piece, "slab", k * low)
-        (mine,) = exchanged_sum([mine], "slab", low, members)
-        pieces.update(received)
-    sent = {offset: swapped(piece, "brick", 1) for offset, piece in pieces.items()}
+        received = exchanged(value, "slab", low, members)
+        mine = total_of([value[:count]] + [other[:count] for other in received.values()])
+        known = sorted(pieces)
+        step = share.shape[0]
+        for k, other in received.items():
+            for i, offset in enumerate(known):
+                pieces[offset ^ k] = other[count + i * step : count + (i + 1) * step]
+        value = jnp.concatenate([mine] + [pieces[o] for o in sorted(pieces)], axis=0)
     residual_grad, down_grad, up_grad, basis_grad = finish(
-        pieces, sent, mine, swapped(mine, "brick", 1), inner, nbasis
+        sorted(pieces), value, swapped(value, "brick", 1), inner, proj.shape[0], nbasis
     )
     return edge_grad, residual_grad, down_grad.T, up_grad, basis_grad
 

time: 72.6 us -> 64.4 us (0.89)
  starting transfers between devices: 34.4 us -> 22.5 us
  waiting for transfers between devices: 9.8 us -> 18.3 us
  local copies, waits for them, and re-layouts: 6.96 us -> 0.11 us
  Pallas kernels: 18.9 us -> 22.1 us
  other arithmetic: 1.2 us -> 0.26 us
    ppermute x22 -> x12, starting transfers between devices: 21.7 us -> 11.8 us  [swapped(): lax.ppermute(value, axis, [(i, i ^ offset) for i in range(lax.axis_size(a...]
    ppermute x22 -> x12, waiting for transfers between devices: 5.97 us -> 15.2 us  [swapped(): lax.ppermute(value, axis, [(i, i ^ offset) for i in range(lax.axis_size(a...]
    unnamed x24 -> x6, local copies, waits for them, and re-layouts: 6.93 us -> 0.05 us
    pallas_call x3, Pallas kernels: 15.4 us -> 18.2 us  [the longest x1 11.3 us: triplets(): pl.pallas_call(triplet_kernel, in_specs=[VMEM] * len(operands) + [HBM] *...]
    ppermute x8, starting transfers between devices: 12.7 us -> 10.8 us  [paired(): return lax.ppermute(value, axis, pairs)]
    pallas_call x1, Pallas kernels: 0.88 us -> 2.01 us  [project(): pl.pallas_call(project_kernel, in_specs=[HBM] * 3, out_specs=[VMEM] * 9,...]
    convert_element_type x6 -> x4, other arithmetic: 1.2 us -> 0.22 us  [total_of(): return sum((part.astype(F32) for part in parts)).astype(BF16)]
    pallas_call x1, Pallas kernels: 1.53 us -> 0.77 us  [collect(): pl.pallas_call(collect_kernel, in_specs=[VMEM] * len(operands), out_specs...]
  transfers between devices with their start and end apart: 30 -> 20, of which waited for: 7 -> 11; matrix products, arithmetic and copies ran while one was open for 2% -> 0% of each run, Pallas kernels for 20% -> 28%
where the time goes in v3:
time: 64.4 us; the launch traced here: 64.2 us
  starting transfers between devices  22.5 us (35%)
  Pallas kernels  22.1 us (34%)
  waiting for transfers between devices  18.3 us (28%)
  between operations  0.85 us (1%)
    ppermute x12, waiting for transfers between devices, swapped(): lax.ppermute(value, axis, [(i, i ^ offset) for i in range(lax.axis_size(a...  15.2 us
    ppermute x12, starting transfers between devices, swapped(): lax.ppermute(value, axis, [(i, i ^ offset) for i in range(lax.axis_size(a...  11.8 us
    pallas_call x1, Pallas kernels, triplets(): pl.pallas_call(triplet_kernel, in_specs=[VMEM] * len(operands) + [HBM] *...  11.3 us
    ppermute x8, starting transfers between devices, paired(): return lax.ppermute(value, axis, pairs)  10.8 us
    pallas_call x1, Pallas kernels, residual(): pl.pallas_call(residual_kernel, in_specs=[VMEM] * 2 + [HBM] * (1 + len(st...  3.64 us
    pallas_call x1, Pallas kernels, edge_gradient(): pl.pallas_call(edge_kernel, in_specs=[VMEM] * 3 + [HBM], out_specs=VMEM,...  3.31 us
    ppermute x8, waiting for transfers between devices, paired(): return lax.ppermute(value, axis, pairs)  3.16 us
    pallas_call x1, Pallas kernels, project(): pl.pallas_call(project_kernel, in_specs=[HBM] * 3, out_specs=[VMEM] * 9,...  2.01 us
  transfers between devices with their start and end apart: 20, of which 11 were waited for; matrix products, arithmetic and copies ran while one was open for 0% of the time, Pallas kernels for 28%

profile of v3, /device:TPU:0, one launch (start us, length us, event | category | flops | bytes accessed | tf_op | source)
XLA Modules:
  0.0 64.2 jit_solution(6399768506756441309)
XLA Ops:
  0.6 2.0 %project.1 = (f32[64,1024]{1,0:T(8,128)S(1)}, bf16[64,1024]{1,0:T(8,128)(2,1)S(1)}, bf16[64,128]{1,0:T(8,128)(2,1)S(1)}, bf16[64,128]{1,0:T(8,128)(2,1)S(1)}, bf...) custom-call(bf16[1024,512]{1,0:T(8,128)(2,1)} %embed_ref.1, ...), custom_call_target="tpu_custom_call" | custom-call | tf_op jit(solution)/shard_map/project/pallas_call | solution.py:139
  2.7 3.0 %collective-permute-start = (bf16[64,128]{1,0:T(8,128)(2,1)S(1)}, bf16[64,128]{1,0:T(8,128)(2,1)S(1)}, u32[]{:S(2)}, u32[]{:S(2)}) collective-permute-start(bf16[64,128]{1,0:T(8,128)(2,1)S(1)} %get-tuple-element.49), channel_id=1, source_target_pairs={{0,8},{8,0},{16,24},{24,16},{1,9},{9,1},{17,25},{25,17},{2,10},{10... | collective-permute-start | bytes 49160 | tf_op jit(solution)/shard_map/ppermute | solution.py:104
  5.7 1.5 %collective-permute-start.1 = (bf16[64,128]{1,0:T(8,128)(2,1)S(1)}, bf16[64,128]{1,0:T(8,128)(2,1)S(1)}, u32[]{:S(2)}, u32[]{:S(2)}) collective-permute-start(bf16[64,128]{1,0:T(8,128)(2,1)S(1)} %get-tuple-element.50), channel_id=1, source_target_pairs={{8,16},{16,8},{24,0},{0,24},{9,17},{17,9},{25,1},{1,25},{10,18},{1... | collective-permute-start | bytes 49160 | tf_op jit(solution)/shard_map/ppermute | solution.py:104
  7.2 3.7 %collective-permute-start.3 = (bf16[64,128]{1,0:T(8,128)(2,1)S(1)}, bf16[64,128]{1,0:T(8,128)(2,1)S(1)}, u32[]{:S(2)}, u32[]{:S(2)}) collective-permute-start(bf16[64,128]{1,0:T(8,128)(2,1)S(1)} %get-tuple-element.52), channel_id=1, source_target_pairs={{1,2},{2,1},{3,4},{4,3},{5,6},{6,5},{7,0},{0,7},{9,10},{10,9},{11,... | collective-permute-start | bytes 49160 | tf_op jit(solution)/shard_map/ppermute | solution.py:104
  10.9 3.6 %residual.1 = (s32[16,1024]{1,0:T(8,128)S(1)}, s32[1,1024]{1,0:T(1,128)S(1)}, bf16[64,512]{1,0:T(8,128)(2,1)S(1)}, bf16[16,64]{1,0:T(8,128)(2,1)S(1)}, bf16[1024...) custom-call(bf16[1024,512]{1,0:T(8,128)(2,1)S(1)} %get-tuple-element.53.embed_ref, ...), custom_call_target="tpu_custom_call" | custom-call | flops 1610612736 | tf_op jit(solution)/shard_map/residual/pallas_call | solution.py:195
  14.7 11.3 %triplets.1 = (f32[64,1024]{1,0:T(8,128)S(1)}, bf16[64,128]{1,0:T(8,128)(2,1)S(1)}, bf16[64,128]{1,0:T(8,128)(2,1)S(1)}, bf16[64,128]{1,0:T(8,128)(2,1)S(1)}, bf...) custom-call(bf16[64,1024]{1,0:T(8,128)(2,1)S(1)} %get-tuple-element.48.proj_ref, ...), custom_call_target="tpu_custom_call" | custom-call | flops 12884901888 | tf_op jit(solution)/shard_map/triplets/pallas_call | solution.py:349
  26.0 0.1 add_convert_fusion
  26.1 0.6 collective-permute-start.10
  26.7 1.5 %collective-permute-start.11 = (bf16[256,128]{1,0:T(8,128)(2,1)S(1)}, bf16[256,128]{1,0:T(8,128)(2,1)S(1)}, u32[]{:S(2)}, u32[]{:S(2)}) collective-permute-start(bf16[256,128]{1,0:T(8,128)(2,1)S(1)} %get-tuple-element.92), channel_id=1, source_target_pairs={{0,8},{8,0},{16,24},{24,16},{1,9},{9,1},{17,25},{25,17},{2,10},{10... | collective-permute-start | bytes 196616 | tf_op jit(solution)/shard_map/ppermute | solution.py:495
  28.1 1.5 %collective-permute-start.9 = (bf16[256,128]{1,0:T(8,128)(2,1)S(1)}, bf16[256,128]{1,0:T(8,128)(2,1)S(1)}, u32[]{:S(2)}, u32[]{:S(2)}) collective-permute-start(bf16[256,128]{1,0:T(8,128)(2,1)S(1)} %get-tuple-element.91), channel_id=1, source_target_pairs={{0,24},{8,16},{16,8},{24,0},{1,25},{9,17},{17,9},{25,1},{2,26},{10... | collective-permute-start | bytes 196616 | tf_op jit(solution)/shard_map/ppermute | solution.py:495
  29.6 1.5 %collective-permute-start.5 = (bf16[64,128]{1,0:T(8,128)(2,1)S(1)}, bf16[64,128]{1,0:T(8,128)(2,1)S(1)}, u32[]{:S(2)}, u32[]{:S(2)}) collective-permute-start(bf16[64,128]{1,0:T(8,128)(2,1)S(1)} %get-tuple-element.65), channel_id=1, source_target_pairs={{0,8},{8,0},{16,24},{24,16},{1,9},{9,1},{17,25},{25,17},{2,10},{10... | collective-permute-start | bytes 49160 | tf_op jit(solution)/shard_map/ppermute | solution.py:104
  31.1 0.5 collective-permute-start.6
  31.6 0.6 collective-permute-start.8
  32.2 1.3 %collective-permute-done.9 = bf16[256,128]{1,0:T(8,128)(2,1)S(1)} collective-permute-done((bf16[256,128]{1,0:T(8,128)(2,1)S(1)}, bf16[256,128]{1,0:T(8,128)(2,1)S(1)}, u32[]{:S(2)}, u32[]{:S(2)}) %collective-permute-start.9) | collective-permute-done | bytes 65568 | tf_op jit(solution)/shard_map/ppermute | solution.py:495
  33.5 0.2 collective-permute-done.5.b0_ref
  33.7 2.0 %collective-permute-done.6.b1_ref = bf16[64,128]{1,0:T(8,128)(2,1)S(1)} collective-permute-done((bf16[64,128]{1,0:T(8,128)(2,1)S(1)}, bf16[64,128]{1,0:T(8,128)(2,1)S(1)}, u32[]{:S(2)}, u32[]{:S(2)}) %collective-permute-start.6) | collective-permute-done | bytes 16416 | tf_op jit(solution)/shard_map/ppermute | solution.py:104
  35.8 0.9 %collective-permute-done.8.b3_ref = bf16[64,128]{1,0:T(8,128)(2,1)S(1)} collective-permute-done((bf16[64,128]{1,0:T(8,128)(2,1)S(1)}, bf16[64,128]{1,0:T(8,128)(2,1)S(1)}, u32[]{:S(2)}, u32[]{:S(2)}) %collective-permute-start.8) | collective-permute-done | bytes 16416 | tf_op jit(solution)/shard_map/ppermute | solution.py:104
  36.7 0.8 %collect.1 = (bf16[64,1024]{1,0:T(8,128)(2,1)S(1)}, bf16[288,128]{1,0:T(8,128)(2,1)S(1)}, bf16[288,128]{1,0:T(8,128)(2,1)S(1)}) custom-call(f32[64,1024]{1,0:T(8,128)S(1)} %get-tuple-element.58.own_ref, bf16[64,128]{1,0:T(8,128)(2,1)S(1)} %collective-permute-done.5.b0_ref, bf16[64,128]{1,0:T(8,128)(2,1)S(1)} %collective-permute-done.6.b1_ref, ...), custom_call_target="tpu_custom_call" | custom-call | tf_op jit(solution)/shard_map/collect/pallas_call | solution.py:412
  37.5 1.3 %collective-permute-done.12 = bf16[288,128]{1,0:T(8,128)(2,1)S(1)} collective-permute-done((bf16[288,128]{1,0:T(8,128)(2,1)S(1)}, bf16[288,128]{1,0:T(8,128)(2,1)S(1)}, u32[]{:S(2)}, u32[]{:S(2)}) %collective-permute-start.12) | collective-permute-done | bytes 73760 | tf_op jit(solution)/shard_map/ppermute | solution.py:495
  38.8 0.6 collective-permute-start.13
  39.4 3.8 %collective-permute-start.15 = (bf16[544,128]{1,0:T(8,128)(2,1)S(1)}, bf16[544,128]{1,0:T(8,128)(2,1)S(1)}, u32[]{:S(2)}, u32[]{:S(2)}) collective-permute-start(bf16[544,128]{1,0:T(8,128)(2,1)S(1)} %constant_dynamic-update-slice_fusion), channel_id=1, source_target_pairs={{0,2},{1,3},{2,0},{3,1},{4,6},{5,7},{6,4},{7,5},{8,10},{9,11},{10,... | collective-permute-start | bytes 417800 | tf_op jit(solution)/shard_map/ppermute | solution.py:495
  43.3 3.3 %edge_gradient.1 = bf16[1024,512]{1,0:T(8,128)(2,1)} custom-call(bf16[512,512]{1,0:T(8,128)(2,1)S(1)} %copy-done, bf16[64,1024]{1,0:T(8,128)(2,1)S(1)} %get-tuple-element.82.dpre_ref, bf16[64,512]{1,0:T(8,128)(2,1)S(1)} %get-tuple-element.83.down_ref, bf16[1024,512]{1,0:T(8,128)(2,1)} %get-tuple-element.84.dres_hbm), custom_call_target="tpu_custom_call" | custom-call | flops 1207959552 | tf_op jit(solution)/shard_map/edge_gradient/pallas_call | solution.py:441
  46.6 0.8 %collective-permute-done.13 = bf16[544,128]{1,0:T(8,128)(2,1)S(1)} collective-permute-done((bf16[544,128]{1,0:T(8,128)(2,1)S(1)}, bf16[544,128]{1,0:T(8,128)(2,1)S(1)}, u32[]{:S(2)}, u32[]{:S(2)}) %collective-permute-start.13) | collective-permute-done | bytes 139296 | tf_op jit(solution)/shard_map/ppermute | solution.py:495
  47.3 4.7 %collective-permute-done.14 = bf16[544,128]{1,0:T(8,128)(2,1)S(1)} collective-permute-done((bf16[544,128]{1,0:T(8,128)(2,1)S(1)}, bf16[544,128]{1,0:T(8,128)(2,1)S(1)}, u32[]{:S(2)}, u32[]{:S(2)}) %collective-permute-start.14) | collective-permute-done | bytes 139296 | tf_op jit(solution)/shard_map/ppermute | solution.py:495
  52.0 0.1 add_convert_fusion.1
  52.1 2.5 %collective-permute-start.16 = (bf16[544,128]{1,0:T(8,128)(2,1)S(1)}, bf16[544,128]{1,0:T(8,128)(2,1)S(1)}, u32[]{:S(2)}, u32[]{:S(2)}) collective-permute-start(bf16[544,128]{1,0:T(8,128)(2,1)S(1)} %add_convert_fusion.1), channel_id=1, source_target_pairs={{0,24},{8,16},{16,8},{24,0},{1,25},{9,17},{17,9},{25,1},{2,26},{10... | collective-permute-start | bytes 417800 | tf_op jit(solution)/shard_map/ppermute | solution.py:495
  54.6 0.5 collective-permute-start.17
  55.1 0.5 collective-permute-start.18
  55.6 3.1 %collective-permute-done.16 = bf16[544,128]{1,0:T(8,128)(2,1)S(1)} collective-permute-done((bf16[544,128]{1,0:T(8,128)(2,1)S(1)}, bf16[544,128]{1,0:T(8,128)(2,1)S(1)}, u32[]{:S(2)}, u32[]{:S(2)}) %collective-permute-start.16) | collective-permute-done | bytes 139296 | tf_op jit(solution)/shard_map/ppermute | solution.py:495
  58.7 2.5 %collective-permute-done.17 = bf16[544,128]{1,0:T(8,128)(2,1)S(1)} collective-permute-done((bf16[544,128]{1,0:T(8,128)(2,1)S(1)}, bf16[544,128]{1,0:T(8,128)(2,1)S(1)}, u32[]{:S(2)}, u32[]{:S(2)}) %collective-permute-start.17) | collective-permute-done | bytes 139296 | tf_op jit(solution)/shard_map/ppermute | solution.py:495
  61.5 1.6 %collective-permute-done.19.refs_1_ = bf16[1312,128]{1,0:T(8,128)(2,1)S(1)} collective-permute-done((bf16[1312,128]{1,0:T(8,128)(2,1)S(1)}, bf16[1312,128]{1,0:T(8,128)(2,1)S(1)}, u32[]{:S(2)}, u32[]{:S(2)}) %collective-permute-start.19) | collective-permute-done | bytes 335904 | tf_op jit(solution)/shard_map/ppermute | solution.py:495
  63.1 1.1 %finish.1 = (f32[512,512]{1,0:T(8,128)}, f32[64,512]{1,0:T(8,128)}, f32[64,512]{1,0:T(8,128)}, f32[16,64]{1,0:T(8,128)}) custom-call(bf16[1312,128]{1,0:T(8,128)(2,1)S(1)} %slice_dynamic-update-slice_fusion.refs_0_, bf16[1312,128]{1,0:T(8,128)(2,1)S(1)} %collective-permute-done.19.refs_1_), custom_call_target="tpu_custom_call" | custom-call | tf_op jit(solution)/shard_map/finish/pallas_call | solution.py:478
  (28 shorter events, 0.5 us)
Async XLA Ops:
  0.6 10.2 %copy-start = (bf16[512,512]{1,0:T(8,128)(2,1)S(1)}, bf16[512,512]{1,0:T(8,128)(2,1)}, u32[]{:S(2)}) copy-start(bf16[512,512]{1,0:T(8,128)(2,1)} %weight_ref.3) | copy-start | bytes 1572868
  2.7 12.0 %collective-permute-start = (bf16[64,128]{1,0:T(8,128)(2,1)S(1)}, bf16[64,128]{1,0:T(8,128)(2,1)S(1)}, u32[]{:S(2)}, u32[]{:S(2)}) collective-permute-start(bf16[64,128]{1,0:T(8,128)(2,1)S(1)} %get-tuple-element.49), channel_id=1, source_target_pairs={{0,8},{8,0},{16,24},{24,16},{1,9},{9,1},{17,25},{25,17},{2,10},{10... | collective-permute-start | bytes 49160 | tf_op jit(solution)/shard_map/ppermute | solution.py:104
  5.7 9.0 %collective-permute-start.1 = (bf16[64,128]{1,0:T(8,128)(2,1)S(1)}, bf16[64,128]{1,0:T(8,128)(2,1)S(1)}, u32[]{:S(2)}, u32[]{:S(2)}) collective-permute-start(bf16[64,128]{1,0:T(8,128)(2,1)S(1)} %get-tuple-element.50), channel_id=1, source_target_pairs={{8,16},{16,8},{24,0},{0,24},{9,17},{17,9},{25,1},{1,25},{10,18},{1... | collective-permute-start | bytes 49160 | tf_op jit(solution)/shard_map/ppermute | solution.py:104
  7.2 7.5 %collective-permute-start.2 = (bf16[64,128]{1,0:T(8,128)(2,1)S(1)}, bf16[64,128]{1,0:T(8,128)(2,1)S(1)}, u32[]{:S(2)}, u32[]{:S(2)}) collective-permute-start(bf16[64,128]{1,0:T(8,128)(2,1)S(1)} %get-tuple-element.51), channel_id=1, source_target_pairs={{0,1},{1,0},{2,3},{3,2},{4,5},{5,4},{6,7},{7,6},{8,9},{9,8},{10,11... | collective-permute-start | bytes 49160 | tf_op jit(solution)/shard_map/ppermute | solution.py:104
  7.2 7.5 %collective-permute-start.3 = (bf16[64,128]{1,0:T(8,128)(2,1)S(1)}, bf16[64,128]{1,0:T(8,128)(2,1)S(1)}, u32[]{:S(2)}, u32[]{:S(2)}) collective-permute-start(bf16[64,128]{1,0:T(8,128)(2,1)S(1)} %get-tuple-element.52), channel_id=1, source_target_pairs={{1,2},{2,1},{3,4},{4,3},{5,6},{6,5},{7,0},{0,7},{9,10},{10,9},{11,... | collective-permute-start | bytes 49160 | tf_op jit(solution)/shard_map/ppermute | solution.py:104
  14.5 11.4 %collective-permute-start.4 = (bf16[1024,128]{1,0:T(8,128)(2,1)S(1)}, bf16[1024,128]{1,0:T(8,128)(2,1)S(1)}, u32[]{:S(2)}, u32[]{:S(2)}) collective-permute-start(bf16[1024,128]{1,0:T(8,128)(2,1)S(1)} %get-tuple-element.64), channel_id=1, source_target_pairs={{0,1},{1,0},{2,3},{3,2},{4,5},{5,4},{6,7},{7,6},{8,9},{9,8},{10,11... | collective-permute-start | bytes 786440 | tf_op jit(solution)/shard_map/ppermute | solution.py:495
  26.1 5.5 %collective-permute-start.10 = (bf16[256,128]{1,0:T(8,128)(2,1)S(1)}, bf16[256,128]{1,0:T(8,128)(2,1)S(1)}, u32[]{:S(2)}, u32[]{:S(2)}) collective-permute-start(bf16[256,128]{1,0:T(8,128)(2,1)S(1)} %get-tuple-element.93), channel_id=1, source_target_pairs={{0,16},{8,24},{16,0},{24,8},{1,17},{9,25},{17,1},{25,9},{2,18},{10... | collective-permute-start | bytes 196616 | tf_op jit(solution)/shard_map/ppermute | solution.py:495
  26.7 5.0 %collective-permute-start.11 = (bf16[256,128]{1,0:T(8,128)(2,1)S(1)}, bf16[256,128]{1,0:T(8,128)(2,1)S(1)}, u32[]{:S(2)}, u32[]{:S(2)}) collective-permute-start(bf16[256,128]{1,0:T(8,128)(2,1)S(1)} %get-tuple-element.92), channel_id=1, source_target_pairs={{0,8},{8,0},{16,24},{24,16},{1,9},{9,1},{17,25},{25,17},{2,10},{10... | collective-permute-start | bytes 196616 | tf_op jit(solution)/shard_map/ppermute | solution.py:495
  28.1 5.3 %collective-permute-start.9 = (bf16[256,128]{1,0:T(8,128)(2,1)S(1)}, bf16[256,128]{1,0:T(8,128)(2,1)S(1)}, u32[]{:S(2)}, u32[]{:S(2)}) collective-permute-start(bf16[256,128]{1,0:T(8,128)(2,1)S(1)} %get-tuple-element.91), channel_id=1, source_target_pairs={{0,24},{8,16},{16,8},{24,0},{1,25},{9,17},{17,9},{25,1},{2,26},{10... | collective-permute-start | bytes 196616 | tf_op jit(solution)/shard_map/ppermute | solution.py:495
  29.6 4.1 %collective-permute-start.5 = (bf16[64,128]{1,0:T(8,128)(2,1)S(1)}, bf16[64,128]{1,0:T(8,128)(2,1)S(1)}, u32[]{:S(2)}, u32[]{:S(2)}) collective-permute-start(bf16[64,128]{1,0:T(8,128)(2,1)S(1)} %get-tuple-element.65), channel_id=1, source_target_pairs={{0,8},{8,0},{16,24},{24,16},{1,9},{9,1},{17,25},{25,17},{2,10},{10... | collective-permute-start | bytes 49160 | tf_op jit(solution)/shard_map/ppermute | solution.py:104
  31.1 4.6 %collective-permute-start.6 = (bf16[64,128]{1,0:T(8,128)(2,1)S(1)}, bf16[64,128]{1,0:T(8,128)(2,1)S(1)}, u32[]{:S(2)}, u32[]{:S(2)}) collective-permute-start(bf16[64,128]{1,0:T(8,128)(2,1)S(1)} %get-tuple-element.66), channel_id=1, source_target_pairs={{8,16},{16,8},{24,0},{0,24},{9,17},{17,9},{25,1},{1,25},{10,18},{1... | collective-permute-start | bytes 49160 | tf_op jit(solution)/shard_map/ppermute | solution.py:104
  31.6 4.2 %collective-permute-start.7 = (bf16[64,128]{1,0:T(8,128)(2,1)S(1)}, bf16[64,128]{1,0:T(8,128)(2,1)S(1)}, u32[]{:S(2)}, u32[]{:S(2)}) collective-permute-start(bf16[64,128]{1,0:T(8,128)(2,1)S(1)} %get-tuple-element.67), channel_id=1, source_target_pairs={{0,1},{1,0},{2,3},{3,2},{4,5},{5,4},{6,7},{7,6},{8,9},{9,8},{10,11... | collective-permute-start | bytes 49160 | tf_op jit(solution)/shard_map/ppermute | solution.py:104
  31.6 5.0 %collective-permute-start.8 = (bf16[64,128]{1,0:T(8,128)(2,1)S(1)}, bf16[64,128]{1,0:T(8,128)(2,1)S(1)}, u32[]{:S(2)}, u32[]{:S(2)}) collective-permute-start(bf16[64,128]{1,0:T(8,128)(2,1)S(1)} %get-tuple-element.68), channel_id=1, source_target_pairs={{1,2},{2,1},{3,4},{4,3},{5,6},{6,5},{7,0},{0,7},{9,10},{10,9},{11,... | collective-permute-start | bytes 49160 | tf_op jit(solution)/shard_map/ppermute | solution.py:104
  37.4 1.3 %collective-permute-start.12 = (bf16[288,128]{1,0:T(8,128)(2,1)S(1)}, bf16[288,128]{1,0:T(8,128)(2,1)S(1)}, u32[]{:S(2)}, u32[]{:S(2)}) collective-permute-start(bf16[288,128]{1,0:T(8,128)(2,1)S(1)} %get-tuple-element.78), channel_id=1, source_target_pairs={{0,1},{1,0},{2,3},{3,2},{4,5},{5,4},{6,7},{7,6},{8,9},{9,8},{10,11... | collective-permute-start | bytes 221192 | tf_op jit(solution)/shard_map/ppermute | solution.py:495
  38.8 8.5 %collective-permute-start.13 = (bf16[544,128]{1,0:T(8,128)(2,1)S(1)}, bf16[544,128]{1,0:T(8,128)(2,1)S(1)}, u32[]{:S(2)}, u32[]{:S(2)}) collective-permute-start(bf16[544,128]{1,0:T(8,128)(2,1)S(1)} %constant_dynamic-update-slice_fusion), channel_id=1, source_target_pairs={{0,6},{1,7},{2,4},{3,5},{4,2},{5,3},{6,0},{7,1},{8,14},{9,15},{10,... | collective-permute-start | bytes 417800 | tf_op jit(solution)/shard_map/ppermute | solution.py:495
  39.4 12.6 %collective-permute-start.14 = (bf16[544,128]{1,0:T(8,128)(2,1)S(1)}, bf16[544,128]{1,0:T(8,128)(2,1)S(1)}, u32[]{:S(2)}, u32[]{:S(2)}) collective-permute-start(bf16[544,128]{1,0:T(8,128)(2,1)S(1)} %constant_dynamic-update-slice_fusion), channel_id=1, source_target_pairs={{0,4},{1,5},{2,6},{3,7},{4,0},{5,1},{6,2},{7,3},{8,12},{9,13},{10,... | collective-permute-start | bytes 417800 | tf_op jit(solution)/shard_map/ppermute | solution.py:495
  39.4 12.6 %collective-permute-start.15 = (bf16[544,128]{1,0:T(8,128)(2,1)S(1)}, bf16[544,128]{1,0:T(8,128)(2,1)S(1)}, u32[]{:S(2)}, u32[]{:S(2)}) collective-permute-start(bf16[544,128]{1,0:T(8,128)(2,1)S(1)} %constant_dynamic-update-slice_fusion), channel_id=1, source_target_pairs={{0,2},{1,3},{2,0},{3,1},{4,6},{5,7},{6,4},{7,5},{8,10},{9,11},{10,... | collective-permute-start | bytes 417800 | tf_op jit(solution)/shard_map/ppermute | solution.py:495
  52.1 6.7 %collective-permute-start.16 = (bf16[544,128]{1,0:T(8,128)(2,1)S(1)}, bf16[544,128]{1,0:T(8,128)(2,1)S(1)}, u32[]{:S(2)}, u32[]{:S(2)}) collective-permute-start(bf16[544,128]{1,0:T(8,128)(2,1)S(1)} %add_convert_fusion.1), channel_id=1, source_target_pairs={{0,24},{8,16},{16,8},{24,0},{1,25},{9,17},{17,9},{25,1},{2,26},{10... | collective-permute-start | bytes 417800 | tf_op jit(solution)/shard_map/ppermute | solution.py:495
  54.6 6.6 %collective-permute-start.17 = (bf16[544,128]{1,0:T(8,128)(2,1)S(1)}, bf16[544,128]{1,0:T(8,128)(2,1)S(1)}, u32[]{:S(2)}, u32[]{:S(2)}) collective-permute-start(bf16[544,128]{1,0:T(8,128)(2,1)S(1)} %add_convert_fusion.1), channel_id=1, source_target_pairs={{0,16},{8,24},{16,0},{24,8},{1,17},{9,25},{17,1},{25,9},{2,18},{10... | collective-permute-start | bytes 417800 | tf_op jit(solution)/shard_map/ppermute | solution.py:495
  55.1 6.2 %collective-permute-start.18 = (bf16[544,128]{1,0:T(8,128)(2,1)S(1)}, bf16[544,128]{1,0:T(8,128)(2,1)S(1)}, u32[]{:S(2)}, u32[]{:S(2)}) collective-permute-start(bf16[544,128]{1,0:T(8,128)(2,1)S(1)} %add_convert_fusion.1), channel_id=1, source_target_pairs={{0,8},{8,0},{16,24},{24,16},{1,9},{9,1},{17,25},{25,17},{2,10},{10... | collective-permute-start | bytes 417800 | tf_op jit(solution)/shard_map/ppermute | solution.py:495
  61.4 1.7 %collective-permute-start.19 = (bf16[1312,128]{1,0:T(8,128)(2,1)S(1)}, bf16[1312,128]{1,0:T(8,128)(2,1)S(1)}, u32[]{:S(2)}, u32[]{:S(2)}) collective-permute-start(bf16[1312,128]{1,0:T(8,128)(2,1)S(1)} %slice_dynamic-update-slice_fusion.refs_0_), channel_id=1, source_target_pairs={{0,1},{1,0},{2,3},{3,2},{4,5},{5,4},{6,7},{7,6},{8,9},{9,8},{10,11... | collective-permute-start | bytes 1007624 | tf_op jit(solution)/shard_map/ppermute | solution.py:495

commit v4 on v3

--- a/solution.py
+++ b/solution.py
@@ -110,48 +110,40 @@
     return [sent[k] for k in range(4)]
 
 
-def project_kernel(
-    embed_ref, down_ref, rows_ref, pre_ref, proj_ref, s0, s1, s2, s3, embed_v, down_v, rows_v, sems
-):
+def select_kernel(embed_ref, rows_ref, s0, s1, s2, s3, embed_v, rows_v, sems):
     copies = [
-        pltpu.make_async_copy(source, target, sems.at[i])
-        for i, (source, target) in enumerate(
-            ((embed_ref, embed_v), (down_ref, down_v), (rows_ref, rows_v))
-        )
+        pltpu.make_async_copy(rows_ref, rows_v, sems.at[0]),
+        pltpu.make_async_copy(embed_ref, embed_v, sems.at[1]),
     ]
     for copy in copies:
         copy.start()
     for copy in copies:
         copy.wait()
-    pre = dot(down_v[...], embed_v[...], NT)
-    pre_ref[...] = pre
-    proj = (pre * sigmoid(pre)).astype(BF16)
-    proj_ref[...] = proj
-    table = stacked(proj)
+    rows = embed_v.shape[0]
     for index, send_ref in zip(pair_lists(rows_v), (s0, s1, s2, s3)):
-        picked = dot(table, onehot(index & (LANES - 1)), NN)
-        send_ref[...] = chosen(picked, index // LANES, proj.shape[0]).astype(BF16)
-
-
-def project(embed, down_t, outgoing):
-    rows, width = embed.shape[0], down_t.shape[0]
-    ghost = jax.ShapeDtypeStruct((width, outgoing.shape[1]), BF16)
+        spots = lax.broadcasted_iota(jnp.int32, (rows, index.shape[1]), 0).astype(jnp.int16)
+        hot = jnp.where(spots == index.astype(jnp.int16), jnp.ones((), BF16), jnp.zeros((), BF16))
+        send_ref[...] = dot(hot, embed_v[...], TN).astype(BF16)
+
+
+def select(embed, outgoing):
+    ghost = jax.ShapeDtypeStruct((outgoing.shape[1], embed.shape[1]), BF16)
     return pl.pallas_call(
-        project_kernel,
-        in_specs=[HBM] * 3,
-        out_specs=[VMEM] * 9,
-        out_shape=[pltpu.VMEM((width, rows), F32), pltpu.VMEM((width, rows), BF16)]
-        + in_vmem(*[ghost] * 4, embed, down_t, outgoing),
-        scratch_shapes=[pltpu.SemaphoreType.DMA((3,))],
+        select_kernel,
+        in_specs=[HBM] * 2,
+        out_specs=[VMEM] * 6,
+        out_shape=in_vmem(*[ghost] * 4, embed, outgoing),
+        scratch_shapes=[pltpu.SemaphoreType.DMA((2,))],
         compiler_params=limits(12),
-        name="project",
-    )(*in_hbm(embed, down_t, outgoing))
+        name="select",
+    )(*in_hbm(embed, outgoing))
 
 
 def residual_kernel(embed_ref, weight_ref, cotangent_ref, *refs):
-    count = (len(refs) - 7) // 2
+    count = (len(refs) - 9) // 2
     sources, targets = refs[:count], refs[count : 2 * count]
-    dres_ref, mine_ref, other_ref, cotangent_v, dres_v, grad_ref, sems = refs[2 * count :]
+    dres_ref, mine_ref, other_ref, pre_ref, proj_ref = refs[2 * count : 2 * count + 5]
+    cotangent_v, dres_v, grad_ref, sems = refs[2 * count + 5 :]
     rows = embed_ref.shape[0]
     block = min(rows, LANES)
     spans = [pl.ds(start, block) for start in range(0, rows, block)]
@@ -175,6 +167,10 @@
         read.wait()
         dres_v[at, :] = (cotangent_v[at, :].astype(F32) * grad).astype(BF16)
         write.start()
+    copies[0].wait()
+    pre = dot(targets[0][...], embed_ref[...], NT)
+    pre_ref[...] = pre
+    proj_ref[...] = (pre * sigmoid(pre)).astype(BF16)
     grad_ref[...] = dot(embed_ref[...], dres_v[...], TN).astype(BF16)
     half = grad_ref.shape[0] // 2
     upper = lax.axis_index("brick") % 2
@@ -185,18 +181,23 @@
             to = pl.ds((part * len(columns) + c) * step, step)
             mine_ref[to, :] = grad_ref[pl.ds(upper * half + part * step, step), column]
             other_ref[to, :] = grad_ref[pl.ds((1 - upper) * half + part * step, step), column]
-    for copy in writes + copies:
+    for copy in writes + copies[1:]:
         copy.wait()
 
 
-def residual(embed, weight, cotangent, *staged):
+def residual(embed, weight, cotangent, down_t, *staged):
+    staged = (down_t, *staged)
+    width, rows = down_t.shape[0], embed.shape[0]
     half = jax.ShapeDtypeStruct((weight.size // 256, 128), BF16)
     blocks = embed.shape[0] // min(embed.shape[0], LANES)
     return pl.pallas_call(
         residual_kernel,
         in_specs=[VMEM] * 2 + [HBM] * (1 + len(staged)),
-        out_specs=[VMEM] * len(staged) + [HBM] + [VMEM] * 2,
-        out_shape=in_vmem(*staged) + [pltpu.HBM(embed.shape, BF16)] + in_vmem(half, half),
+        out_specs=[VMEM] * len(staged) + [HBM] + [VMEM] * 4,
+        out_shape=in_vmem(*staged)
+        + [pltpu.HBM(embed.shape, BF16)]
+        + in_vmem(half, half)
+        + [pltpu.VMEM((width, rows), F32), pltpu.VMEM((width, rows), BF16)],
         scratch_shapes=[
             pltpu.VMEM(embed.shape, BF16),
             pltpu.VMEM(embed.shape, BF16),
@@ -211,6 +212,9 @@
 
 def triplet_kernel(
     proj_ref,
+    pre_ref,
+    embed_ref,
+    down_ref,
     g0_ref,
     g1_ref,
     g2_ref,
@@ -224,9 +228,11 @@
     own_ref,
     t0_ref,
     t1_ref,
-    t2_ref,
     t3_ref,
-    grads_ref,
+    mine_ref,
+    other_ref,
+    ghost_embed_ref,
+    rest_ref,
     table_ref,
     weight_ref,
     hot_ref,
@@ -247,13 +253,16 @@
     trips = index_ref.shape[0]
     nbasis = bw_ref.shape[0]
     own_groups = rows // LANES
-    blocks = []
-    for a_ref, b_ref, axis in ((g0_ref, g1_ref, "slab"), (g2_ref, g3_ref, "brick")):
+    ghost = g0_ref.shape[0]
+    for first, a_ref, b_ref, axis in ((0, g0_ref, g1_ref, "slab"), (2, g2_ref, g3_ref, "brick")):
         odd = parity(axis)
         a, b = a_ref[...], b_ref[...]
-        blocks += [jnp.where(odd, a, b), jnp.where(odd, b, a)]
+        ghost_embed_ref[first * ghost : (first + 1) * ghost, :] = jnp.where(odd, a, b)
+        ghost_embed_ref[(first + 1) * ghost : (first + 2) * ghost, :] = jnp.where(odd, b, a)
+    ghost_pre = dot(down_ref[...], ghost_embed_ref[...], NT)
+    ghost_grad = silu_grad(ghost_pre)
     table_ref[: own_groups * width, :] = stacked(proj_ref[...])
-    table_ref[own_groups * width :, :] = stacked(jnp.concatenate(blocks, axis=1))
+    table_ref[own_groups * width :, :] = stacked((ghost_pre * sigmoid(ghost_pre)).astype(BF16))
     groups = table_ref.shape[0] // width
     tiles = rows // LANES
 
@@ -298,7 +307,7 @@
     read_cotangent.wait()
     cotangent = cotangent_ref[...]
     inner = cotangent.shape[1]
-    grads_ref[:, :inner] = dot(act, cotangent, NN).astype(BF16)
+    rest_ref[:, inner : 2 * inner] = dot(act, cotangent, NN).astype(BF16)
     dsum = dot(up_ref[...], cotangent, NT)
     dt_ref[...] = dsum * (sig * (1.0 + tsum * (1.0 - sig)))
     acc_ref[...] = jnp.zeros_like(acc_ref)
@@ -316,35 +325,56 @@
 
     lax.fori_loop(0, trips, backward, 0, unroll=8)
 
-    own_ref[...] = unstacked(acc_ref[: own_groups * width, :], width)
-    ghost_terms = unstacked(acc_ref[own_groups * width :, :], width).astype(BF16)
-    ghost = t0_ref.shape[1]
-    for first, axis, a_ref, b_ref in ((0, "slab", t0_ref, t1_ref), (2, "brick", t2_ref, t3_ref)):
+    own = unstacked(acc_ref[: own_groups * width, :], width)
+    own_ref[...] = own
+    ghost_terms = unstacked(acc_ref[own_groups * width :, :], width)
+    sides = []
+    for first, axis in ((0, "slab"), (2, "brick")):
         odd = parity(axis)
-        prev = ghost_terms[:, first * ghost : (first + 1) * ghost]
-        following = ghost_terms[:, (first + 1) * ghost : (first + 2) * ghost]
-        a_ref[...] = jnp.where(odd, prev, following)
-        b_ref[...] = jnp.where(odd, following, prev)
+        prev = ghost_terms[:, first * ghost : (first + 1) * ghost].astype(BF16)
+        following = ghost_terms[:, (first + 1) * ghost : (first + 2) * ghost].astype(BF16)
+        sides += [jnp.where(odd, prev, following), jnp.where(odd, following, prev)]
+    t0_ref[...], t1_ref[...], t3_ref[...] = sides[0], sides[1], sides[3]
+    down_grad = dot((own * silu_grad(pre_ref[...])).astype(BF16), embed_ref[...], NN)
+    down_grad += dot((ghost_terms * ghost_grad).astype(BF16), ghost_embed_ref[...], NN)
+    rest_ref[:, :inner] = down_grad.astype(BF16)
     full = dot(dw_ref[...], basis_ref[...], NT).reshape(trips, width, span)
     kept = jnp.sum(jnp.where(own_slot, full, 0.0), axis=0)
     folded = dot(kept, fold, NT, lax.Precision.HIGHEST)
-    pad = grads_ref.shape[1] - inner - nbasis
-    grads_ref[:, inner:] = jnp.concatenate(
+    pad = rest_ref.shape[1] - 2 * inner - nbasis
+    rest_ref[:, 2 * inner :] = jnp.concatenate(
         [folded, jnp.zeros((width, pad), F32)], axis=1
     ).astype(BF16)
-
-
-def triplets(proj, ghosts, basis, index, count, up_weight, cotangent, basis_weight):
+    half = width // 2
+    upper = lax.axis_index("brick") % 2
+    columns = blocks_of(rest_ref.shape[1])
+    for c, column in enumerate(columns):
+        to = pl.ds(c * half, half)
+        mine_ref[to, :] = rest_ref[pl.ds(upper * half, half), column]
+        other_ref[to, :] = rest_ref[pl.ds((1 - upper) * half, half), column]
+    used, total = len(columns) * half, mine_ref.shape[0]
+    if used < total:
+        mine_ref[used:, :] = jnp.zeros((total - used, 128), BF16)
+        other_ref[used:total, :] = jnp.zeros((total - used, 128), BF16)
+    for c, column in enumerate(blocks_of(ghost)):
+        other_ref[pl.ds(total + c * width, width), :] = sides[2][:, column]
+
+
+def triplets(
+    proj, pre, embed, down_t, ghosts, basis, index, count, up_weight, cotangent, basis_weight
+):
     width, rows = proj.shape
     trips = index.shape[0]
-    ghost = ghosts[0].shape[1]
-    inner = cotangent.shape[1]
+    ghost, inner = ghosts[0].shape
     groups = (rows + 4 * ghost) // LANES
-    operands = (proj, *ghosts, index, count, up_weight, basis_weight)
+    operands = (proj, pre, embed, down_t, *ghosts, index, count, up_weight, basis_weight)
+    unit = 16 * lax.axis_size("slab")
+    total = 2 * inner + 128
+    shared = -(-(width * total // 256) // unit) * unit
     out_shape = (
         [pltpu.VMEM((width, rows), F32)]
-        + in_vmem(*ghosts)
-        + [pltpu.VMEM((width, inner + 128), BF16)]
+        + [pltpu.VMEM((width, ghost), BF16)] * 3
+        + [pltpu.VMEM((shared, 128), BF16), pltpu.VMEM((shared + width * ghost // 128, 128), BF16)]
     )
     return pl.pallas_call(
         triplet_kernel,
@@ -352,6 +382,8 @@
         out_specs=[VMEM] * len(out_shape),
         out_shape=out_shape,
         scratch_shapes=[
+            pltpu.VMEM((4 * ghost, inner), BF16),
+            pltpu.VMEM((width, total), BF16),
             pltpu.VMEM((groups * width, LANES), BF16),
             pltpu.VMEM((trips * width, rows), F32),
             pltpu.VMEM((trips, LANES, rows), BF16),
@@ -370,7 +402,7 @@
     )(*operands, *in_hbm(basis, cotangent))
 
 
-def collect_kernel(
+def edge_kernel(
     own_ref,
     b0_ref,
     b1_ref,
@@ -378,50 +410,14 @@
     b3_ref,
     rows_ref,
     pre_ref,
-    embed_ref,
-    grads_ref,
-    dpre_ref,
-    mine_ref,
-    other_ref,
-    all_ref,
+    weight_ref,
+    down_ref,
+    dres_hbm,
+    out_ref,
+    dres_ref,
+    sems,
 ):
     width, rows = own_ref.shape
-    groups = rows // LANES
-    acc = jnp.zeros((groups * width, LANES), F32)
-    for index, back_ref in zip(pair_lists(rows_ref), (b0_ref, b1_ref, b2_ref, b3_ref)):
-        acc += dot(spread(back_ref[...], index // LANES, groups), onehot(index & (LANES - 1)), NT)
-    dproj = own_ref[...] + unstacked(acc, width)
-    dpre = (dproj * silu_grad(pre_ref[...])).astype(BF16)
-    dpre_ref[...] = dpre
-    inner = embed_ref.shape[1]
-    all_ref[:, :inner] = dot(dpre, embed_ref[...], NN).astype(BF16)
-    all_ref[:, inner:] = grads_ref[...]
-    half = width // 2
-    upper = lax.axis_index("brick") % 2
-    for c, column in enumerate(blocks_of(all_ref.shape[1])):
-        to = pl.ds(c * half, half)
-        mine_ref[to, :] = all_ref[pl.ds(upper * half, half), column]
-        other_ref[to, :] = all_ref[pl.ds((1 - upper) * half, half), column]
-
-
-def collect(own, backs, outgoing, pre, embed, grads):
-    width = own.shape[0]
-    total = embed.shape[1] + grads.shape[1]
-    half = pltpu.VMEM((width * total // 256, 128), BF16)
-    operands = (own, *backs, outgoing, pre, embed, grads)
-    return pl.pallas_call(
-        collect_kernel,
-        in_specs=[VMEM] * len(operands),
-        out_specs=[VMEM] * 3,
-        out_shape=[pltpu.VMEM(own.shape, BF16), half, half],
-        scratch_shapes=[pltpu.VMEM((width, total), BF16)],
-        compiler_params=limits(12),
-        name="collect",
-    )(*operands)
-
-
-def edge_kernel(weight_ref, dpre_ref, down_ref, dres_hbm, out_ref, dres_ref, sems):
-    rows = dres_ref.shape[0]
     block = min(rows, LANES)
     spans = [pl.ds(start, block) for start in range(0, rows, block)]
     reads = [
@@ -430,17 +426,24 @@
     ]
     for read in reads:
         read.start()
-    for at, read in zip(spans, reads):
-        down_term = dot(dpre_ref[:, at], down_ref[...], TN)
+    groups = rows // LANES
+    acc = jnp.zeros((groups * width, LANES), F32)
+    for index, back_ref in zip(pair_lists(rows_ref), (b0_ref, b1_ref, b2_ref, b3_ref)):
+        acc += dot(spread(back_ref[...], index // LANES, groups), onehot(index & (LANES - 1)), NT)
+    dproj = own_ref[...] + unstacked(acc, width)
+    dpre = (dproj * silu_grad(pre_ref[...])).astype(BF16)
+    for i, (at, read) in enumerate(zip(spans, reads)):
+        down_term = dot(dpre[:, i * block : (i + 1) * block], down_ref[...], TN)
         read.wait()
         out_ref[at, :] = (dot(dres_ref[at, :], weight_ref[...], NT) + down_term).astype(BF16)
 
 
-def edge_gradient(dres, weight, dpre, down_t):
+def edge_gradient(own, backs, outgoing, pre, weight, down_t, dres):
     rows, inner = dres.shape
+    operands = (own, *backs, outgoing, pre, weight, down_t)
     return pl.pallas_call(
         edge_kernel,
-        in_specs=[VMEM] * 3 + [HBM],
+        in_specs=[VMEM] * len(operands) + [HBM],
         out_specs=VMEM,
         out_shape=jax.ShapeDtypeStruct((rows, inner), BF16),
         scratch_shapes=[
@@ -450,31 +453,39 @@
         compiler_params=limits(12),
         cost_estimate=cost(4 * rows * inner * (inner + down_t.shape[0])),
         name="edge_gradient",
-    )(weight, dpre, down_t, *in_hbm(dres))
-
-
-def finish_kernel(offsets, mine_ref, other_ref, residual_ref, down_ref, up_ref, basis_ref, all_ref):
+    )(*operands, *in_hbm(dres))
+
+
+def finish_kernel(
+    offsets, mine_ref, other_ref, residual_ref, down_ref, up_ref, basis_ref, all_ref, part_ref
+):
     upper = lax.axis_index("brick") % 2
     slab = lax.axis_index("slab")
-    rows, inner = all_ref.shape[0] // 2, down_ref.shape[1]
     half = residual_ref.shape[0] // 2
     step = half // len(offsets)
     columns = blocks_of(residual_ref.shape[1])
+    block = mine_ref.shape[0] // len(offsets)
+    tail = len(columns) * step
+    share = block - tail
     for source, side in ((mine_ref, upper), (other_ref, 1 - upper)):
-        for c, column in enumerate(blocks_of(all_ref.shape[1])):
-            all_ref[pl.ds(side * rows, rows), column] = source[pl.ds(c * rows, rows), :].astype(F32)
-        first = rows * all_ref.shape[1] // 128
         for i, offset in enumerate(offsets):
             place = pl.ds(side * half + (slab ^ offset) * step, step)
             for c, column in enumerate(columns):
-                at = pl.ds(first + (i * len(columns) + c) * step, step)
+                at = pl.ds(i * block + c * step, step)
                 residual_ref[place, column] = source[at, :].astype(F32)
+            place = pl.ds((side * len(offsets) + (slab ^ offset)) * share, share)
+            part_ref[place, :] = source[pl.ds(i * block + tail, share), :].astype(F32)
+    rows, inner = all_ref.shape[0] // 2, down_ref.shape[1]
+    for side in range(2):
+        for c, column in enumerate(blocks_of(all_ref.shape[1])):
+            at = pl.ds(side * len(offsets) * share + c * rows, rows)
+            all_ref[pl.ds(side * rows, rows), column] = part_ref[at, :]
     down_ref[...] = all_ref[:, :inner]
     up_ref[...] = all_ref[:, inner : 2 * inner]
     basis_ref[...] = all_ref[:, 2 * inner :].T[: basis_ref.shape[0], :]
 
 
-def finish(offsets, mine, other, inner, width, nbasis):
+def finish(offsets, mine, other, shared, inner, width, nbasis):
     return pl.pallas_call(
         lambda *refs: finish_kernel(offsets, *refs),
         in_specs=[VMEM] * 2,
@@ -485,7 +496,10 @@
             jax.ShapeDtypeStruct((width, inner), F32),
             jax.ShapeDtypeStruct((nbasis, width), F32),
         ],
-        scratch_shapes=[pltpu.VMEM((width, 2 * inner + 128), F32)],
+        scratch_shapes=[
+            pltpu.VMEM((width, 2 * inner + 128), F32),
+            pltpu.VMEM((2 * shared, 128), F32),
+        ],
         compiler_params=limits(12),
         name="finish",
     )(mine, other)
@@ -508,15 +522,24 @@
     return sum(part.astype(F32) for part in parts).astype(BF16)
 
 
-def scattered_sum(value, axis, low, members):
+def scattered_sum(values, axis, low, members, riders):
     digit = (lax.axis_index(axis) // low) % members
-    rows = value.shape[0] // members
-
-    def piece(k):
+
+    def piece(value, k):
+        rows = value.shape[0] // members
         return lax.dynamic_slice_in_dim(value, (digit ^ k) * rows, rows, 0)
 
-    parts = [swapped(piece(k), axis, k * low) for k in range(members - 1, 0, -1)]
-    return total_of([piece(0)] + parts)
+    sums = [[piece(value, 0)] for value in values]
+    arrived = {}
+    for k in range(members - 1, 0, -1):
+        sent = [piece(value, k) for value in values] + riders.get(k, [])
+        received = swapped(jnp.concatenate(sent, axis=0), axis, k * low)
+        start = 0
+        for total in sums:
+            total.append(received[start : start + total[0].shape[0]])
+            start += total[0].shape[0]
+        arrived[k] = received[start:]
+    return [total_of(total) for total in sums], arrived
 
 
 def exchanged(value, axis, low, members):
@@ -538,14 +561,13 @@
     rows, inner = embed.shape
     trips, nbasis = basis.shape[:2]
 
-    pre, proj, *rest = project(embed, down_weight.T, outgoing_edge_rows)
-    ghosts = pair_exchange(rest[:4])
-    embed_v, down_v, outgoing_v = rest[4:]
-
-    index_v, count_v, up_v, bw_v, dres, mine, other = residual(
+    *sends, embed_v, outgoing_v = select(embed, outgoing_edge_rows)
+    ghosts = pair_exchange(sends)
+    down_v, index_v, count_v, up_v, bw_v, dres, mine, other, pre, proj = residual(
         embed_v,
         residual_weight,
         cotangent,
+        down_weight.T,
         triplet_row_index,
         triplet_slot_count.reshape(1, rows),
         up_weight,
@@ -553,8 +575,11 @@
     )
     share = total_of([mine, swapped(other, "brick", 1)])
 
-    own, *terms, grads = triplets(
+    own, first, second, last, mine, other = triplets(
         proj,
+        pre,
+        embed_v,
+        down_v,
         ghosts,
         basis.reshape(trips * nbasis, rows),
         index_v,
@@ -563,34 +588,39 @@
         cotangent,
         bw_v,
     )
-    *terms, share = lax.optimization_barrier((*terms, share))
-    backs = pair_exchange(terms)
+    mine, other, share = lax.optimization_barrier((mine, other, share))
+    received = swapped(other, "brick", 1)
+    shared = mine.shape[0]
+    mine = total_of([mine, received[:shared]])
+    ring = lax.axis_size("slab")
+    riders = {1: [first]}
+    if ring == 4:
+        riders[3] = [second]
+    backs = [None, None, received[shared:], paired(last, "brick", 1)]
     slab_groups = groups_of("slab", 1)
     for low, members in reversed(slab_groups):
-        share = scattered_sum(share, "slab", low, members)
-    *backs, share = lax.optimization_barrier((*backs, share))
-    dpre, mine, other = collect(own, backs, outgoing_v, pre, embed_v, grads)
-
-    mine = total_of([mine, swapped(other, "brick", 1)])
-    mine, dpre = lax.optimization_barrier((mine, dpre))
-    edge_grad = edge_gradient(dres, residual_weight, dpre, down_v)
-    count = mine.shape[0]
-    value = jnp.concatenate([mine, share], axis=0)
+        (share, mine), arrived = scattered_sum(
+            [share, mine], "slab", low, members, riders if low == 1 else {}
+        )
+    backs[0] = arrived[1]
+    backs[1] = arrived[3] if ring == 4 else paired(second, "slab", 1)
+    edge_grad = edge_gradient(own, backs, outgoing_v, pre, residual_weight, down_v, dres)
+
+    value = jnp.concatenate([share, mine], axis=0)
     for low, members in groups_of("brick", 2):
         value = total_of([value, *exchanged(value, "brick", low, members).values()])
     value, edge_grad = lax.optimization_barrier((value, edge_grad))
-    pieces = {0: value[count:]}
+    pieces = {0: value}
     for low, members in slab_groups:
-        received = exchanged(value, "slab", low, members)
-        mine = total_of([value[:count]] + [other[:count] for other in received.values()])
         known = sorted(pieces)
-        step = share.shape[0]
-        for k, other in received.items():
+        value = jnp.concatenate([pieces[o] for o in known], axis=0)
+        for k, other in exchanged(value, "slab", low, members).items():
             for i, offset in enumerate(known):
-                pieces[offset ^ k] = other[count + i * step : count + (i + 1) * step]
-        value = jnp.concatenate([mine] + [pieces[o] for o in sorted(pieces)], axis=0)
+                step = pieces[offset].shape[0]
+                pieces[offset ^ k] = other[i * step : (i + 1) * step]
+    value = jnp.concatenate([pieces[o] for o in sorted(pieces)], axis=0)
     residual_grad, down_grad, up_grad, basis_grad = finish(
-        sorted(pieces), value, swapped(value, "brick", 1), inner, proj.shape[0], nbasis
+        sorted(pieces), value, swapped(value, "brick", 1), shared, inner, proj.shape[0], nbasis
     )
     return edge_grad, residual_grad, down_grad.T, up_grad, basis_grad
 

time: 64.4 us -> 59.5 us (0.924)
  waiting for transfers between devices: 18.3 us -> 11 us
  local copies, waits for them, and re-layouts: 0.11 us -> 3.1 us
  starting transfers between devices: 22.5 us -> 20.7 us
  other arithmetic: 0.26 us -> 1.19 us
    ppermute x12, waiting for transfers between devices: 15.2 us -> 11 us  [swapped(): lax.ppermute(value, axis, [(i, i ^ offset) for i in range(lax.axis_size(a...]
    ppermute x8 -> x5, waiting for transfers between devices: 3.16 us -> 0.01 us  [paired(): return lax.ppermute(value, axis, pairs)]
    unnamed x6 -> x13, local copies, waits for them, and re-layouts: 0.05 us -> 3.05 us
    ppermute x8 -> x5, starting transfers between devices: 10.8 us -> 8.41 us  [paired(): return lax.ppermute(value, axis, pairs)]
    convert_element_type x4 -> x5, other arithmetic: 0.22 us -> 1.16 us  [total_of(): return sum((part.astype(F32) for part in parts)).astype(BF16)]
    pallas_call x3 -> x2, Pallas kernels: 6.08 us -> 5.91 us  [the longest x1 3.82 us: edge_gradient(): pl.pallas_call(edge_kernel, in_specs=[VMEM] * len(operands) + [HBM], out_...]
  transfers between devices with their start and end apart: 20 -> 17, of which waited for: 11 -> 7; matrix products, arithmetic and copies ran while one was open for 0% -> 0% of each run, Pallas kernels for 28% -> 32%
where the time goes in v4:
time: 59.5 us; the launch traced here: 59.2 us
  Pallas kernels  22.4 us (38%)
  starting transfers between devices  20.7 us (35%)
  waiting for transfers between devices  11 us (18%)
  local copies, waits for them, and re-layouts  3.1 us (5%)
  other arithmetic  1.19 us (2%)
  between operations  0.82 us (1%)
    ppermute x12, starting transfers between devices, swapped(): lax.ppermute(value, axis, [(i, i ^ offset) for i in range(lax.axis_size(a...  12.3 us
    pallas_call x1, Pallas kernels, triplets(): pl.pallas_call(triplet_kernel, in_specs=[VMEM] * len(operands) + [HBM] *...  11.7 us
    ppermute x12, waiting for transfers between devices, swapped(): lax.ppermute(value, axis, [(i, i ^ offset) for i in range(lax.axis_size(a...  11 us
    ppermute x5, starting transfers between devices, paired(): return lax.ppermute(value, axis, pairs)  8.41 us
    pallas_call x1, Pallas kernels, edge_gradient(): pl.pallas_call(edge_kernel, in_specs=[VMEM] * len(operands) + [HBM], out_...  3.82 us
    pallas_call x1, Pallas kernels, residual(): pl.pallas_call(residual_kernel, in_specs=[VMEM] * 2 + [HBM] * (1 + len(st...  3.66 us
    unnamed x13, local copies, waits for them, and re-layouts  3.05 us
    pallas_call x1, Pallas kernels, select(): pl.pallas_call(select_kernel, in_specs=[HBM] * 2, out_specs=[VMEM] * 6, o...  2.09 us
  transfers between devices with their start and end apart: 17, of which 7 were waited for; matrix products, arithmetic and copies ran while one was open for 0% of the time, Pallas kernels for 32%

profile of v4, /device:TPU:0, one launch (start us, length us, event | category | flops | bytes accessed | tf_op | source)
XLA Modules:
  0.0 59.2 jit_solution(17182251886920664340)
XLA Ops:
  0.6 2.1 %select.5 = (bf16[128,512]{1,0:T(8,128)(2,1)S(1)}, bf16[128,512]{1,0:T(8,128)(2,1)S(1)}, bf16[128,512]{1,0:T(8,128)(2,1)S(1)}, bf16[128,512]{1,0:T(8,128)(2,1)S(...) custom-call(bf16[1024,512]{1,0:T(8,128)(2,1)} %embed_ref.1, s32[4,128]{1,0:T(4,128)} %rows_ref.1), custom_call_target="tpu_custom_call" | custom-call | tf_op jit(solution)/shard_map/select/pallas_call | solution.py:131
  2.7 3.0 %collective-permute-start = (bf16[128,512]{1,0:T(8,128)(2,1)S(1)}, bf16[128,512]{1,0:T(8,128)(2,1)S(1)}, u32[]{:S(2)}, u32[]{:S(2)}) collective-permute-start(bf16[128,512]{1,0:T(8,128)(2,1)S(1)} %get-tuple-element.40), channel_id=1, source_target_pairs={{0,8},{8,0},{16,24},{24,16},{1,9},{9,1},{17,25},{25,17},{2,10},{10... | collective-permute-start | bytes 393224 | tf_op jit(solution)/shard_map/ppermute | solution.py:104
  5.7 1.5 %collective-permute-start.1 = (bf16[128,512]{1,0:T(8,128)(2,1)S(1)}, bf16[128,512]{1,0:T(8,128)(2,1)S(1)}, u32[]{:S(2)}, u32[]{:S(2)}) collective-permute-start(bf16[128,512]{1,0:T(8,128)(2,1)S(1)} %get-tuple-element.41), channel_id=1, source_target_pairs={{8,16},{16,8},{24,0},{0,24},{9,17},{17,9},{25,1},{1,25},{10,18},{1... | collective-permute-start | bytes 393224 | tf_op jit(solution)/shard_map/ppermute | solution.py:104
  7.2 3.7 %collective-permute-start.3 = (bf16[128,512]{1,0:T(8,128)(2,1)S(1)}, bf16[128,512]{1,0:T(8,128)(2,1)S(1)}, u32[]{:S(2)}, u32[]{:S(2)}) collective-permute-start(bf16[128,512]{1,0:T(8,128)(2,1)S(1)} %get-tuple-element.43), channel_id=1, source_target_pairs={{1,2},{2,1},{3,4},{4,3},{5,6},{6,5},{7,0},{0,7},{9,10},{10,9},{11,... | collective-permute-start | bytes 393224 | tf_op jit(solution)/shard_map/ppermute | solution.py:104
  10.9 3.7 %residual.1 = (bf16[64,512]{1,0:T(8,128)(2,1)S(1)}, s32[16,1024]{1,0:T(8,128)S(1)}, s32[1,1024]{1,0:T(1,128)S(1)}, bf16[64,512]{1,0:T(8,128)(2,1)S(1)}, bf16[16,...) custom-call(bf16[1024,512]{1,0:T(8,128)(2,1)S(1)} %get-tuple-element, ...), custom_call_target="tpu_custom_call" | custom-call | flops 1610612736 | tf_op jit(solution)/shard_map/residual/pallas_call | solution.py:193
  14.6 0.6 %copy-done.1 = bf16[64,1024]{1,0:T(8,128)(2,1)} copy-done((bf16[64,1024]{1,0:T(8,128)(2,1)}, bf16[64,1024]{1,0:T(8,128)(2,1)S(1)}, u32[]{:S(2)}) %copy-start.1) | copy-done | bytes 131096
  15.3 0.6 %copy-done.3 = bf16[64,512]{1,0:T(8,128)(2,1)} copy-done((bf16[64,512]{1,0:T(8,128)(2,1)}, bf16[64,512]{1,0:T(8,128)(2,1)S(1)}, u32[]{:S(2)}) %copy-start.3) | copy-done | bytes 65560
  15.9 0.9 %copy-done.2 = bf16[64,1024]{1,0:T(8,128)(2,1)S(1)} copy-done((bf16[64,1024]{1,0:T(8,128)(2,1)S(1)}, bf16[64,1024]{1,0:T(8,128)(2,1)}, u32[]{:S(2)}) %copy-start.2) | copy-done | bytes 131096
  16.8 0.8 %copy-done.4 = bf16[64,512]{1,0:T(8,128)(2,1)S(1)} copy-done((bf16[64,512]{1,0:T(8,128)(2,1)S(1)}, bf16[64,512]{1,0:T(8,128)(2,1)}, u32[]{:S(2)}) %copy-start.4) | copy-done | bytes 65560
  17.7 11.7 %triplets.1 = (f32[64,1024]{1,0:T(8,128)S(1)}, bf16[64,128]{1,0:T(8,128)(2,1)S(1)}, bf16[64,128]{1,0:T(8,128)(2,1)S(1)}, bf16[64,128]{1,0:T(8,128)(2,1)S(1)}, bf...) custom-call(bf16[64,1024]{1,0:T(8,128)(2,1)S(1)} %copy-done.2, f32[64,1024]{1,0:T(8,128)S(1)} %get-tuple-element.38.pre_ref, ...), custom_call_target="tpu_custom_call" | custom-call | flops 12884901888 | tf_op jit(solution)/shard_map/triplets/pallas_call | solution.py:379
  29.4 1.0 %add_convert_fusion = bf16[1024,128]{1,0:T(8,128)(2,1)S(1)} fusion(bf16[1024,128]{1,0:T(8,128)(2,1)} %collective-permute-done.4, bf16[1024,128]{1,0:T(8,128)(2,1)S(1)} %get-tuple-element.50), kind=kLoop, calls=%fused_computation | loop fusion | flops 524288 | bytes 786432 | tf_op jit(solution)/shard_map/convert_element_type | solution.py:522
  30.5 0.6 collective-permute-start.5
  31.0 0.9 %collective-permute-done.5 = bf16[384,128]{1,0:T(8,128)(2,1)S(1)} collective-permute-done((bf16[384,128]{1,0:T(8,128)(2,1)S(1)}, bf16[384,128]{1,0:T(8,128)(2,1)S(1)}, u32[]{:S(2)}, u32[]{:S(2)}) %collective-permute-start.5) | collective-permute-done | bytes 98336 | tf_op jit(solution)/shard_map/ppermute | solution.py:509
  32.0 1.5 %collective-permute-start.6 = (bf16[400,128]{1,0:T(8,128)(2,1)S(1)}, bf16[400,128]{1,0:T(8,128)(2,1)S(1)}, u32[]{:S(2)}, u32[]{:S(2)}) collective-permute-start(bf16[400,128]{1,0:T(8,128)(2,1)S(1)} %pad_maximum_fusion), channel_id=1, source_target_pairs={{0,24},{8,16},{16,8},{24,0},{1,25},{9,17},{17,9},{25,1},{2,26},{10... | collective-permute-start | bytes 307208 | tf_op jit(solution)/shard_map/ppermute | solution.py:509
  33.6 0.6 %collective-permute-start.8 = (bf16[400,128]{1,0:T(8,128)(2,1)S(1)}, bf16[400,128]{1,0:T(8,128)(2,1)S(1)}, u32[]{:S(2)}, u32[]{:S(2)}) collective-permute-start(bf16[400,128]{1,0:T(8,128)(2,1)S(1)} %pad_maximum_fusion.1), channel_id=1, source_target_pairs={{0,8},{8,0},{16,24},{24,16},{1,9},{9,1},{17,25},{25,17},{2,10},{10... | collective-permute-start | bytes 307208 | tf_op jit(solution)/shard_map/ppermute | solution.py:509
  34.2 1.5 %collective-permute-start.7 = (bf16[336,128]{1,0:T(8,128)(2,1)S(1)}, bf16[336,128]{1,0:T(8,128)(2,1)S(1)}, u32[]{:S(2)}, u32[]{:S(2)}) collective-permute-start(bf16[336,128]{1,0:T(8,128)(2,1)S(1)} %pad_maximum_fusion.2), channel_id=1, source_target_pairs={{0,16},{8,24},{16,0},{24,8},{1,17},{9,25},{17,1},{25,9},{2,18},{10... | collective-permute-start | bytes 258056 | tf_op jit(solution)/shard_map/ppermute | solution.py:509
  35.7 0.2 collective-permute-start.12
  35.9 4.1 %collective-permute-done.7 = bf16[336,128]{1,0:T(8,128)(2,1)S(1)} collective-permute-done((bf16[336,128]{1,0:T(8,128)(2,1)S(1)}, bf16[336,128]{1,0:T(8,128)(2,1)S(1)}, u32[]{:S(2)}, u32[]{:S(2)}) %collective-permute-start.7) | collective-permute-done | bytes 86048 | tf_op jit(solution)/shard_map/ppermute | solution.py:509
  40.1 0.3 collective-permute-start.10
  40.4 1.4 %collective-permute-start.11 = (bf16[336,128]{1,0:T(8,128)(2,1)S(1)}, bf16[336,128]{1,0:T(8,128)(2,1)S(1)}, u32[]{:S(2)}, u32[]{:S(2)}) collective-permute-start(bf16[336,128]{1,0:T(8,128)(2,1)S(1)} %pad_maximum_fusion.3), channel_id=1, source_target_pairs={{0,2},{1,3},{2,0},{3,1},{4,6},{5,7},{6,4},{7,5},{8,10},{9,11},{10,... | collective-permute-start | bytes 258056 | tf_op jit(solution)/shard_map/ppermute | solution.py:509
  41.8 2.7 %collective-permute-start.9 = (bf16[336,128]{1,0:T(8,128)(2,1)S(1)}, bf16[336,128]{1,0:T(8,128)(2,1)S(1)}, u32[]{:S(2)}, u32[]{:S(2)}) collective-permute-start(bf16[336,128]{1,0:T(8,128)(2,1)S(1)} %pad_maximum_fusion.3), channel_id=1, source_target_pairs={{0,6},{1,7},{2,4},{3,5},{4,2},{5,3},{6,0},{7,1},{8,14},{9,15},{10,... | collective-permute-start | bytes 258056 | tf_op jit(solution)/shard_map/ppermute | solution.py:509
  44.6 3.8 %edge_gradient.1 = bf16[1024,512]{1,0:T(8,128)(2,1)} custom-call(f32[64,1024]{1,0:T(8,128)S(1)} %get-tuple-element.57.own_ref, bf16[64,128]{1,0:T(8,128)(2,1)S(1)} %slice.47.b0_ref, bf16[64,128]{1,0:T(8,128)(2,1)S(1)} %slice.48.b1_ref, bf16[64,128]{1,0:T(8,128)(2,1)S(1)} %slice.49.b2_ref, bf16[64,128]{1,0:T(8,128)(2,1)S(1)} %collective-permute-done.12.b3_ref, ...), custom_call_target="tpu_custom_call" | custom-call | flops 1207959552 | tf_op jit(solution)/shard_map/edge_gradient/pallas_call | solution.py:444
  48.4 0.2 collective-permute-done.9
  48.6 1.6 %collective-permute-start.13 = (bf16[336,128]{1,0:T(8,128)(2,1)S(1)}, bf16[336,128]{1,0:T(8,128)(2,1)S(1)}, u32[]{:S(2)}, u32[]{:S(2)}) collective-permute-start(bf16[336,128]{1,0:T(8,128)(2,1)S(1)} %add_convert_fusion.1), channel_id=1, source_target_pairs={{0,8},{8,0},{16,24},{24,16},{1,9},{9,1},{17,25},{25,17},{2,10},{10... | collective-permute-start | bytes 258056 | tf_op jit(solution)/shard_map/ppermute | solution.py:509
  50.2 0.7 %collective-permute-start.14 = (bf16[336,128]{1,0:T(8,128)(2,1)S(1)}, bf16[336,128]{1,0:T(8,128)(2,1)S(1)}, u32[]{:S(2)}, u32[]{:S(2)}) collective-permute-start(bf16[336,128]{1,0:T(8,128)(2,1)S(1)} %add_convert_fusion.1), channel_id=1, source_target_pairs={{0,16},{8,24},{16,0},{24,8},{1,17},{9,25},{17,1},{25,9},{2,18},{10... | collective-permute-start | bytes 258056 | tf_op jit(solution)/shard_map/ppermute | solution.py:509
  50.9 1.2 %collective-permute-start.15 = (bf16[336,128]{1,0:T(8,128)(2,1)S(1)}, bf16[336,128]{1,0:T(8,128)(2,1)S(1)}, u32[]{:S(2)}, u32[]{:S(2)}) collective-permute-start(bf16[336,128]{1,0:T(8,128)(2,1)S(1)} %add_convert_fusion.1), channel_id=1, source_target_pairs={{0,24},{8,16},{16,8},{24,0},{1,25},{9,17},{17,9},{25,1},{2,26},{10... | collective-permute-start | bytes 258056 | tf_op jit(solution)/shard_map/ppermute | solution.py:509
  52.2 1.5 %collective-permute-done.13 = bf16[336,128]{1,0:T(8,128)(2,1)S(1)} collective-permute-done((bf16[336,128]{1,0:T(8,128)(2,1)S(1)}, bf16[336,128]{1,0:T(8,128)(2,1)S(1)}, u32[]{:S(2)}, u32[]{:S(2)}) %collective-permute-start.13) | collective-permute-done | bytes 86048 | tf_op jit(solution)/shard_map/ppermute | solution.py:509
  53.8 1.3 %collective-permute-done.14 = bf16[336,128]{1,0:T(8,128)(2,1)S(1)} collective-permute-done((bf16[336,128]{1,0:T(8,128)(2,1)S(1)}, bf16[336,128]{1,0:T(8,128)(2,1)S(1)}, u32[]{:S(2)}, u32[]{:S(2)}) %collective-permute-start.14) | collective-permute-done | bytes 86048 | tf_op jit(solution)/shard_map/ppermute | solution.py:509
  55.0 1.3 %collective-permute-done.15 = bf16[336,128]{1,0:T(8,128)(2,1)S(1)} collective-permute-done((bf16[336,128]{1,0:T(8,128)(2,1)S(1)}, bf16[336,128]{1,0:T(8,128)(2,1)S(1)}, u32[]{:S(2)}, u32[]{:S(2)}) %collective-permute-start.15) | collective-permute-done | bytes 86048 | tf_op jit(solution)/shard_map/ppermute | solution.py:509
  56.3 0.1 collective-permute-start.16
  56.4 1.6 %collective-permute-done.16.refs_1_ = bf16[1344,128]{1,0:T(8,128)(2,1)S(1)} collective-permute-done((bf16[1344,128]{1,0:T(8,128)(2,1)S(1)}, bf16[1344,128]{1,0:T(8,128)(2,1)S(1)}, u32[]{:S(2)}, u32[]{:S(2)}) %collective-permute-start.16) | collective-permute-done | bytes 344096 | tf_op jit(solution)/shard_map/ppermute | solution.py:509
  58.1 1.1 %finish.1 = (f32[512,512]{1,0:T(8,128)}, f32[64,512]{1,0:T(8,128)}, f32[64,512]{1,0:T(8,128)}, f32[16,64]{1,0:T(8,128)}) custom-call(bf16[1344,128]{1,0:T(8,128)(2,1)S(1)} %constant_dynamic-update-slice_fusion.refs_0_, bf16[1344,128]{1,0:T(8,128)(2,1)S(1)} %collective-permute-done.16.refs_1_), custom_call_target="tpu_custom_call" | custom-call | tf_op jit(solution)/shard_map/finish/pallas_call | solution.py:489
  (35 shorter events, 0.3 us)
Async XLA Ops:
  0.6 10.3 %copy-start = (bf16[512,512]{1,0:T(8,128)(2,1)S(1)}, bf16[512,512]{1,0:T(8,128)(2,1)}, u32[]{:S(2)}) copy-start(bf16[512,512]{1,0:T(8,128)(2,1)} %weight_ref.3) | copy-start | bytes 1572868
  2.7 13.2 %collective-permute-start = (bf16[128,512]{1,0:T(8,128)(2,1)S(1)}, bf16[128,512]{1,0:T(8,128)(2,1)S(1)}, u32[]{:S(2)}, u32[]{:S(2)}) collective-permute-start(bf16[128,512]{1,0:T(8,128)(2,1)S(1)} %get-tuple-element.40), channel_id=1, source_target_pairs={{0,8},{8,0},{16,24},{24,16},{1,9},{9,1},{17,25},{25,17},{2,10},{10... | collective-permute-start | bytes 393224 | tf_op jit(solution)/shard_map/ppermute | solution.py:104
  5.7 10.2 %collective-permute-start.1 = (bf16[128,512]{1,0:T(8,128)(2,1)S(1)}, bf16[128,512]{1,0:T(8,128)(2,1)S(1)}, u32[]{:S(2)}, u32[]{:S(2)}) collective-permute-start(bf16[128,512]{1,0:T(8,128)(2,1)S(1)} %get-tuple-element.41), channel_id=1, source_target_pairs={{8,16},{16,8},{24,0},{0,24},{9,17},{17,9},{25,1},{1,25},{10,18},{1... | collective-permute-start | bytes 393224 | tf_op jit(solution)/shard_map/ppermute | solution.py:104
  7.2 8.7 %collective-permute-start.2 = (bf16[128,512]{1,0:T(8,128)(2,1)S(1)}, bf16[128,512]{1,0:T(8,128)(2,1)S(1)}, u32[]{:S(2)}, u32[]{:S(2)}) collective-permute-start(bf16[128,512]{1,0:T(8,128)(2,1)S(1)} %get-tuple-element.42), channel_id=1, source_target_pairs={{0,1},{1,0},{2,3},{3,2},{4,5},{5,4},{6,7},{7,6},{8,9},{9,8},{10,11... | collective-permute-start | bytes 393224 | tf_op jit(solution)/shard_map/ppermute | solution.py:104
  7.2 8.7 %collective-permute-start.3 = (bf16[128,512]{1,0:T(8,128)(2,1)S(1)}, bf16[128,512]{1,0:T(8,128)(2,1)S(1)}, u32[]{:S(2)}, u32[]{:S(2)}) collective-permute-start(bf16[128,512]{1,0:T(8,128)(2,1)S(1)} %get-tuple-element.43), channel_id=1, source_target_pairs={{1,2},{2,1},{3,4},{4,3},{5,6},{6,5},{7,0},{0,7},{9,10},{10,9},{11,... | collective-permute-start | bytes 393224 | tf_op jit(solution)/shard_map/ppermute | solution.py:104
  14.6 0.7 %copy-start.1 = (bf16[64,1024]{1,0:T(8,128)(2,1)}, bf16[64,1024]{1,0:T(8,128)(2,1)S(1)}, u32[]{:S(2)}) copy-start(bf16[64,1024]{1,0:T(8,128)(2,1)S(1)} %get-tuple-element.37.proj_ref) | copy-start | bytes 393220
  15.3 0.6 %copy-start.3 = (bf16[64,512]{1,0:T(8,128)(2,1)}, bf16[64,512]{1,0:T(8,128)(2,1)S(1)}, u32[]{:S(2)}) copy-start(bf16[64,512]{1,0:T(8,128)(2,1)S(1)} %get-tuple-element.46.up_ref) | copy-start | bytes 196612
  15.9 13.5 %collective-permute-start.4 = (bf16[1024,128]{1,0:T(8,128)(2,1)S(1)}, bf16[1024,128]{1,0:T(8,128)(2,1)}, u32[]{:S(2)}, u32[]{:S(2)}) collective-permute-start(bf16[1024,128]{1,0:T(8,128)(2,1)S(1)} %get-tuple-element.51), channel_id=1, source_target_pairs={{0,1},{1,0},{2,3},{3,2},{4,5},{5,4},{6,7},{7,6},{8,9},{9,8},{10,11... | collective-permute-start | bytes 786440 | tf_op jit(solution)/shard_map/ppermute | solution.py:509
  15.9 0.9 %copy-start.2 = (bf16[64,1024]{1,0:T(8,128)(2,1)S(1)}, bf16[64,1024]{1,0:T(8,128)(2,1)}, u32[]{:S(2)}) copy-start(bf16[64,1024]{1,0:T(8,128)(2,1)} %copy-done.1) | copy-start | bytes 393220
  16.8 0.8 %copy-start.4 = (bf16[64,512]{1,0:T(8,128)(2,1)S(1)}, bf16[64,512]{1,0:T(8,128)(2,1)}, u32[]{:S(2)}) copy-start(bf16[64,512]{1,0:T(8,128)(2,1)} %copy-done.3) | copy-start | bytes 196612
  30.5 1.5 %collective-permute-start.5 = (bf16[384,128]{1,0:T(8,128)(2,1)S(1)}, bf16[384,128]{1,0:T(8,128)(2,1)S(1)}, u32[]{:S(2)}, u32[]{:S(2)}) collective-permute-start(bf16[384,128]{1,0:T(8,128)(2,1)S(1)} %get-tuple-element.54), channel_id=1, source_target_pairs={{0,1},{1,0},{2,3},{3,2},{4,5},{5,4},{6,7},{7,6},{8,9},{9,8},{10,11... | collective-permute-start | bytes 294920 | tf_op jit(solution)/shard_map/ppermute | solution.py:509
  32.0 8.0 %collective-permute-start.6 = (bf16[400,128]{1,0:T(8,128)(2,1)S(1)}, bf16[400,128]{1,0:T(8,128)(2,1)S(1)}, u32[]{:S(2)}, u32[]{:S(2)}) collective-permute-start(bf16[400,128]{1,0:T(8,128)(2,1)S(1)} %pad_maximum_fusion), channel_id=1, source_target_pairs={{0,24},{8,16},{16,8},{24,0},{1,25},{9,17},{17,9},{25,1},{2,26},{10... | collective-permute-start | bytes 307208 | tf_op jit(solution)/shard_map/ppermute | solution.py:509
  33.6 6.4 %collective-permute-start.8 = (bf16[400,128]{1,0:T(8,128)(2,1)S(1)}, bf16[400,128]{1,0:T(8,128)(2,1)S(1)}, u32[]{:S(2)}, u32[]{:S(2)}) collective-permute-start(bf16[400,128]{1,0:T(8,128)(2,1)S(1)} %pad_maximum_fusion.1), channel_id=1, source_target_pairs={{0,8},{8,0},{16,24},{24,16},{1,9},{9,1},{17,25},{25,17},{2,10},{10... | collective-permute-start | bytes 307208 | tf_op jit(solution)/shard_map/ppermute | solution.py:509
  34.2 5.8 %collective-permute-start.7 = (bf16[336,128]{1,0:T(8,128)(2,1)S(1)}, bf16[336,128]{1,0:T(8,128)(2,1)S(1)}, u32[]{:S(2)}, u32[]{:S(2)}) collective-permute-start(bf16[336,128]{1,0:T(8,128)(2,1)S(1)} %pad_maximum_fusion.2), channel_id=1, source_target_pairs={{0,16},{8,24},{16,0},{24,8},{1,17},{9,25},{17,1},{25,9},{2,18},{10... | collective-permute-start | bytes 258056 | tf_op jit(solution)/shard_map/ppermute | solution.py:509
  35.7 8.9 %collective-permute-start.12 = (bf16[64,128]{1,0:T(8,128)(2,1)S(1)}, bf16[64,128]{1,0:T(8,128)(2,1)S(1)}, u32[]{:S(2)}, u32[]{:S(2)}) collective-permute-start(bf16[64,128]{1,0:T(8,128)(2,1)S(1)} %get-tuple-element.58), channel_id=1, source_target_pairs={{1,2},{2,1},{3,4},{4,3},{5,6},{6,5},{7,0},{0,7},{9,10},{10,9},{11,... | collective-permute-start | bytes 49160 | tf_op jit(solution)/shard_map/ppermute | solution.py:104
  40.1 8.3 %collective-permute-start.10 = (bf16[336,128]{1,0:T(8,128)(2,1)S(1)}, bf16[336,128]{1,0:T(8,128)(2,1)S(1)}, u32[]{:S(2)}, u32[]{:S(2)}) collective-permute-start(bf16[336,128]{1,0:T(8,128)(2,1)S(1)} %pad_maximum_fusion.3), channel_id=1, source_target_pairs={{0,4},{1,5},{2,6},{3,7},{4,0},{5,1},{6,2},{7,3},{8,12},{9,13},{10,... | collective-permute-start | bytes 258056 | tf_op jit(solution)/shard_map/ppermute | solution.py:509
  40.4 8.0 %collective-permute-start.11 = (bf16[336,128]{1,0:T(8,128)(2,1)S(1)}, bf16[336,128]{1,0:T(8,128)(2,1)S(1)}, u32[]{:S(2)}, u32[]{:S(2)}) collective-permute-start(bf16[336,128]{1,0:T(8,128)(2,1)S(1)} %pad_maximum_fusion.3), channel_id=1, source_target_pairs={{0,2},{1,3},{2,0},{3,1},{4,6},{5,7},{6,4},{7,5},{8,10},{9,11},{10,... | collective-permute-start | bytes 258056 | tf_op jit(solution)/shard_map/ppermute | solution.py:509
  41.8 6.8 %collective-permute-start.9 = (bf16[336,128]{1,0:T(8,128)(2,1)S(1)}, bf16[336,128]{1,0:T(8,128)(2,1)S(1)}, u32[]{:S(2)}, u32[]{:S(2)}) collective-permute-start(bf16[336,128]{1,0:T(8,128)(2,1)S(1)} %pad_maximum_fusion.3), channel_id=1, source_target_pairs={{0,6},{1,7},{2,4},{3,5},{4,2},{5,3},{6,0},{7,1},{8,14},{9,15},{10,... | collective-permute-start | bytes 258056 | tf_op jit(solution)/shard_map/ppermute | solution.py:509
  48.6 5.1 %collective-permute-start.13 = (bf16[336,128]{1,0:T(8,128)(2,1)S(1)}, bf16[336,128]{1,0:T(8,128)(2,1)S(1)}, u32[]{:S(2)}, u32[]{:S(2)}) collective-permute-start(bf16[336,128]{1,0:T(8,128)(2,1)S(1)} %add_convert_fusion.1), channel_id=1, source_target_pairs={{0,8},{8,0},{16,24},{24,16},{1,9},{9,1},{17,25},{25,17},{2,10},{10... | collective-permute-start | bytes 258056 | tf_op jit(solution)/shard_map/ppermute | solution.py:509
  50.2 4.8 %collective-permute-start.14 = (bf16[336,128]{1,0:T(8,128)(2,1)S(1)}, bf16[336,128]{1,0:T(8,128)(2,1)S(1)}, u32[]{:S(2)}, u32[]{:S(2)}) collective-permute-start(bf16[336,128]{1,0:T(8,128)(2,1)S(1)} %add_convert_fusion.1), channel_id=1, source_target_pairs={{0,16},{8,24},{16,0},{24,8},{1,17},{9,25},{17,1},{25,9},{2,18},{10... | collective-permute-start | bytes 258056 | tf_op jit(solution)/shard_map/ppermute | solution.py:509
  50.9 5.4 %collective-permute-start.15 = (bf16[336,128]{1,0:T(8,128)(2,1)S(1)}, bf16[336,128]{1,0:T(8,128)(2,1)S(1)}, u32[]{:S(2)}, u32[]{:S(2)}) collective-permute-start(bf16[336,128]{1,0:T(8,128)(2,1)S(1)} %add_convert_fusion.1), channel_id=1, source_target_pairs={{0,24},{8,16},{16,8},{24,0},{1,25},{9,17},{17,9},{25,1},{2,26},{10... | collective-permute-start | bytes 258056 | tf_op jit(solution)/shard_map/ppermute | solution.py:509
  56.3 1.7 %collective-permute-start.16 = (bf16[1344,128]{1,0:T(8,128)(2,1)S(1)}, bf16[1344,128]{1,0:T(8,128)(2,1)S(1)}, u32[]{:S(2)}, u32[]{:S(2)}) collective-permute-start(bf16[1344,128]{1,0:T(8,128)(2,1)S(1)} %constant_dynamic-update-slice_fusion.refs_0_), channel_id=1, source_target_pairs={{0,1},{1,0},{2,3},{3,2},{4,5},{5,4},{6,7},{7,6},{8,9},{9,8},{10,11... | collective-permute-start | bytes 1032200 | tf_op jit(solution)/shard_map/ppermute | solution.py:509

commit v5 on v4

--- a/solution.py
+++ b/solution.py
@@ -28,8 +28,8 @@
     return [pltpu.with_memory_space_constraint(a, pltpu.HBM) for a in arrays]
 
 
-def limits(mib):
-    return pltpu.CompilerParams(vmem_limit_bytes=mib * 2**20)
+def limits():
+    return pltpu.CompilerParams(vmem_limit_bytes=30 * 2**20)
 
 
 def cost(flops):
@@ -134,16 +134,16 @@
         out_specs=[VMEM] * 6,
         out_shape=in_vmem(*[ghost] * 4, embed, outgoing),
         scratch_shapes=[pltpu.SemaphoreType.DMA((2,))],
-        compiler_params=limits(12),
+        compiler_params=limits(),
         name="select",
     )(*in_hbm(embed, outgoing))
 
 
 def residual_kernel(embed_ref, weight_ref, cotangent_ref, *refs):
-    count = (len(refs) - 9) // 2
+    count = (len(refs) - 8) // 2
     sources, targets = refs[:count], refs[count : 2 * count]
-    dres_ref, mine_ref, other_ref, pre_ref, proj_ref = refs[2 * count : 2 * count + 5]
-    cotangent_v, dres_v, grad_ref, sems = refs[2 * count + 5 :]
+    dres_ref, mine_ref, other_ref, pre_ref = refs[2 * count : 2 * count + 4]
+    cotangent_v, dres_v, grad_ref, sems = refs[2 * count + 4 :]
     rows = embed_ref.shape[0]
     block = min(rows, LANES)
     spans = [pl.ds(start, block) for start in range(0, rows, block)]
@@ -168,9 +168,7 @@
         dres_v[at, :] = (cotangent_v[at, :].astype(F32) * grad).astype(BF16)
         write.start()
     copies[0].wait()
-    pre = dot(targets[0][...], embed_ref[...], NT)
-    pre_ref[...] = pre
-    proj_ref[...] = (pre * sigmoid(pre)).astype(BF16)
+    pre_ref[...] = dot(targets[0][...], embed_ref[...], NT)
     grad_ref[...] = dot(embed_ref[...], dres_v[...], TN).astype(BF16)
     half = grad_ref.shape[0] // 2
     upper = lax.axis_index("brick") % 2
@@ -193,25 +191,24 @@
     return pl.pallas_call(
         residual_kernel,
         in_specs=[VMEM] * 2 + [HBM] * (1 + len(staged)),
-        out_specs=[VMEM] * len(staged) + [HBM] + [VMEM] * 4,
+        out_specs=[VMEM] * len(staged) + [HBM] + [VMEM] * 3,
         out_shape=in_vmem(*staged)
         + [pltpu.HBM(embed.shape, BF16)]
         + in_vmem(half, half)
-        + [pltpu.VMEM((width, rows), F32), pltpu.VMEM((width, rows), BF16)],
+        + [pltpu.VMEM((width, rows), F32)],
         scratch_shapes=[
             pltpu.VMEM(embed.shape, BF16),
             pltpu.VMEM(embed.shape, BF16),
             pltpu.VMEM(weight.shape, BF16),
             pltpu.SemaphoreType.DMA((2 * blocks + len(staged),)),
         ],
-        compiler_params=limits(16),
+        compiler_params=limits(),
         cost_estimate=cost(6 * embed.size * weight.shape[1]),
         name="residual",
     )(embed, weight, *in_hbm(cotangent, *staged))
 
 
 def triplet_kernel(
-    proj_ref,
     pre_ref,
     embed_ref,
     down_ref,
@@ -221,10 +218,10 @@
     g3_ref,
     index_ref,
     count_ref,
-    up_ref,
     bw_ref,
     basis_hbm,
     cotangent_hbm,
+    up_hbm,
     own_ref,
     t0_ref,
     t1_ref,
@@ -243,13 +240,16 @@
     acc_ref,
     basis_ref,
     cotangent_ref,
+    up_ref,
     sems,
 ):
     read_basis = pltpu.make_async_copy(basis_hbm, basis_ref, sems.at[0])
     read_cotangent = pltpu.make_async_copy(cotangent_hbm, cotangent_ref, sems.at[1])
+    read_up = pltpu.make_async_copy(up_hbm, up_ref, sems.at[2])
     read_basis.start()
     read_cotangent.start()
-    width, rows = proj_ref.shape
+    read_up.start()
+    width, rows = pre_ref.shape
     trips = index_ref.shape[0]
     nbasis = bw_ref.shape[0]
     own_groups = rows // LANES
@@ -261,7 +261,8 @@
         ghost_embed_ref[(first + 1) * ghost : (first + 2) * ghost, :] = jnp.where(odd, b, a)
     ghost_pre = dot(down_ref[...], ghost_embed_ref[...], NT)
     ghost_grad = silu_grad(ghost_pre)
-    table_ref[: own_groups * width, :] = stacked(proj_ref[...])
+    own_pre = pre_ref[...]
+    table_ref[: own_groups * width, :] = stacked((own_pre * sigmoid(own_pre)).astype(BF16))
     table_ref[own_groups * width :, :] = stacked((ghost_pre * sigmoid(ghost_pre)).astype(BF16))
     groups = table_ref.shape[0] // width
     tiles = rows // LANES
@@ -305,6 +306,7 @@
     sig = sigmoid(tsum)
     act = (tsum * sig).astype(BF16)
     read_cotangent.wait()
+    read_up.wait()
     cotangent = cotangent_ref[...]
     inner = cotangent.shape[1]
     rest_ref[:, inner : 2 * inner] = dot(act, cotangent, NN).astype(BF16)
@@ -361,13 +363,13 @@
 
 
 def triplets(
-    proj, pre, embed, down_t, ghosts, basis, index, count, up_weight, cotangent, basis_weight
+    pre, embed, down_t, ghosts, basis, index, count, up_weight, cotangent, basis_weight
 ):
-    width, rows = proj.shape
+    width, rows = pre.shape
     trips = index.shape[0]
     ghost, inner = ghosts[0].shape
     groups = (rows + 4 * ghost) // LANES
-    operands = (proj, pre, embed, down_t, *ghosts, index, count, up_weight, basis_weight)
+    operands = (pre, embed, down_t, *ghosts, index, count, basis_weight)
     unit = 16 * lax.axis_size("slab")
     total = 2 * inner + 128
     shared = -(-(width * total // 256) // unit) * unit
@@ -378,7 +380,7 @@
     )
     return pl.pallas_call(
         triplet_kernel,
-        in_specs=[VMEM] * len(operands) + [HBM] * 2,
+        in_specs=[VMEM] * len(operands) + [HBM] * 3,
         out_specs=[VMEM] * len(out_shape),
         out_shape=out_shape,
         scratch_shapes=[
@@ -394,12 +396,13 @@
             pltpu.VMEM((groups * width, LANES), F32),
             pltpu.VMEM(basis.shape, BF16),
             pltpu.VMEM(cotangent.shape, BF16),
-            pltpu.SemaphoreType.DMA((2,)),
+            pltpu.VMEM(up_weight.shape, BF16),
+            pltpu.SemaphoreType.DMA((3,)),
         ],
-        compiler_params=limits(28),
+        compiler_params=limits(),
         cost_estimate=cost(8 * trips * rows * width * (rows + 4 * ghost)),
         name="triplets",
-    )(*operands, *in_hbm(basis, cotangent))
+    )(*operands, *in_hbm(basis, cotangent, up_weight))
 
 
 def edge_kernel(
@@ -450,7 +453,7 @@
             pltpu.VMEM((rows, inner), BF16),
             pltpu.SemaphoreType.DMA((rows // min(rows, LANES),)),
         ],
-        compiler_params=limits(12),
+        compiler_params=limits(),
         cost_estimate=cost(4 * rows * inner * (inner + down_t.shape[0])),
         name="edge_gradient",
     )(*operands, *in_hbm(dres))
@@ -500,7 +503,7 @@
             pltpu.VMEM((width, 2 * inner + 128), F32),
             pltpu.VMEM((2 * shared, 128), F32),
         ],
-        compiler_params=limits(12),
+        compiler_params=limits(),
         name="finish",
     )(mine, other)
 
@@ -563,20 +566,18 @@
 
     *sends, embed_v, outgoing_v = select(embed, outgoing_edge_rows)
     ghosts = pair_exchange(sends)
-    down_v, index_v, count_v, up_v, bw_v, dres, mine, other, pre, proj = residual(
+    down_v, index_v, count_v, bw_v, dres, mine, other, pre = residual(
         embed_v,
         residual_weight,
         cotangent,
         down_weight.T,
         triplet_row_index,
         triplet_slot_count.reshape(1, rows),
-        up_weight,
         basis_weight,
     )
     share = total_of([mine, swapped(other, "brick", 1)])
 
     own, first, second, last, mine, other = triplets(
-        proj,
         pre,
         embed_v,
         down_v,
@@ -584,11 +585,10 @@
         basis.reshape(trips * nbasis, rows),
         index_v,
         count_v,
-        up_v,
+        up_weight,
         cotangent,
         bw_v,
     )
-    mine, other, share = lax.optimization_barrier((mine, other, share))
     received = swapped(other, "brick", 1)
     shared = mine.shape[0]
     mine = total_of([mine, received[:shared]])
@@ -620,7 +620,7 @@
                 pieces[offset ^ k] = other[i * step : (i + 1) * step]
     value = jnp.concatenate([pieces[o] for o in sorted(pieces)], axis=0)
     residual_grad, down_grad, up_grad, basis_grad = finish(
-        sorted(pieces), value, swapped(value, "brick", 1), shared, inner, proj.shape[0], nbasis
+        sorted(pieces), value, swapped(value, "brick", 1), shared, inner, pre.shape[0], nbasis
     )
     return edge_grad, residual_grad, down_grad.T, up_grad, basis_grad
 

time: 59.5 us -> 56.9 us (0.956)
  local copies, waits for them, and re-layouts: 3.1 us -> 0.1 us
  starting transfers between devices: 20.7 us -> 22.1 us
  other arithmetic: 1.19 us -> 0.24 us
    unnamed x13 -> x5, local copies, waits for them, and re-layouts: 3.05 us -> 0.04 us
    ppermute x5, starting transfers between devices: 8.41 us -> 9.81 us  [paired(): return lax.ppermute(value, axis, pairs)]
    convert_element_type x5, other arithmetic: 1.16 us -> 0.21 us  [total_of(): return sum((part.astype(F32) for part in parts)).astype(BF16)]
  transfers between devices with their start and end apart: 17 -> 17, of which waited for: 7 -> 9; matrix products, arithmetic and copies ran while one was open for 0% -> 0% of each run, Pallas kernels for 32% -> 13%
where the time goes in v5:
time: 56.9 us; the launch traced here: 56.7 us
  Pallas kernels  22.5 us (40%)
  starting transfers between devices  22.1 us (39%)
  waiting for transfers between devices  10.9 us (19%)
  between operations  0.81 us (1%)
    ppermute x12, starting transfers between devices, swapped(): lax.ppermute(value, axis, [(i, i ^ offset) for i in range(lax.axis_size(a...  12.3 us
    pallas_call x1, Pallas kernels, triplets(): pl.pallas_call(triplet_kernel, in_specs=[VMEM] * len(operands) + [HBM] *...  11.8 us
    ppermute x12, waiting for transfers between devices, swapped(): lax.ppermute(value, axis, [(i, i ^ offset) for i in range(lax.axis_size(a...  10.9 us
    ppermute x5, starting transfers between devices, paired(): return lax.ppermute(value, axis, pairs)  9.81 us
    pallas_call x1, Pallas kernels, edge_gradient(): pl.pallas_call(edge_kernel, in_specs=[VMEM] * len(operands) + [HBM], out_...  3.82 us
    pallas_call x1, Pallas kernels, residual(): pl.pallas_call(residual_kernel, in_specs=[VMEM] * 2 + [HBM] * (1 + len(st...  3.67 us
    pallas_call x1, Pallas kernels, select(): pl.pallas_call(select_kernel, in_specs=[HBM] * 2, out_specs=[VMEM] * 6, o...  2.08 us
  transfers between devices with their start and end apart: 17, of which 9 were waited for; matrix products, arithmetic and copies ran while one was open for 0% of the time, Pallas kernels for 13%

profile of v5, /device:TPU:0, one launch (start us, length us, event | category | flops | bytes accessed | tf_op | source)
XLA Modules:
  0.0 56.7 jit_solution(9234020054749252671)
XLA Ops:
  0.6 2.1 %select.5 = (bf16[128,512]{1,0:T(8,128)(2,1)S(1)}, bf16[128,512]{1,0:T(8,128)(2,1)S(1)}, bf16[128,512]{1,0:T(8,128)(2,1)S(1)}, bf16[128,512]{1,0:T(8,128)(2,1)S(...) custom-call(bf16[1024,512]{1,0:T(8,128)(2,1)} %embed_ref.1, s32[4,128]{1,0:T(4,128)} %rows_ref.1), custom_call_target="tpu_custom_call" | custom-call | tf_op jit(solution)/shard_map/select/pallas_call | solution.py:131
  2.7 3.0 %collective-permute-start.1 = (bf16[128,512]{1,0:T(8,128)(2,1)S(1)}, bf16[128,512]{1,0:T(8,128)(2,1)S(1)}, u32[]{:S(2)}, u32[]{:S(2)}) collective-permute-start(bf16[128,512]{1,0:T(8,128)(2,1)S(1)} %get-tuple-element.36), channel_id=1, source_target_pairs={{0,8},{8,0},{16,24},{24,16},{1,9},{9,1},{17,25},{25,17},{2,10},{10... | collective-permute-start | bytes 393224 | tf_op jit(solution)/shard_map/ppermute | solution.py:104
  5.7 1.5 %collective-permute-start.2 = (bf16[128,512]{1,0:T(8,128)(2,1)S(1)}, bf16[128,512]{1,0:T(8,128)(2,1)S(1)}, u32[]{:S(2)}, u32[]{:S(2)}) collective-permute-start(bf16[128,512]{1,0:T(8,128)(2,1)S(1)} %get-tuple-element.37), channel_id=1, source_target_pairs={{8,16},{16,8},{24,0},{0,24},{9,17},{17,9},{25,1},{1,25},{10,18},{1... | collective-permute-start | bytes 393224 | tf_op jit(solution)/shard_map/ppermute | solution.py:104
  7.2 3.7 %collective-permute-start.4 = (bf16[128,512]{1,0:T(8,128)(2,1)S(1)}, bf16[128,512]{1,0:T(8,128)(2,1)S(1)}, u32[]{:S(2)}, u32[]{:S(2)}) collective-permute-start(bf16[128,512]{1,0:T(8,128)(2,1)S(1)} %get-tuple-element.39), channel_id=1, source_target_pairs={{1,2},{2,1},{3,4},{4,3},{5,6},{6,5},{7,0},{0,7},{9,10},{10,9},{11,... | collective-permute-start | bytes 393224 | tf_op jit(solution)/shard_map/ppermute | solution.py:104
  10.9 3.7 %residual.1 = (bf16[64,512]{1,0:T(8,128)(2,1)S(1)}, s32[16,1024]{1,0:T(8,128)S(1)}, s32[1,1024]{1,0:T(1,128)S(1)}, bf16[16,64]{1,0:T(8,128)(2,1)S(1)}, bf16[1024...) custom-call(bf16[1024,512]{1,0:T(8,128)(2,1)S(1)} %get-tuple-element.3, ...), custom_call_target="tpu_custom_call" | custom-call | flops 1610612736 | tf_op jit(solution)/shard_map/residual/pallas_call | solution.py:191
  14.7 11.8 %triplets.1 = (f32[64,1024]{1,0:T(8,128)S(1)}, bf16[64,128]{1,0:T(8,128)(2,1)S(1)}, bf16[64,128]{1,0:T(8,128)(2,1)S(1)}, bf16[64,128]{1,0:T(8,128)(2,1)S(1)}, bf...) custom-call(f32[64,1024]{1,0:T(8,128)S(1)} %get-tuple-element.34.pre_ref, ...), custom_call_target="tpu_custom_call" | custom-call | flops 12884901888 | tf_op jit(solution)/shard_map/triplets/pallas_call | solution.py:381
  26.5 0.1 collective-permute-start.5
  26.5 0.5 collective-permute-start
  27.0 0.8 %collective-permute-done.5 = bf16[384,128]{1,0:T(8,128)(2,1)S(1)} collective-permute-done((bf16[384,128]{1,0:T(8,128)(2,1)S(1)}, bf16[384,128]{1,0:T(8,128)(2,1)S(1)}, u32[]{:S(2)}, u32[]{:S(2)}) %collective-permute-start.5) | collective-permute-done | bytes 98336 | tf_op jit(solution)/shard_map/ppermute | solution.py:512
  27.9 0.3 collective-permute-done
  28.2 0.1 add_convert_fusion
  28.3 1.5 %collective-permute-start.6 = (bf16[400,128]{1,0:T(8,128)(2,1)S(1)}, bf16[400,128]{1,0:T(8,128)(2,1)S(1)}, u32[]{:S(2)}, u32[]{:S(2)}) collective-permute-start(bf16[400,128]{1,0:T(8,128)(2,1)S(1)} %pad_maximum_fusion), channel_id=1, source_target_pairs={{0,24},{8,16},{16,8},{24,0},{1,25},{9,17},{17,9},{25,1},{2,26},{10... | collective-permute-start | bytes 307208 | tf_op jit(solution)/shard_map/ppermute | solution.py:512
  29.8 0.6 %collective-permute-start.8 = (bf16[400,128]{1,0:T(8,128)(2,1)S(1)}, bf16[400,128]{1,0:T(8,128)(2,1)S(1)}, u32[]{:S(2)}, u32[]{:S(2)}) collective-permute-start(bf16[400,128]{1,0:T(8,128)(2,1)S(1)} %pad_maximum_fusion.1), channel_id=1, source_target_pairs={{0,8},{8,0},{16,24},{24,16},{1,9},{9,1},{17,25},{25,17},{2,10},{10... | collective-permute-start | bytes 307208 | tf_op jit(solution)/shard_map/ppermute | solution.py:512
  30.4 1.5 %collective-permute-start.7 = (bf16[336,128]{1,0:T(8,128)(2,1)S(1)}, bf16[336,128]{1,0:T(8,128)(2,1)S(1)}, u32[]{:S(2)}, u32[]{:S(2)}) collective-permute-start(bf16[336,128]{1,0:T(8,128)(2,1)S(1)} %pad_maximum_fusion.2), channel_id=1, source_target_pairs={{0,16},{8,24},{16,0},{24,8},{1,17},{9,25},{17,1},{25,9},{2,18},{10... | collective-permute-start | bytes 258056 | tf_op jit(solution)/shard_map/ppermute | solution.py:512
  32.0 1.6 %collective-permute-start.12 = (bf16[64,128]{1,0:T(8,128)(2,1)S(1)}, bf16[64,128]{1,0:T(8,128)(2,1)S(1)}, u32[]{:S(2)}, u32[]{:S(2)}) collective-permute-start(bf16[64,128]{1,0:T(8,128)(2,1)S(1)} %get-tuple-element.48), channel_id=1, source_target_pairs={{1,2},{2,1},{3,4},{4,3},{5,6},{6,5},{7,0},{0,7},{9,10},{10,9},{11,... | collective-permute-start | bytes 49160 | tf_op jit(solution)/shard_map/ppermute | solution.py:104
  33.6 2.7 %collective-permute-done.7 = bf16[336,128]{1,0:T(8,128)(2,1)S(1)} collective-permute-done((bf16[336,128]{1,0:T(8,128)(2,1)S(1)}, bf16[336,128]{1,0:T(8,128)(2,1)S(1)}, u32[]{:S(2)}, u32[]{:S(2)}) %collective-permute-start.7) | collective-permute-done | bytes 86048 | tf_op jit(solution)/shard_map/ppermute | solution.py:512
  36.4 1.2 %collective-permute-start.10 = (bf16[336,128]{1,0:T(8,128)(2,1)S(1)}, bf16[336,128]{1,0:T(8,128)(2,1)S(1)}, u32[]{:S(2)}, u32[]{:S(2)}) collective-permute-start(bf16[336,128]{1,0:T(8,128)(2,1)S(1)} %pad_maximum_fusion.3), channel_id=1, source_target_pairs={{0,4},{1,5},{2,6},{3,7},{4,0},{5,1},{6,2},{7,3},{8,12},{9,13},{10,... | collective-permute-start | bytes 258056 | tf_op jit(solution)/shard_map/ppermute | solution.py:512
  37.6 1.9 %collective-permute-start.11 = (bf16[336,128]{1,0:T(8,128)(2,1)S(1)}, bf16[336,128]{1,0:T(8,128)(2,1)S(1)}, u32[]{:S(2)}, u32[]{:S(2)}) collective-permute-start(bf16[336,128]{1,0:T(8,128)(2,1)S(1)} %pad_maximum_fusion.3), channel_id=1, source_target_pairs={{0,2},{1,3},{2,0},{3,1},{4,6},{5,7},{6,4},{7,5},{8,10},{9,11},{10,... | collective-permute-start | bytes 258056 | tf_op jit(solution)/shard_map/ppermute | solution.py:512
  39.5 1.4 %collective-permute-start.9 = (bf16[336,128]{1,0:T(8,128)(2,1)S(1)}, bf16[336,128]{1,0:T(8,128)(2,1)S(1)}, u32[]{:S(2)}, u32[]{:S(2)}) collective-permute-start(bf16[336,128]{1,0:T(8,128)(2,1)S(1)} %pad_maximum_fusion.3), channel_id=1, source_target_pairs={{0,6},{1,7},{2,4},{3,5},{4,2},{5,3},{6,0},{7,1},{8,14},{9,15},{10,... | collective-permute-start | bytes 258056 | tf_op jit(solution)/shard_map/ppermute | solution.py:512
  40.9 3.8 %edge_gradient.1 = bf16[1024,512]{1,0:T(8,128)(2,1)} custom-call(f32[64,1024]{1,0:T(8,128)S(1)} %get-tuple-element.47.own_ref, bf16[64,128]{1,0:T(8,128)(2,1)S(1)} %slice.47.b0_ref, bf16[64,128]{1,0:T(8,128)(2,1)S(1)} %slice.48.b1_ref, bf16[64,128]{1,0:T(8,128)(2,1)S(1)} %slice.49.b2_ref, bf16[64,128]{1,0:T(8,128)(2,1)S(1)} %collective-permute-done.12.b3_ref, ...), custom_call_target="tpu_custom_call" | custom-call | flops 1207959552 | tf_op jit(solution)/shard_map/edge_gradient/pallas_call | solution.py:447
  44.7 0.1 collective-permute-done.11
  44.8 1.1 %collective-permute-done.9 = bf16[336,128]{1,0:T(8,128)(2,1)S(1)} collective-permute-done((bf16[336,128]{1,0:T(8,128)(2,1)S(1)}, bf16[336,128]{1,0:T(8,128)(2,1)S(1)}, u32[]{:S(2)}, u32[]{:S(2)}) %collective-permute-start.9) | collective-permute-done | bytes 86048 | tf_op jit(solution)/shard_map/ppermute | solution.py:512
  45.9 0.1 add_convert_fusion.1
  45.9 1.6 %collective-permute-start.13 = (bf16[336,128]{1,0:T(8,128)(2,1)S(1)}, bf16[336,128]{1,0:T(8,128)(2,1)S(1)}, u32[]{:S(2)}, u32[]{:S(2)}) collective-permute-start(bf16[336,128]{1,0:T(8,128)(2,1)S(1)} %add_convert_fusion.1), channel_id=1, source_target_pairs={{0,8},{8,0},{16,24},{24,16},{1,9},{9,1},{17,25},{25,17},{2,10},{10... | collective-permute-start | bytes 258056 | tf_op jit(solution)/shard_map/ppermute | solution.py:512
  47.5 0.9 %collective-permute-start.14 = (bf16[336,128]{1,0:T(8,128)(2,1)S(1)}, bf16[336,128]{1,0:T(8,128)(2,1)S(1)}, u32[]{:S(2)}, u32[]{:S(2)}) collective-permute-start(bf16[336,128]{1,0:T(8,128)(2,1)S(1)} %add_convert_fusion.1), channel_id=1, source_target_pairs={{0,16},{8,24},{16,0},{24,8},{1,17},{9,25},{17,1},{25,9},{2,18},{10... | collective-permute-start | bytes 258056 | tf_op jit(solution)/shard_map/ppermute | solution.py:512
  48.4 1.1 %collective-permute-start.15 = (bf16[336,128]{1,0:T(8,128)(2,1)S(1)}, bf16[336,128]{1,0:T(8,128)(2,1)S(1)}, u32[]{:S(2)}, u32[]{:S(2)}) collective-permute-start(bf16[336,128]{1,0:T(8,128)(2,1)S(1)} %add_convert_fusion.1), channel_id=1, source_target_pairs={{0,24},{8,16},{16,8},{24,0},{1,25},{9,17},{17,9},{25,1},{2,26},{10... | collective-permute-start | bytes 258056 | tf_op jit(solution)/shard_map/ppermute | solution.py:512
  49.5 1.6 %collective-permute-done.13 = bf16[336,128]{1,0:T(8,128)(2,1)S(1)} collective-permute-done((bf16[336,128]{1,0:T(8,128)(2,1)S(1)}, bf16[336,128]{1,0:T(8,128)(2,1)S(1)}, u32[]{:S(2)}, u32[]{:S(2)}) %collective-permute-start.13) | collective-permute-done | bytes 86048 | tf_op jit(solution)/shard_map/ppermute | solution.py:512
  51.1 0.9 %collective-permute-done.14 = bf16[336,128]{1,0:T(8,128)(2,1)S(1)} collective-permute-done((bf16[336,128]{1,0:T(8,128)(2,1)S(1)}, bf16[336,128]{1,0:T(8,128)(2,1)S(1)}, u32[]{:S(2)}, u32[]{:S(2)}) %collective-permute-start.14) | collective-permute-done | bytes 86048 | tf_op jit(solution)/shard_map/ppermute | solution.py:512
  52.0 1.7 %collective-permute-done.15 = bf16[336,128]{1,0:T(8,128)(2,1)S(1)} collective-permute-done((bf16[336,128]{1,0:T(8,128)(2,1)S(1)}, bf16[336,128]{1,0:T(8,128)(2,1)S(1)}, u32[]{:S(2)}, u32[]{:S(2)}) %collective-permute-start.15) | collective-permute-done | bytes 86048 | tf_op jit(solution)/shard_map/ppermute | solution.py:512
  53.8 0.1 collective-permute-start.16
  53.9 1.6 %collective-permute-done.16.refs_1_ = bf16[1344,128]{1,0:T(8,128)(2,1)S(1)} collective-permute-done((bf16[1344,128]{1,0:T(8,128)(2,1)S(1)}, bf16[1344,128]{1,0:T(8,128)(2,1)S(1)}, u32[]{:S(2)}, u32[]{:S(2)}) %collective-permute-start.16) | collective-permute-done | bytes 344096 | tf_op jit(solution)/shard_map/ppermute | solution.py:512
  55.5 1.1 %finish.1 = (f32[512,512]{1,0:T(8,128)}, f32[64,512]{1,0:T(8,128)}, f32[64,512]{1,0:T(8,128)}, f32[16,64]{1,0:T(8,128)}) custom-call(bf16[1344,128]{1,0:T(8,128)(2,1)S(1)} %constant_dynamic-update-slice_fusion.refs_0_, bf16[1344,128]{1,0:T(8,128)(2,1)S(1)} %collective-permute-done.16.refs_1_), custom_call_target="tpu_custom_call" | custom-call | tf_op jit(solution)/shard_map/finish/pallas_call | solution.py:492
  (27 shorter events, 0.2 us)
Async XLA Ops:
  0.6 10.3 %copy-start = (bf16[512,512]{1,0:T(8,128)(2,1)S(1)}, bf16[512,512]{1,0:T(8,128)(2,1)}, u32[]{:S(2)}) copy-start(bf16[512,512]{1,0:T(8,128)(2,1)} %weight_ref.3) | copy-start | bytes 1572868
  2.7 11.9 %collective-permute-start.1 = (bf16[128,512]{1,0:T(8,128)(2,1)S(1)}, bf16[128,512]{1,0:T(8,128)(2,1)S(1)}, u32[]{:S(2)}, u32[]{:S(2)}) collective-permute-start(bf16[128,512]{1,0:T(8,128)(2,1)S(1)} %get-tuple-element.36), channel_id=1, source_target_pairs={{0,8},{8,0},{16,24},{24,16},{1,9},{9,1},{17,25},{25,17},{2,10},{10... | collective-permute-start | bytes 393224 | tf_op jit(solution)/shard_map/ppermute | solution.py:104
  5.7 8.9 %collective-permute-start.2 = (bf16[128,512]{1,0:T(8,128)(2,1)S(1)}, bf16[128,512]{1,0:T(8,128)(2,1)S(1)}, u32[]{:S(2)}, u32[]{:S(2)}) collective-permute-start(bf16[128,512]{1,0:T(8,128)(2,1)S(1)} %get-tuple-element.37), channel_id=1, source_target_pairs={{8,16},{16,8},{24,0},{0,24},{9,17},{17,9},{25,1},{1,25},{10,18},{1... | collective-permute-start | bytes 393224 | tf_op jit(solution)/shard_map/ppermute | solution.py:104
  7.2 7.4 %collective-permute-start.3 = (bf16[128,512]{1,0:T(8,128)(2,1)S(1)}, bf16[128,512]{1,0:T(8,128)(2,1)S(1)}, u32[]{:S(2)}, u32[]{:S(2)}) collective-permute-start(bf16[128,512]{1,0:T(8,128)(2,1)S(1)} %get-tuple-element.38), channel_id=1, source_target_pairs={{0,1},{1,0},{2,3},{3,2},{4,5},{5,4},{6,7},{7,6},{8,9},{9,8},{10,11... | collective-permute-start | bytes 393224 | tf_op jit(solution)/shard_map/ppermute | solution.py:104
  7.2 7.4 %collective-permute-start.4 = (bf16[128,512]{1,0:T(8,128)(2,1)S(1)}, bf16[128,512]{1,0:T(8,128)(2,1)S(1)}, u32[]{:S(2)}, u32[]{:S(2)}) collective-permute-start(bf16[128,512]{1,0:T(8,128)(2,1)S(1)} %get-tuple-element.39), channel_id=1, source_target_pairs={{1,2},{2,1},{3,4},{4,3},{5,6},{6,5},{7,0},{0,7},{9,10},{10,9},{11,... | collective-permute-start | bytes 393224 | tf_op jit(solution)/shard_map/ppermute | solution.py:104
  26.5 1.4 %collective-permute-start.5 = (bf16[384,128]{1,0:T(8,128)(2,1)S(1)}, bf16[384,128]{1,0:T(8,128)(2,1)S(1)}, u32[]{:S(2)}, u32[]{:S(2)}) collective-permute-start(bf16[384,128]{1,0:T(8,128)(2,1)S(1)} %get-tuple-element.44), channel_id=1, source_target_pairs={{0,1},{1,0},{2,3},{3,2},{4,5},{5,4},{6,7},{7,6},{8,9},{9,8},{10,11... | collective-permute-start | bytes 294920 | tf_op jit(solution)/shard_map/ppermute | solution.py:512
  26.5 1.7 %collective-permute-start = (bf16[1024,128]{1,0:T(8,128)(2,1)S(1)}, bf16[1024,128]{1,0:T(8,128)(2,1)S(1)}, u32[]{:S(2)}, u32[]{:S(2)}) collective-permute-start(bf16[1024,128]{1,0:T(8,128)(2,1)S(1)} %get-tuple-element.33), channel_id=1, source_target_pairs={{0,1},{1,0},{2,3},{3,2},{4,5},{5,4},{6,7},{7,6},{8,9},{9,8},{10,11... | collective-permute-start | bytes 786440 | tf_op jit(solution)/shard_map/ppermute | solution.py:512
  28.3 8.0 %collective-permute-start.6 = (bf16[400,128]{1,0:T(8,128)(2,1)S(1)}, bf16[400,128]{1,0:T(8,128)(2,1)S(1)}, u32[]{:S(2)}, u32[]{:S(2)}) collective-permute-start(bf16[400,128]{1,0:T(8,128)(2,1)S(1)} %pad_maximum_fusion), channel_id=1, source_target_pairs={{0,24},{8,16},{16,8},{24,0},{1,25},{9,17},{17,9},{25,1},{2,26},{10... | collective-permute-start | bytes 307208 | tf_op jit(solution)/shard_map/ppermute | solution.py:512
  29.8 6.5 %collective-permute-start.8 = (bf16[400,128]{1,0:T(8,128)(2,1)S(1)}, bf16[400,128]{1,0:T(8,128)(2,1)S(1)}, u32[]{:S(2)}, u32[]{:S(2)}) collective-permute-start(bf16[400,128]{1,0:T(8,128)(2,1)S(1)} %pad_maximum_fusion.1), channel_id=1, source_target_pairs={{0,8},{8,0},{16,24},{24,16},{1,9},{9,1},{17,25},{25,17},{2,10},{10... | collective-permute-start | bytes 307208 | tf_op jit(solution)/shard_map/ppermute | solution.py:512
  30.4 5.8 %collective-permute-start.7 = (bf16[336,128]{1,0:T(8,128)(2,1)S(1)}, bf16[336,128]{1,0:T(8,128)(2,1)S(1)}, u32[]{:S(2)}, u32[]{:S(2)}) collective-permute-start(bf16[336,128]{1,0:T(8,128)(2,1)S(1)} %pad_maximum_fusion.2), channel_id=1, source_target_pairs={{0,16},{8,24},{16,0},{24,8},{1,17},{9,25},{17,1},{25,9},{2,18},{10... | collective-permute-start | bytes 258056 | tf_op jit(solution)/shard_map/ppermute | solution.py:512
  32.0 8.9 %collective-permute-start.12 = (bf16[64,128]{1,0:T(8,128)(2,1)S(1)}, bf16[64,128]{1,0:T(8,128)(2,1)S(1)}, u32[]{:S(2)}, u32[]{:S(2)}) collective-permute-start(bf16[64,128]{1,0:T(8,128)(2,1)S(1)} %get-tuple-element.48), channel_id=1, source_target_pairs={{1,2},{2,1},{3,4},{4,3},{5,6},{6,5},{7,0},{0,7},{9,10},{10,9},{11,... | collective-permute-start | bytes 49160 | tf_op jit(solution)/shard_map/ppermute | solution.py:104
  36.4 8.3 %collective-permute-start.10 = (bf16[336,128]{1,0:T(8,128)(2,1)S(1)}, bf16[336,128]{1,0:T(8,128)(2,1)S(1)}, u32[]{:S(2)}, u32[]{:S(2)}) collective-permute-start(bf16[336,128]{1,0:T(8,128)(2,1)S(1)} %pad_maximum_fusion.3), channel_id=1, source_target_pairs={{0,4},{1,5},{2,6},{3,7},{4,0},{5,1},{6,2},{7,3},{8,12},{9,13},{10,... | collective-permute-start | bytes 258056 | tf_op jit(solution)/shard_map/ppermute | solution.py:512
  37.6 7.2 %collective-permute-start.11 = (bf16[336,128]{1,0:T(8,128)(2,1)S(1)}, bf16[336,128]{1,0:T(8,128)(2,1)S(1)}, u32[]{:S(2)}, u32[]{:S(2)}) collective-permute-start(bf16[336,128]{1,0:T(8,128)(2,1)S(1)} %pad_maximum_fusion.3), channel_id=1, source_target_pairs={{0,2},{1,3},{2,0},{3,1},{4,6},{5,7},{6,4},{7,5},{8,10},{9,11},{10,... | collective-permute-start | bytes 258056 | tf_op jit(solution)/shard_map/ppermute | solution.py:512
  39.5 6.4 %collective-permute-start.9 = (bf16[336,128]{1,0:T(8,128)(2,1)S(1)}, bf16[336,128]{1,0:T(8,128)(2,1)S(1)}, u32[]{:S(2)}, u32[]{:S(2)}) collective-permute-start(bf16[336,128]{1,0:T(8,128)(2,1)S(1)} %pad_maximum_fusion.3), channel_id=1, source_target_pairs={{0,6},{1,7},{2,4},{3,5},{4,2},{5,3},{6,0},{7,1},{8,14},{9,15},{10,... | collective-permute-start | bytes 258056 | tf_op jit(solution)/shard_map/ppermute | solution.py:512
  45.9 5.1 %collective-permute-start.13 = (bf16[336,128]{1,0:T(8,128)(2,1)S(1)}, bf16[336,128]{1,0:T(8,128)(2,1)S(1)}, u32[]{:S(2)}, u32[]{:S(2)}) collective-permute-start(bf16[336,128]{1,0:T(8,128)(2,1)S(1)} %add_convert_fusion.1), channel_id=1, source_target_pairs={{0,8},{8,0},{16,24},{24,16},{1,9},{9,1},{17,25},{25,17},{2,10},{10... | collective-permute-start | bytes 258056 | tf_op jit(solution)/shard_map/ppermute | solution.py:512
  47.5 4.5 %collective-permute-start.14 = (bf16[336,128]{1,0:T(8,128)(2,1)S(1)}, bf16[336,128]{1,0:T(8,128)(2,1)S(1)}, u32[]{:S(2)}, u32[]{:S(2)}) collective-permute-start(bf16[336,128]{1,0:T(8,128)(2,1)S(1)} %add_convert_fusion.1), channel_id=1, source_target_pairs={{0,16},{8,24},{16,0},{24,8},{1,17},{9,25},{17,1},{25,9},{2,18},{10... | collective-permute-start | bytes 258056 | tf_op jit(solution)/shard_map/ppermute | solution.py:512
  48.4 5.4 %collective-permute-start.15 = (bf16[336,128]{1,0:T(8,128)(2,1)S(1)}, bf16[336,128]{1,0:T(8,128)(2,1)S(1)}, u32[]{:S(2)}, u32[]{:S(2)}) collective-permute-start(bf16[336,128]{1,0:T(8,128)(2,1)S(1)} %add_convert_fusion.1), channel_id=1, source_target_pairs={{0,24},{8,16},{16,8},{24,0},{1,25},{9,17},{17,9},{25,1},{2,26},{10... | collective-permute-start | bytes 258056 | tf_op jit(solution)/shard_map/ppermute | solution.py:512
  53.8 1.7 %collective-permute-start.16 = (bf16[1344,128]{1,0:T(8,128)(2,1)S(1)}, bf16[1344,128]{1,0:T(8,128)(2,1)S(1)}, u32[]{:S(2)}, u32[]{:S(2)}) collective-permute-start(bf16[1344,128]{1,0:T(8,128)(2,1)S(1)} %constant_dynamic-update-slice_fusion.refs_0_), channel_id=1, source_target_pairs={{0,1},{1,0},{2,3},{3,2},{4,5},{5,4},{6,7},{7,6},{8,9},{9,8},{10,11... | collective-permute-start | bytes 1032200 | tf_op jit(solution)/shard_map/ppermute | solution.py:512

commit v6 on v5

--- a/solution.py
+++ b/solution.py
@@ -110,40 +110,44 @@
     return [sent[k] for k in range(4)]
 
 
-def select_kernel(embed_ref, rows_ref, s0, s1, s2, s3, embed_v, rows_v, sems):
+def select_kernel(
+    embed_ref, rows_ref, weight_ref, s0, s1, s2, s3, embed_v, rows_v, weight_v, sems
+):
     copies = [
         pltpu.make_async_copy(rows_ref, rows_v, sems.at[0]),
         pltpu.make_async_copy(embed_ref, embed_v, sems.at[1]),
+        pltpu.make_async_copy(weight_ref, weight_v, sems.at[2]),
     ]
     for copy in copies:
         copy.start()
-    for copy in copies:
+    for copy in copies[:2]:
         copy.wait()
     rows = embed_v.shape[0]
     for index, send_ref in zip(pair_lists(rows_v), (s0, s1, s2, s3)):
         spots = lax.broadcasted_iota(jnp.int32, (rows, index.shape[1]), 0).astype(jnp.int16)
         hot = jnp.where(spots == index.astype(jnp.int16), jnp.ones((), BF16), jnp.zeros((), BF16))
         send_ref[...] = dot(hot, embed_v[...], TN).astype(BF16)
-
-
-def select(embed, outgoing):
+    copies[2].wait()
+
+
+def select(embed, outgoing, weight):
     ghost = jax.ShapeDtypeStruct((outgoing.shape[1], embed.shape[1]), BF16)
     return pl.pallas_call(
         select_kernel,
-        in_specs=[HBM] * 2,
-        out_specs=[VMEM] * 6,
-        out_shape=in_vmem(*[ghost] * 4, embed, outgoing),
-        scratch_shapes=[pltpu.SemaphoreType.DMA((2,))],
+        in_specs=[HBM] * 3,
+        out_specs=[VMEM] * 7,
+        out_shape=in_vmem(*[ghost] * 4, embed, outgoing, weight),
+        scratch_shapes=[pltpu.SemaphoreType.DMA((3,))],
         compiler_params=limits(),
         name="select",
-    )(*in_hbm(embed, outgoing))
-
-
-def residual_kernel(embed_ref, weight_ref, cotangent_ref, *refs):
-    count = (len(refs) - 8) // 2
+    )(*in_hbm(embed, outgoing, weight))
+
+
+def residual_kernel(embed_ref, weight_ref, cotangent_ref, basis_hbm, bw_hbm, *refs):
+    count = (len(refs) - 11) // 2
     sources, targets = refs[:count], refs[count : 2 * count]
-    dres_ref, mine_ref, other_ref, pre_ref = refs[2 * count : 2 * count + 4]
-    cotangent_v, dres_v, grad_ref, sems = refs[2 * count + 4 :]
+    dres_ref, mine_ref, other_ref, pre_ref, slots_ref = refs[2 * count : 2 * count + 5]
+    cotangent_v, dres_v, grad_ref, basis_ref, bw_ref, sems = refs[2 * count + 5 :]
     rows = embed_ref.shape[0]
     block = min(rows, LANES)
     spans = [pl.ds(start, block) for start in range(0, rows, block)]
@@ -157,7 +161,9 @@
     ]
     copies = [
         pltpu.make_async_copy(source, target, sems.at[2 * len(spans) + i])
-        for i, (source, target) in enumerate(zip(sources, targets))
+        for i, (source, target) in enumerate(
+            zip((*sources, basis_hbm, bw_hbm), (*targets, basis_ref, bw_ref))
+        )
     ]
     for copy in reads + copies:
         copy.start()
@@ -179,46 +185,67 @@
             to = pl.ds((part * len(columns) + c) * step, step)
             mine_ref[to, :] = grad_ref[pl.ds(upper * half + part * step, step), column]
             other_ref[to, :] = grad_ref[pl.ds((1 - upper) * half + part * step, step), column]
-    for copy in writes + copies[1:]:
+    for copy in copies[1:]:
         copy.wait()
-
-
-def residual(embed, weight, cotangent, down_t, *staged):
+    nbasis, width = bw_ref.shape
+    span = basis_ref.shape[0]
+    trips = span // nbasis
+    fold = jnp.where(
+        lax.broadcasted_iota(jnp.int32, (nbasis, span), 1) % nbasis
+        == lax.broadcasted_iota(jnp.int32, (nbasis, span), 0),
+        1.0,
+        0.0,
+    )
+    wide = dot(bw_ref[...], fold.astype(BF16), TN).astype(BF16)
+    own_slot = lax.broadcasted_iota(jnp.int32, (trips, width, span), 0) == (
+        lax.broadcasted_iota(jnp.int32, (trips, width, span), 2) // nbasis
+    )
+    diagonal = jnp.where(own_slot, wide[None], jnp.zeros((), BF16)).reshape(trips * width, span)
+    slots_ref[...] = dot(diagonal, basis_ref[...], NN)
+
+    for copy in writes:
+        copy.wait()
+
+
+def residual(embed, weight, cotangent, basis, basis_weight, down_t, *staged):
     staged = (down_t, *staged)
     width, rows = down_t.shape[0], embed.shape[0]
+    trips = basis.shape[0] // basis_weight.shape[0]
     half = jax.ShapeDtypeStruct((weight.size // 256, 128), BF16)
     blocks = embed.shape[0] // min(embed.shape[0], LANES)
     return pl.pallas_call(
         residual_kernel,
-        in_specs=[VMEM] * 2 + [HBM] * (1 + len(staged)),
-        out_specs=[VMEM] * len(staged) + [HBM] + [VMEM] * 3,
+        in_specs=[VMEM] * 2 + [HBM] * (3 + len(staged)),
+        out_specs=[VMEM] * len(staged) + [HBM] + [VMEM] * 4,
         out_shape=in_vmem(*staged)
         + [pltpu.HBM(embed.shape, BF16)]
         + in_vmem(half, half)
-        + [pltpu.VMEM((width, rows), F32)],
+        + [pltpu.VMEM((width, rows), F32), pltpu.VMEM((trips * width, rows), F32)],
         scratch_shapes=[
             pltpu.VMEM(embed.shape, BF16),
             pltpu.VMEM(embed.shape, BF16),
             pltpu.VMEM(weight.shape, BF16),
-            pltpu.SemaphoreType.DMA((2 * blocks + len(staged),)),
+            pltpu.VMEM(basis.shape, BF16),
+            pltpu.VMEM(basis_weight.shape, BF16),
+            pltpu.SemaphoreType.DMA((2 * blocks + len(staged) + 2,)),
         ],
         compiler_params=limits(),
         cost_estimate=cost(6 * embed.size * weight.shape[1]),
         name="residual",
-    )(embed, weight, *in_hbm(cotangent, *staged))
+    )(embed, weight, *in_hbm(cotangent, basis, basis_weight, *staged))
 
 
 def triplet_kernel(
     pre_ref,
     embed_ref,
     down_ref,
+    g1_ref,
+    g3_ref,
     g0_ref,
-    g1_ref,
     g2_ref,
-    g3_ref,
     index_ref,
     count_ref,
-    bw_ref,
+    weight_ref,
     basis_hbm,
     cotangent_hbm,
     up_hbm,
@@ -231,10 +258,8 @@
     ghost_embed_ref,
     rest_ref,
     table_ref,
-    weight_ref,
     hot_ref,
     picked_ref,
-    dw_ref,
     tsum_ref,
     dt_ref,
     acc_ref,
@@ -251,7 +276,7 @@
     read_up.start()
     width, rows = pre_ref.shape
     trips = index_ref.shape[0]
-    nbasis = bw_ref.shape[0]
+    nbasis = basis_ref.shape[0] // trips
     own_groups = rows // LANES
     ghost = g0_ref.shape[0]
     for first, a_ref, b_ref, axis in ((0, g0_ref, g1_ref, "slab"), (2, g2_ref, g3_ref, "brick")):
@@ -267,21 +292,6 @@
     groups = table_ref.shape[0] // width
     tiles = rows // LANES
 
-    span = trips * nbasis
-    fold = jnp.where(
-        lax.broadcasted_iota(jnp.int32, (nbasis, span), 1) % nbasis
-        == lax.broadcasted_iota(jnp.int32, (nbasis, span), 0),
-        1.0,
-        0.0,
-    )
-    wide = dot(bw_ref[...], fold.astype(BF16), TN).astype(BF16)
-    own_slot = lax.broadcasted_iota(jnp.int32, (trips, width, span), 0) == (
-        lax.broadcasted_iota(jnp.int32, (trips, width, span), 2) // nbasis
-    )
-    diagonal = jnp.where(own_slot, wide[None], jnp.zeros((), BF16)).reshape(trips * width, span)
-    read_basis.wait()
-    weight_ref[...] = dot(diagonal, basis_ref[...], NN)
-
     tsum_ref[...] = jnp.zeros_like(tsum_ref)
 
     def lookup(j, t):
@@ -300,11 +310,12 @@
             tsum_ref[:, at] += weight_ref[pl.ds(j * width, width), at] * picked
         return carry
 
-    lax.fori_loop(0, trips, forward, 0, unroll=8)
+    lax.fori_loop(0, trips, forward, 0, unroll=16)
 
     tsum = tsum_ref[...]
     sig = sigmoid(tsum)
     act = (tsum * sig).astype(BF16)
+    read_basis.wait()
     read_cotangent.wait()
     read_up.wait()
     cotangent = cotangent_ref[...]
@@ -316,16 +327,18 @@
 
     def backward(j, carry):
         parts = []
+        dws = []
         for t in range(tiles):
             at, low, high = lookup(j, t)
             dt = dt_ref[:, at]
-            dw_ref[pl.ds(j * width, width), at] = (dt * picked_ref[j, :, at].astype(F32)).astype(BF16)
+            dws.append((dt * picked_ref[j, :, at].astype(F32)).astype(BF16))
             terms = (dt * weight_ref[pl.ds(j * width, width), at]).astype(BF16)
             parts.append(spread(terms, high, groups))
         acc_ref[...] += dot(jnp.concatenate(parts, axis=1), hot_ref[j], NT)
-        return carry
-
-    lax.fori_loop(0, trips, backward, 0, unroll=8)
+        slot_basis = basis_ref[pl.ds(pl.multiple_of(j * nbasis, nbasis), nbasis), :]
+        return carry + dot(slot_basis, jnp.concatenate(dws, axis=1), NT)
+
+    basis_grad = lax.fori_loop(0, trips, backward, jnp.zeros((nbasis, width), F32), unroll=8)
 
     own = unstacked(acc_ref[: own_groups * width, :], width)
     own_ref[...] = own
@@ -340,13 +353,8 @@
     down_grad = dot((own * silu_grad(pre_ref[...])).astype(BF16), embed_ref[...], NN)
     down_grad += dot((ghost_terms * ghost_grad).astype(BF16), ghost_embed_ref[...], NN)
     rest_ref[:, :inner] = down_grad.astype(BF16)
-    full = dot(dw_ref[...], basis_ref[...], NT).reshape(trips, width, span)
-    kept = jnp.sum(jnp.where(own_slot, full, 0.0), axis=0)
-    folded = dot(kept, fold, NT, lax.Precision.HIGHEST)
-    pad = rest_ref.shape[1] - 2 * inner - nbasis
-    rest_ref[:, 2 * inner :] = jnp.concatenate(
-        [folded, jnp.zeros((width, pad), F32)], axis=1
-    ).astype(BF16)
+    rest_ref[:, 2 * inner :] = jnp.zeros((width, rest_ref.shape[1] - 2 * inner), BF16)
+    rest_ref[:nbasis, 2 * inner : 2 * inner + width] = basis_grad.astype(BF16)
     half = width // 2
     upper = lax.axis_index("brick") % 2
     columns = blocks_of(rest_ref.shape[1])
@@ -363,13 +371,14 @@
 
 
 def triplets(
-    pre, embed, down_t, ghosts, basis, index, count, up_weight, cotangent, basis_weight
+    pre, embed, down_t, ghosts, basis, index, count, up_weight, cotangent, weights
 ):
     width, rows = pre.shape
     trips = index.shape[0]
     ghost, inner = ghosts[0].shape
     groups = (rows + 4 * ghost) // LANES
-    operands = (pre, embed, down_t, *ghosts, index, count, basis_weight)
+    ordered = [ghosts[k] for k in (1, 3, 0, 2)]
+    operands = (pre, embed, down_t, *ordered, index, count, weights)
     unit = 16 * lax.axis_size("slab")
     total = 2 * inner + 128
     shared = -(-(width * total // 256) // unit) * unit
@@ -387,10 +396,8 @@
             pltpu.VMEM((4 * ghost, inner), BF16),
             pltpu.VMEM((width, total), BF16),
             pltpu.VMEM((groups * width, LANES), BF16),
-            pltpu.VMEM((trips * width, rows), F32),
             pltpu.VMEM((trips, LANES, rows), BF16),
             pltpu.VMEM((trips, width, rows), BF16),
-            pltpu.VMEM((trips * width, rows), BF16),
             pltpu.VMEM((width, rows), F32),
             pltpu.VMEM((width, rows), F32),
             pltpu.VMEM((groups * width, LANES), F32),
@@ -485,7 +492,8 @@
             all_ref[pl.ds(side * rows, rows), column] = part_ref[at, :]
     down_ref[...] = all_ref[:, :inner]
     up_ref[...] = all_ref[:, inner : 2 * inner]
-    basis_ref[...] = all_ref[:, 2 * inner :].T[: basis_ref.shape[0], :]
+    nbasis, width = basis_ref.shape
+    basis_ref[...] = all_ref[:nbasis, 2 * inner : 2 * inner + width]
 
 
 def finish(offsets, mine, other, shared, inner, width, nbasis):
@@ -564,16 +572,18 @@
     rows, inner = embed.shape
     trips, nbasis = basis.shape[:2]
 
-    *sends, embed_v, outgoing_v = select(embed, outgoing_edge_rows)
+    *sends, embed_v, outgoing_v, weight_v = select(embed, outgoing_edge_rows, residual_weight)
     ghosts = pair_exchange(sends)
-    down_v, index_v, count_v, bw_v, dres, mine, other, pre = residual(
+    basis = basis.reshape(trips * nbasis, rows)
+    down_v, index_v, count_v, dres, mine, other, pre, weights = residual(
         embed_v,
-        residual_weight,
+        weight_v,
         cotangent,
+        basis,
+        basis_weight,
         down_weight.T,
         triplet_row_index,
         triplet_slot_count.reshape(1, rows),
-        basis_weight,
     )
     share = total_of([mine, swapped(other, "brick", 1)])
 
@@ -582,12 +592,12 @@
         embed_v,
         down_v,
         ghosts,
-        basis.reshape(trips * nbasis, rows),
+        basis,
         index_v,
         count_v,
         up_weight,
         cotangent,
-        bw_v,
+        weights,
     )
     received = swapped(other, "brick", 1)
     shared = mine.shape[0]
@@ -604,7 +614,7 @@
         )
     backs[0] = arrived[1]
     backs[1] = arrived[3] if ring == 4 else paired(second, "slab", 1)
-    edge_grad = edge_gradient(own, backs, outgoing_v, pre, residual_weight, down_v, dres)
+    edge_grad = edge_gradient(own, backs, outgoing_v, pre, weight_v, down_v, dres)
 
     value = jnp.concatenate([share, mine], axis=0)
     for low, members in groups_of("brick", 2):

time: 56.9 us -> 54.8 us (0.963)
  starting transfers between devices: 22.1 us -> 20.6 us
  Pallas kernels: 22.5 us -> 21.8 us
    pallas_call x1, Pallas kernels: 11.8 us -> 10.2 us  [triplets(): pl.pallas_call(triplet_kernel, in_specs=[VMEM] * len(operands) + [HBM] *...]
    ppermute x5, starting transfers between devices: 9.81 us -> 8.24 us  [paired(): return lax.ppermute(value, axis, pairs)]
    pallas_call x2, Pallas kernels: 5.75 us -> 6.59 us  [the longest x1 4.55 us: residual(): pl.pallas_call(residual_kernel, in_specs=[VMEM] * 2 + [HBM] * (3 + len(st...]
  transfers between devices with their start and end apart: 17 -> 17, of which waited for: 9 -> 8; matrix products, arithmetic and copies ran while one was open for 0% -> 0% of each run, Pallas kernels for 13% -> 15%
where the time goes in v6:
time: 54.8 us; the launch traced here: 54.6 us
  Pallas kernels  21.8 us (40%)
  starting transfers between devices  20.6 us (38%)
  waiting for transfers between devices  11.2 us (20%)
  between operations  0.8 us (1%)
    ppermute x12, starting transfers between devices, swapped(): lax.ppermute(value, axis, [(i, i ^ offset) for i in range(lax.axis_size(a...  12.3 us
    ppermute x12, waiting for transfers between devices, swapped(): lax.ppermute(value, axis, [(i, i ^ offset) for i in range(lax.axis_size(a...  11.2 us
    pallas_call x1, Pallas kernels, triplets(): pl.pallas_call(triplet_kernel, in_specs=[VMEM] * len(operands) + [HBM] *...  10.2 us
    ppermute x5, starting transfers between devices, paired(): return lax.ppermute(value, axis, pairs)  8.24 us
    pallas_call x1, Pallas kernels, residual(): pl.pallas_call(residual_kernel, in_specs=[VMEM] * 2 + [HBM] * (3 + len(st...  4.55 us
    pallas_call x1, Pallas kernels, edge_gradient(): pl.pallas_call(edge_kernel, in_specs=[VMEM] * len(operands) + [HBM], out_...  3.82 us
    pallas_call x1, Pallas kernels, select(): pl.pallas_call(select_kernel, in_specs=[HBM] * 3, out_specs=[VMEM] * 7, o...  2.03 us
    pallas_call x1, Pallas kernels, finish(): pl.pallas_call(lambda *refs: finish_kernel(offsets, *refs), in_specs=[VME...  1.15 us
  transfers between devices with their start and end apart: 17, of which 8 were waited for; matrix products, arithmetic and copies ran while one was open for 0% of the time, Pallas kernels for 15%

profile of v6, /device:TPU:0, one launch (start us, length us, event | category | flops | bytes accessed | tf_op | source)
XLA Modules:
  0.0 54.6 jit_solution(15093730736913505340)
XLA Ops:
  0.6 2.0 %select.5 = (bf16[128,512]{1,0:T(8,128)(2,1)S(1)}, bf16[128,512]{1,0:T(8,128)(2,1)S(1)}, bf16[128,512]{1,0:T(8,128)(2,1)S(1)}, bf16[128,512]{1,0:T(8,128)(2,1)S(...) custom-call(bf16[1024,512]{1,0:T(8,128)(2,1)} %embed_ref.1, ...), custom_call_target="tpu_custom_call" | custom-call | tf_op jit(solution)/shard_map/select/pallas_call | solution.py:135
  2.7 4.0 %collective-permute-start.1 = (bf16[128,512]{1,0:T(8,128)(2,1)S(1)}, bf16[128,512]{1,0:T(8,128)(2,1)S(1)}, u32[]{:S(2)}, u32[]{:S(2)}) collective-permute-start(bf16[128,512]{1,0:T(8,128)(2,1)S(1)} %get-tuple-element.38), channel_id=1, source_target_pairs={{8,16},{16,8},{24,0},{0,24},{9,17},{17,9},{25,1},{1,25},{10,18},{1... | collective-permute-start | bytes 393224 | tf_op jit(solution)/shard_map/ppermute | solution.py:104
  6.6 2.8 %collective-permute-start.2 = (bf16[128,512]{1,0:T(8,128)(2,1)S(1)}, bf16[128,512]{1,0:T(8,128)(2,1)S(1)}, u32[]{:S(2)}, u32[]{:S(2)}) collective-permute-start(bf16[128,512]{1,0:T(8,128)(2,1)S(1)} %get-tuple-element.39), channel_id=1, source_target_pairs={{1,2},{2,1},{3,4},{4,3},{5,6},{6,5},{7,0},{0,7},{9,10},{10,9},{11,... | collective-permute-start | bytes 393224 | tf_op jit(solution)/shard_map/ppermute | solution.py:104
  9.4 0.5 collective-permute-start.3
  9.9 0.0 collective-permute-start.4
  9.9 4.6 %residual.1 = (bf16[64,512]{1,0:T(8,128)(2,1)S(1)}, s32[16,1024]{1,0:T(8,128)S(1)}, s32[1,1024]{1,0:T(1,128)S(1)}, bf16[1024,512]{1,0:T(8,128)(2,1)}, bf16[1024,...) custom-call(bf16[1024,512]{1,0:T(8,128)(2,1)S(1)} %get-tuple-element.32., ...), custom_call_target="tpu_custom_call" | custom-call | flops 1610612736 | tf_op jit(solution)/shard_map/residual/pallas_call | solution.py:216
  14.5 10.2 %triplets.1 = (f32[64,1024]{1,0:T(8,128)S(1)}, bf16[64,128]{1,0:T(8,128)(2,1)S(1)}, bf16[64,128]{1,0:T(8,128)(2,1)S(1)}, bf16[64,128]{1,0:T(8,128)(2,1)S(1)}, bf...) custom-call(f32[64,1024]{1,0:T(8,128)S(1)} %get-tuple-element.36.pre_ref, ...), custom_call_target="tpu_custom_call" | custom-call | flops 12884901888 | tf_op jit(solution)/shard_map/triplets/pallas_call | solution.py:390
  24.7 0.6 %collective-permute-start.5 = (bf16[384,128]{1,0:T(8,128)(2,1)S(1)}, bf16[384,128]{1,0:T(8,128)(2,1)S(1)}, u32[]{:S(2)}, u32[]{:S(2)}) collective-permute-start(bf16[384,128]{1,0:T(8,128)(2,1)S(1)} %get-tuple-element.46), channel_id=1, source_target_pairs={{0,1},{1,0},{2,3},{3,2},{4,5},{5,4},{6,7},{7,6},{8,9},{9,8},{10,11... | collective-permute-start | bytes 294920 | tf_op jit(solution)/shard_map/ppermute | solution.py:520
  25.3 0.1 collective-permute-start
  25.4 0.9 %collective-permute-done.5 = bf16[384,128]{1,0:T(8,128)(2,1)S(1)} collective-permute-done((bf16[384,128]{1,0:T(8,128)(2,1)S(1)}, bf16[384,128]{1,0:T(8,128)(2,1)S(1)}, u32[]{:S(2)}, u32[]{:S(2)}) %collective-permute-start.5) | collective-permute-done | bytes 98336 | tf_op jit(solution)/shard_map/ppermute | solution.py:520
  26.3 0.5 collective-permute-done
  26.9 0.1 add_convert_fusion
  27.0 1.5 %collective-permute-start.6 = (bf16[400,128]{1,0:T(8,128)(2,1)S(1)}, bf16[400,128]{1,0:T(8,128)(2,1)S(1)}, u32[]{:S(2)}, u32[]{:S(2)}) collective-permute-start(bf16[400,128]{1,0:T(8,128)(2,1)S(1)} %pad_maximum_fusion), channel_id=1, source_target_pairs={{0,24},{8,16},{16,8},{24,0},{1,25},{9,17},{17,9},{25,1},{2,26},{10... | collective-permute-start | bytes 307208 | tf_op jit(solution)/shard_map/ppermute | solution.py:520
  28.5 0.6 %collective-permute-start.8 = (bf16[400,128]{1,0:T(8,128)(2,1)S(1)}, bf16[400,128]{1,0:T(8,128)(2,1)S(1)}, u32[]{:S(2)}, u32[]{:S(2)}) collective-permute-start(bf16[400,128]{1,0:T(8,128)(2,1)S(1)} %pad_maximum_fusion.1), channel_id=1, source_target_pairs={{0,8},{8,0},{16,24},{24,16},{1,9},{9,1},{17,25},{25,17},{2,10},{10... | collective-permute-start | bytes 307208 | tf_op jit(solution)/shard_map/ppermute | solution.py:520
  29.1 1.5 %collective-permute-start.7 = (bf16[336,128]{1,0:T(8,128)(2,1)S(1)}, bf16[336,128]{1,0:T(8,128)(2,1)S(1)}, u32[]{:S(2)}, u32[]{:S(2)}) collective-permute-start(bf16[336,128]{1,0:T(8,128)(2,1)S(1)} %pad_maximum_fusion.2), channel_id=1, source_target_pairs={{0,16},{8,24},{16,0},{24,8},{1,17},{9,25},{17,1},{25,9},{2,18},{10... | collective-permute-start | bytes 258056 | tf_op jit(solution)/shard_map/ppermute | solution.py:520
  30.6 1.0 %collective-permute-start.12 = (bf16[64,128]{1,0:T(8,128)(2,1)S(1)}, bf16[64,128]{1,0:T(8,128)(2,1)S(1)}, u32[]{:S(2)}, u32[]{:S(2)}) collective-permute-start(bf16[64,128]{1,0:T(8,128)(2,1)S(1)} %get-tuple-element.50), channel_id=1, source_target_pairs={{1,2},{2,1},{3,4},{4,3},{5,6},{6,5},{7,0},{0,7},{9,10},{10,9},{11,... | collective-permute-start | bytes 49160 | tf_op jit(solution)/shard_map/ppermute | solution.py:104
  31.6 3.1 %collective-permute-done.7 = bf16[336,128]{1,0:T(8,128)(2,1)S(1)} collective-permute-done((bf16[336,128]{1,0:T(8,128)(2,1)S(1)}, bf16[336,128]{1,0:T(8,128)(2,1)S(1)}, u32[]{:S(2)}, u32[]{:S(2)}) %collective-permute-start.7) | collective-permute-done | bytes 86048 | tf_op jit(solution)/shard_map/ppermute | solution.py:520
  34.8 1.2 %collective-permute-start.10 = (bf16[336,128]{1,0:T(8,128)(2,1)S(1)}, bf16[336,128]{1,0:T(8,128)(2,1)S(1)}, u32[]{:S(2)}, u32[]{:S(2)}) collective-permute-start(bf16[336,128]{1,0:T(8,128)(2,1)S(1)} %pad_maximum_fusion.3), channel_id=1, source_target_pairs={{0,4},{1,5},{2,6},{3,7},{4,0},{5,1},{6,2},{7,3},{8,12},{9,13},{10,... | collective-permute-start | bytes 258056 | tf_op jit(solution)/shard_map/ppermute | solution.py:520
  36.0 1.5 %collective-permute-start.11 = (bf16[336,128]{1,0:T(8,128)(2,1)S(1)}, bf16[336,128]{1,0:T(8,128)(2,1)S(1)}, u32[]{:S(2)}, u32[]{:S(2)}) collective-permute-start(bf16[336,128]{1,0:T(8,128)(2,1)S(1)} %pad_maximum_fusion.3), channel_id=1, source_target_pairs={{0,2},{1,3},{2,0},{3,1},{4,6},{5,7},{6,4},{7,5},{8,10},{9,11},{10,... | collective-permute-start | bytes 258056 | tf_op jit(solution)/shard_map/ppermute | solution.py:520
  37.5 1.7 %collective-permute-start.9 = (bf16[336,128]{1,0:T(8,128)(2,1)S(1)}, bf16[336,128]{1,0:T(8,128)(2,1)S(1)}, u32[]{:S(2)}, u32[]{:S(2)}) collective-permute-start(bf16[336,128]{1,0:T(8,128)(2,1)S(1)} %pad_maximum_fusion.3), channel_id=1, source_target_pairs={{0,6},{1,7},{2,4},{3,5},{4,2},{5,3},{6,0},{7,1},{8,14},{9,15},{10,... | collective-permute-start | bytes 258056 | tf_op jit(solution)/shard_map/ppermute | solution.py:520
  39.3 3.8 %edge_gradient.1 = bf16[1024,512]{1,0:T(8,128)(2,1)} custom-call(f32[64,1024]{1,0:T(8,128)S(1)} %get-tuple-element.49.own_ref, bf16[64,128]{1,0:T(8,128)(2,1)S(1)} %slice.47.b0_ref, bf16[64,128]{1,0:T(8,128)(2,1)S(1)} %slice.48.b1_ref, bf16[64,128]{1,0:T(8,128)(2,1)S(1)} %slice.49.b2_ref, bf16[64,128]{1,0:T(8,128)(2,1)S(1)} %collective-permute-done.12.b3_ref, ...), custom_call_target="tpu_custom_call" | custom-call | flops 1207959552 | tf_op jit(solution)/shard_map/edge_gradient/pallas_call | solution.py:454
  43.1 0.9 %collective-permute-done.11 = bf16[336,128]{1,0:T(8,128)(2,1)S(1)} collective-permute-done((bf16[336,128]{1,0:T(8,128)(2,1)S(1)}, bf16[336,128]{1,0:T(8,128)(2,1)S(1)}, u32[]{:S(2)}, u32[]{:S(2)}) %collective-permute-start.11) | collective-permute-done | bytes 86048 | tf_op jit(solution)/shard_map/ppermute | solution.py:520
  44.0 0.1 add_convert_fusion.1
  44.1 1.6 %collective-permute-start.13 = (bf16[336,128]{1,0:T(8,128)(2,1)S(1)}, bf16[336,128]{1,0:T(8,128)(2,1)S(1)}, u32[]{:S(2)}, u32[]{:S(2)}) collective-permute-start(bf16[336,128]{1,0:T(8,128)(2,1)S(1)} %add_convert_fusion.1), channel_id=1, source_target_pairs={{0,8},{8,0},{16,24},{24,16},{1,9},{9,1},{17,25},{25,17},{2,10},{10... | collective-permute-start | bytes 258056 | tf_op jit(solution)/shard_map/ppermute | solution.py:520
  45.6 0.8 %collective-permute-start.14 = (bf16[336,128]{1,0:T(8,128)(2,1)S(1)}, bf16[336,128]{1,0:T(8,128)(2,1)S(1)}, u32[]{:S(2)}, u32[]{:S(2)}) collective-permute-start(bf16[336,128]{1,0:T(8,128)(2,1)S(1)} %add_convert_fusion.1), channel_id=1, source_target_pairs={{0,16},{8,24},{16,0},{24,8},{1,17},{9,25},{17,1},{25,9},{2,18},{10... | collective-permute-start | bytes 258056 | tf_op jit(solution)/shard_map/ppermute | solution.py:520
  46.4 1.2 %collective-permute-start.15 = (bf16[336,128]{1,0:T(8,128)(2,1)S(1)}, bf16[336,128]{1,0:T(8,128)(2,1)S(1)}, u32[]{:S(2)}, u32[]{:S(2)}) collective-permute-start(bf16[336,128]{1,0:T(8,128)(2,1)S(1)} %add_convert_fusion.1), channel_id=1, source_target_pairs={{0,24},{8,16},{16,8},{24,0},{1,25},{9,17},{17,9},{25,1},{2,26},{10... | collective-permute-start | bytes 258056 | tf_op jit(solution)/shard_map/ppermute | solution.py:520
  47.6 1.9 %collective-permute-done.13 = bf16[336,128]{1,0:T(8,128)(2,1)S(1)} collective-permute-done((bf16[336,128]{1,0:T(8,128)(2,1)S(1)}, bf16[336,128]{1,0:T(8,128)(2,1)S(1)}, u32[]{:S(2)}, u32[]{:S(2)}) %collective-permute-start.13) | collective-permute-done | bytes 86048 | tf_op jit(solution)/shard_map/ppermute | solution.py:520
  49.5 0.9 %collective-permute-done.14 = bf16[336,128]{1,0:T(8,128)(2,1)S(1)} collective-permute-done((bf16[336,128]{1,0:T(8,128)(2,1)S(1)}, bf16[336,128]{1,0:T(8,128)(2,1)S(1)}, u32[]{:S(2)}, u32[]{:S(2)}) %collective-permute-start.14) | collective-permute-done | bytes 86048 | tf_op jit(solution)/shard_map/ppermute | solution.py:520
  50.4 1.4 %collective-permute-done.15 = bf16[336,128]{1,0:T(8,128)(2,1)S(1)} collective-permute-done((bf16[336,128]{1,0:T(8,128)(2,1)S(1)}, bf16[336,128]{1,0:T(8,128)(2,1)S(1)}, u32[]{:S(2)}, u32[]{:S(2)}) %collective-permute-start.15) | collective-permute-done | bytes 86048 | tf_op jit(solution)/shard_map/ppermute | solution.py:520
  51.8 0.1 collective-permute-start.16
  51.9 1.6 %collective-permute-done.16.refs_1_ = bf16[1344,128]{1,0:T(8,128)(2,1)S(1)} collective-permute-done((bf16[1344,128]{1,0:T(8,128)(2,1)S(1)}, bf16[1344,128]{1,0:T(8,128)(2,1)S(1)}, u32[]{:S(2)}, u32[]{:S(2)}) %collective-permute-start.16) | collective-permute-done | bytes 344096 | tf_op jit(solution)/shard_map/ppermute | solution.py:520
  53.5 1.1 %finish.1 = (f32[512,512]{1,0:T(8,128)}, f32[64,512]{1,0:T(8,128)}, f32[64,512]{1,0:T(8,128)}, f32[16,64]{1,0:T(8,128)}) custom-call(bf16[1344,128]{1,0:T(8,128)(2,1)S(1)} %constant_dynamic-update-slice_fusion.refs_0_, bf16[1344,128]{1,0:T(8,128)(2,1)S(1)} %collective-permute-done.16.refs_1_), custom_call_target="tpu_custom_call" | custom-call | tf_op jit(solution)/shard_map/finish/pallas_call | solution.py:500
  (25 shorter events, 0.2 us)
Async XLA Ops:
  2.7 11.8 %collective-permute-start.1 = (bf16[128,512]{1,0:T(8,128)(2,1)S(1)}, bf16[128,512]{1,0:T(8,128)(2,1)S(1)}, u32[]{:S(2)}, u32[]{:S(2)}) collective-permute-start(bf16[128,512]{1,0:T(8,128)(2,1)S(1)} %get-tuple-element.38), channel_id=1, source_target_pairs={{8,16},{16,8},{24,0},{0,24},{9,17},{17,9},{25,1},{1,25},{10,18},{1... | collective-permute-start | bytes 393224 | tf_op jit(solution)/shard_map/ppermute | solution.py:104
  6.6 7.9 %collective-permute-start.2 = (bf16[128,512]{1,0:T(8,128)(2,1)S(1)}, bf16[128,512]{1,0:T(8,128)(2,1)S(1)}, u32[]{:S(2)}, u32[]{:S(2)}) collective-permute-start(bf16[128,512]{1,0:T(8,128)(2,1)S(1)} %get-tuple-element.39), channel_id=1, source_target_pairs={{1,2},{2,1},{3,4},{4,3},{5,6},{6,5},{7,0},{0,7},{9,10},{10,9},{11,... | collective-permute-start | bytes 393224 | tf_op jit(solution)/shard_map/ppermute | solution.py:104
  9.4 5.1 %collective-permute-start.3 = (bf16[128,512]{1,0:T(8,128)(2,1)S(1)}, bf16[128,512]{1,0:T(8,128)(2,1)S(1)}, u32[]{:S(2)}, u32[]{:S(2)}) collective-permute-start(bf16[128,512]{1,0:T(8,128)(2,1)S(1)} %get-tuple-element.40), channel_id=1, source_target_pairs={{0,8},{8,0},{16,24},{24,16},{1,9},{9,1},{17,25},{25,17},{2,10},{10... | collective-permute-start | bytes 393224 | tf_op jit(solution)/shard_map/ppermute | solution.py:104
  9.9 4.6 %collective-permute-start.4 = (bf16[128,512]{1,0:T(8,128)(2,1)S(1)}, bf16[128,512]{1,0:T(8,128)(2,1)S(1)}, u32[]{:S(2)}, u32[]{:S(2)}) collective-permute-start(bf16[128,512]{1,0:T(8,128)(2,1)S(1)} %get-tuple-element.41), channel_id=1, source_target_pairs={{0,1},{1,0},{2,3},{3,2},{4,5},{5,4},{6,7},{7,6},{8,9},{9,8},{10,11... | collective-permute-start | bytes 393224 | tf_op jit(solution)/shard_map/ppermute | solution.py:104
  24.7 1.5 %collective-permute-start.5 = (bf16[384,128]{1,0:T(8,128)(2,1)S(1)}, bf16[384,128]{1,0:T(8,128)(2,1)S(1)}, u32[]{:S(2)}, u32[]{:S(2)}) collective-permute-start(bf16[384,128]{1,0:T(8,128)(2,1)S(1)} %get-tuple-element.46), channel_id=1, source_target_pairs={{0,1},{1,0},{2,3},{3,2},{4,5},{5,4},{6,7},{7,6},{8,9},{9,8},{10,11... | collective-permute-start | bytes 294920 | tf_op jit(solution)/shard_map/ppermute | solution.py:520
  25.3 1.5 %collective-permute-start = (bf16[1024,128]{1,0:T(8,128)(2,1)S(1)}, bf16[1024,128]{1,0:T(8,128)(2,1)S(1)}, u32[]{:S(2)}, u32[]{:S(2)}) collective-permute-start(bf16[1024,128]{1,0:T(8,128)(2,1)S(1)} %get-tuple-element.35), channel_id=1, source_target_pairs={{0,1},{1,0},{2,3},{3,2},{4,5},{5,4},{6,7},{7,6},{8,9},{9,8},{10,11... | collective-permute-start | bytes 786440 | tf_op jit(solution)/shard_map/ppermute | solution.py:520
  27.0 7.7 %collective-permute-start.6 = (bf16[400,128]{1,0:T(8,128)(2,1)S(1)}, bf16[400,128]{1,0:T(8,128)(2,1)S(1)}, u32[]{:S(2)}, u32[]{:S(2)}) collective-permute-start(bf16[400,128]{1,0:T(8,128)(2,1)S(1)} %pad_maximum_fusion), channel_id=1, source_target_pairs={{0,24},{8,16},{16,8},{24,0},{1,25},{9,17},{17,9},{25,1},{2,26},{10... | collective-permute-start | bytes 307208 | tf_op jit(solution)/shard_map/ppermute | solution.py:520
  28.5 6.2 %collective-permute-start.8 = (bf16[400,128]{1,0:T(8,128)(2,1)S(1)}, bf16[400,128]{1,0:T(8,128)(2,1)S(1)}, u32[]{:S(2)}, u32[]{:S(2)}) collective-permute-start(bf16[400,128]{1,0:T(8,128)(2,1)S(1)} %pad_maximum_fusion.1), channel_id=1, source_target_pairs={{0,8},{8,0},{16,24},{24,16},{1,9},{9,1},{17,25},{25,17},{2,10},{10... | collective-permute-start | bytes 307208 | tf_op jit(solution)/shard_map/ppermute | solution.py:520
  29.1 5.6 %collective-permute-start.7 = (bf16[336,128]{1,0:T(8,128)(2,1)S(1)}, bf16[336,128]{1,0:T(8,128)(2,1)S(1)}, u32[]{:S(2)}, u32[]{:S(2)}) collective-permute-start(bf16[336,128]{1,0:T(8,128)(2,1)S(1)} %pad_maximum_fusion.2), channel_id=1, source_target_pairs={{0,16},{8,24},{16,0},{24,8},{1,17},{9,25},{17,1},{25,9},{2,18},{10... | collective-permute-start | bytes 258056 | tf_op jit(solution)/shard_map/ppermute | solution.py:520
  30.6 8.7 %collective-permute-start.12 = (bf16[64,128]{1,0:T(8,128)(2,1)S(1)}, bf16[64,128]{1,0:T(8,128)(2,1)S(1)}, u32[]{:S(2)}, u32[]{:S(2)}) collective-permute-start(bf16[64,128]{1,0:T(8,128)(2,1)S(1)} %get-tuple-element.50), channel_id=1, source_target_pairs={{1,2},{2,1},{3,4},{4,3},{5,6},{6,5},{7,0},{0,7},{9,10},{10,9},{11,... | collective-permute-start | bytes 49160 | tf_op jit(solution)/shard_map/ppermute | solution.py:104
  34.8 8.3 %collective-permute-start.10 = (bf16[336,128]{1,0:T(8,128)(2,1)S(1)}, bf16[336,128]{1,0:T(8,128)(2,1)S(1)}, u32[]{:S(2)}, u32[]{:S(2)}) collective-permute-start(bf16[336,128]{1,0:T(8,128)(2,1)S(1)} %pad_maximum_fusion.3), channel_id=1, source_target_pairs={{0,4},{1,5},{2,6},{3,7},{4,0},{5,1},{6,2},{7,3},{8,12},{9,13},{10,... | collective-permute-start | bytes 258056 | tf_op jit(solution)/shard_map/ppermute | solution.py:520
  36.0 8.0 %collective-permute-start.11 = (bf16[336,128]{1,0:T(8,128)(2,1)S(1)}, bf16[336,128]{1,0:T(8,128)(2,1)S(1)}, u32[]{:S(2)}, u32[]{:S(2)}) collective-permute-start(bf16[336,128]{1,0:T(8,128)(2,1)S(1)} %pad_maximum_fusion.3), channel_id=1, source_target_pairs={{0,2},{1,3},{2,0},{3,1},{4,6},{5,7},{6,4},{7,5},{8,10},{9,11},{10,... | collective-permute-start | bytes 258056 | tf_op jit(solution)/shard_map/ppermute | solution.py:520
  37.5 6.5 %collective-permute-start.9 = (bf16[336,128]{1,0:T(8,128)(2,1)S(1)}, bf16[336,128]{1,0:T(8,128)(2,1)S(1)}, u32[]{:S(2)}, u32[]{:S(2)}) collective-permute-start(bf16[336,128]{1,0:T(8,128)(2,1)S(1)} %pad_maximum_fusion.3), channel_id=1, source_target_pairs={{0,6},{1,7},{2,4},{3,5},{4,2},{5,3},{6,0},{7,1},{8,14},{9,15},{10,... | collective-permute-start | bytes 258056 | tf_op jit(solution)/shard_map/ppermute | solution.py:520
  44.1 5.4 %collective-permute-start.13 = (bf16[336,128]{1,0:T(8,128)(2,1)S(1)}, bf16[336,128]{1,0:T(8,128)(2,1)S(1)}, u32[]{:S(2)}, u32[]{:S(2)}) collective-permute-start(bf16[336,128]{1,0:T(8,128)(2,1)S(1)} %add_convert_fusion.1), channel_id=1, source_target_pairs={{0,8},{8,0},{16,24},{24,16},{1,9},{9,1},{17,25},{25,17},{2,10},{10... | collective-permute-start | bytes 258056 | tf_op jit(solution)/shard_map/ppermute | solution.py:520
  45.6 4.8 %collective-permute-start.14 = (bf16[336,128]{1,0:T(8,128)(2,1)S(1)}, bf16[336,128]{1,0:T(8,128)(2,1)S(1)}, u32[]{:S(2)}, u32[]{:S(2)}) collective-permute-start(bf16[336,128]{1,0:T(8,128)(2,1)S(1)} %add_convert_fusion.1), channel_id=1, source_target_pairs={{0,16},{8,24},{16,0},{24,8},{1,17},{9,25},{17,1},{25,9},{2,18},{10... | collective-permute-start | bytes 258056 | tf_op jit(solution)/shard_map/ppermute | solution.py:520
  46.4 5.4 %collective-permute-start.15 = (bf16[336,128]{1,0:T(8,128)(2,1)S(1)}, bf16[336,128]{1,0:T(8,128)(2,1)S(1)}, u32[]{:S(2)}, u32[]{:S(2)}) collective-permute-start(bf16[336,128]{1,0:T(8,128)(2,1)S(1)} %add_convert_fusion.1), channel_id=1, source_target_pairs={{0,24},{8,16},{16,8},{24,0},{1,25},{9,17},{17,9},{25,1},{2,26},{10... | collective-permute-start | bytes 258056 | tf_op jit(solution)/shard_map/ppermute | solution.py:520
  51.8 1.7 %collective-permute-start.16 = (bf16[1344,128]{1,0:T(8,128)(2,1)S(1)}, bf16[1344,128]{1,0:T(8,128)(2,1)S(1)}, u32[]{:S(2)}, u32[]{:S(2)}) collective-permute-start(bf16[1344,128]{1,0:T(8,128)(2,1)S(1)} %constant_dynamic-update-slice_fusion.refs_0_), channel_id=1, source_target_pairs={{0,1},{1,0},{2,3},{3,2},{4,5},{5,4},{6,7},{7,6},{8,9},{9,8},{10,11... | collective-permute-start | bytes 1032200 | tf_op jit(solution)/shard_map/ppermute | solution.py:520

commit v7 on v6

--- a/solution.py
+++ b/solution.py
@@ -113,31 +113,47 @@
 def select_kernel(
     embed_ref, rows_ref, weight_ref, s0, s1, s2, s3, embed_v, rows_v, weight_v, sems
 ):
+    block = min(embed_ref.shape[0], LANES)
+    spans = [pl.ds(start, block) for start in range(0, embed_ref.shape[0], block)]
+    reads = [
+        pltpu.make_async_copy(embed_ref.at[at, :], embed_v.at[at, :], sems.at[2 + i])
+        for i, at in enumerate(spans)
+    ]
     copies = [
         pltpu.make_async_copy(rows_ref, rows_v, sems.at[0]),
-        pltpu.make_async_copy(embed_ref, embed_v, sems.at[1]),
-        pltpu.make_async_copy(weight_ref, weight_v, sems.at[2]),
+        pltpu.make_async_copy(weight_ref, weight_v, sems.at[1]),
     ]
-    for copy in copies:
+    for copy in (copies[0], *reads, copies[1]):
         copy.start()
-    for copy in copies[:2]:
-        copy.wait()
+    copies[0].wait()
     rows = embed_v.shape[0]
-    for index, send_ref in zip(pair_lists(rows_v), (s0, s1, s2, s3)):
-        spots = lax.broadcasted_iota(jnp.int32, (rows, index.shape[1]), 0).astype(jnp.int16)
-        hot = jnp.where(spots == index.astype(jnp.int16), jnp.ones((), BF16), jnp.zeros((), BF16))
-        send_ref[...] = dot(hot, embed_v[...], TN).astype(BF16)
-    copies[2].wait()
+    hots = []
+    for index in pair_lists(rows_v):
+        ghost = index.shape[1]
+        column = jnp.broadcast_to(index.astype(F32), (128, ghost)).T
+        wide = jnp.concatenate([column] * (rows // 128), axis=1).astype(jnp.int32).astype(jnp.int16)
+        spots = lax.broadcasted_iota(jnp.int32, (ghost, rows), 1).astype(jnp.int16)
+        hots.append(jnp.where(spots == wide, jnp.ones((), BF16), jnp.zeros((), BF16)))
+    hot = jnp.concatenate(hots, axis=0)
+    total = jnp.zeros((hot.shape[0], embed_v.shape[1]), F32)
+    for i, (at, read) in enumerate(zip(spans, reads)):
+        read.wait()
+        total = total + dot(hot[:, i * block : (i + 1) * block], embed_v[at, :], NN)
+    ghost = s0.shape[0]
+    for i, send_ref in enumerate((s0, s1, s2, s3)):
+        send_ref[...] = total[i * ghost : (i + 1) * ghost].astype(BF16)
+    copies[1].wait()
 
 
 def select(embed, outgoing, weight):
+    rows = embed.shape[0]
     ghost = jax.ShapeDtypeStruct((outgoing.shape[1], embed.shape[1]), BF16)
     return pl.pallas_call(
         select_kernel,
         in_specs=[HBM] * 3,
         out_specs=[VMEM] * 7,
         out_shape=in_vmem(*[ghost] * 4, embed, outgoing, weight),
-        scratch_shapes=[pltpu.SemaphoreType.DMA((3,))],
+        scratch_shapes=[pltpu.SemaphoreType.DMA((2 + rows // min(rows, LANES),))],
         compiler_params=limits(),
         name="select",
     )(*in_hbm(embed, outgoing, weight))
@@ -325,20 +341,27 @@
     dt_ref[...] = dsum * (sig * (1.0 + tsum * (1.0 - sig)))
     acc_ref[...] = jnp.zeros_like(acc_ref)
 
-    def backward(j, carry):
-        parts = []
-        dws = []
-        for t in range(tiles):
-            at, low, high = lookup(j, t)
-            dt = dt_ref[:, at]
-            dws.append((dt * picked_ref[j, :, at].astype(F32)).astype(BF16))
-            terms = (dt * weight_ref[pl.ds(j * width, width), at]).astype(BF16)
-            parts.append(spread(terms, high, groups))
-        acc_ref[...] += dot(jnp.concatenate(parts, axis=1), hot_ref[j], NT)
-        slot_basis = basis_ref[pl.ds(pl.multiple_of(j * nbasis, nbasis), nbasis), :]
+    def backward(step, carry):
+        parts, dws, hots, bases = [], [], [], []
+        for k in range(group):
+            j = step * group + k
+            for t in range(tiles):
+                at, low, high = lookup(j, t)
+                dt = dt_ref[:, at]
+                dws.append((dt * picked_ref[j, :, at].astype(F32)).astype(BF16))
+                terms = (dt * weight_ref[pl.ds(j * width, width), at]).astype(BF16)
+                parts.append(spread(terms, high, groups))
+            hots.append(hot_ref[j])
+            bases.append(basis_ref[pl.ds(pl.multiple_of(j * nbasis, nbasis), nbasis), :])
+        hot = jnp.concatenate(hots, axis=1)
+        acc_ref[...] += dot(jnp.concatenate(parts, axis=1), hot, NT)
+        slot_basis = jnp.concatenate(bases, axis=1)
         return carry + dot(slot_basis, jnp.concatenate(dws, axis=1), NT)
 
-    basis_grad = lax.fori_loop(0, trips, backward, jnp.zeros((nbasis, width), F32), unroll=8)
+    group = 2 if trips % 2 == 0 else 1
+    basis_grad = lax.fori_loop(
+        0, trips // group, backward, jnp.zeros((nbasis, width), F32), unroll=4
+    )
 
     own = unstacked(acc_ref[: own_groups * width, :], width)
     own_ref[...] = own

time: 54.8 us -> 54.6 us (level)
  no operation moved by 1% of the time
where the time goes in v7:
time: 54.6 us; the launch traced here: 54.4 us
  Pallas kernels  21.5 us (39%)
  starting transfers between devices  20.6 us (38%)
  waiting for transfers between devices  11.2 us (21%)
  between operations  0.8 us (1%)
    ppermute x12, starting transfers between devices, swapped(): lax.ppermute(value, axis, [(i, i ^ offset) for i in range(lax.axis_size(a...  12.4 us
    ppermute x12, waiting for transfers between devices, swapped(): lax.ppermute(value, axis, [(i, i ^ offset) for i in range(lax.axis_size(a...  11.2 us
    pallas_call x1, Pallas kernels, triplets(): pl.pallas_call(triplet_kernel, in_specs=[VMEM] * len(operands) + [HBM] *...  10.1 us
    ppermute x5, starting transfers between devices, paired(): return lax.ppermute(value, axis, pairs)  8.25 us
    pallas_call x1, Pallas kernels, residual(): pl.pallas_call(residual_kernel, in_specs=[VMEM] * 2 + [HBM] * (3 + len(st...  4.56 us
    pallas_call x1, Pallas kernels, edge_gradient(): pl.pallas_call(edge_kernel, in_specs=[VMEM] * len(operands) + [HBM], out_...  3.82 us
    pallas_call x1, Pallas kernels, select(): pl.pallas_call(select_kernel, in_specs=[HBM] * 3, out_specs=[VMEM] * 7, o...  1.9 us
    pallas_call x1, Pallas kernels, finish(): pl.pallas_call(lambda *refs: finish_kernel(offsets, *refs), in_specs=[VME...  1.15 us
  transfers between devices with their start and end apart: 17, of which 8 were waited for; matrix products, arithmetic and copies ran while one was open for 0% of the time, Pallas kernels for 15%

profile of v7, /device:TPU:0, one launch (start us, length us, event | category | flops | bytes accessed | tf_op | source)
XLA Modules:
  0.0 54.4 jit_solution(1487135273827852017)
XLA Ops:
  0.6 1.9 %select.5 = (bf16[128,512]{1,0:T(8,128)(2,1)S(1)}, bf16[128,512]{1,0:T(8,128)(2,1)S(1)}, bf16[128,512]{1,0:T(8,128)(2,1)S(1)}, bf16[128,512]{1,0:T(8,128)(2,1)S(...) custom-call(bf16[1024,512]{1,0:T(8,128)(2,1)} %embed_ref.1, ...), custom_call_target="tpu_custom_call" | custom-call | tf_op jit(solution)/shard_map/select/pallas_call | solution.py:151
  2.5 4.0 %collective-permute-start.1 = (bf16[128,512]{1,0:T(8,128)(2,1)S(1)}, bf16[128,512]{1,0:T(8,128)(2,1)S(1)}, u32[]{:S(2)}, u32[]{:S(2)}) collective-permute-start(bf16[128,512]{1,0:T(8,128)(2,1)S(1)} %get-tuple-element.38), channel_id=1, source_target_pairs={{8,16},{16,8},{24,0},{0,24},{9,17},{17,9},{25,1},{1,25},{10,18},{1... | collective-permute-start | bytes 393224 | tf_op jit(solution)/shard_map/ppermute | solution.py:104
  6.5 2.7 %collective-permute-start.2 = (bf16[128,512]{1,0:T(8,128)(2,1)S(1)}, bf16[128,512]{1,0:T(8,128)(2,1)S(1)}, u32[]{:S(2)}, u32[]{:S(2)}) collective-permute-start(bf16[128,512]{1,0:T(8,128)(2,1)S(1)} %get-tuple-element.39), channel_id=1, source_target_pairs={{1,2},{2,1},{3,4},{4,3},{5,6},{6,5},{7,0},{0,7},{9,10},{10,9},{11,... | collective-permute-start | bytes 393224 | tf_op jit(solution)/shard_map/ppermute | solution.py:104
  9.3 0.5 %collective-permute-start.3 = (bf16[128,512]{1,0:T(8,128)(2,1)S(1)}, bf16[128,512]{1,0:T(8,128)(2,1)S(1)}, u32[]{:S(2)}, u32[]{:S(2)}) collective-permute-start(bf16[128,512]{1,0:T(8,128)(2,1)S(1)} %get-tuple-element.40), channel_id=1, source_target_pairs={{0,8},{8,0},{16,24},{24,16},{1,9},{9,1},{17,25},{25,17},{2,10},{10... | collective-permute-start | bytes 393224 | tf_op jit(solution)/shard_map/ppermute | solution.py:104
  9.8 0.0 collective-permute-start.4
  9.8 4.6 %residual.1 = (bf16[64,512]{1,0:T(8,128)(2,1)S(1)}, s32[16,1024]{1,0:T(8,128)S(1)}, s32[1,1024]{1,0:T(1,128)S(1)}, bf16[1024,512]{1,0:T(8,128)(2,1)}, bf16[1024,...) custom-call(bf16[1024,512]{1,0:T(8,128)(2,1)S(1)} %get-tuple-element.32., ...), custom_call_target="tpu_custom_call" | custom-call | flops 1610612736 | tf_op jit(solution)/shard_map/residual/pallas_call | solution.py:232
  14.4 10.1 %triplets.1 = (f32[64,1024]{1,0:T(8,128)S(1)}, bf16[64,128]{1,0:T(8,128)(2,1)S(1)}, bf16[64,128]{1,0:T(8,128)(2,1)S(1)}, bf16[64,128]{1,0:T(8,128)(2,1)S(1)}, bf...) custom-call(f32[64,1024]{1,0:T(8,128)S(1)} %get-tuple-element.36.pre_ref, ...), custom_call_target="tpu_custom_call" | custom-call | flops 12884901888 | tf_op jit(solution)/shard_map/triplets/pallas_call | solution.py:413
  24.5 0.6 %collective-permute-start.5 = (bf16[384,128]{1,0:T(8,128)(2,1)S(1)}, bf16[384,128]{1,0:T(8,128)(2,1)S(1)}, u32[]{:S(2)}, u32[]{:S(2)}) collective-permute-start(bf16[384,128]{1,0:T(8,128)(2,1)S(1)} %get-tuple-element.46), channel_id=1, source_target_pairs={{0,1},{1,0},{2,3},{3,2},{4,5},{5,4},{6,7},{7,6},{8,9},{9,8},{10,11... | collective-permute-start | bytes 294920 | tf_op jit(solution)/shard_map/ppermute | solution.py:543
  25.1 0.1 collective-permute-start
  25.2 0.9 %collective-permute-done.5 = bf16[384,128]{1,0:T(8,128)(2,1)S(1)} collective-permute-done((bf16[384,128]{1,0:T(8,128)(2,1)S(1)}, bf16[384,128]{1,0:T(8,128)(2,1)S(1)}, u32[]{:S(2)}, u32[]{:S(2)}) %collective-permute-start.5) | collective-permute-done | bytes 98336 | tf_op jit(solution)/shard_map/ppermute | solution.py:543
  26.1 0.5 collective-permute-done
  26.6 0.1 add_convert_fusion
  26.8 1.5 %collective-permute-start.6 = (bf16[400,128]{1,0:T(8,128)(2,1)S(1)}, bf16[400,128]{1,0:T(8,128)(2,1)S(1)}, u32[]{:S(2)}, u32[]{:S(2)}) collective-permute-start(bf16[400,128]{1,0:T(8,128)(2,1)S(1)} %pad_maximum_fusion), channel_id=1, source_target_pairs={{0,24},{8,16},{16,8},{24,0},{1,25},{9,17},{17,9},{25,1},{2,26},{10... | collective-permute-start | bytes 307208 | tf_op jit(solution)/shard_map/ppermute | solution.py:543
  28.3 0.6 %collective-permute-start.8 = (bf16[400,128]{1,0:T(8,128)(2,1)S(1)}, bf16[400,128]{1,0:T(8,128)(2,1)S(1)}, u32[]{:S(2)}, u32[]{:S(2)}) collective-permute-start(bf16[400,128]{1,0:T(8,128)(2,1)S(1)} %pad_maximum_fusion.1), channel_id=1, source_target_pairs={{0,8},{8,0},{16,24},{24,16},{1,9},{9,1},{17,25},{25,17},{2,10},{10... | collective-permute-start | bytes 307208 | tf_op jit(solution)/shard_map/ppermute | solution.py:543
  28.9 1.5 %collective-permute-start.7 = (bf16[336,128]{1,0:T(8,128)(2,1)S(1)}, bf16[336,128]{1,0:T(8,128)(2,1)S(1)}, u32[]{:S(2)}, u32[]{:S(2)}) collective-permute-start(bf16[336,128]{1,0:T(8,128)(2,1)S(1)} %pad_maximum_fusion.2), channel_id=1, source_target_pairs={{0,16},{8,24},{16,0},{24,8},{1,17},{9,25},{17,1},{25,9},{2,18},{10... | collective-permute-start | bytes 258056 | tf_op jit(solution)/shard_map/ppermute | solution.py:543
  30.4 1.0 %collective-permute-start.12 = (bf16[64,128]{1,0:T(8,128)(2,1)S(1)}, bf16[64,128]{1,0:T(8,128)(2,1)S(1)}, u32[]{:S(2)}, u32[]{:S(2)}) collective-permute-start(bf16[64,128]{1,0:T(8,128)(2,1)S(1)} %get-tuple-element.50), channel_id=1, source_target_pairs={{1,2},{2,1},{3,4},{4,3},{5,6},{6,5},{7,0},{0,7},{9,10},{10,9},{11,... | collective-permute-start | bytes 49160 | tf_op jit(solution)/shard_map/ppermute | solution.py:104
  31.4 3.1 %collective-permute-done.7 = bf16[336,128]{1,0:T(8,128)(2,1)S(1)} collective-permute-done((bf16[336,128]{1,0:T(8,128)(2,1)S(1)}, bf16[336,128]{1,0:T(8,128)(2,1)S(1)}, u32[]{:S(2)}, u32[]{:S(2)}) %collective-permute-start.7) | collective-permute-done | bytes 86048 | tf_op jit(solution)/shard_map/ppermute | solution.py:543
  34.6 1.1 %collective-permute-start.10 = (bf16[336,128]{1,0:T(8,128)(2,1)S(1)}, bf16[336,128]{1,0:T(8,128)(2,1)S(1)}, u32[]{:S(2)}, u32[]{:S(2)}) collective-permute-start(bf16[336,128]{1,0:T(8,128)(2,1)S(1)} %pad_maximum_fusion.3), channel_id=1, source_target_pairs={{0,4},{1,5},{2,6},{3,7},{4,0},{5,1},{6,2},{7,3},{8,12},{9,13},{10,... | collective-permute-start | bytes 258056 | tf_op jit(solution)/shard_map/ppermute | solution.py:543
  35.7 1.6 %collective-permute-start.11 = (bf16[336,128]{1,0:T(8,128)(2,1)S(1)}, bf16[336,128]{1,0:T(8,128)(2,1)S(1)}, u32[]{:S(2)}, u32[]{:S(2)}) collective-permute-start(bf16[336,128]{1,0:T(8,128)(2,1)S(1)} %pad_maximum_fusion.3), channel_id=1, source_target_pairs={{0,2},{1,3},{2,0},{3,1},{4,6},{5,7},{6,4},{7,5},{8,10},{9,11},{10,... | collective-permute-start | bytes 258056 | tf_op jit(solution)/shard_map/ppermute | solution.py:543
  37.3 1.7 %collective-permute-start.9 = (bf16[336,128]{1,0:T(8,128)(2,1)S(1)}, bf16[336,128]{1,0:T(8,128)(2,1)S(1)}, u32[]{:S(2)}, u32[]{:S(2)}) collective-permute-start(bf16[336,128]{1,0:T(8,128)(2,1)S(1)} %pad_maximum_fusion.3), channel_id=1, source_target_pairs={{0,6},{1,7},{2,4},{3,5},{4,2},{5,3},{6,0},{7,1},{8,14},{9,15},{10,... | collective-permute-start | bytes 258056 | tf_op jit(solution)/shard_map/ppermute | solution.py:543
  39.1 3.8 %edge_gradient.1 = bf16[1024,512]{1,0:T(8,128)(2,1)} custom-call(f32[64,1024]{1,0:T(8,128)S(1)} %get-tuple-element.49.own_ref, bf16[64,128]{1,0:T(8,128)(2,1)S(1)} %slice.47.b0_ref, bf16[64,128]{1,0:T(8,128)(2,1)S(1)} %slice.48.b1_ref, bf16[64,128]{1,0:T(8,128)(2,1)S(1)} %slice.49.b2_ref, bf16[64,128]{1,0:T(8,128)(2,1)S(1)} %collective-permute-done.12.b3_ref, ...), custom_call_target="tpu_custom_call" | custom-call | flops 1207959552 | tf_op jit(solution)/shard_map/edge_gradient/pallas_call | solution.py:477
  42.9 0.9 %collective-permute-done.11 = bf16[336,128]{1,0:T(8,128)(2,1)S(1)} collective-permute-done((bf16[336,128]{1,0:T(8,128)(2,1)S(1)}, bf16[336,128]{1,0:T(8,128)(2,1)S(1)}, u32[]{:S(2)}, u32[]{:S(2)}) %collective-permute-start.11) | collective-permute-done | bytes 86048 | tf_op jit(solution)/shard_map/ppermute | solution.py:543
  43.8 0.1 add_convert_fusion.1
  43.8 1.6 %collective-permute-start.13 = (bf16[336,128]{1,0:T(8,128)(2,1)S(1)}, bf16[336,128]{1,0:T(8,128)(2,1)S(1)}, u32[]{:S(2)}, u32[]{:S(2)}) collective-permute-start(bf16[336,128]{1,0:T(8,128)(2,1)S(1)} %add_convert_fusion.1), channel_id=1, source_target_pairs={{0,8},{8,0},{16,24},{24,16},{1,9},{9,1},{17,25},{25,17},{2,10},{10... | collective-permute-start | bytes 258056 | tf_op jit(solution)/shard_map/ppermute | solution.py:543
  45.4 0.8 %collective-permute-start.14 = (bf16[336,128]{1,0:T(8,128)(2,1)S(1)}, bf16[336,128]{1,0:T(8,128)(2,1)S(1)}, u32[]{:S(2)}, u32[]{:S(2)}) collective-permute-start(bf16[336,128]{1,0:T(8,128)(2,1)S(1)} %add_convert_fusion.1), channel_id=1, source_target_pairs={{0,16},{8,24},{16,0},{24,8},{1,17},{9,25},{17,1},{25,9},{2,18},{10... | collective-permute-start | bytes 258056 | tf_op jit(solution)/shard_map/ppermute | solution.py:543
  46.2 1.2 %collective-permute-start.15 = (bf16[336,128]{1,0:T(8,128)(2,1)S(1)}, bf16[336,128]{1,0:T(8,128)(2,1)S(1)}, u32[]{:S(2)}, u32[]{:S(2)}) collective-permute-start(bf16[336,128]{1,0:T(8,128)(2,1)S(1)} %add_convert_fusion.1), channel_id=1, source_target_pairs={{0,24},{8,16},{16,8},{24,0},{1,25},{9,17},{17,9},{25,1},{2,26},{10... | collective-permute-start | bytes 258056 | tf_op jit(solution)/shard_map/ppermute | solution.py:543
  47.4 1.9 %collective-permute-done.13 = bf16[336,128]{1,0:T(8,128)(2,1)S(1)} collective-permute-done((bf16[336,128]{1,0:T(8,128)(2,1)S(1)}, bf16[336,128]{1,0:T(8,128)(2,1)S(1)}, u32[]{:S(2)}, u32[]{:S(2)}) %collective-permute-start.13) | collective-permute-done | bytes 86048 | tf_op jit(solution)/shard_map/ppermute | solution.py:543
  49.3 0.9 %collective-permute-done.14 = bf16[336,128]{1,0:T(8,128)(2,1)S(1)} collective-permute-done((bf16[336,128]{1,0:T(8,128)(2,1)S(1)}, bf16[336,128]{1,0:T(8,128)(2,1)S(1)}, u32[]{:S(2)}, u32[]{:S(2)}) %collective-permute-start.14) | collective-permute-done | bytes 86048 | tf_op jit(solution)/shard_map/ppermute | solution.py:543
  50.2 1.4 %collective-permute-done.15 = bf16[336,128]{1,0:T(8,128)(2,1)S(1)} collective-permute-done((bf16[336,128]{1,0:T(8,128)(2,1)S(1)}, bf16[336,128]{1,0:T(8,128)(2,1)S(1)}, u32[]{:S(2)}, u32[]{:S(2)}) %collective-permute-start.15) | collective-permute-done | bytes 86048 | tf_op jit(solution)/shard_map/ppermute | solution.py:543
  51.6 0.1 collective-permute-start.16
  51.7 1.6 %collective-permute-done.16.refs_1_ = bf16[1344,128]{1,0:T(8,128)(2,1)S(1)} collective-permute-done((bf16[1344,128]{1,0:T(8,128)(2,1)S(1)}, bf16[1344,128]{1,0:T(8,128)(2,1)S(1)}, u32[]{:S(2)}, u32[]{:S(2)}) %collective-permute-start.16) | collective-permute-done | bytes 344096 | tf_op jit(solution)/shard_map/ppermute | solution.py:543
  53.3 1.1 %finish.1 = (f32[512,512]{1,0:T(8,128)}, f32[64,512]{1,0:T(8,128)}, f32[64,512]{1,0:T(8,128)}, f32[16,64]{1,0:T(8,128)}) custom-call(bf16[1344,128]{1,0:T(8,128)(2,1)S(1)} %constant_dynamic-update-slice_fusion.refs_0_, bf16[1344,128]{1,0:T(8,128)(2,1)S(1)} %collective-permute-done.16.refs_1_), custom_call_target="tpu_custom_call" | custom-call | tf_op jit(solution)/shard_map/finish/pallas_call | solution.py:523
  (25 shorter events, 0.2 us)
Async XLA Ops:
  2.5 11.8 %collective-permute-start.1 = (bf16[128,512]{1,0:T(8,128)(2,1)S(1)}, bf16[128,512]{1,0:T(8,128)(2,1)S(1)}, u32[]{:S(2)}, u32[]{:S(2)}) collective-permute-start(bf16[128,512]{1,0:T(8,128)(2,1)S(1)} %get-tuple-element.38), channel_id=1, source_target_pairs={{8,16},{16,8},{24,0},{0,24},{9,17},{17,9},{25,1},{1,25},{10,18},{1... | collective-permute-start | bytes 393224 | tf_op jit(solution)/shard_map/ppermute | solution.py:104
  6.5 7.9 %collective-permute-start.2 = (bf16[128,512]{1,0:T(8,128)(2,1)S(1)}, bf16[128,512]{1,0:T(8,128)(2,1)S(1)}, u32[]{:S(2)}, u32[]{:S(2)}) collective-permute-start(bf16[128,512]{1,0:T(8,128)(2,1)S(1)} %get-tuple-element.39), channel_id=1, source_target_pairs={{1,2},{2,1},{3,4},{4,3},{5,6},{6,5},{7,0},{0,7},{9,10},{10,9},{11,... | collective-permute-start | bytes 393224 | tf_op jit(solution)/shard_map/ppermute | solution.py:104
  9.3 5.1 %collective-permute-start.3 = (bf16[128,512]{1,0:T(8,128)(2,1)S(1)}, bf16[128,512]{1,0:T(8,128)(2,1)S(1)}, u32[]{:S(2)}, u32[]{:S(2)}) collective-permute-start(bf16[128,512]{1,0:T(8,128)(2,1)S(1)} %get-tuple-element.40), channel_id=1, source_target_pairs={{0,8},{8,0},{16,24},{24,16},{1,9},{9,1},{17,25},{25,17},{2,10},{10... | collective-permute-start | bytes 393224 | tf_op jit(solution)/shard_map/ppermute | solution.py:104
  9.8 4.6 %collective-permute-start.4 = (bf16[128,512]{1,0:T(8,128)(2,1)S(1)}, bf16[128,512]{1,0:T(8,128)(2,1)S(1)}, u32[]{:S(2)}, u32[]{:S(2)}) collective-permute-start(bf16[128,512]{1,0:T(8,128)(2,1)S(1)} %get-tuple-element.41), channel_id=1, source_target_pairs={{0,1},{1,0},{2,3},{3,2},{4,5},{5,4},{6,7},{7,6},{8,9},{9,8},{10,11... | collective-permute-start | bytes 393224 | tf_op jit(solution)/shard_map/ppermute | solution.py:104
  24.5 1.5 %collective-permute-start.5 = (bf16[384,128]{1,0:T(8,128)(2,1)S(1)}, bf16[384,128]{1,0:T(8,128)(2,1)S(1)}, u32[]{:S(2)}, u32[]{:S(2)}) collective-permute-start(bf16[384,128]{1,0:T(8,128)(2,1)S(1)} %get-tuple-element.46), channel_id=1, source_target_pairs={{0,1},{1,0},{2,3},{3,2},{4,5},{5,4},{6,7},{7,6},{8,9},{9,8},{10,11... | collective-permute-start | bytes 294920 | tf_op jit(solution)/shard_map/ppermute | solution.py:543
  25.1 1.5 %collective-permute-start = (bf16[1024,128]{1,0:T(8,128)(2,1)S(1)}, bf16[1024,128]{1,0:T(8,128)(2,1)S(1)}, u32[]{:S(2)}, u32[]{:S(2)}) collective-permute-start(bf16[1024,128]{1,0:T(8,128)(2,1)S(1)} %get-tuple-element.35), channel_id=1, source_target_pairs={{0,1},{1,0},{2,3},{3,2},{4,5},{5,4},{6,7},{7,6},{8,9},{9,8},{10,11... | collective-permute-start | bytes 786440 | tf_op jit(solution)/shard_map/ppermute | solution.py:543
  26.8 7.7 %collective-permute-start.6 = (bf16[400,128]{1,0:T(8,128)(2,1)S(1)}, bf16[400,128]{1,0:T(8,128)(2,1)S(1)}, u32[]{:S(2)}, u32[]{:S(2)}) collective-permute-start(bf16[400,128]{1,0:T(8,128)(2,1)S(1)} %pad_maximum_fusion), channel_id=1, source_target_pairs={{0,24},{8,16},{16,8},{24,0},{1,25},{9,17},{17,9},{25,1},{2,26},{10... | collective-permute-start | bytes 307208 | tf_op jit(solution)/shard_map/ppermute | solution.py:543
  28.3 6.2 %collective-permute-start.8 = (bf16[400,128]{1,0:T(8,128)(2,1)S(1)}, bf16[400,128]{1,0:T(8,128)(2,1)S(1)}, u32[]{:S(2)}, u32[]{:S(2)}) collective-permute-start(bf16[400,128]{1,0:T(8,128)(2,1)S(1)} %pad_maximum_fusion.1), channel_id=1, source_target_pairs={{0,8},{8,0},{16,24},{24,16},{1,9},{9,1},{17,25},{25,17},{2,10},{10... | collective-permute-start | bytes 307208 | tf_op jit(solution)/shard_map/ppermute | solution.py:543
  28.9 5.6 %collective-permute-start.7 = (bf16[336,128]{1,0:T(8,128)(2,1)S(1)}, bf16[336,128]{1,0:T(8,128)(2,1)S(1)}, u32[]{:S(2)}, u32[]{:S(2)}) collective-permute-start(bf16[336,128]{1,0:T(8,128)(2,1)S(1)} %pad_maximum_fusion.2), channel_id=1, source_target_pairs={{0,16},{8,24},{16,0},{24,8},{1,17},{9,25},{17,1},{25,9},{2,18},{10... | collective-permute-start | bytes 258056 | tf_op jit(solution)/shard_map/ppermute | solution.py:543
  30.4 8.7 %collective-permute-start.12 = (bf16[64,128]{1,0:T(8,128)(2,1)S(1)}, bf16[64,128]{1,0:T(8,128)(2,1)S(1)}, u32[]{:S(2)}, u32[]{:S(2)}) collective-permute-start(bf16[64,128]{1,0:T(8,128)(2,1)S(1)} %get-tuple-element.50), channel_id=1, source_target_pairs={{1,2},{2,1},{3,4},{4,3},{5,6},{6,5},{7,0},{0,7},{9,10},{10,9},{11,... | collective-permute-start | bytes 49160 | tf_op jit(solution)/shard_map/ppermute | solution.py:104
  34.6 8.3 %collective-permute-start.10 = (bf16[336,128]{1,0:T(8,128)(2,1)S(1)}, bf16[336,128]{1,0:T(8,128)(2,1)S(1)}, u32[]{:S(2)}, u32[]{:S(2)}) collective-permute-start(bf16[336,128]{1,0:T(8,128)(2,1)S(1)} %pad_maximum_fusion.3), channel_id=1, source_target_pairs={{0,4},{1,5},{2,6},{3,7},{4,0},{5,1},{6,2},{7,3},{8,12},{9,13},{10,... | collective-permute-start | bytes 258056 | tf_op jit(solution)/shard_map/ppermute | solution.py:543
  35.7 8.0 %collective-permute-start.11 = (bf16[336,128]{1,0:T(8,128)(2,1)S(1)}, bf16[336,128]{1,0:T(8,128)(2,1)S(1)}, u32[]{:S(2)}, u32[]{:S(2)}) collective-permute-start(bf16[336,128]{1,0:T(8,128)(2,1)S(1)} %pad_maximum_fusion.3), channel_id=1, source_target_pairs={{0,2},{1,3},{2,0},{3,1},{4,6},{5,7},{6,4},{7,5},{8,10},{9,11},{10,... | collective-permute-start | bytes 258056 | tf_op jit(solution)/shard_map/ppermute | solution.py:543
  37.3 6.5 %collective-permute-start.9 = (bf16[336,128]{1,0:T(8,128)(2,1)S(1)}, bf16[336,128]{1,0:T(8,128)(2,1)S(1)}, u32[]{:S(2)}, u32[]{:S(2)}) collective-permute-start(bf16[336,128]{1,0:T(8,128)(2,1)S(1)} %pad_maximum_fusion.3), channel_id=1, source_target_pairs={{0,6},{1,7},{2,4},{3,5},{4,2},{5,3},{6,0},{7,1},{8,14},{9,15},{10,... | collective-permute-start | bytes 258056 | tf_op jit(solution)/shard_map/ppermute | solution.py:543
  43.8 5.4 %collective-permute-start.13 = (bf16[336,128]{1,0:T(8,128)(2,1)S(1)}, bf16[336,128]{1,0:T(8,128)(2,1)S(1)}, u32[]{:S(2)}, u32[]{:S(2)}) collective-permute-start(bf16[336,128]{1,0:T(8,128)(2,1)S(1)} %add_convert_fusion.1), channel_id=1, source_target_pairs={{0,8},{8,0},{16,24},{24,16},{1,9},{9,1},{17,25},{25,17},{2,10},{10... | collective-permute-start | bytes 258056 | tf_op jit(solution)/shard_map/ppermute | solution.py:543
  45.4 4.8 %collective-permute-start.14 = (bf16[336,128]{1,0:T(8,128)(2,1)S(1)}, bf16[336,128]{1,0:T(8,128)(2,1)S(1)}, u32[]{:S(2)}, u32[]{:S(2)}) collective-permute-start(bf16[336,128]{1,0:T(8,128)(2,1)S(1)} %add_convert_fusion.1), channel_id=1, source_target_pairs={{0,16},{8,24},{16,0},{24,8},{1,17},{9,25},{17,1},{25,9},{2,18},{10... | collective-permute-start | bytes 258056 | tf_op jit(solution)/shard_map/ppermute | solution.py:543
  46.2 5.4 %collective-permute-start.15 = (bf16[336,128]{1,0:T(8,128)(2,1)S(1)}, bf16[336,128]{1,0:T(8,128)(2,1)S(1)}, u32[]{:S(2)}, u32[]{:S(2)}) collective-permute-start(bf16[336,128]{1,0:T(8,128)(2,1)S(1)} %add_convert_fusion.1), channel_id=1, source_target_pairs={{0,24},{8,16},{16,8},{24,0},{1,25},{9,17},{17,9},{25,1},{2,26},{10... | collective-permute-start | bytes 258056 | tf_op jit(solution)/shard_map/ppermute | solution.py:543
  51.6 1.7 %collective-permute-start.16 = (bf16[1344,128]{1,0:T(8,128)(2,1)S(1)}, bf16[1344,128]{1,0:T(8,128)(2,1)S(1)}, u32[]{:S(2)}, u32[]{:S(2)}) collective-permute-start(bf16[1344,128]{1,0:T(8,128)(2,1)S(1)} %constant_dynamic-update-slice_fusion.refs_0_), channel_id=1, source_target_pairs={{0,1},{1,0},{2,3},{3,2},{4,5},{5,4},{6,7},{7,6},{8,9},{9,8},{10,11... | collective-permute-start | bytes 1032200 | tf_op jit(solution)/shard_map/ppermute | solution.py:543

commit v8 on v7

--- a/solution.py
+++ b/solution.py
@@ -489,25 +489,26 @@
     )(*operands, *in_hbm(dres))
 
 
-def finish_kernel(
-    offsets, mine_ref, other_ref, residual_ref, down_ref, up_ref, basis_ref, all_ref, part_ref
-):
+def finish_kernel(offsets, *refs):
+    count = len(offsets)
+    kept, sent = refs[:count], refs[count : 2 * count]
+    residual_ref, down_ref, up_ref, basis_ref, all_ref, part_ref = refs[2 * count :]
     upper = lax.axis_index("brick") % 2
     slab = lax.axis_index("slab")
     half = residual_ref.shape[0] // 2
     step = half // len(offsets)
     columns = blocks_of(residual_ref.shape[1])
-    block = mine_ref.shape[0] // len(offsets)
+    block = kept[0].shape[0]
     tail = len(columns) * step
     share = block - tail
-    for source, side in ((mine_ref, upper), (other_ref, 1 - upper)):
-        for i, offset in enumerate(offsets):
+    for sources, side in ((kept, upper), (sent, 1 - upper)):
+        for source, offset in zip(sources, offsets):
             place = pl.ds(side * half + (slab ^ offset) * step, step)
             for c, column in enumerate(columns):
-                at = pl.ds(i * block + c * step, step)
+                at = pl.ds(c * step, step)
                 residual_ref[place, column] = source[at, :].astype(F32)
             place = pl.ds((side * len(offsets) + (slab ^ offset)) * share, share)
-            part_ref[place, :] = source[pl.ds(i * block + tail, share), :].astype(F32)
+            part_ref[place, :] = source[pl.ds(tail, share), :].astype(F32)
     rows, inner = all_ref.shape[0] // 2, down_ref.shape[1]
     for side in range(2):
         for c, column in enumerate(blocks_of(all_ref.shape[1])):
@@ -519,10 +520,10 @@
     basis_ref[...] = all_ref[:nbasis, 2 * inner : 2 * inner + width]
 
 
-def finish(offsets, mine, other, shared, inner, width, nbasis):
+def finish(offsets, kept, sent, shared, inner, width, nbasis):
     return pl.pallas_call(
         lambda *refs: finish_kernel(offsets, *refs),
-        in_specs=[VMEM] * 2,
+        in_specs=[VMEM] * (2 * len(offsets)),
         out_specs=[VMEM] * 4,
         out_shape=[
             jax.ShapeDtypeStruct((inner, inner), F32),
@@ -536,7 +537,7 @@
         ],
         compiler_params=limits(),
         name="finish",
-    )(mine, other)
+    )(*kept, *sent)
 
 
 def swapped(value, axis, offset):
@@ -651,9 +652,11 @@
             for i, offset in enumerate(known):
                 step = pieces[offset].shape[0]
                 pieces[offset ^ k] = other[i * step : (i + 1) * step]
-    value = jnp.concatenate([pieces[o] for o in sorted(pieces)], axis=0)
+    offsets = sorted(pieces)
+    kept = [pieces[o] for o in offsets]
+    sent = [swapped(piece, "brick", 1) for piece in kept]
     residual_grad, down_grad, up_grad, basis_grad = finish(
-        sorted(pieces), value, swapped(value, "brick", 1), shared, inner, pre.shape[0], nbasis
+        offsets, kept, sent, shared, inner, pre.shape[0], nbasis
     )
     return edge_grad, residual_grad, down_grad.T, up_grad, basis_grad
 

time: 54.6 us -> 54.2 us (level)
    ppermute x12 -> x15, waiting for transfers between devices: 11.2 us -> 10.8 us  [swapped(): lax.ppermute(value, axis, [(i, i ^ offset) for i in range(lax.axis_size(a...]
    ppermute x12 -> x15, starting transfers between devices: 12.4 us -> 12.3 us  [swapped(): lax.ppermute(value, axis, [(i, i ^ offset) for i in range(lax.axis_size(a...]
  transfers between devices with their start and end apart: 17 -> 20, of which waited for: 8 -> 8; matrix products, arithmetic and copies ran while one was open for 0% -> 0% of each run, Pallas kernels for 15% -> 16%
where the time goes in v8:
time: 54.2 us; the launch traced here: 54 us
  Pallas kernels  21.5 us (40%)
  starting transfers between devices  20.5 us (38%)
  waiting for transfers between devices  10.8 us (20%)
  between operations  0.79 us (1%)
    ppermute x15, starting transfers between devices, swapped(): lax.ppermute(value, axis, [(i, i ^ offset) for i in range(lax.axis_size(a...  12.3 us
    ppermute x15, waiting for transfers between devices, swapped(): lax.ppermute(value, axis, [(i, i ^ offset) for i in range(lax.axis_size(a...  10.8 us
    pallas_call x1, Pallas kernels, triplets(): pl.pallas_call(triplet_kernel, in_specs=[VMEM] * len(operands) + [HBM] *...  10.1 us
    ppermute x5, starting transfers between devices, paired(): return lax.ppermute(value, axis, pairs)  8.25 us
    pallas_call x1, Pallas kernels, residual(): pl.pallas_call(residual_kernel, in_specs=[VMEM] * 2 + [HBM] * (3 + len(st...  4.56 us
    pallas_call x1, Pallas kernels, edge_gradient(): pl.pallas_call(edge_kernel, in_specs=[VMEM] * len(operands) + [HBM], out_...  3.82 us
    pallas_call x1, Pallas kernels, select(): pl.pallas_call(select_kernel, in_specs=[HBM] * 3, out_specs=[VMEM] * 7, o...  1.9 us
    pallas_call x1, Pallas kernels, finish(): pl.pallas_call(lambda *refs: finish_kernel(offsets, *refs), in_specs=[VME...  1.15 us
  transfers between devices with their start and end apart: 20, of which 8 were waited for; matrix products, arithmetic and copies ran while one was open for 0% of the time, Pallas kernels for 16%

profile of v8, /device:TPU:0, one launch (start us, length us, event | category | flops | bytes accessed | tf_op | source)
XLA Modules:
  0.0 54.0 jit_solution(7733376939171684883)
XLA Ops:
  0.6 1.9 %select.5 = (bf16[128,512]{1,0:T(8,128)(2,1)S(1)}, bf16[128,512]{1,0:T(8,128)(2,1)S(1)}, bf16[128,512]{1,0:T(8,128)(2,1)S(1)}, bf16[128,512]{1,0:T(8,128)(2,1)S(...) custom-call(bf16[1024,512]{1,0:T(8,128)(2,1)} %embed_ref.1, ...), custom_call_target="tpu_custom_call" | custom-call | tf_op jit(solution)/shard_map/select/pallas_call | solution.py:151
  2.5 4.0 %collective-permute-start.1 = (bf16[128,512]{1,0:T(8,128)(2,1)S(1)}, bf16[128,512]{1,0:T(8,128)(2,1)S(1)}, u32[]{:S(2)}, u32[]{:S(2)}) collective-permute-start(bf16[128,512]{1,0:T(8,128)(2,1)S(1)} %get-tuple-element.38), channel_id=1, source_target_pairs={{8,16},{16,8},{24,0},{0,24},{9,17},{17,9},{25,1},{1,25},{10,18},{1... | collective-permute-start | bytes 393224 | tf_op jit(solution)/shard_map/ppermute | solution.py:104
  6.5 2.7 %collective-permute-start.2 = (bf16[128,512]{1,0:T(8,128)(2,1)S(1)}, bf16[128,512]{1,0:T(8,128)(2,1)S(1)}, u32[]{:S(2)}, u32[]{:S(2)}) collective-permute-start(bf16[128,512]{1,0:T(8,128)(2,1)S(1)} %get-tuple-element.39), channel_id=1, source_target_pairs={{1,2},{2,1},{3,4},{4,3},{5,6},{6,5},{7,0},{0,7},{9,10},{10,9},{11,... | collective-permute-start | bytes 393224 | tf_op jit(solution)/shard_map/ppermute | solution.py:104
  9.3 0.5 %collective-permute-start.3 = (bf16[128,512]{1,0:T(8,128)(2,1)S(1)}, bf16[128,512]{1,0:T(8,128)(2,1)S(1)}, u32[]{:S(2)}, u32[]{:S(2)}) collective-permute-start(bf16[128,512]{1,0:T(8,128)(2,1)S(1)} %get-tuple-element.40), channel_id=1, source_target_pairs={{0,8},{8,0},{16,24},{24,16},{1,9},{9,1},{17,25},{25,17},{2,10},{10... | collective-permute-start | bytes 393224 | tf_op jit(solution)/shard_map/ppermute | solution.py:104
  9.8 0.0 collective-permute-start.4
  9.8 4.6 %residual.1 = (bf16[64,512]{1,0:T(8,128)(2,1)S(1)}, s32[16,1024]{1,0:T(8,128)S(1)}, s32[1,1024]{1,0:T(1,128)S(1)}, bf16[1024,512]{1,0:T(8,128)(2,1)}, bf16[1024,...) custom-call(bf16[1024,512]{1,0:T(8,128)(2,1)S(1)} %get-tuple-element.32., ...), custom_call_target="tpu_custom_call" | custom-call | flops 1610612736 | tf_op jit(solution)/shard_map/residual/pallas_call | solution.py:232
  14.4 0.0 collective-permute-done.2.g3_ref
  14.4 10.1 %triplets.1 = (f32[64,1024]{1,0:T(8,128)S(1)}, bf16[64,128]{1,0:T(8,128)(2,1)S(1)}, bf16[64,128]{1,0:T(8,128)(2,1)S(1)}, bf16[64,128]{1,0:T(8,128)(2,1)S(1)}, bf...) custom-call(f32[64,1024]{1,0:T(8,128)S(1)} %get-tuple-element.36.pre_ref, ...), custom_call_target="tpu_custom_call" | custom-call | flops 12884901888 | tf_op jit(solution)/shard_map/triplets/pallas_call | solution.py:413
  24.5 0.6 %collective-permute-start.5 = (bf16[384,128]{1,0:T(8,128)(2,1)S(1)}, bf16[384,128]{1,0:T(8,128)(2,1)S(1)}, u32[]{:S(2)}, u32[]{:S(2)}) collective-permute-start(bf16[384,128]{1,0:T(8,128)(2,1)S(1)} %get-tuple-element.46), channel_id=1, source_target_pairs={{0,1},{1,0},{2,3},{3,2},{4,5},{5,4},{6,7},{7,6},{8,9},{9,8},{10,11... | collective-permute-start | bytes 294920 | tf_op jit(solution)/shard_map/ppermute | solution.py:544
  25.1 0.1 collective-permute-start
  25.2 0.9 %collective-permute-done.5 = bf16[384,128]{1,0:T(8,128)(2,1)S(1)} collective-permute-done((bf16[384,128]{1,0:T(8,128)(2,1)S(1)}, bf16[384,128]{1,0:T(8,128)(2,1)S(1)}, u32[]{:S(2)}, u32[]{:S(2)}) %collective-permute-start.5) | collective-permute-done | bytes 98336 | tf_op jit(solution)/shard_map/ppermute | solution.py:544
  26.1 0.5 collective-permute-done
  26.6 0.1 add_convert_fusion
  26.8 1.5 %collective-permute-start.6 = (bf16[400,128]{1,0:T(8,128)(2,1)S(1)}, bf16[400,128]{1,0:T(8,128)(2,1)S(1)}, u32[]{:S(2)}, u32[]{:S(2)}) collective-permute-start(bf16[400,128]{1,0:T(8,128)(2,1)S(1)} %pad_maximum_fusion), channel_id=1, source_target_pairs={{0,24},{8,16},{16,8},{24,0},{1,25},{9,17},{17,9},{25,1},{2,26},{10... | collective-permute-start | bytes 307208 | tf_op jit(solution)/shard_map/ppermute | solution.py:544
  28.3 0.6 %collective-permute-start.8 = (bf16[400,128]{1,0:T(8,128)(2,1)S(1)}, bf16[400,128]{1,0:T(8,128)(2,1)S(1)}, u32[]{:S(2)}, u32[]{:S(2)}) collective-permute-start(bf16[400,128]{1,0:T(8,128)(2,1)S(1)} %pad_maximum_fusion.1), channel_id=1, source_target_pairs={{0,8},{8,0},{16,24},{24,16},{1,9},{9,1},{17,25},{25,17},{2,10},{10... | collective-permute-start | bytes 307208 | tf_op jit(solution)/shard_map/ppermute | solution.py:544
  28.9 1.5 %collective-permute-start.7 = (bf16[336,128]{1,0:T(8,128)(2,1)S(1)}, bf16[336,128]{1,0:T(8,128)(2,1)S(1)}, u32[]{:S(2)}, u32[]{:S(2)}) collective-permute-start(bf16[336,128]{1,0:T(8,128)(2,1)S(1)} %pad_maximum_fusion.2), channel_id=1, source_target_pairs={{0,16},{8,24},{16,0},{24,8},{1,17},{9,25},{17,1},{25,9},{2,18},{10... | collective-permute-start | bytes 258056 | tf_op jit(solution)/shard_map/ppermute | solution.py:544
  30.4 1.0 %collective-permute-start.12 = (bf16[64,128]{1,0:T(8,128)(2,1)S(1)}, bf16[64,128]{1,0:T(8,128)(2,1)S(1)}, u32[]{:S(2)}, u32[]{:S(2)}) collective-permute-start(bf16[64,128]{1,0:T(8,128)(2,1)S(1)} %get-tuple-element.50), channel_id=1, source_target_pairs={{1,2},{2,1},{3,4},{4,3},{5,6},{6,5},{7,0},{0,7},{9,10},{10,9},{11,... | collective-permute-start | bytes 49160 | tf_op jit(solution)/shard_map/ppermute | solution.py:104
  31.4 3.1 %collective-permute-done.7 = bf16[336,128]{1,0:T(8,128)(2,1)S(1)} collective-permute-done((bf16[336,128]{1,0:T(8,128)(2,1)S(1)}, bf16[336,128]{1,0:T(8,128)(2,1)S(1)}, u32[]{:S(2)}, u32[]{:S(2)}) %collective-permute-start.7) | collective-permute-done | bytes 86048 | tf_op jit(solution)/shard_map/ppermute | solution.py:544
  34.6 1.1 %collective-permute-start.10 = (bf16[336,128]{1,0:T(8,128)(2,1)S(1)}, bf16[336,128]{1,0:T(8,128)(2,1)S(1)}, u32[]{:S(2)}, u32[]{:S(2)}) collective-permute-start(bf16[336,128]{1,0:T(8,128)(2,1)S(1)} %pad_maximum_fusion.3), channel_id=1, source_target_pairs={{0,4},{1,5},{2,6},{3,7},{4,0},{5,1},{6,2},{7,3},{8,12},{9,13},{10,... | collective-permute-start | bytes 258056 | tf_op jit(solution)/shard_map/ppermute | solution.py:544
  35.7 1.6 %collective-permute-start.11 = (bf16[336,128]{1,0:T(8,128)(2,1)S(1)}, bf16[336,128]{1,0:T(8,128)(2,1)S(1)}, u32[]{:S(2)}, u32[]{:S(2)}) collective-permute-start(bf16[336,128]{1,0:T(8,128)(2,1)S(1)} %pad_maximum_fusion.3), channel_id=1, source_target_pairs={{0,2},{1,3},{2,0},{3,1},{4,6},{5,7},{6,4},{7,5},{8,10},{9,11},{10,... | collective-permute-start | bytes 258056 | tf_op jit(solution)/shard_map/ppermute | solution.py:544
  37.3 1.7 %collective-permute-start.9 = (bf16[336,128]{1,0:T(8,128)(2,1)S(1)}, bf16[336,128]{1,0:T(8,128)(2,1)S(1)}, u32[]{:S(2)}, u32[]{:S(2)}) collective-permute-start(bf16[336,128]{1,0:T(8,128)(2,1)S(1)} %pad_maximum_fusion.3), channel_id=1, source_target_pairs={{0,6},{1,7},{2,4},{3,5},{4,2},{5,3},{6,0},{7,1},{8,14},{9,15},{10,... | collective-permute-start | bytes 258056 | tf_op jit(solution)/shard_map/ppermute | solution.py:544
  39.1 3.8 %edge_gradient.1 = bf16[1024,512]{1,0:T(8,128)(2,1)} custom-call(f32[64,1024]{1,0:T(8,128)S(1)} %get-tuple-element.49.own_ref, bf16[64,128]{1,0:T(8,128)(2,1)S(1)} %slice.47.b0_ref, bf16[64,128]{1,0:T(8,128)(2,1)S(1)} %slice.48.b1_ref, bf16[64,128]{1,0:T(8,128)(2,1)S(1)} %slice.49.b2_ref, bf16[64,128]{1,0:T(8,128)(2,1)S(1)} %collective-permute-done.12.b3_ref, ...), custom_call_target="tpu_custom_call" | custom-call | flops 1207959552 | tf_op jit(solution)/shard_map/edge_gradient/pallas_call | solution.py:477
  42.9 0.9 %collective-permute-done.11 = bf16[336,128]{1,0:T(8,128)(2,1)S(1)} collective-permute-done((bf16[336,128]{1,0:T(8,128)(2,1)S(1)}, bf16[336,128]{1,0:T(8,128)(2,1)S(1)}, u32[]{:S(2)}, u32[]{:S(2)}) %collective-permute-start.11) | collective-permute-done | bytes 86048 | tf_op jit(solution)/shard_map/ppermute | solution.py:544
  43.8 0.1 add_convert_fusion.1.refs_0_
  43.8 1.6 %collective-permute-start.13 = (bf16[336,128]{1,0:T(8,128)(2,1)S(1)}, bf16[336,128]{1,0:T(8,128)(2,1)S(1)}, u32[]{:S(2)}, u32[]{:S(2)}) collective-permute-start(bf16[336,128]{1,0:T(8,128)(2,1)S(1)} %add_convert_fusion.1.refs_0_), channel_id=1, source_target_pairs={{0,8},{8,0},{16,24},{24,16},{1,9},{9,1},{17,25},{25,17},{2,10},{10... | collective-permute-start | bytes 258056 | tf_op jit(solution)/shard_map/ppermute | solution.py:544
  45.4 0.8 %collective-permute-start.14 = (bf16[336,128]{1,0:T(8,128)(2,1)S(1)}, bf16[336,128]{1,0:T(8,128)(2,1)S(1)}, u32[]{:S(2)}, u32[]{:S(2)}) collective-permute-start(bf16[336,128]{1,0:T(8,128)(2,1)S(1)} %add_convert_fusion.1.refs_0_), channel_id=1, source_target_pairs={{0,16},{8,24},{16,0},{24,8},{1,17},{9,25},{17,1},{25,9},{2,18},{10... | collective-permute-start | bytes 258056 | tf_op jit(solution)/shard_map/ppermute | solution.py:544
  46.2 1.2 %collective-permute-start.15 = (bf16[336,128]{1,0:T(8,128)(2,1)S(1)}, bf16[336,128]{1,0:T(8,128)(2,1)S(1)}, u32[]{:S(2)}, u32[]{:S(2)}) collective-permute-start(bf16[336,128]{1,0:T(8,128)(2,1)S(1)} %add_convert_fusion.1.refs_0_), channel_id=1, source_target_pairs={{0,24},{8,16},{16,8},{24,0},{1,25},{9,17},{17,9},{25,1},{2,26},{10... | collective-permute-start | bytes 258056 | tf_op jit(solution)/shard_map/ppermute | solution.py:544
  47.4 1.9 %collective-permute-done.13.refs_1_ = bf16[336,128]{1,0:T(8,128)(2,1)S(1)} collective-permute-done((bf16[336,128]{1,0:T(8,128)(2,1)S(1)}, bf16[336,128]{1,0:T(8,128)(2,1)S(1)}, u32[]{:S(2)}, u32[]{:S(2)}) %collective-permute-start.13) | collective-permute-done | bytes 86048 | tf_op jit(solution)/shard_map/ppermute | solution.py:544
  49.3 0.9 %collective-permute-done.14.refs_2_ = bf16[336,128]{1,0:T(8,128)(2,1)S(1)} collective-permute-done((bf16[336,128]{1,0:T(8,128)(2,1)S(1)}, bf16[336,128]{1,0:T(8,128)(2,1)S(1)}, u32[]{:S(2)}, u32[]{:S(2)}) %collective-permute-start.14) | collective-permute-done | bytes 86048 | tf_op jit(solution)/shard_map/ppermute | solution.py:544
  50.2 1.4 %collective-permute-done.15.refs_3_ = bf16[336,128]{1,0:T(8,128)(2,1)S(1)} collective-permute-done((bf16[336,128]{1,0:T(8,128)(2,1)S(1)}, bf16[336,128]{1,0:T(8,128)(2,1)S(1)}, u32[]{:S(2)}, u32[]{:S(2)}) %collective-permute-start.15) | collective-permute-done | bytes 86048 | tf_op jit(solution)/shard_map/ppermute | solution.py:544
  51.6 1.3 %collective-permute-done.19.refs_7_ = bf16[336,128]{1,0:T(8,128)(2,1)S(1)} collective-permute-done((bf16[336,128]{1,0:T(8,128)(2,1)S(1)}, bf16[336,128]{1,0:T(8,128)(2,1)S(1)}, u32[]{:S(2)}, u32[]{:S(2)}) %collective-permute-start.19) | collective-permute-done | bytes 86048 | tf_op jit(solution)/shard_map/ppermute | solution.py:544
  52.9 1.1 %finish.1 = (f32[512,512]{1,0:T(8,128)}, f32[64,512]{1,0:T(8,128)}, f32[64,512]{1,0:T(8,128)}, f32[16,64]{1,0:T(8,128)}) custom-call(bf16[336,128]{1,0:T(8,128)(2,1)S(1)} %add_convert_fusion.1.refs_0_, bf16[336,128]{1,0:T(8,128)(2,1)S(1)} %collective-permute-done.13.refs_1_, bf16[336,128]{1,0:T(8,128)(2,1)S(1)} %collective-permute-done.14.refs_2_, ...), custom_call_target="tpu_custom_call" | custom-call | tf_op jit(solution)/shard_map/finish/pallas_call | solution.py:524
  (27 shorter events, 0.2 us)
Async XLA Ops:
  2.5 11.8 %collective-permute-start.1 = (bf16[128,512]{1,0:T(8,128)(2,1)S(1)}, bf16[128,512]{1,0:T(8,128)(2,1)S(1)}, u32[]{:S(2)}, u32[]{:S(2)}) collective-permute-start(bf16[128,512]{1,0:T(8,128)(2,1)S(1)} %get-tuple-element.38), channel_id=1, source_target_pairs={{8,16},{16,8},{24,0},{0,24},{9,17},{17,9},{25,1},{1,25},{10,18},{1... | collective-permute-start | bytes 393224 | tf_op jit(solution)/shard_map/ppermute | solution.py:104
  6.5 7.9 %collective-permute-start.2 = (bf16[128,512]{1,0:T(8,128)(2,1)S(1)}, bf16[128,512]{1,0:T(8,128)(2,1)S(1)}, u32[]{:S(2)}, u32[]{:S(2)}) collective-permute-start(bf16[128,512]{1,0:T(8,128)(2,1)S(1)} %get-tuple-element.39), channel_id=1, source_target_pairs={{1,2},{2,1},{3,4},{4,3},{5,6},{6,5},{7,0},{0,7},{9,10},{10,9},{11,... | collective-permute-start | bytes 393224 | tf_op jit(solution)/shard_map/ppermute | solution.py:104
  9.3 5.1 %collective-permute-start.3 = (bf16[128,512]{1,0:T(8,128)(2,1)S(1)}, bf16[128,512]{1,0:T(8,128)(2,1)S(1)}, u32[]{:S(2)}, u32[]{:S(2)}) collective-permute-start(bf16[128,512]{1,0:T(8,128)(2,1)S(1)} %get-tuple-element.40), channel_id=1, source_target_pairs={{0,8},{8,0},{16,24},{24,16},{1,9},{9,1},{17,25},{25,17},{2,10},{10... | collective-permute-start | bytes 393224 | tf_op jit(solution)/shard_map/ppermute | solution.py:104
  9.8 4.6 %collective-permute-start.4 = (bf16[128,512]{1,0:T(8,128)(2,1)S(1)}, bf16[128,512]{1,0:T(8,128)(2,1)S(1)}, u32[]{:S(2)}, u32[]{:S(2)}) collective-permute-start(bf16[128,512]{1,0:T(8,128)(2,1)S(1)} %get-tuple-element.41), channel_id=1, source_target_pairs={{0,1},{1,0},{2,3},{3,2},{4,5},{5,4},{6,7},{7,6},{8,9},{9,8},{10,11... | collective-permute-start | bytes 393224 | tf_op jit(solution)/shard_map/ppermute | solution.py:104
  24.5 1.5 %collective-permute-start.5 = (bf16[384,128]{1,0:T(8,128)(2,1)S(1)}, bf16[384,128]{1,0:T(8,128)(2,1)S(1)}, u32[]{:S(2)}, u32[]{:S(2)}) collective-permute-start(bf16[384,128]{1,0:T(8,128)(2,1)S(1)} %get-tuple-element.46), channel_id=1, source_target_pairs={{0,1},{1,0},{2,3},{3,2},{4,5},{5,4},{6,7},{7,6},{8,9},{9,8},{10,11... | collective-permute-start | bytes 294920 | tf_op jit(solution)/shard_map/ppermute | solution.py:544
  25.1 1.5 %collective-permute-start = (bf16[1024,128]{1,0:T(8,128)(2,1)S(1)}, bf16[1024,128]{1,0:T(8,128)(2,1)S(1)}, u32[]{:S(2)}, u32[]{:S(2)}) collective-permute-start(bf16[1024,128]{1,0:T(8,128)(2,1)S(1)} %get-tuple-element.35), channel_id=1, source_target_pairs={{0,1},{1,0},{2,3},{3,2},{4,5},{5,4},{6,7},{7,6},{8,9},{9,8},{10,11... | collective-permute-start | bytes 786440 | tf_op jit(solution)/shard_map/ppermute | solution.py:544
  26.8 7.7 %collective-permute-start.6 = (bf16[400,128]{1,0:T(8,128)(2,1)S(1)}, bf16[400,128]{1,0:T(8,128)(2,1)S(1)}, u32[]{:S(2)}, u32[]{:S(2)}) collective-permute-start(bf16[400,128]{1,0:T(8,128)(2,1)S(1)} %pad_maximum_fusion), channel_id=1, source_target_pairs={{0,24},{8,16},{16,8},{24,0},{1,25},{9,17},{17,9},{25,1},{2,26},{10... | collective-permute-start | bytes 307208 | tf_op jit(solution)/shard_map/ppermute | solution.py:544
  28.3 6.2 %collective-permute-start.8 = (bf16[400,128]{1,0:T(8,128)(2,1)S(1)}, bf16[400,128]{1,0:T(8,128)(2,1)S(1)}, u32[]{:S(2)}, u32[]{:S(2)}) collective-permute-start(bf16[400,128]{1,0:T(8,128)(2,1)S(1)} %pad_maximum_fusion.1), channel_id=1, source_target_pairs={{0,8},{8,0},{16,24},{24,16},{1,9},{9,1},{17,25},{25,17},{2,10},{10... | collective-permute-start | bytes 307208 | tf_op jit(solution)/shard_map/ppermute | solution.py:544
  28.9 5.6 %collective-permute-start.7 = (bf16[336,128]{1,0:T(8,128)(2,1)S(1)}, bf16[336,128]{1,0:T(8,128)(2,1)S(1)}, u32[]{:S(2)}, u32[]{:S(2)}) collective-permute-start(bf16[336,128]{1,0:T(8,128)(2,1)S(1)} %pad_maximum_fusion.2), channel_id=1, source_target_pairs={{0,16},{8,24},{16,0},{24,8},{1,17},{9,25},{17,1},{25,9},{2,18},{10... | collective-permute-start | bytes 258056 | tf_op jit(solution)/shard_map/ppermute | solution.py:544
  30.4 8.7 %collective-permute-start.12 = (bf16[64,128]{1,0:T(8,128)(2,1)S(1)}, bf16[64,128]{1,0:T(8,128)(2,1)S(1)}, u32[]{:S(2)}, u32[]{:S(2)}) collective-permute-start(bf16[64,128]{1,0:T(8,128)(2,1)S(1)} %get-tuple-element.50), channel_id=1, source_target_pairs={{1,2},{2,1},{3,4},{4,3},{5,6},{6,5},{7,0},{0,7},{9,10},{10,9},{11,... | collective-permute-start | bytes 49160 | tf_op jit(solution)/shard_map/ppermute | solution.py:104
  34.6 8.3 %collective-permute-start.10 = (bf16[336,128]{1,0:T(8,128)(2,1)S(1)}, bf16[336,128]{1,0:T(8,128)(2,1)S(1)}, u32[]{:S(2)}, u32[]{:S(2)}) collective-permute-start(bf16[336,128]{1,0:T(8,128)(2,1)S(1)} %pad_maximum_fusion.3), channel_id=1, source_target_pairs={{0,4},{1,5},{2,6},{3,7},{4,0},{5,1},{6,2},{7,3},{8,12},{9,13},{10,... | collective-permute-start | bytes 258056 | tf_op jit(solution)/shard_map/ppermute | solution.py:544
  35.7 8.0 %collective-permute-start.11 = (bf16[336,128]{1,0:T(8,128)(2,1)S(1)}, bf16[336,128]{1,0:T(8,128)(2,1)S(1)}, u32[]{:S(2)}, u32[]{:S(2)}) collective-permute-start(bf16[336,128]{1,0:T(8,128)(2,1)S(1)} %pad_maximum_fusion.3), channel_id=1, source_target_pairs={{0,2},{1,3},{2,0},{3,1},{4,6},{5,7},{6,4},{7,5},{8,10},{9,11},{10,... | collective-permute-start | bytes 258056 | tf_op jit(solution)/shard_map/ppermute | solution.py:544
  37.3 6.5 %collective-permute-start.9 = (bf16[336,128]{1,0:T(8,128)(2,1)S(1)}, bf16[336,128]{1,0:T(8,128)(2,1)S(1)}, u32[]{:S(2)}, u32[]{:S(2)}) collective-permute-start(bf16[336,128]{1,0:T(8,128)(2,1)S(1)} %pad_maximum_fusion.3), channel_id=1, source_target_pairs={{0,6},{1,7},{2,4},{3,5},{4,2},{5,3},{6,0},{7,1},{8,14},{9,15},{10,... | collective-permute-start | bytes 258056 | tf_op jit(solution)/shard_map/ppermute | solution.py:544
  43.8 5.4 %collective-permute-start.13 = (bf16[336,128]{1,0:T(8,128)(2,1)S(1)}, bf16[336,128]{1,0:T(8,128)(2,1)S(1)}, u32[]{:S(2)}, u32[]{:S(2)}) collective-permute-start(bf16[336,128]{1,0:T(8,128)(2,1)S(1)} %add_convert_fusion.1.refs_0_), channel_id=1, source_target_pairs={{0,8},{8,0},{16,24},{24,16},{1,9},{9,1},{17,25},{25,17},{2,10},{10... | collective-permute-start | bytes 258056 | tf_op jit(solution)/shard_map/ppermute | solution.py:544
  45.4 4.8 %collective-permute-start.14 = (bf16[336,128]{1,0:T(8,128)(2,1)S(1)}, bf16[336,128]{1,0:T(8,128)(2,1)S(1)}, u32[]{:S(2)}, u32[]{:S(2)}) collective-permute-start(bf16[336,128]{1,0:T(8,128)(2,1)S(1)} %add_convert_fusion.1.refs_0_), channel_id=1, source_target_pairs={{0,16},{8,24},{16,0},{24,8},{1,17},{9,25},{17,1},{25,9},{2,18},{10... | collective-permute-start | bytes 258056 | tf_op jit(solution)/shard_map/ppermute | solution.py:544
  46.2 5.4 %collective-permute-start.15 = (bf16[336,128]{1,0:T(8,128)(2,1)S(1)}, bf16[336,128]{1,0:T(8,128)(2,1)S(1)}, u32[]{:S(2)}, u32[]{:S(2)}) collective-permute-start(bf16[336,128]{1,0:T(8,128)(2,1)S(1)} %add_convert_fusion.1.refs_0_), channel_id=1, source_target_pairs={{0,24},{8,16},{16,8},{24,0},{1,25},{9,17},{17,9},{25,1},{2,26},{10... | collective-permute-start | bytes 258056 | tf_op jit(solution)/shard_map/ppermute | solution.py:544
  47.4 4.2 %collective-permute-start.16 = (bf16[336,128]{1,0:T(8,128)(2,1)S(1)}, bf16[336,128]{1,0:T(8,128)(2,1)S(1)}, u32[]{:S(2)}, u32[]{:S(2)}) collective-permute-start(bf16[336,128]{1,0:T(8,128)(2,1)S(1)} %add_convert_fusion.1.refs_0_), channel_id=1, source_target_pairs={{0,1},{1,0},{2,3},{3,2},{4,5},{5,4},{6,7},{7,6},{8,9},{9,8},{10,11... | collective-permute-start | bytes 258056 | tf_op jit(solution)/shard_map/ppermute | solution.py:544
  49.2 2.3 %collective-permute-start.17 = (bf16[336,128]{1,0:T(8,128)(2,1)S(1)}, bf16[336,128]{1,0:T(8,128)(2,1)S(1)}, u32[]{:S(2)}, u32[]{:S(2)}) collective-permute-start(bf16[336,128]{1,0:T(8,128)(2,1)S(1)} %collective-permute-done.13.refs_1_), channel_id=1, source_target_pairs={{0,1},{1,0},{2,3},{3,2},{4,5},{5,4},{6,7},{7,6},{8,9},{9,8},{10,11... | collective-permute-start | bytes 258056 | tf_op jit(solution)/shard_map/ppermute | solution.py:544
  50.2 1.4 %collective-permute-start.18 = (bf16[336,128]{1,0:T(8,128)(2,1)S(1)}, bf16[336,128]{1,0:T(8,128)(2,1)S(1)}, u32[]{:S(2)}, u32[]{:S(2)}) collective-permute-start(bf16[336,128]{1,0:T(8,128)(2,1)S(1)} %collective-permute-done.14.refs_2_), channel_id=1, source_target_pairs={{0,1},{1,0},{2,3},{3,2},{4,5},{5,4},{6,7},{7,6},{8,9},{9,8},{10,11... | collective-permute-start | bytes 258056 | tf_op jit(solution)/shard_map/ppermute | solution.py:544
  51.6 1.3 %collective-permute-start.19 = (bf16[336,128]{1,0:T(8,128)(2,1)S(1)}, bf16[336,128]{1,0:T(8,128)(2,1)S(1)}, u32[]{:S(2)}, u32[]{:S(2)}) collective-permute-start(bf16[336,128]{1,0:T(8,128)(2,1)S(1)} %collective-permute-done.15.refs_3_), channel_id=1, source_target_pairs={{0,1},{1,0},{2,3},{3,2},{4,5},{5,4},{6,7},{7,6},{8,9},{9,8},{10,11... | collective-permute-start | bytes 258056 | tf_op jit(solution)/shard_map/ppermute | solution.py:544
